TPU v7x, 32 devices: a whole 2x2x4 slice. The times are simulated.
32 devices in a mesh: grp: 2 (over y), ep: 4 (over z), hd: 2 (over x), sub: 2 (over core).
Axes of the slice: x: 2, y: 2, z: 4, core: 2. Of those that a mesh axis runs over, the one named last changes fastest.
Arguments:
- queries: bfloat16 [2048, 4096], P(('grp', 'ep'), 'hd'), parts along dimension 0, may hold values from -1024 to 1024
- cache_keys: bfloat16 [2048, 512], P(('grp', 'ep', 'sub')), parts along dimension 0, may hold values from -4 to 4
- cache_values: bfloat16 [2048, 512], P(('grp', 'ep', 'sub')), parts along dimension 0, may hold values from -12 to 12
- page_len: int32 [16], P(('grp', 'ep', 'sub')), parts along dimension 0, may hold values from 1 to 128, 512 in all
- new_keys: bfloat16 [2048, 512], P(('grp', 'ep', 'sub')), parts along dimension 0, may hold values from -6 to 6
- new_values: bfloat16 [2048, 512], P(('grp', 'ep', 'sub')), parts along dimension 0, may hold values from -6 to 6
- out_proj: bfloat16 [4096, 2048], P('hd', 'sub'), may hold values from -0.09375 to 0.09375
- residual: bfloat16 [2048, 2048], P(('grp', 'ep', 'hd'), 'sub'), parts along dimension 0, may hold values from -6 to 6
- norm_gain: bfloat16 [2048], replicated, may hold values from 0.099609375 to 1.8984375
- gate_up: bfloat16 [8, 2, 384, 2048], P(('ep', 'hd'), None, 'sub'), may hold values from -0.125 to 0.125
- w_down: bfloat16 [8, 384, 2048], P(('ep', 'hd'), 'sub'), may hold values from -0.3125 to 0.3125
- expert_ids: int32 [2048, 8], P(('grp', 'ep', 'hd')), parts along dimension 0, may hold values from 0 to 7, as said below
- gates: bfloat16 [2048, 8], P(('grp', 'ep', 'hd')), parts along dimension 0, may hold values from 0.049804688 to 0.5
Outputs:
- layer_out: bfloat16 [2048, 2048], P(('grp', 'ep', 'hd'), 'sub'), parts along dimension 0
There are 2 independent parts, one for each index of `grp`. A program takes and returns all parts, laid end to end along the dimension named above; an argument that names none is the same for every part. Nothing has to cross between parts.
Inputs may be any that keep to these rules, and one draw needn't show every extreme that they name: `expert_ids`: expert x belongs to group x // 2. Each row names 8 different experts, exactly two in each of 4 different groups. Among the rows of one block b (rows b * 128 to (b + 1) * 128 - 1), each group is named by at most 128 rows and each expert by at most 128; in every block some group is named by exactly 128 rows and some expert by exactly 128.
All inputs are finite; a program needn't handle non-finite values. No bound on the sum of `page_len` on one device may be relied on, other than what follows from the above.
Results may differ from a plain program's by a relative error of at most 0.02.
Values may be sent and summed in bfloat16 or wider, within the bound.
No kernel may reach another device: no remote copies, remote signals or barrier semaphores. Data moves between devices by JAX's collectives and lax.ppermute only.
A program may use at most 64 MiB of HBM per device.

v0:
```python
import math

import jax
import jax.numpy as jnp
from jax import lax
from jax.sharding import PartitionSpec as P

QH = 32
KVH = 4
HD = 128
GROUPS_ROW = 4


NEG_FILL = -1e30
EPSILON = 1e-06
KEY_BLOCK = 1024
FAR_RANK = 1073741824


def joined(x, axis, join):
    gathered = jax.tree.map(
        lambda a, kind: lax.all_gather(a.astype(kind), axis),
        x,
        jax.tree.map(lambda a: jnp.bfloat16 if a.dtype == jnp.float32 else a.dtype, x),
    )

    def take(source):
        return jax.tree.map(
            lambda a, own: lax.dynamic_index_in_dim(a, source, 0, False).astype(own.dtype),
            gathered,
            x,
        )

    return lax.fori_loop(
        1, lax.axis_size(axis), lambda source, state: join(state, take(source)), take(0)
    )


def block_sizes(block_rows, group_total, experts_group):
    group_slots = min(block_rows, 3 * GROUPS_ROW * block_rows // (2 * group_total))
    return (group_slots, 2 * group_slots // experts_group)


def attend_block(fold_state, packed, key_rank, query_heads, row_ids, kv_heads):
    running_max, weight_sum, weighted = fold_state
    half_cols = packed.shape[1] // 2
    length = packed.shape[0]
    key_part = packed[:, :half_cols].reshape(length, kv_heads, half_cols // kv_heads)
    value_part = packed[:, half_cols:].reshape(length, kv_heads, half_cols // kv_heads)
    scores = jnp.einsum(
        "rkqd,lkd->rkql", query_heads, key_part, preferred_element_type=jnp.float32
    ) * (1.0 / math.sqrt(HD))
    allowed = (key_rank[None, :] <= row_ids[:, None])[:, None, None, :]
    masked = jnp.where(allowed, scores, NEG_FILL)
    new_max = jnp.maximum(running_max, jnp.max(masked, axis=3))
    factor = jnp.exp(running_max - new_max)
    exp_terms = jnp.where(allowed, jnp.exp(scores - new_max[..., None]), 0.0)
    weight_sum = weight_sum * factor + jnp.sum(exp_terms, axis=3)
    weighted = weighted * factor[..., None] + jnp.einsum(
        "rkql,lkd->rkqd",
        exp_terms.astype(jnp.bfloat16),
        value_part,
        preferred_element_type=jnp.float32,
    )
    return (new_max, weight_sum, weighted)


def join_parts(first_part, second_part):
    first_max, first_sum, first_weighted = first_part
    second_max, second_sum, second_weighted = second_part
    joint_max = jnp.maximum(first_max, second_max)
    first_factor = jnp.exp(first_max - joint_max)
    second_factor = jnp.exp(second_max - joint_max)
    joint_sum = first_sum * first_factor + second_sum * second_factor
    joint_weighted = (
        first_weighted * first_factor[..., None] + second_weighted * second_factor[..., None]
    )
    return (joint_max, joint_sum, joint_weighted)


def shards(
    queries,
    cache_keys,
    cache_values,
    page_len,
    new_keys,
    new_values,
    out_proj,
    residual,
    norm_gain,
    gate_up,
    w_down,
    expert_ids,
    gates,
):
    query_rows = queries.shape[0]
    heads_here = queries.shape[1] // HD
    group_width = QH // KVH
    kv_heads = max(1, heads_here // group_width)
    per_kv = heads_here // kv_heads
    kv_first = lax.axis_index("hd") * heads_here // group_width

    def kv_columns(source):
        return lax.dynamic_slice_in_dim(source, kv_first * HD, kv_heads * HD, 1)

    local_keys = jnp.concatenate([kv_columns(cache_keys), kv_columns(new_keys)], axis=0)
    local_values = jnp.concatenate([kv_columns(cache_values), kv_columns(new_values)], axis=0)
    packed_local = jnp.concatenate([local_keys, local_values], axis=1)
    cache_rows = cache_keys.shape[0]
    new_rows = new_keys.shape[0]
    cache_rank = jnp.where(
        jnp.arange(cache_rows, dtype=jnp.int32) < page_len[0], -1, FAR_RANK
    ).astype(jnp.int32)
    new_block = lax.axis_index("ep") * lax.axis_size("sub") + lax.axis_index("sub")
    new_rank = new_block * new_rows + jnp.arange(new_rows, dtype=jnp.int32)
    rank_local = jnp.concatenate([cache_rank, new_rank], axis=0)
    row_ids = lax.axis_index("ep") * query_rows + jnp.arange(query_rows, dtype=jnp.int32)
    query_heads = queries.reshape(query_rows, kv_heads, per_kv, HD)

    def fold_keys(fold_state, piece_data):
        packed, key_rank = piece_data
        length = packed.shape[0]
        if length > KEY_BLOCK and length % KEY_BLOCK == 0:
            block_count = length // KEY_BLOCK

            def scan_step(inner_state, block_data):
                return (
                    attend_block(
                        inner_state, block_data[0], block_data[1], query_heads, row_ids, kv_heads
                    ),
                    None,
                )

            fold_state, _ = lax.scan(
                scan_step,
                fold_state,
                (
                    packed.reshape(block_count, KEY_BLOCK, packed.shape[1]),
                    key_rank.reshape(block_count, KEY_BLOCK),
                ),
            )
            return fold_state
        return attend_block(fold_state, packed, key_rank, query_heads, row_ids, kv_heads)

    start_state = (
        jnp.full((query_rows, kv_heads, per_kv), NEG_FILL, jnp.float32),
        jnp.zeros((query_rows, kv_heads, per_kv), jnp.float32),
        jnp.zeros((query_rows, kv_heads, per_kv, HD), jnp.float32),
    )
    fold_state = fold_keys(
        start_state,
        (
            lax.all_gather(packed_local, "ep", axis=0, tiled=True),
            lax.all_gather(rank_local, "ep", axis=0, tiled=True),
        ),
    )
    running_max, weight_sum, weighted = joined(fold_state, "sub", join_parts)
    attended = (
        (weighted / weight_sum[..., None]).reshape(query_rows, heads_here * HD).astype(jnp.bfloat16)
    )
    projected = lax.psum_scatter(
        jnp.dot(attended, out_proj, preferred_element_type=jnp.float32).astype(jnp.bfloat16),
        "hd",
        scatter_dimension=0,
        tiled=True,
    ).astype(jnp.float32)
    hidden_half = (residual.astype(jnp.float32) + projected).astype(jnp.bfloat16)
    widened = hidden_half.astype(jnp.float32)
    features = norm_gain.shape[0]
    half_width = hidden_half.shape[1]
    square_sum = lax.psum(jnp.sum(widened * widened, axis=1), "sub")
    gain_half = lax.dynamic_slice_in_dim(
        norm_gain, lax.axis_index("sub") * half_width, half_width, 0
    )
    normed = (
        widened
        * lax.rsqrt(square_sum[:, None] / features + EPSILON)
        * gain_half.astype(jnp.float32)
    ).astype(jnp.bfloat16)
    pair_weights = gate_up[0].reshape(-1, features)
    hidden_units = w_down.shape[1]
    group_total = lax.axis_size("ep")
    group_experts = lax.axis_size("hd")
    all_experts = group_total * group_experts
    block_rows = expert_ids.shape[0]
    group_slots, expert_slots = block_sizes(block_rows, group_total, group_experts)
    chosen = (
        expert_ids[:, :, None] == jnp.arange(all_experts, dtype=jnp.int32)[None, None, :]
    ).astype(jnp.int32)
    named_count = jnp.sum(chosen, axis=1)
    earlier = jnp.cumsum(named_count, axis=0) - named_count
    slot_index = jnp.sum(chosen * earlier[:, None, :], axis=2)
    position = expert_ids * expert_slots + slot_index
    slot_columns = jnp.arange(all_experts * expert_slots, dtype=jnp.int32)
    gate_table = jnp.sum(
        jnp.where(
            position[:, :, None] == slot_columns[None, None, :],
            gates.astype(jnp.float32)[:, :, None],
            0.0,
        ),
        axis=1,
    ).astype(jnp.bfloat16)
    placed = (gate_table != 0).astype(jnp.bfloat16)
    outgoing = jnp.einsum("rq,rd->qd", placed, normed, preferred_element_type=jnp.float32).astype(
        jnp.bfloat16
    )
    outgoing = outgoing.reshape(all_experts, expert_slots, normed.shape[1])
    arrived = lax.all_to_all(outgoing, ("ep", "hd"), split_axis=0, concat_axis=0, tiled=True)
    lead_shape = arrived.shape[:-1]
    rows_in = arrived.reshape(-1, arrived.shape[-1])
    rows_in = lax.all_gather(rows_in, "sub", axis=1, tiled=True)
    projected_pair = jnp.einsum(
        "rd,fd->rf", rows_in, pair_weights, preferred_element_type=jnp.float32
    )
    activation = (
        jax.nn.silu(projected_pair[:, :hidden_units]) * projected_pair[:, hidden_units:]
    ).astype(jnp.bfloat16)
    partial_out = jnp.dot(activation, w_down[0], preferred_element_type=jnp.float32)
    expert_out = lax.psum_scatter(
        partial_out.astype(jnp.bfloat16), "sub", scatter_dimension=1, tiled=True
    )
    results = expert_out.reshape(lead_shape + (expert_out.shape[1],))
    returned = lax.all_to_all(results, ("ep", "hd"), split_axis=0, concat_axis=0, tiled=True)
    mixture = jnp.dot(
        gate_table,
        returned.reshape(all_experts * expert_slots, half_width),
        preferred_element_type=jnp.float32,
    )
    return (widened + mixture).astype(jnp.bfloat16)


def solution(mesh):
    return jax.shard_map(
        shards,
        mesh=mesh,
        in_specs=(
            P(("grp", "ep"), "hd"),
            P(("grp", "ep", "sub"), None),
            P(("grp", "ep", "sub"), None),
            P(("grp", "ep", "sub")),
            P(("grp", "ep", "sub"), None),
            P(("grp", "ep", "sub"), None),
            P("hd", "sub"),
            P(("grp", "ep", "hd"), "sub"),
            P(),
            P(("ep", "hd"), None, "sub", None),
            P(("ep", "hd"), "sub", None),
            P(("grp", "ep", "hd"), None),
            P(("grp", "ep", "hd"), None),
        ),
        out_specs=P(("grp", "ep", "hd"), "sub"),
        check_vma=False,
    )
```

profile of v0, /device:TPU:0, one launch (start us, length us, event | category | flops | bytes accessed | tf_op | source)
XLA Modules:
  0.0 255.9 jit_solution(14275604198719664992)
XLA Ops:
  6.5 1.0 constant_dynamic-slice_fusion.2
  7.7 0.1 copy.58
  7.8 0.9 constant_dynamic-slice_fusion
  8.8 0.1 copy.60
  8.9 0.7 maximum_maximum_fusion
  10.4 1.5 copy.61
  11.9 12.7 %all-gather.3 = s32[4,1,256]{2,1,0:T(1,128)S(1)} all-gather(s32[1,1,256]{2,1,0:T(1,128)S(1)} %bitcast.65), channel_id=1, replica_groups=mesh['grp'=2,'ep'=4,'hd'=2,'sub'=2] {'ep'}, dimensions={0}, use_global_device_ids=true | all-gather | bytes 5120 | tf_op jit(solution)/shard_map/all_gather | solution.py:154
  24.6 0.2 broadcast_compare_fusion
  24.8 17.9 %all-gather.8.cloned.1.call-done = bf16[1024,512]{0,1:T(8,128)(2,1)} async-done(((bf16[256,512]{0,1:T(8,128)(2,1)}), bf16[1024,512]{0,1:T(8,128)(2,1)}) %all-gather.8.cloned.1.call-update) | async-done | bytes 1048592 | tf_op jit(solution)/shard_map/all_gather | solution.py:153
  42.7 1.3 fusion.36
  44.0 7.3 %fusion = (f32[256,2,8]{0,2,1:T(8,128)S(1)}, f32[2,1024,256,8]{2,1,3,0:T(8,128)}) fusion(pred[256,1024]{0,1:T(8,128)(4,1)S(1)} %broadcast_compare_fusion, bf16[1024,2,128,1]{0,2,3,1:T(8,128)(2,1)S(1)} %bitcast.59, bf16[256,2,8,128]{3,2,1,0:T(8,128)(2,1)S(1)} %bitcast.58), kind=kOutput, calls=%fused_computation.2 | convolution fusion | flops 1086320640 | bytes 18628608 | tf_op jit(solution)/shard_map/rkqd,lkd->rkql/dot_general | solution.py:50
  51.3 9.1 %fusion.3 = f32[256,2,8]{0,2,1:T(8,128)S(1)} fusion(f32[2,1024,256,8]{2,1,3,0:T(8,128)} %get-tuple-element.37, f32[256,2,8]{0,2,1:T(8,128)S(1)} %broadcast_maximum_fusion, pred[256,1024]{0,1:T(8,128)(4,1)S(1)} %broadcast_compare_fusion), kind=kLoop, calls=%fused_computation.5 | loop fusion | flops 16773120 | bytes 17072128 | tf_op jit(solution)/shard_map/reduce_sum | solution.py:58
  60.4 10.3 %fusion.8 = bf16[256,2,8,128]{0,3,2,1:T(8,128)(2,1)} fusion(bf16[1024,2,128,1]{0,2,3,1:T(8,128)(2,1)S(1)} %bitcast.63, f32[2,1024,256,8]{2,1,3,0:T(8,128)} %get-tuple-element.37, f32[256,2,8]{0,2,1:T(8,128)S(1)} %broadcast_maximum_fusion, pred[256,1024]{0,1:T(8,128)(4,1)S(1)} %broadcast_compare_fusion, f32[256,2,8]{0,2,1:T(8,128)S(1)} %get-tuple-element.34), kind=kOutput, calls=%fused_computation.13 | convolution fusion | flops 1091567616 | bytes 18644992 | tf_op jit(solution)/shard_map/rkql,lkd->rkqd/dot_general | solution.py:59
  70.7 1.8 all-gather.2
  72.6 1.8 all-gather.1
  74.4 5.1 %all-gather.12.cloned.1.call-done = bf16[512,2,8,128]{0,3,2,1:T(8,128)(2,1)} async-done(((bf16[256,2,8,128]{0,3,2,1:T(8,128)(2,1)}), bf16[512,2,8,128]{0,3,2,1:T(8,128)(2,1)}) %all-gather.12.cloned.1.call-update) | async-done | bytes 2097168 | tf_op jit(solution)/shard_map/all_gather | solution.py:22
  79.5 2.1 divide_convert_fusion
  81.6 4.3 %convolution_convert_fusion.2 = bf16[256,1024]{1,0:T(8,128)(2,1)} fusion(bf16[256,2048]{0,1:T(8,128)(2,1)S(1)} %bitcast.61, bf16[2048,1024]{1,0:T(8,128)(2,1)} %param.19), kind=kOutput, calls=%fused_computation.16 | convolution fusion | flops 1074003968 | bytes 5767168 | tf_op jit(solution)/shard_map/dot_general | solution.py:162
  85.9 0.2 all-gather.10.cloned.1.call-start
  86.3 0.2 reduce_window_sum.11
  86.8 1.3 select_reduce_fusion
  88.2 13.7 %reduce-scatter.3.cloned.1.call-done = bf16[128,1024]{1,0:T(8,128)(2,1)} async-done(((bf16[256,1024]{1,0:T(8,128)(2,1)}), bf16[128,1024]{1,0:T(8,128)(2,1)}) %reduce-scatter.3.cloned.1.call-update) | async-done | bytes 262160 | tf_op jit(solution)/shard_map/reduce_scatter | solution.py:161
  101.8 1.1 fusion.16
  103.0 2.5 psum.7
  105.4 1.7 convolution_convert_fusion.1
  107.2 53.0 %all_to_all.10 = bf16[8,128,1024]{2,1,0:T(8,128)(2,1)} all-to-all(bf16[8,128,1024]{2,1,0:T(8,128)(2,1)S(1)} %bitcast.57), channel_id=1, replica_groups=mesh['grp'=2,'ep'=4,'hd'=2,'sub'=2] {'ep','hd'}, dimensions={0} | all-to-all | bytes 4194304 | tf_op jit(solution)/shard_map/all_to_all | solution.py:208
  160.3 12.8 %all-gather.10.cloned.1.call-done = bf16[1024,2048]{1,0:T(8,128)(2,1)} async-done(((bf16[1024,1024]{1,0:T(8,128)(2,1)}), bf16[1024,2048]{1,0:T(8,128)(2,1)}) %all-gather.10.cloned.1.call-update) | async-done | bytes 4194320 | tf_op jit(solution)/shard_map/all_gather | solution.py:211
  173.1 4.1 %fusion.37 = f32[1024,384]{0,1:T(8,128)S(1)} fusion(bf16[1024,2048]{1,0:T(8,128)(2,1)} %all-gather.10.cloned.1.call-done, bf16[384,2048]{1,0:T(8,128)(2,1)S(1)} %bitcast.54), kind=kOutput, calls=%fused_computation.69 | convolution fusion | flops 1610612736 | bytes 7340032 | tf_op jit(solution)/shard_map/rd,fd->rf/dot_general | solution.py:212
  177.2 3.2 %convolution_convert_fusion = bf16[1024,2048]{1,0:T(8,128)(2,1)} fusion(bf16[1,192,2048]{2,1,0:T(8,128)(2,1)S(1)} %copy-done.6, f32[1024,384]{0,1:T(8,128)S(1)} %fusion.37), kind=kOutput, calls=%fused_computation.11 | convolution fusion | flops 808583168 | bytes 6553600 | tf_op jit(solution)/shard_map/dot_general | solution.py:218
  180.4 13.4 %reduce-scatter.5.cloned.1.call-done = bf16[1024,1024]{1,0:T(8,128)(2,1)} async-done(((bf16[1024,2048]{1,0:T(8,128)(2,1)}), bf16[1024,1024]{1,0:T(8,128)(2,1)}) %reduce-scatter.5.cloned.1.call-update) | async-done | bytes 2097168 | tf_op jit(solution)/shard_map/reduce_scatter | solution.py:219
  193.8 54.4 %all_to_all.11 = bf16[8,128,1024]{2,1,0:T(8,128)(2,1)S(1)} all-to-all(bf16[8,128,1024]{2,1,0:T(8,128)(2,1)} %bitcast.60), channel_id=1, replica_groups=mesh['grp'=2,'ep'=4,'hd'=2,'sub'=2] {'ep','hd'}, dimensions={0} | all-to-all | bytes 4194304 | tf_op jit(solution)/shard_map/all_to_all | solution.py:223
  248.2 1.2 fusion.11
  (42 shorter events, 1.0 us)
Async XLA Ops:
  6.5 166.5 %copy-start = (bf16[1,2,192,2048]{3,2,1,0:T(8,128)(2,1)S(1)}, bf16[1,2,192,2048]{3,2,1,0:T(8,128)(2,1)}, u32[]{:S(2)}) copy-start(bf16[1,2,192,2048]{3,2,1,0:T(8,128)(2,1)} %param.22) | copy-start | bytes 4718596
  6.5 36.2 %all-gather.8.cloned.1.call-start = ((), (), s32[]{:S(2)}) async-start(), calls=%async_computation.4 | async-start | bytes 1310720 | tf_op jit(solution)/shard_map/all_gather | solution.py:153
  9.7 69.8 %all-gather.12.cloned.1.call-start = ((), (), s32[]{:S(2)}) async-start(), calls=%async_computation.8 | async-start | bytes 3145728 | tf_op jit(solution)/shard_map/all_gather | solution.py:22
  70.7 31.1 %reduce-scatter.3.cloned.1.call-start = ((), (), s32[]{:S(2)}) async-start(), calls=%async_computation.5 | async-start | bytes 786432 | tf_op jit(solution)/shard_map/reduce_scatter | solution.py:161
  81.6 4.6 %copy-start.3 = (s32[128,8]{0,1:T(8,128)S(1)}, s32[128,8]{0,1:T(8,128)}, u32[]{:S(2)}) copy-start(s32[128,8]{0,1:T(8,128)} %param.24) | copy-start | bytes 12292
  81.6 5.1 %copy-start.4 = (bf16[128,8]{0,1:T(8,128)(2,1)S(1)}, bf16[128,8]{0,1:T(8,128)(2,1)}, u32[]{:S(2)}) copy-start(bf16[128,8]{0,1:T(8,128)(2,1)} %param.25) | copy-start | bytes 6148
  81.6 5.2 %copy-start.5 = (bf16[2048]{0:T(1024)(128)(2,1)S(1)}, bf16[2048]{0:T(1024)(128)(2,1)}, u32[]{:S(2)}) copy-start(bf16[2048]{0:T(1024)(128)(2,1)} %param.21) | copy-start | bytes 12292
  81.6 20.3 %copy-start.1 = (bf16[128,1024]{1,0:T(8,128)(2,1)S(1)}, bf16[128,1024]{1,0:T(8,128)(2,1)}, u32[]{:S(2)}) copy-start(bf16[128,1024]{1,0:T(8,128)(2,1)} %param.20) | copy-start | bytes 786436
  85.9 87.2 %all-gather.10.cloned.1.call-start = ((), (), s32[]{:S(2)}) async-start(), calls=%async_computation.6 | async-start | bytes 6291456 | tf_op jit(solution)/shard_map/all_gather | solution.py:211
  160.2 33.6 %reduce-scatter.5.cloned.1.call-start = ((), (), s32[]{:S(2)}) async-start(), calls=%async_computation.7 | async-start | bytes 6291456 | tf_op jit(solution)/shard_map/reduce_scatter | solution.py:219
  173.1 4.1 %copy-start.6 = (bf16[1,192,2048]{2,1,0:T(8,128)(2,1)S(1)}, bf16[1,192,2048]{2,1,0:T(8,128)(2,1)}, u32[]{:S(2)}) copy-start(bf16[1,192,2048]{2,1,0:T(8,128)(2,1)} %param.23) | copy-start | bytes 2359300
  180.4 67.8 %copy-start.2 = (bf16[128,1024]{1,0:T(8,128)(2,1)S(1)}, bf16[128,1024]{1,0:T(8,128)(2,1)}, u32[]{:S(2)}) copy-start(bf16[128,1024]{1,0:T(8,128)(2,1)} %reduce-scatter.3.cloned.1.call-done) | copy-start | bytes 786436
Sparse Core Ops, SparseCore 0:
  9.8 32.8 all-gather.7
  70.8 8.6 all-gather.11
  86.0 15.7 reduce-scatter.2
  160.3 12.6 all-gather.9
  180.6 13.2 reduce-scatter.4
where the time goes:
time: 256 us
  blocking collectives  126 us (49%)
  waiting for transfers between devices  62.9 us (25%)
  matrix products  32.1 us (13%)
  other arithmetic  14.9 us (6%)
  between operations  14 us (5%)
  local copies, waits for them, and re-layouts  5.46 us (2%)
    all_to_all x1, blocking collectives, shards(): lax.all_to_all(results, ('ep', 'hd'), split_axis=0, concat_axis=0, tiled=...  54.4 us
    all_to_all x1, blocking collectives, shards(): lax.all_to_all(outgoing, ('ep', 'hd'), split_axis=0, concat_axis=0, tiled...  53 us
    all_gather x1, waiting for transfers between devices, shards(): lax.all_gather(packed_local, 'ep', axis=0, tiled=True)  17.9 us
    reduce_scatter x1, waiting for transfers between devices, shards(): lax.psum_scatter(jnp.dot(attended, out_proj, preferred_element_type=jnp.f...  13.7 us
    reduce_scatter x1, waiting for transfers between devices, shards(): lax.psum_scatter(partial_out.astype(jnp.bfloat16), 'sub', scatter_dimensi...  13.4 us
    all_gather x1, waiting for transfers between devices, shards(): rows_in = lax.all_gather(rows_in, 'sub', axis=1, tiled=True)  12.8 us
    all_gather x1, blocking collectives, shards(): lax.all_gather(rank_local, 'ep', axis=0, tiled=True)  12.7 us
    dot_general x1, matrix products, attend_block(): jnp.einsum('rkql,lkd->rkqd', exp_terms.astype(jnp.bfloat16), value_part,...  10.3 us
  transfers between devices with their start and end apart: 5, of which 5 were waited for; matrix products, arithmetic and copies ran while one was open for 1% of the time, Pallas kernels for 0%

commit v1 on v0

v1 whole, which is shorter than its diff:
```python
import math

import jax
import jax.numpy as jnp
from jax import lax
from jax.experimental import pallas as pl
from jax.experimental.pallas import tpu as pltpu
from jax.sharding import PartitionSpec as P

QH = 32
KVH = 4
HD = 128
GROUPS_ROW = 4
NEG_FILL = -1e30
EPSILON = 1e-06
MASK_ROWS = 16
LANES = 128
MIB = 1024 * 1024
CONTRACT_LAST = (((1,), (1,)), ((), ()))


def block_sizes(block_rows, group_total, experts_group):
    group_slots = min(block_rows, 3 * GROUPS_ROW * block_rows // (2 * group_total))
    return (group_slots, 2 * group_slots // experts_group)


def cycle(size, step=1):
    return [(i, (i + step) % size) for i in range(size)]


def sub_copies(x):
    size = lax.axis_size("sub")
    return [x] + [lax.ppermute(x, "sub", cycle(size, step)) for step in range(1, size)]


def by_sub(copies):
    size = len(copies)
    me = lax.axis_index("sub")
    ordered = []
    for target in range(size):
        value = copies[0]
        for step in range(1, size):
            value = jnp.where((me - step) % size == target, copies[step], value)
        ordered.append(value)
    return ordered


def sub_exchange(x, axis):
    size = lax.axis_size("sub")
    me = lax.axis_index("sub")
    length = x.shape[axis] // size

    def part(index):
        return lax.dynamic_slice_in_dim(x, index * length, length, axis)

    came = [part(me)]
    for step in range(1, size):
        came.append(lax.ppermute(part((me + step) % size), "sub", cycle(size, step)))
    return came


def pack_keys(cache_keys, cache_values, new_keys, new_values, page_len, kv_heads, heads_here):
    width = kv_heads * HD
    cache_rows, new_rows = cache_keys.shape[0], new_keys.shape[0]
    group_width = QH // KVH
    rows = cache_rows + new_rows + MASK_ROWS

    def kernel(page_ref, ck_ref, cv_ref, nk_ref, nv_ref, out_ref):
        first = lax.axis_index("hd") * heads_here // group_width
        columns = pl.ds(pl.multiple_of(first * HD, HD), width)
        out_ref[:cache_rows, :width] = ck_ref[:, columns]
        out_ref[:cache_rows, width:] = cv_ref[:, columns]
        out_ref[cache_rows : cache_rows + new_rows, :width] = nk_ref[:, columns]
        out_ref[cache_rows : cache_rows + new_rows, width:] = nv_ref[:, columns]
        lane = lax.broadcasted_iota(jnp.int32, (MASK_ROWS, 2 * width), 1)
        bias = jnp.where(lane < page_ref[0], 0.0, NEG_FILL)
        out_ref[cache_rows + new_rows :, :] = bias.astype(out_ref.dtype)

    vmem = pl.BlockSpec(memory_space=pltpu.VMEM)
    return pl.pallas_call(
        kernel,
        out_shape=jax.ShapeDtypeStruct((rows, 2 * width), cache_keys.dtype),
        in_specs=[pl.BlockSpec(memory_space=pltpu.SMEM)] + [vmem] * 4,
        out_specs=vmem,
        name="pack_keys",
    )(page_len, cache_keys, cache_values, new_keys, new_values)


def attend(queries, stages, state, cache_rows, kv_heads, last):
    n_hd, n_sub, rows, columns = queries.shape
    heads = columns // HD
    per_kv = heads // kv_heads
    width = kv_heads * HD
    stack = 2 if per_kv % 2 == 0 else 1
    all_rows = n_hd * rows
    hops = [hop for hop, blocks in stages for _ in blocks]
    sources = [step for _, blocks in stages for step in range(len(blocks))]
    blocks = [block for _, stage_blocks in stages for block in stage_blocks]
    new_rows = blocks[0].shape[0] - cache_rows - MASK_ROWS
    keys = cache_rows + new_rows
    factor = math.log2(math.e) / math.sqrt(HD)
    relative = n_hd == 2

    def kernel(*refs):
        q_ref, refs = refs[0], refs[1:]
        block_refs, refs = refs[: len(blocks)], refs[len(blocks) :]
        if state is not None:
            (m_in, acc_in), refs = refs[:2], refs[2:]
        sub = lax.axis_index("sub")
        ep = lax.axis_index("ep")
        hd = lax.axis_index("hd")
        places = [(hd + j) % n_hd if relative else j for j in range(n_hd)]
        biases = []
        for hop, step, block in zip(hops, sources, block_refs):
            cache_bias = block[keys : keys + 1, :cache_rows].astype(jnp.float32)
            if hop == 0:
                key_id = ((sub - step) % n_sub) * new_rows + lax.broadcasted_iota(
                    jnp.int32, (rows, new_rows), 1
                )
                row_id = lax.broadcasted_iota(jnp.int32, (rows, new_rows), 0)
                parts = [
                    jnp.where(
                        key_id <= row_id + (place * n_sub + sub) * rows, 0.0, NEG_FILL
                    )
                    for place in places
                ]
                new_bias = jnp.concatenate(parts * stack, axis=0)
                cache_bias = jnp.broadcast_to(cache_bias, (stack * all_rows, cache_rows))
            else:
                new_bias = jnp.full(
                    (1, new_rows), jnp.where(ep >= hop, 0.0, NEG_FILL), jnp.float32
                )
            biases.append(jnp.concatenate([cache_bias, new_bias], axis=1))
        ones = jnp.ones((keys, HD), jnp.bfloat16)
        for kv in range(kv_heads):
            key_parts = [block[:keys, kv * HD : (kv + 1) * HD] for block in block_refs]
            value_parts = [
                jnp.concatenate(
                    [block[:keys, width + kv * HD : width + (kv + 1) * HD], ones], axis=1
                )
                for block in block_refs
            ]
            for first in range(kv * per_kv, (kv + 1) * per_kv, stack):
                q = jnp.concatenate(
                    [
                        q_ref[place, sub, :, h * HD : (h + 1) * HD]
                        for h in range(first, first + stack)
                        for place in places
                    ],
                    axis=0,
                )
                terms = [
                    lax.dot_general(q, k, CONTRACT_LAST, preferred_element_type=jnp.float32)
                    * factor
                    + bias
                    for k, bias in zip(key_parts, biases)
                ]
                top = jnp.max(terms[0], axis=1, keepdims=True)
                for term in terms[1:]:
                    top = jnp.maximum(top, jnp.max(term, axis=1, keepdims=True))
                if state is not None:
                    top_in = m_in[first * all_rows : (first + stack) * all_rows, :]
                    top = jnp.maximum(top, top_in)[:, :1]
                acc = None
                for term, v in zip(terms, value_parts):
                    weights = jnp.exp2(term - top).astype(jnp.bfloat16)
                    product = jnp.dot(weights, v, preferred_element_type=jnp.float32)
                    acc = product if acc is None else acc + product
                if state is not None:
                    scale = jnp.exp2(top_in[:, :1] - top)
                    acc = acc + scale * acc_in[first * all_rows : (first + stack) * all_rows, :]
                if last:
                    out = (acc[:, :HD] / acc[:, HD:]).astype(jnp.bfloat16)
                    for s in range(stack):
                        refs[0][:, (first + s) * HD : (first + s + 1) * HD] = out[
                            s * all_rows : (s + 1) * all_rows
                        ]
                else:
                    refs[0][first * all_rows : (first + stack) * all_rows, :] = jnp.broadcast_to(
                        top, (stack * all_rows, LANES)
                    )
                    refs[1][first * all_rows : (first + stack) * all_rows, :] = acc

    vmem = pl.BlockSpec(memory_space=pltpu.VMEM)
    if last:
        out_shape = jax.ShapeDtypeStruct((all_rows, columns), jnp.bfloat16)
        out_specs = vmem
    else:
        out_shape = (
            jax.ShapeDtypeStruct((heads * all_rows, LANES), jnp.float32),
            jax.ShapeDtypeStruct((heads * all_rows, 2 * HD), jnp.float32),
        )
        out_specs = (vmem, vmem)
    operands = [queries] + blocks + (list(state) if state is not None else [])
    scores = all_rows * heads * keys * len(blocks)
    return pl.pallas_call(
        kernel,
        out_shape=out_shape,
        in_specs=[vmem] * len(operands),
        out_specs=out_specs,
        compiler_params=pltpu.CompilerParams(vmem_limit_bytes=24 * MIB),
        cost_estimate=pl.CostEstimate(
            flops=6 * scores * HD, bytes_accessed=4 * MIB, transcendentals=scores
        ),
        name="attend",
    )(*operands)


def apply_expert(inputs, gate_up, w_down):
    features = w_down[0].shape[1]
    hidden = w_down[0].shape[0]
    rows = sum(x.shape[0] for x in inputs)

    def kernel(*refs):
        x_refs, refs = refs[: len(inputs)], refs[len(inputs) :]
        gu_refs, refs = refs[: len(gate_up)], refs[len(gate_up) :]
        down_refs, (out_ref,) = refs[: len(w_down)], refs[len(w_down) :]
        mine = lax.axis_index("ep") * lax.axis_size("hd") + lax.axis_index("hd")
        joined = jnp.concatenate([x[...] for x in x_refs], axis=0)
        x = joined[:, :features]
        table = joined[:, features:].astype(jnp.float32)
        lane = lax.broadcasted_iota(jnp.int32, table.shape, 1)
        gate = jnp.sum(jnp.where(lane == mine, table, 0.0), axis=1, keepdims=True)
        total = None
        for gu, down in zip(gu_refs, down_refs):
            gate_part = lax.dot_general(
                x, gu[0], CONTRACT_LAST, preferred_element_type=jnp.float32
            )
            up_part = lax.dot_general(x, gu[1], CONTRACT_LAST, preferred_element_type=jnp.float32)
            activation = (gate_part / (1.0 + jnp.exp(-gate_part)) * up_part).astype(jnp.bfloat16)
            product = jnp.dot(activation, down[...], preferred_element_type=jnp.float32)
            total = product if total is None else total + product
        out_ref[...] = gate * total.astype(jnp.bfloat16).astype(jnp.float32)

    vmem = pl.BlockSpec(memory_space=pltpu.VMEM)
    operands = list(inputs) + list(gate_up) + list(w_down)
    return pl.pallas_call(
        kernel,
        out_shape=jax.ShapeDtypeStruct((rows, features), jnp.float32),
        in_specs=[vmem] * len(operands),
        out_specs=vmem,
        compiler_params=pltpu.CompilerParams(vmem_limit_bytes=24 * MIB),
        cost_estimate=pl.CostEstimate(
            flops=6 * rows * hidden * len(w_down) * features,
            bytes_accessed=6 * MIB,
            transcendentals=rows * hidden * len(w_down),
        ),
        name="apply_expert",
    )(*operands)


def chip_ring(n_ep, n_hd):
    if n_hd == 2:
        return [z * 2 for z in range(n_ep)] + [z * 2 + 1 for z in reversed(range(n_ep))]
    return list(range(n_ep * n_hd))


def dense_experts(normed, gate_table, gate_up, w_down):
    axes = ("ep", "hd")
    walk = chip_ring(lax.axis_size("ep"), lax.axis_size("hd"))
    size = len(walk)
    ahead = [(walk[i], walk[(i + 1) % size]) for i in range(size)]
    back = [(b, a) for a, b in ahead]
    rows, features = normed.shape
    half = rows // 2
    reach = size // 2
    own = jnp.concatenate([normed, gate_table], axis=1)
    from_back, from_ahead = [own], [own]
    for hop in range(1, reach + 1):
        behind, before = from_back[-1], from_ahead[-1]
        if hop == reach:
            behind, before = behind[:half], before[half:]
        from_back.append(lax.ppermute(behind, axes, ahead))
        from_ahead.append(lax.ppermute(before, axes, back))
    mine = apply_expert([own], gate_up, w_down)
    outs = []
    for hop in range(1, reach + 1):
        both = apply_expert([from_back[hop], from_ahead[hop]], gate_up, w_down)
        cut = both.shape[0] // 2
        outs.append((both[:cut], both[cut:]))
    to_back, to_ahead = outs[-1]
    for hop in range(reach - 1, -1, -1):
        to_back = lax.ppermute(to_back.astype(jnp.bfloat16), axes, back).astype(jnp.float32)
        to_ahead = lax.ppermute(to_ahead.astype(jnp.bfloat16), axes, ahead).astype(jnp.float32)
        if hop == reach - 1:
            empty = jnp.zeros((rows - half, features), jnp.float32)
            to_back = jnp.concatenate([to_back, empty], axis=0)
            to_ahead = jnp.concatenate([empty, to_ahead], axis=0)
        if hop > 0:
            to_back = to_back + outs[hop - 1][0]
            to_ahead = to_ahead + outs[hop - 1][1]
    return mine + to_back + to_ahead


def sparse_experts(widened, normed, gate_up, w_down, expert_ids, gates, features):
    half_width = normed.shape[1]
    pair_weights = gate_up[0].reshape(-1, features)
    hidden_units = w_down.shape[1]
    group_total = lax.axis_size("ep")
    group_experts = lax.axis_size("hd")
    all_experts = group_total * group_experts
    block_rows = expert_ids.shape[0]
    group_slots, expert_slots = block_sizes(block_rows, group_total, group_experts)
    chosen = (
        expert_ids[:, :, None] == jnp.arange(all_experts, dtype=jnp.int32)[None, None, :]
    ).astype(jnp.int32)
    named_count = jnp.sum(chosen, axis=1)
    earlier = jnp.cumsum(named_count, axis=0) - named_count
    slot_index = jnp.sum(chosen * earlier[:, None, :], axis=2)
    position = expert_ids * expert_slots + slot_index
    slot_columns = jnp.arange(all_experts * expert_slots, dtype=jnp.int32)
    gate_table = jnp.sum(
        jnp.where(
            position[:, :, None] == slot_columns[None, None, :],
            gates.astype(jnp.float32)[:, :, None],
            0.0,
        ),
        axis=1,
    ).astype(jnp.bfloat16)
    placed = (gate_table != 0).astype(jnp.bfloat16)
    outgoing = jnp.einsum("rq,rd->qd", placed, normed, preferred_element_type=jnp.float32).astype(
        jnp.bfloat16
    )
    outgoing = outgoing.reshape(all_experts, expert_slots, normed.shape[1])
    arrived = lax.all_to_all(outgoing, ("ep", "hd"), split_axis=0, concat_axis=0, tiled=True)
    lead_shape = arrived.shape[:-1]
    rows_in = arrived.reshape(-1, arrived.shape[-1])
    rows_in = lax.all_gather(rows_in, "sub", axis=1, tiled=True)
    projected_pair = jnp.einsum(
        "rd,fd->rf", rows_in, pair_weights, preferred_element_type=jnp.float32
    )
    activation = (
        jax.nn.silu(projected_pair[:, :hidden_units]) * projected_pair[:, hidden_units:]
    ).astype(jnp.bfloat16)
    partial_out = jnp.dot(activation, w_down[0], preferred_element_type=jnp.float32)
    expert_out = lax.psum_scatter(
        partial_out.astype(jnp.bfloat16), "sub", scatter_dimension=1, tiled=True
    )
    results = expert_out.reshape(lead_shape + (expert_out.shape[1],))
    returned = lax.all_to_all(results, ("ep", "hd"), split_axis=0, concat_axis=0, tiled=True)
    mixture = jnp.dot(
        gate_table,
        returned.reshape(all_experts * expert_slots, half_width),
        preferred_element_type=jnp.float32,
    )
    return (widened + mixture).astype(jnp.bfloat16)


def shards(
    queries,
    cache_keys,
    cache_values,
    page_len,
    new_keys,
    new_values,
    out_proj,
    residual,
    norm_gain,
    gate_up,
    w_down,
    expert_ids,
    gates,
):
    n_ep, n_hd, n_sub = lax.axis_size("ep"), lax.axis_size("hd"), lax.axis_size("sub")
    sub = lax.axis_index("sub")
    query_rows = queries.shape[0]
    heads_here = queries.shape[1] // HD
    kv_heads = max(1, heads_here // (QH // KVH))
    rows = query_rows // (n_hd * n_sub)
    features = norm_gain.shape[0]
    cache_rows = cache_keys.shape[0]
    all_experts = n_ep * n_hd * gate_up.shape[0]
    dense = (
        expert_ids.shape[1] == all_experts
        and gate_up.shape[0] == 1
        and n_ep * n_hd % 2 == 0
        and rows % 32 == 0
    )

    packed = pack_keys(
        cache_keys, cache_values, new_keys, new_values, page_len, kv_heads, heads_here
    )
    query_blocks = queries.reshape(n_hd, n_sub, rows, heads_here * HD)
    stages = [(0, sub_copies(packed))]
    travelling = packed
    for hop in range(1, n_ep):
        travelling = lax.ppermute(travelling, "ep", cycle(n_ep))
        stages.append((hop, sub_copies(travelling)))
    projections = sub_copies(out_proj)
    residual_parts = sub_exchange(residual, 0)
    if dense:
        gate_up_parts = sub_copies(gate_up[0])
        w_down_parts = sub_copies(w_down[0])
    state = None
    for index, stage in enumerate(stages):
        state = attend(
            query_blocks, [stage], state, cache_rows, kv_heads, index == len(stages) - 1
        )
    attended = state

    def project(x):
        return jnp.concatenate(
            [jnp.dot(x, w, preferred_element_type=jnp.float32) for w in projections], axis=1
        )

    if n_hd == 2:
        came = lax.ppermute(
            project(attended[rows:]).astype(jnp.bfloat16), "hd", cycle(n_hd)
        )
        projected = project(attended[:rows]) + came.astype(jnp.float32)
    else:
        projected = lax.psum_scatter(
            project(attended).astype(jnp.bfloat16), "hd", scatter_dimension=0, tiled=True
        ).astype(jnp.float32)
    residual_rows = jnp.concatenate(residual_parts, axis=1).astype(jnp.float32)
    hidden = (residual_rows + projected).astype(jnp.bfloat16)
    hidden = jnp.concatenate(by_sub(jnp.split(hidden, n_sub, axis=1)), axis=1)
    widened = hidden.astype(jnp.float32)
    square_sum = jnp.sum(widened * widened, axis=1, keepdims=True)
    normed = (
        widened * lax.rsqrt(square_sum / features + EPSILON) * norm_gain.astype(jnp.float32)
    ).astype(jnp.bfloat16)

    if not dense:
        own_columns = [
            jnp.concatenate(by_sub(sub_exchange(x, 1)), axis=0) for x in (hidden, normed)
        ]
        return sparse_experts(
            own_columns[0].astype(jnp.float32),
            own_columns[1],
            gate_up,
            w_down,
            expert_ids,
            gates,
            features,
        )
    ids_here = lax.dynamic_slice_in_dim(expert_ids, sub * rows, rows, 0)
    gates_here = lax.dynamic_slice_in_dim(gates, sub * rows, rows, 0).astype(jnp.float32)
    gate_table = jnp.sum(
        jnp.where(
            ids_here[:, :, None] == jnp.arange(LANES, dtype=jnp.int32)[None, None, :],
            gates_here[:, :, None],
            0.0,
        ),
        axis=1,
    ).astype(jnp.bfloat16)
    mixture = dense_experts(normed, gate_table, gate_up_parts, w_down_parts)
    layer_rows = (widened + mixture).astype(jnp.bfloat16)
    return jnp.concatenate(by_sub(sub_exchange(layer_rows, 1)), axis=0)


def solution(mesh):
    return jax.shard_map(
        shards,
        mesh=mesh,
        in_specs=(
            P(("grp", "ep"), "hd"),
            P(("grp", "ep", "sub"), None),
            P(("grp", "ep", "sub"), None),
            P(("grp", "ep", "sub")),
            P(("grp", "ep", "sub"), None),
            P(("grp", "ep", "sub"), None),
            P("hd", "sub"),
            P(("grp", "ep", "hd"), "sub"),
            P(),
            P(("ep", "hd"), None, "sub", None),
            P(("ep", "hd"), "sub", None),
            P(("grp", "ep", "hd"), None),
            P(("grp", "ep", "hd"), None),
        ),
        out_specs=P(("grp", "ep", "hd"), "sub"),
        check_vma=False,
    )
```

time: 256 us -> 142 us (0.55)
  blocking collectives: 126 us -> 0 us
  Pallas kernels: 0 us -> 26 us
  matrix products: 32.1 us -> 7.98 us
  starting transfers between devices: 0.35 us -> 22 us
  between operations: 14 us -> 1.08 us
  other arithmetic: 14.9 us -> 5.18 us
  waiting for transfers between devices: 62.9 us -> 69.2 us
  local copies, waits for them, and re-layouts: 5.46 us -> 10.3 us
    all_to_all x2 -> x0, blocking collectives: 107 us -> none  [the longest x1 54.4 us: shards(): lax.all_to_all(results, ('ep', 'hd'), split_axis=0, concat_axis=0, tiled=...]
    ppermute x0 -> x29, waiting for transfers between devices: none -> 69.2 us  [the longest x3 27.2 us: shards(): travelling = lax.ppermute(travelling, 'ep', cycle(n_ep))]
    all_gather x3 -> x0, waiting for transfers between devices: 35.8 us -> none  [the longest x1 17.9 us: shards(): lax.all_gather(packed_local, 'ep', axis=0, tiled=True)]
    reduce_scatter x2 -> x0, waiting for transfers between devices: 27.1 us -> none  [the longest x1 13.7 us: shards(): lax.psum_scatter(jnp.dot(attended, out_proj, preferred_element_type=jnp.f...]
    pallas_call x0 -> x10, Pallas kernels: none -> 26 us  [the longest x4 16.5 us: attend(): pl.pallas_call(kernel, out_shape=out_shape, in_specs=[vmem] * len(operand...]
    dot_general x7 -> x4, matrix products: 32.1 us -> 7.98 us  [project(): jnp.dot(x, w, preferred_element_type=jnp.float32)]
    ppermute x0 -> x29, starting transfers between devices: none -> 22 us  [the longest x4 6.92 us: dense_experts(): from_ahead.append(lax.ppermute(before, axes, back))]
    all_gather x3 -> x0, blocking collectives: 16.3 us -> none  [the longest x1 12.7 us: shards(): lax.all_gather(rank_local, 'ep', axis=0, tiled=True)]
  transfers between devices with their start and end apart: 5 -> 29, of which waited for: 5 -> 17; matrix products, arithmetic and copies ran while one was open for 1% -> 8% of each run, Pallas kernels for 0% -> 17%
where the time goes in v1:
time: 142 us
  waiting for transfers between devices  69.2 us (49%)
  Pallas kernels  26 us (18%)
  starting transfers between devices  22 us (15%)
  local copies, waits for them, and re-layouts  10.3 us (7%)
  matrix products  7.98 us (6%)
  other arithmetic  5.18 us (4%)
    ppermute x3, waiting for transfers between devices, shards(): travelling = lax.ppermute(travelling, 'ep', cycle(n_ep))  27.2 us
    ppermute x4, waiting for transfers between devices, dense_experts(): from_back.append(lax.ppermute(behind, axes, ahead))  19.6 us
    pallas_call x4, Pallas kernels, attend(): pl.pallas_call(kernel, out_shape=out_shape, in_specs=[vmem] * len(operand...  16.5 us
    ppermute x4, waiting for transfers between devices, dense_experts(): lax.ppermute(to_back.astype(jnp.bfloat16), axes, back).astype(jnp.float32)  13.4 us
    unnamed x38, local copies, waits for them, and re-layouts  8.33 us
    dot_general x4, matrix products, project(): jnp.dot(x, w, preferred_element_type=jnp.float32)  7.98 us
    pallas_call x5, Pallas kernels, apply_expert(): pl.pallas_call(kernel, out_shape=jax.ShapeDtypeStruct((rows, features), j...  7.65 us
    ppermute x4, starting transfers between devices, dense_experts(): from_ahead.append(lax.ppermute(before, axes, back))  6.92 us
  transfers between devices with their start and end apart: 29, of which 17 were waited for; matrix products, arithmetic and copies ran while one was open for 8% of the time, Pallas kernels for 17%

profile of v1, /device:TPU:0, one launch (start us, length us, event | category | flops | bytes accessed | tf_op | source)
XLA Modules:
  0.0 141.7 jit_solution(9790165965158289223)
XLA Ops:
  1.1 1.8 %pack_keys.1.refs_1_ = bf16[272,512]{1,0:T(8,128)(2,1)} custom-call(s32[1]{0:T(128)S(6)} %copy.18.page_ref, bf16[128,512]{1,0:T(8,128)(2,1)} %ck_ref.1, bf16[128,512]{1,0:T(8,128)(2,1)} %cv_ref.1, bf16[128,512]{1,0:T(8,128)(2,1)} %nk_ref.1, bf16[128,512]{1,0:T(8,128)(2,1)} %nv_ref.1), custom_call_target="tpu_custom_call" | custom-call | tf_op jit(solution)/shard_map/pack_keys/pallas_call | solution.py:80
  3.0 2.7 %collective-permute-start.1 = (bf16[272,512]{1,0:T(8,128)(2,1)}, bf16[272,512]{1,0:T(8,128)(2,1)S(1)}, u32[]{:S(2)}, u32[]{:S(2)}) collective-permute-start(bf16[272,512]{1,0:T(8,128)(2,1)} %pack_keys.1.refs_1_), channel_id=1, source_target_pairs={{0,4},{4,8},{8,12},{12,0},{1,5},{5,9},{9,13},{13,1},{2,6},{6,10},{... | collective-permute-start | bytes 835592 | tf_op jit(solution)/shard_map/ppermute | solution.py:387
  5.7 9.4 %collective-permute-done.1.refs_1_ = bf16[272,512]{1,0:T(8,128)(2,1)S(1)} collective-permute-done((bf16[272,512]{1,0:T(8,128)(2,1)}, bf16[272,512]{1,0:T(8,128)(2,1)S(1)}, u32[]{:S(2)}, u32[]{:S(2)}) %collective-permute-start.1) | collective-permute-done | bytes 278560 | tf_op jit(solution)/shard_map/ppermute | solution.py:387
  15.1 10.2 %collective-permute-done.2.refs_1_ = bf16[272,512]{1,0:T(8,128)(2,1)S(1)} collective-permute-done((bf16[272,512]{1,0:T(8,128)(2,1)S(1)}, bf16[272,512]{1,0:T(8,128)(2,1)S(1)}, u32[]{:S(2)}, u32[]{:S(2)}) %collective-permute-start.2) | collective-permute-done | bytes 278560 | tf_op jit(solution)/shard_map/ppermute | solution.py:387
  27.0 7.6 %collective-permute-done.3.refs_1_ = bf16[272,512]{1,0:T(8,128)(2,1)} collective-permute-done((bf16[272,512]{1,0:T(8,128)(2,1)S(1)}, bf16[272,512]{1,0:T(8,128)(2,1)}, u32[]{:S(2)}, u32[]{:S(2)}) %collective-permute-start.3) | collective-permute-done | bytes 278560 | tf_op jit(solution)/shard_map/ppermute | solution.py:387
  34.6 1.7 %constant_dynamic-slice_fusion.3 = (bf16[64,1024]{1,0:T(8,128)(2,1)}, bf16[64,1024]{1,0:T(8,128)(2,1)}) fusion(bf16[128,1024]{1,0:T(8,128)(2,1)} %param.20, s32[]{:T(128)S(6)} %select_n.61, s32[]{:T(128)S(6)} %select_n.63), kind=kLoop, calls=%fused_computation.44 | loop fusion | bytes 524296 | tf_op jit(solution)/shard_map/dynamic_slice | solution.py:54
  39.7 1.6 %attend.4 = (f32[2048,128]{1,0:T(8,128)S(1)}, f32[2048,256]{1,0:T(8,128)S(1)}) custom-call(bf16[2,2,64,2048]{3,2,1,0:T(8,128)(2,1)S(1)} %bitcast.19, bf16[272,512]{1,0:T(8,128)(2,1)S(1)} %copy-done.12, bf16[272,512]{1,0:T(8,128)(2,1)S(1)} %collective-permute-done.7.refs_2_), custom_call_target="tpu_custom_call" | custom-call | flops 805306368 | bytes 4194304 | tf_op jit(solution)/shard_map/attend/pallas_call | solution.py:196
  45.2 4.2 %attend.5 = (f32[2048,128]{1,0:T(8,128)S(1)}, f32[2048,256]{1,0:T(8,128)S(1)}) custom-call(bf16[2,2,64,2048]{3,2,1,0:T(8,128)(2,1)S(1)} %bitcast.20, bf16[272,512]{1,0:T(8,128)(2,1)S(1)} %copy-done.9, bf16[272,512]{1,0:T(8,128)(2,1)S(1)} %copy-done.11, f32[2048,128]{1,0:T(8,128)S(1)} %get-tuple-element.11.refs_3_, f32[2048,256]{1,0:T(8,128)S(1)} %get-tuple-element.12.refs_4_), custom_call_target="tpu_custom_call" | custom-call | flops 805306368 | bytes 4194304 | tf_op jit(solution)/shard_map/attend/pallas_call | solution.py:196
  49.5 5.4 %attend.6 = (f32[2048,128]{1,0:T(8,128)S(1)}, f32[2048,256]{1,0:T(8,128)S(1)}) custom-call(bf16[2,2,64,2048]{3,2,1,0:T(8,128)(2,1)S(1)} %bitcast.21, bf16[272,512]{1,0:T(8,128)(2,1)S(1)} %collective-permute-done.2.refs_1_, bf16[272,512]{1,0:T(8,128)(2,1)} %collective-permute-done.5.refs_2_, f32[2048,128]{1,0:T(8,128)S(1)} %get-tuple-element.13.refs_3_, ...), custom_call_target="tpu_custom_call" | custom-call | flops 805306368 | bytes 4194304 | tf_op jit(solution)/shard_map/attend/pallas_call | solution.py:196
  54.9 5.3 %attend.7 = bf16[128,2048]{1,0:T(8,128)(2,1)S(1)} custom-call(bf16[2,2,64,2048]{3,2,1,0:T(8,128)(2,1)S(1)} %bitcast.22, bf16[272,512]{1,0:T(8,128)(2,1)} %collective-permute-done.3.refs_1_, bf16[272,512]{1,0:T(8,128)(2,1)} %collective-permute-done.4.refs_2_, f32[2048,128]{1,0:T(8,128)S(1)} %get-tuple-element.15.refs_3_, ...), custom_call_target="tpu_custom_call" | custom-call | flops 805306368 | bytes 4194304 | tf_op jit(solution)/shard_map/attend/pallas_call | solution.py:196
  62.1 3.1 %convolution_convert_fusion = bf16[64,1024]{1,0:T(8,128)(2,1)S(1)} fusion(bf16[2048,1024]{1,0:T(8,128)(2,1)} %collective-permute-done.8, bf16[128,2048]{1,0:T(8,128)(2,1)S(1)} %attend.7), kind=kOutput, calls=%fused_computation | convolution fusion | flops 268500992 | bytes 4587520 | tf_op jit(solution)/shard_map/dot_general | solution.py:403
  66.4 3.0 %fusion.14 = f32[64,1024]{1,0:T(8,128)S(1)} fusion(bf16[2048,1024]{1,0:T(8,128)(2,1)} %collective-permute-done.8, bf16[128,2048]{1,0:T(8,128)(2,1)S(1)} %attend.7), kind=kOutput, calls=%fused_computation.32 | convolution fusion | flops 268435456 | bytes 4718592 | tf_op jit(solution)/shard_map/dot_general | solution.py:403
  69.5 4.5 %collective-permute-done.9 = bf16[64,2048]{1,0:T(8,128)(2,1)S(1)} collective-permute-done((bf16[64,2048]{1,0:T(8,128)(2,1)S(1)}, bf16[64,2048]{1,0:T(8,128)(2,1)S(1)}, u32[]{:S(2)}, u32[]{:S(2)}) %collective-permute-start.9) | collective-permute-done | bytes 262176 | tf_op jit(solution)/shard_map/ppermute | solution.py:407
  74.5 2.0 %collective-permute-start.16 = (bf16[64,2176]{1,0:T(8,128)(2,1)S(1)}, bf16[64,2176]{1,0:T(8,128)(2,1)S(1)}, u32[]{:S(2)}, u32[]{:S(2)}) collective-permute-start(bf16[64,2176]{1,0:T(8,128)(2,1)S(1)} %pad_maximum_fusion.refs_0_), channel_id=1, source_target_pairs={{4,0},{8,4},{12,8},{14,12},{10,14},{6,10},{2,6},{0,2},{5,1},{9,5},... | collective-permute-start | bytes 835592 | tf_op jit(solution)/shard_map/ppermute | solution.py:274
  76.6 6.2 %collective-permute-done.12.refs_0_ = bf16[64,2176]{1,0:T(8,128)(2,1)S(1)} collective-permute-done((bf16[64,2176]{1,0:T(8,128)(2,1)S(1)}, bf16[64,2176]{1,0:T(8,128)(2,1)S(1)}, u32[]{:S(2)}, u32[]{:S(2)}) %collective-permute-start.12) | collective-permute-done | bytes 278560 | tf_op jit(solution)/shard_map/ppermute | solution.py:273
  83.1 1.7 %collective-permute-start.17 = (bf16[64,2176]{1,0:T(8,128)(2,1)S(1)}, bf16[64,2176]{1,0:T(8,128)(2,1)S(1)}, u32[]{:S(2)}, u32[]{:S(2)}) collective-permute-start(bf16[64,2176]{1,0:T(8,128)(2,1)S(1)} %collective-permute-done.16.refs_1_), channel_id=1, source_target_pairs={{4,0},{8,4},{12,8},{14,12},{10,14},{6,10},{2,6},{0,2},{5,1},{9,5},... | collective-permute-start | bytes 835592 | tf_op jit(solution)/shard_map/ppermute | solution.py:274
  84.8 5.4 %collective-permute-done.13.refs_0_ = bf16[64,2176]{1,0:T(8,128)(2,1)S(1)} collective-permute-done((bf16[64,2176]{1,0:T(8,128)(2,1)S(1)}, bf16[64,2176]{1,0:T(8,128)(2,1)S(1)}, u32[]{:S(2)}, u32[]{:S(2)}) %collective-permute-start.13) | collective-permute-done | bytes 278560 | tf_op jit(solution)/shard_map/ppermute | solution.py:273
  90.8 1.4 %collective-permute-start.18 = (bf16[64,2176]{1,0:T(8,128)(2,1)S(1)}, bf16[64,2176]{1,0:T(8,128)(2,1)S(1)}, u32[]{:S(2)}, u32[]{:S(2)}) collective-permute-start(bf16[64,2176]{1,0:T(8,128)(2,1)S(1)} %collective-permute-done.17.refs_1_), channel_id=1, source_target_pairs={{4,0},{8,4},{12,8},{14,12},{10,14},{6,10},{2,6},{0,2},{5,1},{9,5},... | collective-permute-start | bytes 835592 | tf_op jit(solution)/shard_map/ppermute | solution.py:274
  92.2 5.0 %collective-permute-done.14.refs_0_ = bf16[64,2176]{1,0:T(8,128)(2,1)S(1)} collective-permute-done((bf16[64,2176]{1,0:T(8,128)(2,1)S(1)}, bf16[64,2176]{1,0:T(8,128)(2,1)S(1)}, u32[]{:S(2)}, u32[]{:S(2)}) %collective-permute-start.14) | collective-permute-done | bytes 278560 | tf_op jit(solution)/shard_map/ppermute | solution.py:273
  97.7 1.7 %collective-permute-start.19 = (bf16[32,2176]{1,0:T(8,128)(2,1)S(1)}, bf16[32,2176]{1,0:T(8,128)(2,1)S(1)}, u32[]{:S(2)}, u32[]{:S(2)}) collective-permute-start(bf16[32,2176]{1,0:T(8,128)(2,1)S(1)} %slice.53), channel_id=1, source_target_pairs={{4,0},{8,4},{12,8},{14,12},{10,14},{6,10},{2,6},{0,2},{5,1},{9,5},... | collective-permute-start | bytes 417800 | tf_op jit(solution)/shard_map/ppermute | solution.py:274
  99.4 2.9 %collective-permute-done.15.refs_0_ = bf16[32,2176]{1,0:T(8,128)(2,1)S(1)} collective-permute-done((bf16[32,2176]{1,0:T(8,128)(2,1)S(1)}, bf16[32,2176]{1,0:T(8,128)(2,1)S(1)}, u32[]{:S(2)}, u32[]{:S(2)}) %collective-permute-start.15) | collective-permute-done | bytes 139296 | tf_op jit(solution)/shard_map/ppermute | solution.py:273
  102.8 1.5 %apply_expert.6 = f32[64,2048]{1,0:T(8,128)S(1)} custom-call(bf16[32,2176]{1,0:T(8,128)(2,1)S(1)} %collective-permute-done.15.refs_0_, bf16[32,2176]{1,0:T(8,128)(2,1)S(1)} %collective-permute-done.19.refs_1_, bf16[2,192,2048]{2,1,0:T(8,128)(2,1)S(1)} %bitcast.8, bf16[2,192,2048]{2,1,0:T(8,128)(2,1)S(1)} %collective-permute-done.10.refs_2_.refs_3_, ...), custom_call_target="tpu_custom_call" | custom-call | flops 301989888 | bytes 6291456 | tf_op jit(solution)/shard_map/apply_expert/pallas_call | solution.py:237
  104.4 1.9 %collective-permute-start.20 = (bf16[32,2048]{1,0:T(8,128)(2,1)S(1)}, bf16[32,2048]{1,0:T(8,128)(2,1)S(1)}, u32[]{:S(2)}, u32[]{:S(2)}) collective-permute-start(bf16[32,2048]{1,0:T(8,128)(2,1)S(1)} %get-tuple-element.25), channel_id=1, source_target_pairs={{4,0},{8,4},{12,8},{14,12},{10,14},{6,10},{2,6},{0,2},{5,1},{9,5},... | collective-permute-start | bytes 393224 | tf_op jit(solution)/shard_map/ppermute | solution.py:283
  106.5 1.5 %apply_expert.7 = f32[128,2048]{1,0:T(8,128)S(1)} custom-call(bf16[64,2176]{1,0:T(8,128)(2,1)S(1)} %collective-permute-done.14.refs_0_, bf16[64,2176]{1,0:T(8,128)(2,1)S(1)} %collective-permute-done.18.refs_1_, bf16[2,192,2048]{2,1,0:T(8,128)(2,1)S(1)} %bitcast.9, bf16[2,192,2048]{2,1,0:T(8,128)(2,1)S(1)} %collective-permute-done.10.refs_2_.refs_3_, ...), custom_call_target="tpu_custom_call" | custom-call | flops 603979776 | bytes 6291456 | tf_op jit(solution)/shard_map/apply_expert/pallas_call | solution.py:237
  108.0 2.8 %collective-permute-done.20 = bf16[32,2048]{1,0:T(8,128)(2,1)S(1)} collective-permute-done((bf16[32,2048]{1,0:T(8,128)(2,1)S(1)}, bf16[32,2048]{1,0:T(8,128)(2,1)S(1)}, u32[]{:S(2)}, u32[]{:S(2)}) %collective-permute-start.20) | collective-permute-done | bytes 131104 | tf_op jit(solution)/shard_map/ppermute | solution.py:283
  110.8 1.8 %collective-permute-done.24 = bf16[32,2048]{1,0:T(8,128)(2,1)S(1)} collective-permute-done((bf16[32,2048]{1,0:T(8,128)(2,1)S(1)}, bf16[32,2048]{1,0:T(8,128)(2,1)S(1)}, u32[]{:S(2)}, u32[]{:S(2)}) %collective-permute-start.24) | collective-permute-done | bytes 131104 | tf_op jit(solution)/shard_map/ppermute | solution.py:284
  114.7 1.5 %apply_expert.8 = f32[128,2048]{1,0:T(8,128)S(1)} custom-call(bf16[64,2176]{1,0:T(8,128)(2,1)S(1)} %collective-permute-done.13.refs_0_, bf16[64,2176]{1,0:T(8,128)(2,1)S(1)} %collective-permute-done.17.refs_1_, bf16[2,192,2048]{2,1,0:T(8,128)(2,1)S(1)} %bitcast.10, bf16[2,192,2048]{2,1,0:T(8,128)(2,1)S(1)} %collective-permute-done.10.refs_2_.refs_3_, ...), custom_call_target="tpu_custom_call" | custom-call | flops 603979776 | bytes 6291456 | tf_op jit(solution)/shard_map/apply_expert/pallas_call | solution.py:237
  116.3 4.9 %collective-permute-done.21 = bf16[64,2048]{1,0:T(8,128)(2,1)S(1)} collective-permute-done((bf16[64,2048]{1,0:T(8,128)(2,1)S(1)}, bf16[64,2048]{1,0:T(8,128)(2,1)S(1)}, u32[]{:S(2)}, u32[]{:S(2)}) %collective-permute-start.21) | collective-permute-done | bytes 262176 | tf_op jit(solution)/shard_map/ppermute | solution.py:283
  122.2 1.5 %collective-permute-start.26 = (bf16[64,2048]{1,0:T(8,128)(2,1)S(1)}, bf16[64,2048]{1,0:T(8,128)(2,1)S(1)}, u32[]{:S(2)}, u32[]{:S(2)}) collective-permute-start(bf16[64,2048]{1,0:T(8,128)(2,1)S(1)} %get-tuple-element.20), channel_id=1, source_target_pairs={{0,4},{4,8},{8,12},{12,14},{14,10},{10,6},{6,2},{2,0},{1,5},{5,9},... | collective-permute-start | bytes 786440 | tf_op jit(solution)/shard_map/ppermute | solution.py:284
  123.7 1.6 %apply_expert.9 = f32[128,2048]{1,0:T(8,128)S(1)} custom-call(bf16[64,2176]{1,0:T(8,128)(2,1)S(1)} %collective-permute-done.12.refs_0_, bf16[64,2176]{1,0:T(8,128)(2,1)S(1)} %collective-permute-done.16.refs_1_, bf16[2,192,2048]{2,1,0:T(8,128)(2,1)S(1)} %bitcast.11, bf16[2,192,2048]{2,1,0:T(8,128)(2,1)S(1)} %collective-permute-done.10.refs_2_.refs_3_, ...), custom_call_target="tpu_custom_call" | custom-call | flops 603979776 | bytes 6291456 | tf_op jit(solution)/shard_map/apply_expert/pallas_call | solution.py:237
  125.3 4.8 %collective-permute-done.22 = bf16[64,2048]{1,0:T(8,128)(2,1)S(1)} collective-permute-done((bf16[64,2048]{1,0:T(8,128)(2,1)S(1)}, bf16[64,2048]{1,0:T(8,128)(2,1)S(1)}, u32[]{:S(2)}, u32[]{:S(2)}) %collective-permute-start.22) | collective-permute-done | bytes 262176 | tf_op jit(solution)/shard_map/ppermute | solution.py:283
  135.3 1.5 %apply_expert.5 = f32[64,2048]{1,0:T(8,128)S(1)} custom-call(bf16[64,2176]{1,0:T(8,128)(2,1)S(1)} %pad_maximum_fusion.refs_0_, bf16[2,192,2048]{2,1,0:T(8,128)(2,1)S(1)} %bitcast.12, bf16[2,192,2048]{2,1,0:T(8,128)(2,1)S(1)} %collective-permute-done.10.refs_2_.refs_3_, bf16[192,2048]{1,0:T(8,128)(2,1)S(1)} %bitcast.18, bf16[192,2048]{1,0:T(8,128)(2,1)S(1)} %copy-done.5), custom_call_target="tpu_custom_call" | custom-call | flops 301989888 | bytes 6291456 | tf_op jit(solution)/shard_map/apply_expert/pallas_call | solution.py:237
  (103 shorter events, 28.2 us)
Async XLA Ops:
  0.0 42.1 %copy-start.1 = (bf16[1,2,192,2048]{3,2,1,0:T(8,128)(2,1)S(1)}, bf16[1,2,192,2048]{3,2,1,0:T(8,128)(2,1)}, u32[]{:S(2)}) copy-start(bf16[1,2,192,2048]{3,2,1,0:T(8,128)(2,1)} %param.22) | copy-start | bytes 4718596
  0.0 62.1 %collective-permute-start.8 = (bf16[2048,1024]{1,0:T(8,128)(2,1)}, bf16[2048,1024]{1,0:T(8,128)(2,1)}, u32[]{:S(2)}, u32[]{:S(2)}) collective-permute-start(bf16[2048,1024]{1,0:T(8,128)(2,1)} %param.19), channel_id=1, source_target_pairs={{0,1},{1,0},{2,3},{3,2},{4,5},{5,4},{6,7},{7,6},{8,9},{9,8},{10,11... | collective-permute-start | bytes 12582920 | tf_op jit(solution)/shard_map/ppermute | solution.py:33
  3.0 12.1 %collective-permute-start.1 = (bf16[272,512]{1,0:T(8,128)(2,1)}, bf16[272,512]{1,0:T(8,128)(2,1)S(1)}, u32[]{:S(2)}, u32[]{:S(2)}) collective-permute-start(bf16[272,512]{1,0:T(8,128)(2,1)} %pack_keys.1.refs_1_), channel_id=1, source_target_pairs={{0,4},{4,8},{8,12},{12,0},{1,5},{5,9},{9,13},{13,1},{2,6},{6,10},{... | collective-permute-start | bytes 835592 | tf_op jit(solution)/shard_map/ppermute | solution.py:387
  15.1 10.2 %collective-permute-start.2 = (bf16[272,512]{1,0:T(8,128)(2,1)S(1)}, bf16[272,512]{1,0:T(8,128)(2,1)S(1)}, u32[]{:S(2)}, u32[]{:S(2)}) collective-permute-start(bf16[272,512]{1,0:T(8,128)(2,1)S(1)} %collective-permute-done.1.refs_1_), channel_id=1, source_target_pairs={{0,4},{4,8},{8,12},{12,0},{1,5},{5,9},{9,13},{13,1},{2,6},{6,10},{... | collective-permute-start | bytes 835592 | tf_op jit(solution)/shard_map/ppermute | solution.py:387
  15.1 21.9 %collective-permute-start.7 = (bf16[272,512]{1,0:T(8,128)(2,1)}, bf16[272,512]{1,0:T(8,128)(2,1)S(1)}, u32[]{:S(2)}, u32[]{:S(2)}) collective-permute-start(bf16[272,512]{1,0:T(8,128)(2,1)} %pack_keys.1.refs_1_), channel_id=1, source_target_pairs={{0,1},{1,0},{2,3},{3,2},{4,5},{5,4},{6,7},{7,6},{8,9},{9,8},{10,11... | collective-permute-start | bytes 835592 | tf_op jit(solution)/shard_map/ppermute | solution.py:33
  25.2 9.4 %collective-permute-start.3 = (bf16[272,512]{1,0:T(8,128)(2,1)S(1)}, bf16[272,512]{1,0:T(8,128)(2,1)}, u32[]{:S(2)}, u32[]{:S(2)}) collective-permute-start(bf16[272,512]{1,0:T(8,128)(2,1)S(1)} %collective-permute-done.2.refs_1_), channel_id=1, source_target_pairs={{0,4},{4,8},{8,12},{12,0},{1,5},{5,9},{9,13},{13,1},{2,6},{6,10},{... | collective-permute-start | bytes 835592 | tf_op jit(solution)/shard_map/ppermute | solution.py:387
  26.2 15.1 %collective-permute-start.6 = (bf16[272,512]{1,0:T(8,128)(2,1)S(1)}, bf16[272,512]{1,0:T(8,128)(2,1)S(1)}, u32[]{:S(2)}, u32[]{:S(2)}) collective-permute-start(bf16[272,512]{1,0:T(8,128)(2,1)S(1)} %collective-permute-done.1.refs_1_), channel_id=1, source_target_pairs={{0,1},{1,0},{2,3},{3,2},{4,5},{5,4},{6,7},{7,6},{8,9},{9,8},{10,11... | collective-permute-start | bytes 835592 | tf_op jit(solution)/shard_map/ppermute | solution.py:33
  26.3 23.2 %collective-permute-start.5 = (bf16[272,512]{1,0:T(8,128)(2,1)S(1)}, bf16[272,512]{1,0:T(8,128)(2,1)}, u32[]{:S(2)}, u32[]{:S(2)}) collective-permute-start(bf16[272,512]{1,0:T(8,128)(2,1)S(1)} %collective-permute-done.2.refs_1_), channel_id=1, source_target_pairs={{0,1},{1,0},{2,3},{3,2},{4,5},{5,4},{6,7},{7,6},{8,9},{9,8},{10,11... | collective-permute-start | bytes 835592 | tf_op jit(solution)/shard_map/ppermute | solution.py:33
  34.6 20.3 %collective-permute-start.4 = (bf16[272,512]{1,0:T(8,128)(2,1)}, bf16[272,512]{1,0:T(8,128)(2,1)}, u32[]{:S(2)}, u32[]{:S(2)}) collective-permute-start(bf16[272,512]{1,0:T(8,128)(2,1)} %collective-permute-done.3.refs_1_), channel_id=1, source_target_pairs={{0,1},{1,0},{2,3},{3,2},{4,5},{5,4},{6,7},{7,6},{8,9},{9,8},{10,11... | collective-permute-start | bytes 835592 | tf_op jit(solution)/shard_map/ppermute | solution.py:33
  37.0 32.4 %collective-permute-start = (bf16[64,1024]{1,0:T(8,128)(2,1)}, bf16[64,1024]{1,0:T(8,128)(2,1)S(1)}, u32[]{:S(2)}, u32[]{:S(2)}) collective-permute-start(bf16[64,1024]{1,0:T(8,128)(2,1)} %get-tuple-element.30), channel_id=1, source_target_pairs={{0,1},{1,0},{2,3},{3,2},{4,5},{5,4},{6,7},{7,6},{8,9},{9,8},{10,11... | collective-permute-start | bytes 393224 | tf_op jit(solution)/shard_map/ppermute | solution.py:58
  42.1 57.3 %collective-permute-start.10 = (bf16[2,192,2048]{2,1,0:T(8,128)(2,1)S(1)}, bf16[2,192,2048]{2,1,0:T(8,128)(2,1)S(1)}, u32[]{:S(2)}, u32[]{:S(2)}) collective-permute-start(bf16[2,192,2048]{2,1,0:T(8,128)(2,1)S(1)} %bitcast.7), channel_id=1, source_target_pairs={{0,1},{1,0},{2,3},{3,2},{4,5},{5,4},{6,7},{7,6},{8,9},{9,8},{10,11... | collective-permute-start | bytes 4718600 | tf_op jit(solution)/shard_map/ppermute | solution.py:33
  65.2 8.8 %collective-permute-start.9 = (bf16[64,2048]{1,0:T(8,128)(2,1)S(1)}, bf16[64,2048]{1,0:T(8,128)(2,1)S(1)}, u32[]{:S(2)}, u32[]{:S(2)}) collective-permute-start(bf16[64,2048]{1,0:T(8,128)(2,1)S(1)} %pad_maximum_fusion.1), channel_id=1, source_target_pairs={{0,2},{2,0},{1,3},{3,1},{4,6},{6,4},{5,7},{7,5},{8,10},{10,8},{9,1... | collective-permute-start | bytes 786440 | tf_op jit(solution)/shard_map/ppermute | solution.py:407
  74.1 28.3 %copy-start.14 = (bf16[64,1024]{1,0:T(8,128)(2,1)}, bf16[64,1024]{1,0:T(8,128)(2,1)S(1)}, u32[]{:S(2)}) copy-start(bf16[64,1024]{1,0:T(8,128)(2,1)S(1)} %get-tuple-element.27) | copy-start | bytes 393220
  74.1 28.3 %copy-start.16 = (bf16[64,1024]{1,0:T(8,128)(2,1)}, bf16[64,1024]{1,0:T(8,128)(2,1)S(1)}, u32[]{:S(2)}) copy-start(bf16[64,1024]{1,0:T(8,128)(2,1)S(1)} %get-tuple-element.28) | copy-start | bytes 393220
  74.5 8.3 %collective-permute-start.12 = (bf16[64,2176]{1,0:T(8,128)(2,1)S(1)}, bf16[64,2176]{1,0:T(8,128)(2,1)S(1)}, u32[]{:S(2)}, u32[]{:S(2)}) collective-permute-start(bf16[64,2176]{1,0:T(8,128)(2,1)S(1)} %pad_maximum_fusion.refs_0_), channel_id=1, source_target_pairs={{0,4},{4,8},{8,12},{12,14},{14,10},{10,6},{6,2},{2,0},{1,5},{5,9},... | collective-permute-start | bytes 835592 | tf_op jit(solution)/shard_map/ppermute | solution.py:273
  74.5 8.6 %collective-permute-start.16 = (bf16[64,2176]{1,0:T(8,128)(2,1)S(1)}, bf16[64,2176]{1,0:T(8,128)(2,1)S(1)}, u32[]{:S(2)}, u32[]{:S(2)}) collective-permute-start(bf16[64,2176]{1,0:T(8,128)(2,1)S(1)} %pad_maximum_fusion.refs_0_), channel_id=1, source_target_pairs={{4,0},{8,4},{12,8},{14,12},{10,14},{6,10},{2,6},{0,2},{5,1},{9,5},... | collective-permute-start | bytes 835592 | tf_op jit(solution)/shard_map/ppermute | solution.py:274
  76.6 22.9 %collective-permute-start.11 = (bf16[192,2048]{1,0:T(8,128)(2,1)S(1)}, bf16[192,2048]{1,0:T(8,128)(2,1)S(1)}, u32[]{:S(2)}, u32[]{:S(2)}) collective-permute-start(bf16[192,2048]{1,0:T(8,128)(2,1)S(1)} %bitcast.13), channel_id=1, source_target_pairs={{0,1},{1,0},{2,3},{3,2},{4,5},{5,4},{6,7},{7,6},{8,9},{9,8},{10,11... | collective-permute-start | bytes 2359304 | tf_op jit(solution)/shard_map/ppermute | solution.py:33
  82.8 7.4 %collective-permute-start.13 = (bf16[64,2176]{1,0:T(8,128)(2,1)S(1)}, bf16[64,2176]{1,0:T(8,128)(2,1)S(1)}, u32[]{:S(2)}, u32[]{:S(2)}) collective-permute-start(bf16[64,2176]{1,0:T(8,128)(2,1)S(1)} %collective-permute-done.12.refs_0_), channel_id=1, source_target_pairs={{0,4},{4,8},{8,12},{12,14},{14,10},{10,6},{6,2},{2,0},{1,5},{5,9},... | collective-permute-start | bytes 835592 | tf_op jit(solution)/shard_map/ppermute | solution.py:273
  83.1 7.7 %collective-permute-start.17 = (bf16[64,2176]{1,0:T(8,128)(2,1)S(1)}, bf16[64,2176]{1,0:T(8,128)(2,1)S(1)}, u32[]{:S(2)}, u32[]{:S(2)}) collective-permute-start(bf16[64,2176]{1,0:T(8,128)(2,1)S(1)} %collective-permute-done.16.refs_1_), channel_id=1, source_target_pairs={{4,0},{8,4},{12,8},{14,12},{10,14},{6,10},{2,6},{0,2},{5,1},{9,5},... | collective-permute-start | bytes 835592 | tf_op jit(solution)/shard_map/ppermute | solution.py:274
  90.2 7.1 %collective-permute-start.14 = (bf16[64,2176]{1,0:T(8,128)(2,1)S(1)}, bf16[64,2176]{1,0:T(8,128)(2,1)S(1)}, u32[]{:S(2)}, u32[]{:S(2)}) collective-permute-start(bf16[64,2176]{1,0:T(8,128)(2,1)S(1)} %collective-permute-done.13.refs_0_), channel_id=1, source_target_pairs={{0,4},{4,8},{8,12},{12,14},{14,10},{10,6},{6,2},{2,0},{1,5},{5,9},... | collective-permute-start | bytes 835592 | tf_op jit(solution)/shard_map/ppermute | solution.py:273
  90.8 6.9 %collective-permute-start.18 = (bf16[64,2176]{1,0:T(8,128)(2,1)S(1)}, bf16[64,2176]{1,0:T(8,128)(2,1)S(1)}, u32[]{:S(2)}, u32[]{:S(2)}) collective-permute-start(bf16[64,2176]{1,0:T(8,128)(2,1)S(1)} %collective-permute-done.17.refs_1_), channel_id=1, source_target_pairs={{4,0},{8,4},{12,8},{14,12},{10,14},{6,10},{2,6},{0,2},{5,1},{9,5},... | collective-permute-start | bytes 835592 | tf_op jit(solution)/shard_map/ppermute | solution.py:274
  97.3 5.1 %collective-permute-start.15 = (bf16[32,2176]{1,0:T(8,128)(2,1)S(1)}, bf16[32,2176]{1,0:T(8,128)(2,1)S(1)}, u32[]{:S(2)}, u32[]{:S(2)}) collective-permute-start(bf16[32,2176]{1,0:T(8,128)(2,1)S(1)} %slice.52), channel_id=1, source_target_pairs={{0,4},{4,8},{8,12},{12,14},{14,10},{10,6},{6,2},{2,0},{1,5},{5,9},... | collective-permute-start | bytes 417800 | tf_op jit(solution)/shard_map/ppermute | solution.py:273
  97.7 5.1 %collective-permute-start.19 = (bf16[32,2176]{1,0:T(8,128)(2,1)S(1)}, bf16[32,2176]{1,0:T(8,128)(2,1)S(1)}, u32[]{:S(2)}, u32[]{:S(2)}) collective-permute-start(bf16[32,2176]{1,0:T(8,128)(2,1)S(1)} %slice.53), channel_id=1, source_target_pairs={{4,0},{8,4},{12,8},{14,12},{10,14},{6,10},{2,6},{0,2},{5,1},{9,5},... | collective-permute-start | bytes 417800 | tf_op jit(solution)/shard_map/ppermute | solution.py:274
  104.4 6.4 %collective-permute-start.20 = (bf16[32,2048]{1,0:T(8,128)(2,1)S(1)}, bf16[32,2048]{1,0:T(8,128)(2,1)S(1)}, u32[]{:S(2)}, u32[]{:S(2)}) collective-permute-start(bf16[32,2048]{1,0:T(8,128)(2,1)S(1)} %get-tuple-element.25), channel_id=1, source_target_pairs={{4,0},{8,4},{12,8},{14,12},{10,14},{6,10},{2,6},{0,2},{5,1},{9,5},... | collective-permute-start | bytes 393224 | tf_op jit(solution)/shard_map/ppermute | solution.py:283
  106.2 6.4 %collective-permute-start.24 = (bf16[32,2048]{1,0:T(8,128)(2,1)S(1)}, bf16[32,2048]{1,0:T(8,128)(2,1)S(1)}, u32[]{:S(2)}, u32[]{:S(2)}) collective-permute-start(bf16[32,2048]{1,0:T(8,128)(2,1)S(1)} %get-tuple-element.26), channel_id=1, source_target_pairs={{0,4},{4,8},{8,12},{12,14},{14,10},{10,6},{6,2},{2,0},{1,5},{5,9},... | collective-permute-start | bytes 393224 | tf_op jit(solution)/shard_map/ppermute | solution.py:284
  112.7 8.6 %collective-permute-start.21 = (bf16[64,2048]{1,0:T(8,128)(2,1)S(1)}, bf16[64,2048]{1,0:T(8,128)(2,1)S(1)}, u32[]{:S(2)}, u32[]{:S(2)}) collective-permute-start(bf16[64,2048]{1,0:T(8,128)(2,1)S(1)} %get-tuple-element.21), channel_id=1, source_target_pairs={{4,0},{8,4},{12,8},{14,12},{10,14},{6,10},{2,6},{0,2},{5,1},{9,5},... | collective-permute-start | bytes 786440 | tf_op jit(solution)/shard_map/ppermute | solution.py:283
  113.6 7.9 %collective-permute-start.25 = (bf16[64,2048]{1,0:T(8,128)(2,1)S(1)}, bf16[64,2048]{1,0:T(8,128)(2,1)S(1)}, u32[]{:S(2)}, u32[]{:S(2)}) collective-permute-start(bf16[64,2048]{1,0:T(8,128)(2,1)S(1)} %get-tuple-element.22), channel_id=1, source_target_pairs={{0,4},{4,8},{8,12},{12,14},{14,10},{10,6},{6,2},{2,0},{1,5},{5,9},... | collective-permute-start | bytes 786440 | tf_op jit(solution)/shard_map/ppermute | solution.py:284
  121.7 8.4 %collective-permute-start.22 = (bf16[64,2048]{1,0:T(8,128)(2,1)S(1)}, bf16[64,2048]{1,0:T(8,128)(2,1)S(1)}, u32[]{:S(2)}, u32[]{:S(2)}) collective-permute-start(bf16[64,2048]{1,0:T(8,128)(2,1)S(1)} %get-tuple-element.19), channel_id=1, source_target_pairs={{4,0},{8,4},{12,8},{14,12},{10,14},{6,10},{2,6},{0,2},{5,1},{9,5},... | collective-permute-start | bytes 786440 | tf_op jit(solution)/shard_map/ppermute | solution.py:283
  122.2 7.9 %collective-permute-start.26 = (bf16[64,2048]{1,0:T(8,128)(2,1)S(1)}, bf16[64,2048]{1,0:T(8,128)(2,1)S(1)}, u32[]{:S(2)}, u32[]{:S(2)}) collective-permute-start(bf16[64,2048]{1,0:T(8,128)(2,1)S(1)} %get-tuple-element.20), channel_id=1, source_target_pairs={{0,4},{4,8},{8,12},{12,14},{14,10},{10,6},{6,2},{2,0},{1,5},{5,9},... | collective-permute-start | bytes 786440 | tf_op jit(solution)/shard_map/ppermute | solution.py:284
  131.0 6.7 %collective-permute-start.23 = (bf16[64,2048]{1,0:T(8,128)(2,1)}, bf16[64,2048]{1,0:T(8,128)(2,1)}, u32[]{:S(2)}, u32[]{:S(2)}) collective-permute-start(bf16[64,2048]{1,0:T(8,128)(2,1)} %get-tuple-element.17), channel_id=1, source_target_pairs={{4,0},{8,4},{12,8},{14,12},{10,14},{6,10},{2,6},{0,2},{5,1},{9,5},... | collective-permute-start | bytes 786440 | tf_op jit(solution)/shard_map/ppermute | solution.py:283
  131.6 6.7 %collective-permute-start.27 = (bf16[64,2048]{1,0:T(8,128)(2,1)}, bf16[64,2048]{1,0:T(8,128)(2,1)}, u32[]{:S(2)}, u32[]{:S(2)}) collective-permute-start(bf16[64,2048]{1,0:T(8,128)(2,1)} %get-tuple-element.18), channel_id=1, source_target_pairs={{0,4},{4,8},{8,12},{12,14},{14,10},{10,6},{6,2},{2,0},{1,5},{5,9},... | collective-permute-start | bytes 786440 | tf_op jit(solution)/shard_map/ppermute | solution.py:284
  139.5 1.4 collective-permute-start.28
  (16 other events, 124.3 us)

commit v2 on v1

--- a/solution.py
+++ b/solution.py
@@ -1,3 +1,4 @@
+import functools
 import math
 
 import jax
@@ -60,145 +61,185 @@
 
 
 def pack_keys(cache_keys, cache_values, new_keys, new_values, page_len, kv_heads, heads_here):
-    width = kv_heads * HD
     cache_rows, new_rows = cache_keys.shape[0], new_keys.shape[0]
     group_width = QH // KVH
     rows = cache_rows + new_rows + MASK_ROWS
 
-    def kernel(page_ref, ck_ref, cv_ref, nk_ref, nv_ref, out_ref):
+    def kernel(page_ref, ck_ref, cv_ref, nk_ref, nv_ref, *out_refs):
         first = lax.axis_index("hd") * heads_here // group_width
-        columns = pl.ds(pl.multiple_of(first * HD, HD), width)
-        out_ref[:cache_rows, :width] = ck_ref[:, columns]
-        out_ref[:cache_rows, width:] = cv_ref[:, columns]
-        out_ref[cache_rows : cache_rows + new_rows, :width] = nk_ref[:, columns]
-        out_ref[cache_rows : cache_rows + new_rows, width:] = nv_ref[:, columns]
-        lane = lax.broadcasted_iota(jnp.int32, (MASK_ROWS, 2 * width), 1)
-        bias = jnp.where(lane < page_ref[0], 0.0, NEG_FILL)
-        out_ref[cache_rows + new_rows :, :] = bias.astype(out_ref.dtype)
+        lane = lax.broadcasted_iota(jnp.int32, (MASK_ROWS, 2 * HD), 1)
+        bias = jnp.where(lane < page_ref[0], 0.0, NEG_FILL).astype(jnp.bfloat16)
+        for kv, out_ref in enumerate(out_refs):
+            columns = pl.ds(pl.multiple_of((first + kv) * HD, HD), HD)
+            out_ref[:cache_rows, :HD] = ck_ref[:, columns]
+            out_ref[:cache_rows, HD:] = cv_ref[:, columns]
+            out_ref[cache_rows : cache_rows + new_rows, :HD] = nk_ref[:, columns]
+            out_ref[cache_rows : cache_rows + new_rows, HD:] = nv_ref[:, columns]
+            out_ref[cache_rows + new_rows :, :] = bias
 
     vmem = pl.BlockSpec(memory_space=pltpu.VMEM)
     return pl.pallas_call(
         kernel,
-        out_shape=jax.ShapeDtypeStruct((rows, 2 * width), cache_keys.dtype),
+        out_shape=[jax.ShapeDtypeStruct((rows, 2 * HD), cache_keys.dtype)] * kv_heads,
         in_specs=[pl.BlockSpec(memory_space=pltpu.SMEM)] + [vmem] * 4,
-        out_specs=vmem,
+        out_specs=[vmem] * kv_heads,
         name="pack_keys",
     )(page_len, cache_keys, cache_values, new_keys, new_values)
 
 
-def attend(queries, stages, state, cache_rows, kv_heads, last):
+def attend(queries, kv, hop, blocks, state, cache_rows, kv_heads, finish=None):
     n_hd, n_sub, rows, columns = queries.shape
-    heads = columns // HD
-    per_kv = heads // kv_heads
-    width = kv_heads * HD
+    per_kv = columns // HD // kv_heads
     stack = 2 if per_kv % 2 == 0 else 1
     all_rows = n_hd * rows
-    hops = [hop for hop, blocks in stages for _ in blocks]
-    sources = [step for _, blocks in stages for step in range(len(blocks))]
-    blocks = [block for _, stage_blocks in stages for block in stage_blocks]
+    part = stack * all_rows
     new_rows = blocks[0].shape[0] - cache_rows - MASK_ROWS
     keys = cache_rows + new_rows
     factor = math.log2(math.e) / math.sqrt(HD)
     relative = n_hd == 2
+    last = finish is not None
+    weights, earlier = finish if last else ([], None)
+    head_columns = per_kv * HD
+    final = last and kv == kv_heads - 1
+    kept_rows = rows if relative else 0
 
     def kernel(*refs):
         q_ref, refs = refs[0], refs[1:]
         block_refs, refs = refs[: len(blocks)], refs[len(blocks) :]
         if state is not None:
             (m_in, acc_in), refs = refs[:2], refs[2:]
+        weight_refs, refs = refs[: len(weights)], refs[len(weights) :]
+        if earlier is not None:
+            earlier_ref, refs = refs[0], refs[1:]
+        if last:
+            results = 1 + (kept_rows > 0 and final)
+            result_refs, refs = refs[:results], refs[results:]
+            head_ref, refs = refs[0], refs[1:]
+            held_refs, sems = refs[: len(weights)], refs[len(weights)]
+            copies = [
+                pltpu.make_async_copy(
+                    w.at[pl.ds(kv * head_columns, head_columns), :], held, sems.at[i]
+                )
+                for i, (w, held) in enumerate(zip(weight_refs, held_refs))
+            ]
+            for copy in copies:
+                copy.start()
+        else:
+            m_out, acc_out = refs
         sub = lax.axis_index("sub")
         ep = lax.axis_index("ep")
         hd = lax.axis_index("hd")
         places = [(hd + j) % n_hd if relative else j for j in range(n_hd)]
         biases = []
-        for hop, step, block in zip(hops, sources, block_refs):
+        for step, block in enumerate(block_refs):
             cache_bias = block[keys : keys + 1, :cache_rows].astype(jnp.float32)
             if hop == 0:
                 key_id = ((sub - step) % n_sub) * new_rows + lax.broadcasted_iota(
                     jnp.int32, (rows, new_rows), 1
                 )
                 row_id = lax.broadcasted_iota(jnp.int32, (rows, new_rows), 0)
-                parts = [
+                seen = [
                     jnp.where(
                         key_id <= row_id + (place * n_sub + sub) * rows, 0.0, NEG_FILL
                     )
                     for place in places
                 ]
-                new_bias = jnp.concatenate(parts * stack, axis=0)
-                cache_bias = jnp.broadcast_to(cache_bias, (stack * all_rows, cache_rows))
+                new_bias = jnp.concatenate(seen * stack, axis=0)
+                cache_bias = jnp.broadcast_to(cache_bias, (part, cache_rows))
             else:
                 new_bias = jnp.full(
                     (1, new_rows), jnp.where(ep >= hop, 0.0, NEG_FILL), jnp.float32
                 )
             biases.append(jnp.concatenate([cache_bias, new_bias], axis=1))
         ones = jnp.ones((keys, HD), jnp.bfloat16)
-        for kv in range(kv_heads):
-            key_parts = [block[:keys, kv * HD : (kv + 1) * HD] for block in block_refs]
-            value_parts = [
-                jnp.concatenate(
-                    [block[:keys, width + kv * HD : width + (kv + 1) * HD], ones], axis=1
-                )
-                for block in block_refs
+        key_parts = [block[:keys, :HD] for block in block_refs]
+        value_parts = [
+            jnp.concatenate([block[:keys, HD:], ones], axis=1) for block in block_refs
+        ]
+        for index in range(per_kv // stack):
+            here = slice(index * part, (index + 1) * part)
+            heads = range(kv * per_kv + index * stack, kv * per_kv + (index + 1) * stack)
+            q = jnp.concatenate(
+                [q_ref[p, sub, :, h * HD : (h + 1) * HD] for h in heads for p in places], axis=0
+            )
+            terms = [
+                lax.dot_general(q, k, CONTRACT_LAST, preferred_element_type=jnp.float32) * factor
+                + bias
+                for k, bias in zip(key_parts, biases)
             ]
-            for first in range(kv * per_kv, (kv + 1) * per_kv, stack):
-                q = jnp.concatenate(
-                    [
-                        q_ref[place, sub, :, h * HD : (h + 1) * HD]
-                        for h in range(first, first + stack)
-                        for place in places
-                    ],
-                    axis=0,
-                )
-                terms = [
-                    lax.dot_general(q, k, CONTRACT_LAST, preferred_element_type=jnp.float32)
-                    * factor
-                    + bias
-                    for k, bias in zip(key_parts, biases)
-                ]
-                top = jnp.max(terms[0], axis=1, keepdims=True)
-                for term in terms[1:]:
-                    top = jnp.maximum(top, jnp.max(term, axis=1, keepdims=True))
-                if state is not None:
-                    top_in = m_in[first * all_rows : (first + stack) * all_rows, :]
-                    top = jnp.maximum(top, top_in)[:, :1]
-                acc = None
-                for term, v in zip(terms, value_parts):
-                    weights = jnp.exp2(term - top).astype(jnp.bfloat16)
-                    product = jnp.dot(weights, v, preferred_element_type=jnp.float32)
-                    acc = product if acc is None else acc + product
-                if state is not None:
-                    scale = jnp.exp2(top_in[:, :1] - top)
-                    acc = acc + scale * acc_in[first * all_rows : (first + stack) * all_rows, :]
-                if last:
-                    out = (acc[:, :HD] / acc[:, HD:]).astype(jnp.bfloat16)
-                    for s in range(stack):
-                        refs[0][:, (first + s) * HD : (first + s + 1) * HD] = out[
-                            s * all_rows : (s + 1) * all_rows
-                        ]
+            top = jnp.max(functools.reduce(jnp.maximum, terms), axis=1, keepdims=True)
+            top = jnp.broadcast_to(top, (part, LANES))
+            if state is not None:
+                top_in = m_in[here, :]
+                top = jnp.maximum(top, top_in)
+            wide_top = jnp.concatenate([top] * (keys // LANES), axis=1)
+            acc = None
+            for term, v in zip(terms, value_parts):
+                exp_terms = jnp.exp2(term - wide_top).astype(jnp.bfloat16)
+                product = jnp.dot(exp_terms, v, preferred_element_type=jnp.float32)
+                acc = product if acc is None else acc + product
+            if state is not None:
+                scale = jnp.exp2(top_in - top)
+                acc = acc + jnp.concatenate([scale, scale], axis=1) * acc_in[here, :]
+            if last:
+                out = (acc[:, :HD] / acc[:, HD:]).astype(jnp.bfloat16)
+                for s in range(stack):
+                    first = (index * stack + s) * HD
+                    head_ref[:, first : first + HD] = out[s * all_rows : (s + 1) * all_rows]
+            else:
+                m_out[here, :] = top
+                acc_out[here, :] = acc
+        if last:
+            for copy in copies:
+                copy.wait()
+            source = head_ref[...]
+            width = held_refs[0].shape[1]
+            for i, held in enumerate(held_refs):
+                here = slice(i * width, (i + 1) * width)
+                product = jnp.dot(source, held[...], preferred_element_type=jnp.float32)
+                if earlier is not None:
+                    product = product + earlier_ref[:, here]
+                if final:
+                    result_refs[-1][:, here] = product[kept_rows:].astype(jnp.bfloat16)
+                    if kept_rows:
+                        result_refs[0][:, here] = product[:kept_rows]
                 else:
-                    refs[0][first * all_rows : (first + stack) * all_rows, :] = jnp.broadcast_to(
-                        top, (stack * all_rows, LANES)
-                    )
-                    refs[1][first * all_rows : (first + stack) * all_rows, :] = acc
+                    result_refs[0][:, here] = product
 
     vmem = pl.BlockSpec(memory_space=pltpu.VMEM)
+    anywhere = pl.BlockSpec(memory_space=pl.ANY)
+    scratch = []
     if last:
-        out_shape = jax.ShapeDtypeStruct((all_rows, columns), jnp.bfloat16)
-        out_specs = vmem
+        features = sum(w.shape[1] for w in weights)
+        if final:
+            out_shape = (
+                jax.ShapeDtypeStruct((kept_rows, features), jnp.float32),
+                jax.ShapeDtypeStruct((all_rows - kept_rows, features), jnp.bfloat16),
+            )[0 if kept_rows else 1 :]
+        else:
+            out_shape = (jax.ShapeDtypeStruct((all_rows, features), jnp.float32),)
+        scratch = [pltpu.VMEM((all_rows, head_columns), jnp.bfloat16)]
+        scratch += [pltpu.VMEM((head_columns, w.shape[1]), w.dtype) for w in weights]
+        scratch += [pltpu.SemaphoreType.DMA((len(weights),))]
     else:
         out_shape = (
-            jax.ShapeDtypeStruct((heads * all_rows, LANES), jnp.float32),
-            jax.ShapeDtypeStruct((heads * all_rows, 2 * HD), jnp.float32),
+            jax.ShapeDtypeStruct((per_kv * all_rows, LANES), jnp.float32),
+            jax.ShapeDtypeStruct((per_kv * all_rows, 2 * HD), jnp.float32),
         )
-        out_specs = (vmem, vmem)
-    operands = [queries] + blocks + (list(state) if state is not None else [])
-    scores = all_rows * heads * keys * len(blocks)
+    operands = [queries] + list(blocks) + (list(state) if state is not None else [])
+    in_specs = [vmem] * len(operands) + [anywhere] * len(weights)
+    operands += list(weights)
+    if earlier is not None:
+        operands.append(earlier)
+        in_specs.append(vmem)
+    scores = all_rows * per_kv * keys * len(blocks)
     return pl.pallas_call(
         kernel,
         out_shape=out_shape,
-        in_specs=[vmem] * len(operands),
-        out_specs=out_specs,
-        compiler_params=pltpu.CompilerParams(vmem_limit_bytes=24 * MIB),
+        in_specs=in_specs,
+        out_specs=tuple(vmem for _ in out_shape),
+        scratch_shapes=scratch,
+        compiler_params=pltpu.CompilerParams(vmem_limit_bytes=16 * MIB),
         cost_estimate=pl.CostEstimate(
             flops=6 * scores * HD, bytes_accessed=4 * MIB, transcendentals=scores
         ),
@@ -239,7 +280,7 @@
         out_shape=jax.ShapeDtypeStruct((rows, features), jnp.float32),
         in_specs=[vmem] * len(operands),
         out_specs=vmem,
-        compiler_params=pltpu.CompilerParams(vmem_limit_bytes=24 * MIB),
+        compiler_params=pltpu.CompilerParams(vmem_limit_bytes=16 * MIB),
         cost_estimate=pl.CostEstimate(
             flops=6 * rows * hidden * len(w_down) * features,
             bytes_accessed=6 * MIB,
@@ -265,19 +306,20 @@
     half = rows // 2
     reach = size // 2
     own = jnp.concatenate([normed, gate_table], axis=1)
-    from_back, from_ahead = [own], [own]
+    behind, before, waiting = own, own, [own]
+    outs = []
     for hop in range(1, reach + 1):
-        behind, before = from_back[-1], from_ahead[-1]
         if hop == reach:
             behind, before = behind[:half], before[half:]
-        from_back.append(lax.ppermute(behind, axes, ahead))
-        from_ahead.append(lax.ppermute(before, axes, back))
-    mine = apply_expert([own], gate_up, w_down)
-    outs = []
-    for hop in range(1, reach + 1):
-        both = apply_expert([from_back[hop], from_ahead[hop]], gate_up, w_down)
-        cut = both.shape[0] // 2
-        outs.append((both[:cut], both[cut:]))
+        behind = lax.ppermute(behind, axes, ahead)
+        before = lax.ppermute(before, axes, back)
+        out = apply_expert(waiting, gate_up, w_down)
+        behind, before, out = lax.optimization_barrier((behind, before, out))
+        outs.append(out)
+        waiting = [behind, before]
+    outs.append(apply_expert(waiting, gate_up, w_down))
+    mine = outs[0]
+    outs = [(x[: x.shape[0] // 2], x[x.shape[0] // 2 :]) for x in outs[1:]]
     to_back, to_ahead = outs[-1]
     for hop in range(reach - 1, -1, -1):
         to_back = lax.ppermute(to_back.astype(jnp.bfloat16), axes, back).astype(jnp.float32)
@@ -381,37 +423,35 @@
         cache_keys, cache_values, new_keys, new_values, page_len, kv_heads, heads_here
     )
     query_blocks = queries.reshape(n_hd, n_sub, rows, heads_here * HD)
-    stages = [(0, sub_copies(packed))]
-    travelling = packed
-    for hop in range(1, n_ep):
-        travelling = lax.ppermute(travelling, "ep", cycle(n_ep))
-        stages.append((hop, sub_copies(travelling)))
     projections = sub_copies(out_proj)
     residual_parts = sub_exchange(residual, 0)
     if dense:
         gate_up_parts = sub_copies(gate_up[0])
         w_down_parts = sub_copies(w_down[0])
-    state = None
-    for index, stage in enumerate(stages):
-        state = attend(
-            query_blocks, [stage], state, cache_rows, kv_heads, index == len(stages) - 1
+    travelling = list(packed)
+    states = [None] * kv_heads
+    earlier = None
+    for hop in range(n_ep):
+        blocks = [sub_copies(x) for x in travelling]
+        onward = [lax.ppermute(x, "ep", cycle(n_ep)) for x in travelling] if hop < n_ep - 1 else []
+        for kv in range(kv_heads):
+            finish = (projections, earlier) if hop == n_ep - 1 else None
+            states[kv] = attend(
+                query_blocks, kv, hop, blocks[kv], states[kv], cache_rows, kv_heads, finish
+            )
+            if finish:
+                earlier = states[kv][0]
+            else:
+                onward[kv], states[kv] = lax.optimization_barrier((onward[kv], states[kv]))
+        travelling = onward
+    sent = states[-1][-1]
+    if n_hd == 2:
+        came = lax.ppermute(sent, "hd", cycle(n_hd))
+        projected = earlier + came.astype(jnp.float32)
+    else:
+        projected = lax.psum_scatter(sent, "hd", scatter_dimension=0, tiled=True).astype(
+            jnp.float32
         )
-    attended = state
-
-    def project(x):
-        return jnp.concatenate(
-            [jnp.dot(x, w, preferred_element_type=jnp.float32) for w in projections], axis=1
-        )
-
-    if n_hd == 2:
-        came = lax.ppermute(
-            project(attended[rows:]).astype(jnp.bfloat16), "hd", cycle(n_hd)
-        )
-        projected = project(attended[:rows]) + came.astype(jnp.float32)
-    else:
-        projected = lax.psum_scatter(
-            project(attended).astype(jnp.bfloat16), "hd", scatter_dimension=0, tiled=True
-        ).astype(jnp.float32)
     residual_rows = jnp.concatenate(residual_parts, axis=1).astype(jnp.float32)
     hidden = (residual_rows + projected).astype(jnp.bfloat16)
     hidden = jnp.concatenate(by_sub(jnp.split(hidden, n_sub, axis=1)), axis=1)

time: 142 us -> 124 us (0.87)
  waiting for transfers between devices: 69.2 us -> 39.8 us
  starting transfers between devices: 22 us -> 30.6 us
  matrix products: 7.98 us -> 0 us
  local copies, waits for them, and re-layouts: 10.3 us -> 16.6 us
  Pallas kernels: 26 us -> 29.7 us
    ppermute x12 -> x15, waiting for transfers between devices: 51.7 us -> 17.7 us  [the longest x4 6.89 us: dense_experts(): before = lax.ppermute(before, axes, back)]
    dot_general x4 -> x0, matrix products: 7.98 us -> none  [project(): jnp.dot(x, w, preferred_element_type=jnp.float32)]
    ppermute x12 -> x15, starting transfers between devices: 12.1 us -> 20.1 us  [the longest x6 9.69 us: shards(): lax.ppermute(x, 'ep', cycle(n_ep))]
    pallas_call x5, Pallas kernels: 7.65 us -> 13.3 us  [apply_expert(): pl.pallas_call(kernel, out_shape=jax.ShapeDtypeStruct((rows, features), j...]
    unnamed x38 -> x42, local copies, waits for them, and re-layouts: 8.33 us -> 13.4 us
    ppermute x4, waiting for transfers between devices: 13.4 us -> 16.2 us  [dense_experts(): lax.ppermute(to_back.astype(jnp.bfloat16), axes, back).astype(jnp.float32)]
    pallas_call x5 -> x9, Pallas kernels: 18.4 us -> 16.3 us  [the longest x8 14.5 us: attend(): pl.pallas_call(kernel, out_shape=out_shape, in_specs=in_specs, out_specs=...]
    ppermute x4, waiting for transfers between devices: 2.76 us -> 4.43 us  [dense_experts(): lax.ppermute(to_ahead.astype(jnp.bfloat16), axes, ahead).astype(jnp.float32)]
  transfers between devices with their start and end apart: 29 -> 36, of which waited for: 17 -> 18; matrix products, arithmetic and copies ran while one was open for 8% -> 6% of each run, Pallas kernels for 17% -> 22%
where the time goes in v2:
time: 124 us; the launch traced here: 123 us
  waiting for transfers between devices  39.8 us (32%)
  starting transfers between devices  30.6 us (25%)
  Pallas kernels  29.7 us (24%)
  local copies, waits for them, and re-layouts  16.6 us (13%)
  other arithmetic  5.22 us (4%)
    ppermute x4, waiting for transfers between devices, dense_experts(): lax.ppermute(to_back.astype(jnp.bfloat16), axes, back).astype(jnp.float32)  16.2 us
    pallas_call x8, Pallas kernels, attend(): pl.pallas_call(kernel, out_shape=out_shape, in_specs=in_specs, out_specs=...  14.5 us
    unnamed x42, local copies, waits for them, and re-layouts  13.4 us
    pallas_call x5, Pallas kernels, apply_expert(): pl.pallas_call(kernel, out_shape=jax.ShapeDtypeStruct((rows, features), j...  13.3 us
    ppermute x6, starting transfers between devices, shards(): lax.ppermute(x, 'ep', cycle(n_ep))  9.69 us
    ppermute x4, waiting for transfers between devices, dense_experts(): before = lax.ppermute(before, axes, back)  6.89 us
    ppermute x4, starting transfers between devices, dense_experts(): behind = lax.ppermute(behind, axes, ahead)  6.75 us
    ppermute x4, waiting for transfers between devices, dense_experts(): behind = lax.ppermute(behind, axes, ahead)  5.62 us
  transfers between devices with their start and end apart: 36, of which 18 were waited for; matrix products, arithmetic and copies ran while one was open for 6% of the time, Pallas kernels for 22%

profile of v2, /device:TPU:0, one launch (start us, length us, event | category | flops | bytes accessed | tf_op | source)
XLA Modules:
  0.0 122.9 jit_solution(3772212672938357067)
XLA Ops:
  1.1 1.8 %pack_keys.1 = (bf16[272,256]{1,0:T(8,128)(2,1)}, bf16[272,256]{1,0:T(8,128)(2,1)}) custom-call(s32[1]{0:T(128)S(6)} %copy.18.page_ref, bf16[128,512]{1,0:T(8,128)(2,1)} %ck_ref.1, bf16[128,512]{1,0:T(8,128)(2,1)} %cv_ref.1, bf16[128,512]{1,0:T(8,128)(2,1)} %nk_ref.1, bf16[128,512]{1,0:T(8,128)(2,1)} %nv_ref.1), custom_call_target="tpu_custom_call" | custom-call | tf_op jit(solution)/shard_map/pack_keys/pallas_call | solution.py:81
  3.0 3.0 %collective-permute-start.9 = (bf16[272,256]{1,0:T(8,128)(2,1)}, bf16[272,256]{1,0:T(8,128)(2,1)S(1)}, u32[]{:S(2)}, u32[]{:S(2)}) collective-permute-start(bf16[272,256]{1,0:T(8,128)(2,1)} %get-tuple-element.67.refs_1_), channel_id=1, source_target_pairs={{0,4},{4,8},{8,12},{12,0},{1,5},{5,9},{9,13},{13,1},{2,6},{6,10},{... | collective-permute-start | bytes 417800 | tf_op jit(solution)/shard_map/ppermute | solution.py:436
  6.0 1.6 %collective-permute-start.1 = (bf16[272,256]{1,0:T(8,128)(2,1)}, bf16[272,256]{1,0:T(8,128)(2,1)S(1)}, u32[]{:S(2)}, u32[]{:S(2)}) collective-permute-start(bf16[272,256]{1,0:T(8,128)(2,1)} %get-tuple-element.51.refs_1_), channel_id=1, source_target_pairs={{0,4},{4,8},{8,12},{12,0},{1,5},{5,9},{9,13},{13,1},{2,6},{6,10},{... | collective-permute-start | bytes 417800 | tf_op jit(solution)/shard_map/ppermute | solution.py:436
  10.8 2.0 %collective-permute-done.9.refs_1_ = bf16[272,256]{1,0:T(8,128)(2,1)S(1)} collective-permute-done((bf16[272,256]{1,0:T(8,128)(2,1)}, bf16[272,256]{1,0:T(8,128)(2,1)S(1)}, u32[]{:S(2)}, u32[]{:S(2)}) %collective-permute-start.9) | collective-permute-done | bytes 139296 | tf_op jit(solution)/shard_map/ppermute | solution.py:436
  16.0 1.6 %collective-permute-start.3 = (bf16[272,256]{1,0:T(8,128)(2,1)S(1)}, bf16[272,256]{1,0:T(8,128)(2,1)}, u32[]{:S(2)}, u32[]{:S(2)}) collective-permute-start(bf16[272,256]{1,0:T(8,128)(2,1)S(1)} %collective-permute-done.1.refs_1_), channel_id=1, source_target_pairs={{0,4},{4,8},{8,12},{12,0},{1,5},{5,9},{9,13},{13,1},{2,6},{6,10},{... | collective-permute-start | bytes 417800 | tf_op jit(solution)/shard_map/ppermute | solution.py:436
  27.7 2.5 %attend.13 = (f32[1024,128]{1,0:T(8,128)S(1)}, f32[1024,256]{1,0:T(8,128)S(1)}) custom-call(bf16[2,2,64,2048]{3,2,1,0:T(8,128)(2,1)S(1)} %bitcast.13, bf16[272,256]{1,0:T(8,128)(2,1)} %collective-permute-done.11.refs_1_, bf16[272,256]{1,0:T(8,128)(2,1)} %collective-permute-done.14.refs_2_, f32[1024,128]{1,0:T(8,128)S(1)} %get-tuple-element.76.refs_3_, ...), custom_call_target="tpu_custom_call" | custom-call | flops 402653184 | bytes 4194304 | tf_op jit(solution)/shard_map/attend/pallas_call | solution.py:236
  32.7 2.0 %attend.10 = (f32[1024,128]{1,0:T(8,128)S(1)}, f32[1024,256]{1,0:T(8,128)S(1)}) custom-call(bf16[2,2,64,2048]{3,2,1,0:T(8,128)(2,1)S(1)} %bitcast.14, bf16[272,256]{1,0:T(8,128)(2,1)} %collective-permute-done.3.refs_1_, bf16[272,256]{1,0:T(8,128)(2,1)} %collective-permute-done.6.refs_2_, f32[1024,128]{1,0:T(8,128)S(1)} %copy-done.17, f32[1024,256]{1,0:T(8,128)S(1)} %copy-done.14), custom_call_target="tpu_custom_call" | custom-call | flops 402653184 | bytes 4194304 | tf_op jit(solution)/shard_map/attend/pallas_call | solution.py:236
  35.2 1.7 %constant_dynamic-slice_fusion.3 = (bf16[64,1024]{1,0:T(8,128)(2,1)}, bf16[64,1024]{1,0:T(8,128)(2,1)}) fusion(bf16[128,1024]{1,0:T(8,128)(2,1)} %param.20, s32[]{:T(128)S(6)} %select_n.61, s32[]{:T(128)S(6)} %select_n.63), kind=kLoop, calls=%fused_computation.27 | loop fusion | bytes 524296 | tf_op jit(solution)/shard_map/dynamic_slice | solution.py:55
  37.5 2.5 %attend.14.refs_7_ = f32[128,2048]{1,0:T(8,128)S(1)} custom-call(bf16[2,2,64,2048]{3,2,1,0:T(8,128)(2,1)S(1)} %bitcast.15, bf16[272,256]{1,0:T(8,128)(2,1)S(1)} %collective-permute-done.13.refs_1_, bf16[272,256]{1,0:T(8,128)(2,1)S(1)} %collective-permute-done.15.refs_2_, f32[1024,128]{1,0:T(8,128)S(1)} %get-tuple-element.81.refs_3_, ...), custom_call_target="tpu_custom_call" | custom-call | flops 402653184 | bytes 4194304 | tf_op jit(solution)/shard_map/attend/pallas_call | solution.py:236
  40.1 3.3 %attend.15 = (f32[64,2048]{1,0:T(8,128)S(1)}, bf16[64,2048]{1,0:T(8,128)(2,1)}) custom-call(bf16[2,2,64,2048]{3,2,1,0:T(8,128)(2,1)S(1)} %bitcast.16, bf16[272,256]{1,0:T(8,128)(2,1)S(1)} %collective-permute-done.5.refs_1_, bf16[272,256]{1,0:T(8,128)(2,1)S(1)} %collective-permute-done.7.refs_2_, f32[1024,128]{1,0:T(8,128)S(1)} %get-tuple-element.65.refs_3_, ...), custom_call_target="tpu_custom_call" | custom-call | flops 402653184 | bytes 4194304 | tf_op jit(solution)/shard_map/attend/pallas_call | solution.py:236
  44.2 1.7 %collective-permute-start.16 = (bf16[64,2048]{1,0:T(8,128)(2,1)}, bf16[64,2048]{1,0:T(8,128)(2,1)S(1)}, u32[]{:S(2)}, u32[]{:S(2)}) collective-permute-start(bf16[64,2048]{1,0:T(8,128)(2,1)} %get-tuple-element.84), channel_id=1, source_target_pairs={{0,2},{2,0},{1,3},{3,1},{4,6},{6,4},{5,7},{7,5},{8,10},{10,8},{9,1... | collective-permute-start | bytes 786440 | tf_op jit(solution)/shard_map/ppermute | solution.py:449
  49.8 3.2 %collective-permute-done.16 = bf16[64,2048]{1,0:T(8,128)(2,1)S(1)} collective-permute-done((bf16[64,2048]{1,0:T(8,128)(2,1)}, bf16[64,2048]{1,0:T(8,128)(2,1)S(1)}, u32[]{:S(2)}, u32[]{:S(2)}) %collective-permute-start.16) | collective-permute-done | bytes 262176 | tf_op jit(solution)/shard_map/ppermute | solution.py:449
  57.9 2.6 %apply_expert.5 = f32[64,2048]{1,0:T(8,128)S(1)} custom-call(bf16[64,2176]{1,0:T(8,128)(2,1)S(1)} %pad_maximum_fusion.refs_0_, bf16[2,192,2048]{2,1,0:T(8,128)(2,1)S(1)} %bitcast.4, bf16[2,192,2048]{2,1,0:T(8,128)(2,1)S(1)} %collective-permute-done.19.refs_2_.refs_3_, bf16[192,2048]{1,0:T(8,128)(2,1)S(1)} %bitcast.18, ...), custom_call_target="tpu_custom_call" | custom-call | flops 301989888 | bytes 6291456 | tf_op jit(solution)/shard_map/apply_expert/pallas_call | solution.py:278
  61.3 1.6 %collective-permute-done.17.refs_0_ = bf16[64,2176]{1,0:T(8,128)(2,1)S(1)} collective-permute-done((bf16[64,2176]{1,0:T(8,128)(2,1)S(1)}, bf16[64,2176]{1,0:T(8,128)(2,1)S(1)}, u32[]{:S(2)}, u32[]{:S(2)}) %collective-permute-start.17) | collective-permute-done | bytes 278560 | tf_op jit(solution)/shard_map/ppermute | solution.py:314
  65.6 2.7 %apply_expert.6 = f32[128,2048]{1,0:T(8,128)S(1)} custom-call(bf16[64,2176]{1,0:T(8,128)(2,1)S(1)} %collective-permute-done.17.refs_0_, bf16[64,2176]{1,0:T(8,128)(2,1)S(1)} %collective-permute-done.18.refs_1_, bf16[2,192,2048]{2,1,0:T(8,128)(2,1)S(1)} %bitcast.5, bf16[2,192,2048]{2,1,0:T(8,128)(2,1)S(1)} %collective-permute-done.19.refs_2_.refs_3_, ...), custom_call_target="tpu_custom_call" | custom-call | flops 603979776 | bytes 6291456 | tf_op jit(solution)/shard_map/apply_expert/pallas_call | solution.py:278
  68.3 2.2 %collective-permute-done.21.refs_0_ = bf16[64,2176]{1,0:T(8,128)(2,1)S(1)} collective-permute-done((bf16[64,2176]{1,0:T(8,128)(2,1)S(1)}, bf16[64,2176]{1,0:T(8,128)(2,1)S(1)}, u32[]{:S(2)}, u32[]{:S(2)}) %collective-permute-start.21) | collective-permute-done | bytes 278560 | tf_op jit(solution)/shard_map/ppermute | solution.py:314
  71.8 1.6 %collective-permute-start.23 = (bf16[64,2176]{1,0:T(8,128)(2,1)S(1)}, bf16[64,2176]{1,0:T(8,128)(2,1)S(1)}, u32[]{:S(2)}, u32[]{:S(2)}) collective-permute-start(bf16[64,2176]{1,0:T(8,128)(2,1)S(1)} %collective-permute-done.21.refs_0_), channel_id=1, source_target_pairs={{0,4},{4,8},{8,12},{12,14},{14,10},{10,6},{6,2},{2,0},{1,5},{5,9},... | collective-permute-start | bytes 835592 | tf_op jit(solution)/shard_map/ppermute | solution.py:314
  73.8 2.7 %apply_expert.7 = f32[128,2048]{1,0:T(8,128)S(1)} custom-call(bf16[64,2176]{1,0:T(8,128)(2,1)S(1)} %collective-permute-done.21.refs_0_, bf16[64,2176]{1,0:T(8,128)(2,1)S(1)} %collective-permute-done.22.refs_1_, bf16[2,192,2048]{2,1,0:T(8,128)(2,1)S(1)} %bitcast.6, bf16[2,192,2048]{2,1,0:T(8,128)(2,1)S(1)} %collective-permute-done.19.refs_2_.refs_3_, ...), custom_call_target="tpu_custom_call" | custom-call | flops 603979776 | bytes 6291456 | tf_op jit(solution)/shard_map/apply_expert/pallas_call | solution.py:278
  76.5 1.8 %collective-permute-done.23.refs_0_ = bf16[64,2176]{1,0:T(8,128)(2,1)S(1)} collective-permute-done((bf16[64,2176]{1,0:T(8,128)(2,1)S(1)}, bf16[64,2176]{1,0:T(8,128)(2,1)S(1)}, u32[]{:S(2)}, u32[]{:S(2)}) %collective-permute-start.23) | collective-permute-done | bytes 278560 | tf_op jit(solution)/shard_map/ppermute | solution.py:314
  78.3 1.6 %collective-permute-done.24.refs_1_ = bf16[64,2176]{1,0:T(8,128)(2,1)S(1)} collective-permute-done((bf16[64,2176]{1,0:T(8,128)(2,1)S(1)}, bf16[64,2176]{1,0:T(8,128)(2,1)S(1)}, u32[]{:S(2)}, u32[]{:S(2)}) %collective-permute-start.24) | collective-permute-done | bytes 278560 | tf_op jit(solution)/shard_map/ppermute | solution.py:315
  79.9 2.5 %collective-permute-start.25 = (bf16[32,2176]{1,0:T(8,128)(2,1)S(1)}, bf16[32,2176]{1,0:T(8,128)(2,1)S(1)}, u32[]{:S(2)}, u32[]{:S(2)}) collective-permute-start(bf16[32,2176]{1,0:T(8,128)(2,1)S(1)} %slice.32), channel_id=1, source_target_pairs={{0,4},{4,8},{8,12},{12,14},{14,10},{10,6},{6,2},{2,0},{1,5},{5,9},... | collective-permute-start | bytes 417800 | tf_op jit(solution)/shard_map/ppermute | solution.py:314
  82.5 2.7 %apply_expert.8 = f32[128,2048]{1,0:T(8,128)S(1)} custom-call(bf16[64,2176]{1,0:T(8,128)(2,1)S(1)} %collective-permute-done.23.refs_0_, bf16[64,2176]{1,0:T(8,128)(2,1)S(1)} %collective-permute-done.24.refs_1_, bf16[2,192,2048]{2,1,0:T(8,128)(2,1)S(1)} %bitcast.7, bf16[2,192,2048]{2,1,0:T(8,128)(2,1)S(1)} %collective-permute-done.19.refs_2_.refs_3_, ...), custom_call_target="tpu_custom_call" | custom-call | flops 603979776 | bytes 6291456 | tf_op jit(solution)/shard_map/apply_expert/pallas_call | solution.py:278
  85.2 3.3 %collective-permute-done.26.refs_1_ = bf16[32,2176]{1,0:T(8,128)(2,1)S(1)} collective-permute-done((bf16[32,2176]{1,0:T(8,128)(2,1)S(1)}, bf16[32,2176]{1,0:T(8,128)(2,1)S(1)}, u32[]{:S(2)}, u32[]{:S(2)}) %collective-permute-start.26) | collective-permute-done | bytes 139296 | tf_op jit(solution)/shard_map/ppermute | solution.py:315
  88.5 2.6 %apply_expert.9 = f32[64,2048]{1,0:T(8,128)S(1)} custom-call(bf16[32,2176]{1,0:T(8,128)(2,1)S(1)} %collective-permute-done.25.refs_0_, bf16[32,2176]{1,0:T(8,128)(2,1)S(1)} %collective-permute-done.26.refs_1_, bf16[2,192,2048]{2,1,0:T(8,128)(2,1)S(1)} %bitcast.8, bf16[2,192,2048]{2,1,0:T(8,128)(2,1)S(1)} %collective-permute-done.19.refs_2_.refs_3_, ...), custom_call_target="tpu_custom_call" | custom-call | flops 301989888 | bytes 6291456 | tf_op jit(solution)/shard_map/apply_expert/pallas_call | solution.py:278
  91.3 2.0 %collective-permute-start.31 = (bf16[32,2048]{1,0:T(8,128)(2,1)S(1)}, bf16[32,2048]{1,0:T(8,128)(2,1)S(1)}, u32[]{:S(2)}, u32[]{:S(2)}) collective-permute-start(bf16[32,2048]{1,0:T(8,128)(2,1)S(1)} %get-tuple-element.106), channel_id=1, source_target_pairs={{0,4},{4,8},{8,12},{12,14},{14,10},{10,6},{6,2},{2,0},{1,5},{5,9},... | collective-permute-start | bytes 393224 | tf_op jit(solution)/shard_map/ppermute | solution.py:326
  93.3 2.9 %collective-permute-done.27 = bf16[32,2048]{1,0:T(8,128)(2,1)S(1)} collective-permute-done((bf16[32,2048]{1,0:T(8,128)(2,1)S(1)}, bf16[32,2048]{1,0:T(8,128)(2,1)S(1)}, u32[]{:S(2)}, u32[]{:S(2)}) %collective-permute-start.27) | collective-permute-done | bytes 131104 | tf_op jit(solution)/shard_map/ppermute | solution.py:325
  96.9 1.6 %collective-permute-start.32 = (bf16[64,2048]{1,0:T(8,128)(2,1)S(1)}, bf16[64,2048]{1,0:T(8,128)(2,1)S(1)}, u32[]{:S(2)}, u32[]{:S(2)}) collective-permute-start(bf16[64,2048]{1,0:T(8,128)(2,1)S(1)} %get-tuple-element.102), channel_id=1, source_target_pairs={{0,4},{4,8},{8,12},{12,14},{14,10},{10,6},{6,2},{2,0},{1,5},{5,9},... | collective-permute-start | bytes 786440 | tf_op jit(solution)/shard_map/ppermute | solution.py:326
  98.5 4.3 %collective-permute-done.28 = bf16[64,2048]{1,0:T(8,128)(2,1)S(1)} collective-permute-done((bf16[64,2048]{1,0:T(8,128)(2,1)S(1)}, bf16[64,2048]{1,0:T(8,128)(2,1)S(1)}, u32[]{:S(2)}, u32[]{:S(2)}) %collective-permute-start.28) | collective-permute-done | bytes 262176 | tf_op jit(solution)/shard_map/ppermute | solution.py:325
  102.8 1.6 %collective-permute-done.32 = bf16[64,2048]{1,0:T(8,128)(2,1)S(1)} collective-permute-done((bf16[64,2048]{1,0:T(8,128)(2,1)S(1)}, bf16[64,2048]{1,0:T(8,128)(2,1)S(1)}, u32[]{:S(2)}, u32[]{:S(2)}) %collective-permute-start.32) | collective-permute-done | bytes 262176 | tf_op jit(solution)/shard_map/ppermute | solution.py:326
  106.7 4.6 %collective-permute-done.29 = bf16[64,2048]{1,0:T(8,128)(2,1)S(1)} collective-permute-done((bf16[64,2048]{1,0:T(8,128)(2,1)S(1)}, bf16[64,2048]{1,0:T(8,128)(2,1)S(1)}, u32[]{:S(2)}, u32[]{:S(2)}) %collective-permute-start.29) | collective-permute-done | bytes 262176 | tf_op jit(solution)/shard_map/ppermute | solution.py:325
  111.3 1.8 %collective-permute-done.33 = bf16[64,2048]{1,0:T(8,128)(2,1)S(1)} collective-permute-done((bf16[64,2048]{1,0:T(8,128)(2,1)S(1)}, bf16[64,2048]{1,0:T(8,128)(2,1)S(1)}, u32[]{:S(2)}, u32[]{:S(2)}) %collective-permute-start.33) | collective-permute-done | bytes 262176 | tf_op jit(solution)/shard_map/ppermute | solution.py:326
  115.2 4.3 %collective-permute-done.30 = bf16[64,2048]{1,0:T(8,128)(2,1)S(1)} collective-permute-done((bf16[64,2048]{1,0:T(8,128)(2,1)S(1)}, bf16[64,2048]{1,0:T(8,128)(2,1)S(1)}, u32[]{:S(2)}, u32[]{:S(2)}) %collective-permute-start.30) | collective-permute-done | bytes 262176 | tf_op jit(solution)/shard_map/ppermute | solution.py:325
  (120 shorter events, 43.7 us)
Async XLA Ops:
  0.0 37.5 %collective-permute-start.8 = (bf16[2048,1024]{1,0:T(8,128)(2,1)}, bf16[2048,1024]{1,0:T(8,128)(2,1)}, u32[]{:S(2)}, u32[]{:S(2)}) collective-permute-start(bf16[2048,1024]{1,0:T(8,128)(2,1)} %refs_5_.3), channel_id=1, source_target_pairs={{0,1},{1,0},{2,3},{3,2},{4,5},{5,4},{6,7},{7,6},{8,9},{9,8},{10,11... | collective-permute-start | bytes 12582920 | tf_op jit(solution)/shard_map/ppermute | solution.py:34
  3.0 9.7 %collective-permute-start.9 = (bf16[272,256]{1,0:T(8,128)(2,1)}, bf16[272,256]{1,0:T(8,128)(2,1)S(1)}, u32[]{:S(2)}, u32[]{:S(2)}) collective-permute-start(bf16[272,256]{1,0:T(8,128)(2,1)} %get-tuple-element.67.refs_1_), channel_id=1, source_target_pairs={{0,4},{4,8},{8,12},{12,0},{1,5},{5,9},{9,13},{13,1},{2,6},{6,10},{... | collective-permute-start | bytes 417800 | tf_op jit(solution)/shard_map/ppermute | solution.py:436
  6.0 7.9 %collective-permute-start.2 = (bf16[272,256]{1,0:T(8,128)(2,1)}, bf16[272,256]{1,0:T(8,128)(2,1)S(1)}, u32[]{:S(2)}, u32[]{:S(2)}) collective-permute-start(bf16[272,256]{1,0:T(8,128)(2,1)} %get-tuple-element.51.refs_1_), channel_id=1, source_target_pairs={{0,1},{1,0},{2,3},{3,2},{4,5},{5,4},{6,7},{7,6},{8,9},{9,8},{10,11... | collective-permute-start | bytes 417800 | tf_op jit(solution)/shard_map/ppermute | solution.py:34
  6.0 9.8 %collective-permute-start.1 = (bf16[272,256]{1,0:T(8,128)(2,1)}, bf16[272,256]{1,0:T(8,128)(2,1)S(1)}, u32[]{:S(2)}, u32[]{:S(2)}) collective-permute-start(bf16[272,256]{1,0:T(8,128)(2,1)} %get-tuple-element.51.refs_1_), channel_id=1, source_target_pairs={{0,4},{4,8},{8,12},{12,0},{1,5},{5,9},{9,13},{13,1},{2,6},{6,10},{... | collective-permute-start | bytes 417800 | tf_op jit(solution)/shard_map/ppermute | solution.py:436
  12.7 8.2 %collective-permute-start.11 = (bf16[272,256]{1,0:T(8,128)(2,1)S(1)}, bf16[272,256]{1,0:T(8,128)(2,1)}, u32[]{:S(2)}, u32[]{:S(2)}) collective-permute-start(bf16[272,256]{1,0:T(8,128)(2,1)S(1)} %collective-permute-done.9.refs_1_), channel_id=1, source_target_pairs={{0,4},{4,8},{8,12},{12,0},{1,5},{5,9},{9,13},{13,1},{2,6},{6,10},{... | collective-permute-start | bytes 417800 | tf_op jit(solution)/shard_map/ppermute | solution.py:436
  15.9 6.8 %collective-permute-start.4 = (bf16[272,256]{1,0:T(8,128)(2,1)S(1)}, bf16[272,256]{1,0:T(8,128)(2,1)S(1)}, u32[]{:S(2)}, u32[]{:S(2)}) collective-permute-start(bf16[272,256]{1,0:T(8,128)(2,1)S(1)} %collective-permute-done.1.refs_1_), channel_id=1, source_target_pairs={{0,1},{1,0},{2,3},{3,2},{4,5},{5,4},{6,7},{7,6},{8,9},{9,8},{10,11... | collective-permute-start | bytes 417800 | tf_op jit(solution)/shard_map/ppermute | solution.py:34
  16.0 9.5 %collective-permute-start.3 = (bf16[272,256]{1,0:T(8,128)(2,1)S(1)}, bf16[272,256]{1,0:T(8,128)(2,1)}, u32[]{:S(2)}, u32[]{:S(2)}) collective-permute-start(bf16[272,256]{1,0:T(8,128)(2,1)S(1)} %collective-permute-done.1.refs_1_), channel_id=1, source_target_pairs={{0,4},{4,8},{8,12},{12,0},{1,5},{5,9},{9,13},{13,1},{2,6},{6,10},{... | collective-permute-start | bytes 417800 | tf_op jit(solution)/shard_map/ppermute | solution.py:436
  20.9 5.4 %collective-permute-start.14 = (bf16[272,256]{1,0:T(8,128)(2,1)}, bf16[272,256]{1,0:T(8,128)(2,1)}, u32[]{:S(2)}, u32[]{:S(2)}) collective-permute-start(bf16[272,256]{1,0:T(8,128)(2,1)} %collective-permute-done.11.refs_1_), channel_id=1, source_target_pairs={{0,1},{1,0},{2,3},{3,2},{4,5},{5,4},{6,7},{7,6},{8,9},{9,8},{10,11... | collective-permute-start | bytes 417800 | tf_op jit(solution)/shard_map/ppermute | solution.py:34
  21.1 9.2 %collective-permute-start.13 = (bf16[272,256]{1,0:T(8,128)(2,1)}, bf16[272,256]{1,0:T(8,128)(2,1)S(1)}, u32[]{:S(2)}, u32[]{:S(2)}) collective-permute-start(bf16[272,256]{1,0:T(8,128)(2,1)} %collective-permute-done.11.refs_1_), channel_id=1, source_target_pairs={{0,4},{4,8},{8,12},{12,0},{1,5},{5,9},{9,13},{13,1},{2,6},{6,10},{... | collective-permute-start | bytes 417800 | tf_op jit(solution)/shard_map/ppermute | solution.py:436
  25.6 9.1 %collective-permute-start.5 = (bf16[272,256]{1,0:T(8,128)(2,1)}, bf16[272,256]{1,0:T(8,128)(2,1)S(1)}, u32[]{:S(2)}, u32[]{:S(2)}) collective-permute-start(bf16[272,256]{1,0:T(8,128)(2,1)} %collective-permute-done.3.refs_1_), channel_id=1, source_target_pairs={{0,4},{4,8},{8,12},{12,0},{1,5},{5,9},{9,13},{13,1},{2,6},{6,10},{... | collective-permute-start | bytes 417800 | tf_op jit(solution)/shard_map/ppermute | solution.py:436
  30.3 7.2 %collective-permute-start.15 = (bf16[272,256]{1,0:T(8,128)(2,1)S(1)}, bf16[272,256]{1,0:T(8,128)(2,1)S(1)}, u32[]{:S(2)}, u32[]{:S(2)}) collective-permute-start(bf16[272,256]{1,0:T(8,128)(2,1)S(1)} %collective-permute-done.13.refs_1_), channel_id=1, source_target_pairs={{0,1},{1,0},{2,3},{3,2},{4,5},{5,4},{6,7},{7,6},{8,9},{9,8},{10,11... | collective-permute-start | bytes 417800 | tf_op jit(solution)/shard_map/ppermute | solution.py:34
  34.7 5.4 %collective-permute-start.7 = (bf16[272,256]{1,0:T(8,128)(2,1)S(1)}, bf16[272,256]{1,0:T(8,128)(2,1)S(1)}, u32[]{:S(2)}, u32[]{:S(2)}) collective-permute-start(bf16[272,256]{1,0:T(8,128)(2,1)S(1)} %collective-permute-done.5.refs_1_), channel_id=1, source_target_pairs={{0,1},{1,0},{2,3},{3,2},{4,5},{5,4},{6,7},{7,6},{8,9},{9,8},{10,11... | collective-permute-start | bytes 417800 | tf_op jit(solution)/shard_map/ppermute | solution.py:34
  36.9 12.9 %collective-permute-start = (bf16[64,1024]{1,0:T(8,128)(2,1)}, bf16[64,1024]{1,0:T(8,128)(2,1)}, u32[]{:S(2)}, u32[]{:S(2)}) collective-permute-start(bf16[64,1024]{1,0:T(8,128)(2,1)} %get-tuple-element.110), channel_id=1, source_target_pairs={{0,1},{1,0},{2,3},{3,2},{4,5},{5,4},{6,7},{7,6},{8,9},{9,8},{10,11... | collective-permute-start | bytes 393224 | tf_op jit(solution)/shard_map/ppermute | solution.py:59
  37.0 19.7 %collective-permute-start.19 = (bf16[2,192,2048]{2,1,0:T(8,128)(2,1)S(1)}, bf16[2,192,2048]{2,1,0:T(8,128)(2,1)S(1)}, u32[]{:S(2)}, u32[]{:S(2)}) collective-permute-start(bf16[2,192,2048]{2,1,0:T(8,128)(2,1)S(1)} %bitcast.3), channel_id=1, source_target_pairs={{0,1},{1,0},{2,3},{3,2},{4,5},{5,4},{6,7},{7,6},{8,9},{9,8},{10,11... | collective-permute-start | bytes 4718600 | tf_op jit(solution)/shard_map/ppermute | solution.py:34
  37.5 19.3 %collective-permute-start.20 = (bf16[192,2048]{1,0:T(8,128)(2,1)}, bf16[192,2048]{1,0:T(8,128)(2,1)}, u32[]{:S(2)}, u32[]{:S(2)}) collective-permute-start(bf16[192,2048]{1,0:T(8,128)(2,1)} %bitcast.17), channel_id=1, source_target_pairs={{0,1},{1,0},{2,3},{3,2},{4,5},{5,4},{6,7},{7,6},{8,9},{9,8},{10,11... | collective-permute-start | bytes 2359304 | tf_op jit(solution)/shard_map/ppermute | solution.py:34
  44.2 8.9 %collective-permute-start.16 = (bf16[64,2048]{1,0:T(8,128)(2,1)}, bf16[64,2048]{1,0:T(8,128)(2,1)S(1)}, u32[]{:S(2)}, u32[]{:S(2)}) collective-permute-start(bf16[64,2048]{1,0:T(8,128)(2,1)} %get-tuple-element.84), channel_id=1, source_target_pairs={{0,2},{2,0},{1,3},{3,1},{4,6},{6,4},{5,7},{7,5},{8,10},{10,8},{9,1... | collective-permute-start | bytes 786440 | tf_op jit(solution)/shard_map/ppermute | solution.py:449
  54.6 8.3 %collective-permute-start.17 = (bf16[64,2176]{1,0:T(8,128)(2,1)S(1)}, bf16[64,2176]{1,0:T(8,128)(2,1)S(1)}, u32[]{:S(2)}, u32[]{:S(2)}) collective-permute-start(bf16[64,2176]{1,0:T(8,128)(2,1)S(1)} %pad_maximum_fusion.refs_0_), channel_id=1, source_target_pairs={{0,4},{4,8},{8,12},{12,14},{14,10},{10,6},{6,2},{2,0},{1,5},{5,9},... | collective-permute-start | bytes 835592 | tf_op jit(solution)/shard_map/ppermute | solution.py:314
  55.8 7.8 %collective-permute-start.18 = (bf16[64,2176]{1,0:T(8,128)(2,1)S(1)}, bf16[64,2176]{1,0:T(8,128)(2,1)S(1)}, u32[]{:S(2)}, u32[]{:S(2)}) collective-permute-start(bf16[64,2176]{1,0:T(8,128)(2,1)S(1)} %pad_maximum_fusion.refs_0_), channel_id=1, source_target_pairs={{4,0},{8,4},{12,8},{14,12},{10,14},{6,10},{2,6},{0,2},{5,1},{9,5},... | collective-permute-start | bytes 835592 | tf_op jit(solution)/shard_map/ppermute | solution.py:315
  63.6 6.9 %collective-permute-start.21 = (bf16[64,2176]{1,0:T(8,128)(2,1)S(1)}, bf16[64,2176]{1,0:T(8,128)(2,1)S(1)}, u32[]{:S(2)}, u32[]{:S(2)}) collective-permute-start(bf16[64,2176]{1,0:T(8,128)(2,1)S(1)} %collective-permute-done.17.refs_0_), channel_id=1, source_target_pairs={{0,4},{4,8},{8,12},{12,14},{14,10},{10,6},{6,2},{2,0},{1,5},{5,9},... | collective-permute-start | bytes 835592 | tf_op jit(solution)/shard_map/ppermute | solution.py:314
  65.2 6.6 %collective-permute-start.22 = (bf16[64,2176]{1,0:T(8,128)(2,1)S(1)}, bf16[64,2176]{1,0:T(8,128)(2,1)S(1)}, u32[]{:S(2)}, u32[]{:S(2)}) collective-permute-start(bf16[64,2176]{1,0:T(8,128)(2,1)S(1)} %collective-permute-done.18.refs_1_), channel_id=1, source_target_pairs={{4,0},{8,4},{12,8},{14,12},{10,14},{6,10},{2,6},{0,2},{5,1},{9,5},... | collective-permute-start | bytes 835592 | tf_op jit(solution)/shard_map/ppermute | solution.py:315
  71.8 6.5 %collective-permute-start.23 = (bf16[64,2176]{1,0:T(8,128)(2,1)S(1)}, bf16[64,2176]{1,0:T(8,128)(2,1)S(1)}, u32[]{:S(2)}, u32[]{:S(2)}) collective-permute-start(bf16[64,2176]{1,0:T(8,128)(2,1)S(1)} %collective-permute-done.21.refs_0_), channel_id=1, source_target_pairs={{0,4},{4,8},{8,12},{12,14},{14,10},{10,6},{6,2},{2,0},{1,5},{5,9},... | collective-permute-start | bytes 835592 | tf_op jit(solution)/shard_map/ppermute | solution.py:314
  73.4 6.5 %collective-permute-start.24 = (bf16[64,2176]{1,0:T(8,128)(2,1)S(1)}, bf16[64,2176]{1,0:T(8,128)(2,1)S(1)}, u32[]{:S(2)}, u32[]{:S(2)}) collective-permute-start(bf16[64,2176]{1,0:T(8,128)(2,1)S(1)} %collective-permute-done.22.refs_1_), channel_id=1, source_target_pairs={{4,0},{8,4},{12,8},{14,12},{10,14},{6,10},{2,6},{0,2},{5,1},{9,5},... | collective-permute-start | bytes 835592 | tf_op jit(solution)/shard_map/ppermute | solution.py:315
  79.9 5.3 %collective-permute-start.25 = (bf16[32,2176]{1,0:T(8,128)(2,1)S(1)}, bf16[32,2176]{1,0:T(8,128)(2,1)S(1)}, u32[]{:S(2)}, u32[]{:S(2)}) collective-permute-start(bf16[32,2176]{1,0:T(8,128)(2,1)S(1)} %slice.32), channel_id=1, source_target_pairs={{0,4},{4,8},{8,12},{12,14},{14,10},{10,6},{6,2},{2,0},{1,5},{5,9},... | collective-permute-start | bytes 417800 | tf_op jit(solution)/shard_map/ppermute | solution.py:314
  82.4 6.1 %collective-permute-start.26 = (bf16[32,2176]{1,0:T(8,128)(2,1)S(1)}, bf16[32,2176]{1,0:T(8,128)(2,1)S(1)}, u32[]{:S(2)}, u32[]{:S(2)}) collective-permute-start(bf16[32,2176]{1,0:T(8,128)(2,1)S(1)} %slice.33), channel_id=1, source_target_pairs={{4,0},{8,4},{12,8},{14,12},{10,14},{6,10},{2,6},{0,2},{5,1},{9,5},... | collective-permute-start | bytes 417800 | tf_op jit(solution)/shard_map/ppermute | solution.py:315
  91.3 5.0 %collective-permute-start.27 = (bf16[32,2048]{1,0:T(8,128)(2,1)S(1)}, bf16[32,2048]{1,0:T(8,128)(2,1)S(1)}, u32[]{:S(2)}, u32[]{:S(2)}) collective-permute-start(bf16[32,2048]{1,0:T(8,128)(2,1)S(1)} %get-tuple-element.105), channel_id=1, source_target_pairs={{4,0},{8,4},{12,8},{14,12},{10,14},{6,10},{2,6},{0,2},{5,1},{9,5},... | collective-permute-start | bytes 393224 | tf_op jit(solution)/shard_map/ppermute | solution.py:325
  91.3 5.0 %collective-permute-start.31 = (bf16[32,2048]{1,0:T(8,128)(2,1)S(1)}, bf16[32,2048]{1,0:T(8,128)(2,1)S(1)}, u32[]{:S(2)}, u32[]{:S(2)}) collective-permute-start(bf16[32,2048]{1,0:T(8,128)(2,1)S(1)} %get-tuple-element.106), channel_id=1, source_target_pairs={{0,4},{4,8},{8,12},{12,14},{14,10},{10,6},{6,2},{2,0},{1,5},{5,9},... | collective-permute-start | bytes 393224 | tf_op jit(solution)/shard_map/ppermute | solution.py:326
  96.4 6.4 %collective-permute-start.28 = (bf16[64,2048]{1,0:T(8,128)(2,1)S(1)}, bf16[64,2048]{1,0:T(8,128)(2,1)S(1)}, u32[]{:S(2)}, u32[]{:S(2)}) collective-permute-start(bf16[64,2048]{1,0:T(8,128)(2,1)S(1)} %get-tuple-element.101), channel_id=1, source_target_pairs={{4,0},{8,4},{12,8},{14,12},{10,14},{6,10},{2,6},{0,2},{5,1},{9,5},... | collective-permute-start | bytes 786440 | tf_op jit(solution)/shard_map/ppermute | solution.py:325
  96.9 7.6 %collective-permute-start.32 = (bf16[64,2048]{1,0:T(8,128)(2,1)S(1)}, bf16[64,2048]{1,0:T(8,128)(2,1)S(1)}, u32[]{:S(2)}, u32[]{:S(2)}) collective-permute-start(bf16[64,2048]{1,0:T(8,128)(2,1)S(1)} %get-tuple-element.102), channel_id=1, source_target_pairs={{0,4},{4,8},{8,12},{12,14},{14,10},{10,6},{6,2},{2,0},{1,5},{5,9},... | collective-permute-start | bytes 786440 | tf_op jit(solution)/shard_map/ppermute | solution.py:326
  104.6 6.7 %collective-permute-start.29 = (bf16[64,2048]{1,0:T(8,128)(2,1)S(1)}, bf16[64,2048]{1,0:T(8,128)(2,1)S(1)}, u32[]{:S(2)}, u32[]{:S(2)}) collective-permute-start(bf16[64,2048]{1,0:T(8,128)(2,1)S(1)} %get-tuple-element.99), channel_id=1, source_target_pairs={{4,0},{8,4},{12,8},{14,12},{10,14},{6,10},{2,6},{0,2},{5,1},{9,5},... | collective-permute-start | bytes 786440 | tf_op jit(solution)/shard_map/ppermute | solution.py:325
  106.1 6.9 %collective-permute-start.33 = (bf16[64,2048]{1,0:T(8,128)(2,1)S(1)}, bf16[64,2048]{1,0:T(8,128)(2,1)S(1)}, u32[]{:S(2)}, u32[]{:S(2)}) collective-permute-start(bf16[64,2048]{1,0:T(8,128)(2,1)S(1)} %get-tuple-element.100), channel_id=1, source_target_pairs={{0,4},{4,8},{8,12},{12,14},{14,10},{10,6},{6,2},{2,0},{1,5},{5,9},... | collective-permute-start | bytes 786440 | tf_op jit(solution)/shard_map/ppermute | solution.py:326
  113.1 6.4 %collective-permute-start.30 = (bf16[64,2048]{1,0:T(8,128)(2,1)S(1)}, bf16[64,2048]{1,0:T(8,128)(2,1)S(1)}, u32[]{:S(2)}, u32[]{:S(2)}) collective-permute-start(bf16[64,2048]{1,0:T(8,128)(2,1)S(1)} %get-tuple-element.97), channel_id=1, source_target_pairs={{4,0},{8,4},{12,8},{14,12},{10,14},{6,10},{2,6},{0,2},{5,1},{9,5},... | collective-permute-start | bytes 786440 | tf_op jit(solution)/shard_map/ppermute | solution.py:325
  114.2 6.4 %collective-permute-start.34 = (bf16[64,2048]{1,0:T(8,128)(2,1)S(1)}, bf16[64,2048]{1,0:T(8,128)(2,1)S(1)}, u32[]{:S(2)}, u32[]{:S(2)}) collective-permute-start(bf16[64,2048]{1,0:T(8,128)(2,1)S(1)} %get-tuple-element.98), channel_id=1, source_target_pairs={{0,4},{4,8},{8,12},{12,14},{14,10},{10,6},{6,2},{2,0},{1,5},{5,9},... | collective-permute-start | bytes 786440 | tf_op jit(solution)/shard_map/ppermute | solution.py:326
  (25 other events, 185.1 us)

commit v3 on v2

--- a/solution.py
+++ b/solution.py
@@ -65,26 +65,179 @@
     group_width = QH // KVH
     rows = cache_rows + new_rows + MASK_ROWS
 
-    def kernel(page_ref, ck_ref, cv_ref, nk_ref, nv_ref, *out_refs):
+    def kernel(page_ref, ck_ref, cv_ref, nk_ref, nv_ref, *refs):
+        out_refs, (mask_ref, sems) = refs[:kv_heads], refs[kv_heads:]
         first = lax.axis_index("hd") * heads_here // group_width
-        lane = lax.broadcasted_iota(jnp.int32, (MASK_ROWS, 2 * HD), 1)
-        bias = jnp.where(lane < page_ref[0], 0.0, NEG_FILL).astype(jnp.bfloat16)
+        copies = []
         for kv, out_ref in enumerate(out_refs):
             columns = pl.ds(pl.multiple_of((first + kv) * HD, HD), HD)
-            out_ref[:cache_rows, :HD] = ck_ref[:, columns]
-            out_ref[:cache_rows, HD:] = cv_ref[:, columns]
-            out_ref[cache_rows : cache_rows + new_rows, :HD] = nk_ref[:, columns]
-            out_ref[cache_rows : cache_rows + new_rows, HD:] = nv_ref[:, columns]
-            out_ref[cache_rows + new_rows :, :] = bias
-
+            cached, new = pl.ds(0, cache_rows), pl.ds(cache_rows, new_rows)
+            for i, (ref, here, lanes) in enumerate(
+                [(ck_ref, cached, 0), (cv_ref, cached, HD), (nk_ref, new, 0), (nv_ref, new, HD)]
+            ):
+                copies.append(
+                    pltpu.make_async_copy(
+                        ref.at[:, columns], out_ref.at[here, pl.ds(lanes, HD)], sems.at[kv, i]
+                    )
+                )
+                copies[-1].start()
+        lane = lax.broadcasted_iota(jnp.int32, (MASK_ROWS, 2 * HD), 1)
+        mask_ref[...] = jnp.where(lane < page_ref[0], 0.0, NEG_FILL).astype(jnp.bfloat16)
+        for kv, out_ref in enumerate(out_refs):
+            copies.append(
+                pltpu.make_async_copy(
+                    mask_ref, out_ref.at[pl.ds(cache_rows + new_rows, MASK_ROWS), :], sems.at[kv, 4]
+                )
+            )
+            copies[-1].start()
+        for copy in copies:
+            copy.wait()
+
+    anywhere = pl.BlockSpec(memory_space=pl.ANY)
+    return pl.pallas_call(
+        kernel,
+        out_shape=[jax.ShapeDtypeStruct((rows, 2 * HD), cache_keys.dtype)] * kv_heads,
+        in_specs=[pl.BlockSpec(memory_space=pltpu.SMEM)] + [anywhere] * 4,
+        out_specs=[anywhere] * kv_heads,
+        scratch_shapes=[
+            pltpu.VMEM((MASK_ROWS, 2 * HD), jnp.bfloat16),
+            pltpu.SemaphoreType.DMA((kv_heads, 5)),
+        ],
+        compiler_params=pltpu.CompilerParams(vmem_limit_bytes=4 * MIB),
+        name="pack_keys",
+    )(page_len, cache_keys, cache_values, new_keys, new_values)
+
+
+def small_kernel(kernel, out_shape, operands, name):
     vmem = pl.BlockSpec(memory_space=pltpu.VMEM)
     return pl.pallas_call(
         kernel,
-        out_shape=[jax.ShapeDtypeStruct((rows, 2 * HD), cache_keys.dtype)] * kv_heads,
-        in_specs=[pl.BlockSpec(memory_space=pltpu.SMEM)] + [vmem] * 4,
-        out_specs=[vmem] * kv_heads,
-        name="pack_keys",
-    )(page_len, cache_keys, cache_values, new_keys, new_values)
+        out_shape=out_shape,
+        in_specs=[vmem] * len(operands),
+        out_specs=[vmem] * len(out_shape),
+        compiler_params=pltpu.CompilerParams(vmem_limit_bytes=8 * MIB),
+        cost_estimate=pl.CostEstimate(flops=MIB, bytes_accessed=MIB, transcendentals=0),
+        name=name,
+    )(*operands)
+
+
+def hand_over(parts):
+    size = len(parts)
+    return [parts[0]] + [
+        lax.ppermute(part, "sub", cycle(size, step)) for step, part in enumerate(parts) if step
+    ]
+
+
+def split_rows(residual, n_sub):
+    rows, columns = residual.shape[0] // n_sub, residual.shape[1]
+
+    def kernel(in_ref, *out_refs):
+        sub = lax.axis_index("sub")
+        for step, out_ref in enumerate(out_refs):
+            first = pl.multiple_of((sub + step) % n_sub * rows, rows)
+            out_ref[...] = in_ref[pl.ds(first, rows), :]
+
+    shape = jax.ShapeDtypeStruct((rows, columns), residual.dtype)
+    return small_kernel(kernel, [shape] * n_sub, [residual], "split_rows")
+
+
+def gates_by_expert(expert_ids, gates, rows):
+    choices, block_rows = expert_ids.shape[1], expert_ids.shape[0]
+
+    def kernel(ids_ref, gates_ref, out_ref):
+        sub = lax.axis_index("sub")
+        expert = lax.broadcasted_iota(jnp.int32, (LANES, block_rows), 0)
+        weights = gates_ref[...].astype(jnp.float32)
+        ids = ids_ref[...]
+        table = jnp.zeros((LANES, block_rows), jnp.float32)
+        for k in range(choices):
+            table = table + jnp.where(ids[k : k + 1, :] == expert, weights[k : k + 1, :], 0.0)
+        table = table.T
+        chosen = table[:rows]
+        for place in range(1, block_rows // rows):
+            chosen = jnp.where(sub == place, table[place * rows : (place + 1) * rows], chosen)
+        out_ref[...] = chosen.astype(jnp.bfloat16)
+
+    shape = jax.ShapeDtypeStruct((rows, LANES), jnp.bfloat16)
+    return small_kernel(kernel, [shape], [expert_ids.T, gates.T], "gates_by_expert")[0]
+
+
+def normalise(kept, came, residual_parts, gain, gate_table):
+    n_sub = len(residual_parts)
+    rows, width = residual_parts[0].shape
+    features = n_sub * width
+    extra = 0 if gate_table is None else LANES
+
+    def kernel(*refs):
+        refs = list(refs)
+        kept_ref = refs.pop(0) if kept is not None else None
+        came_ref = refs.pop(0)
+        part_refs = [refs.pop(0) for _ in residual_parts]
+        gain_ref = refs.pop(0)
+        if extra:
+            gate_ref = refs.pop(0)
+        hidden_ref, normed_ref = refs
+        sub = lax.axis_index("sub")
+        hidden, places, squares = [], [], 0.0
+        for step, part_ref in enumerate(part_refs):
+            here = slice(step * width, (step + 1) * width)
+            projected = came_ref[:, here].astype(jnp.float32)
+            if kept is not None:
+                projected = kept_ref[:, here] + projected
+            value = (part_ref[...].astype(jnp.float32) + projected).astype(jnp.bfloat16)
+            hidden.append(value)
+            place = pl.ds(pl.multiple_of((sub - step) % n_sub * width, width), width)
+            places.append(place)
+            hidden_ref[:, place] = value
+            wide = value.astype(jnp.float32)
+            squares = squares + jnp.sum(wide * wide, axis=1, keepdims=True)
+        scale = lax.rsqrt(squares / features + EPSILON)
+        for value, place in zip(hidden, places):
+            normed = value.astype(jnp.float32) * scale * gain_ref[:, place].astype(jnp.float32)
+            normed_ref[:, place] = normed.astype(jnp.bfloat16)
+        if extra:
+            normed_ref[:, features:] = gate_ref[...]
+
+    operands = ([kept] if kept is not None else []) + [came] + list(residual_parts)
+    operands.append(gain.reshape(1, features))
+    if extra:
+        operands.append(gate_table)
+    out_shape = [
+        jax.ShapeDtypeStruct((rows, features), jnp.bfloat16),
+        jax.ShapeDtypeStruct((rows, features + extra), jnp.bfloat16),
+    ]
+    return small_kernel(kernel, out_shape, operands, "normalise")
+
+
+def add_up(hidden, mine, to_back, to_ahead, n_sub):
+    rows, features = hidden.shape
+    width = features // n_sub
+
+    def kernel(hidden_ref, mine_ref, back_ref, ahead_ref, *out_refs):
+        sub = lax.axis_index("sub")
+        for step, out_ref in enumerate(out_refs):
+            place = pl.ds(pl.multiple_of((sub + step) % n_sub * width, width), width)
+            mixture = mine_ref[:, place] + back_ref[:, place].astype(jnp.float32)
+            mixture = mixture + ahead_ref[:, place].astype(jnp.float32)
+            total = hidden_ref[:, place].astype(jnp.float32) + mixture
+            out_ref[...] = total.astype(jnp.bfloat16)
+
+    shape = jax.ShapeDtypeStruct((rows, width), jnp.bfloat16)
+    return small_kernel(kernel, [shape] * n_sub, [hidden, mine, to_back, to_ahead], "add_up")
+
+
+def stack_rows(parts):
+    n_sub = len(parts)
+    rows, width = parts[0].shape
+
+    def kernel(*refs):
+        sub = lax.axis_index("sub")
+        for step, part_ref in enumerate(refs[:-1]):
+            first = pl.multiple_of((sub - step) % n_sub * rows, rows)
+            refs[-1][pl.ds(first, rows), :] = part_ref[...]
+
+    shape = jax.ShapeDtypeStruct((n_sub * rows, width), parts[0].dtype)
+    return small_kernel(kernel, [shape], parts, "stack_rows")[0]
 
 
 def attend(queries, kv, hop, blocks, state, cache_rows, kv_heads, finish=None):
@@ -296,16 +449,15 @@
     return list(range(n_ep * n_hd))
 
 
-def dense_experts(normed, gate_table, gate_up, w_down):
+def dense_experts(own, gate_up, w_down):
     axes = ("ep", "hd")
     walk = chip_ring(lax.axis_size("ep"), lax.axis_size("hd"))
     size = len(walk)
     ahead = [(walk[i], walk[(i + 1) % size]) for i in range(size)]
     back = [(b, a) for a, b in ahead]
-    rows, features = normed.shape
+    rows, features = own.shape[0], w_down[0].shape[1]
     half = rows // 2
     reach = size // 2
-    own = jnp.concatenate([normed, gate_table], axis=1)
     behind, before, waiting = own, own, [own]
     outs = []
     for hop in range(1, reach + 1):
@@ -314,24 +466,26 @@
         behind = lax.ppermute(behind, axes, ahead)
         before = lax.ppermute(before, axes, back)
         out = apply_expert(waiting, gate_up, w_down)
-        behind, before, out = lax.optimization_barrier((behind, before, out))
+        behind, out = lax.optimization_barrier((behind, out))
         outs.append(out)
         waiting = [behind, before]
     outs.append(apply_expert(waiting, gate_up, w_down))
     mine = outs[0]
     outs = [(x[: x.shape[0] // 2], x[x.shape[0] // 2 :]) for x in outs[1:]]
-    to_back, to_ahead = outs[-1]
+    to_back, to_ahead = [x.astype(jnp.bfloat16) for x in outs[-1]]
     for hop in range(reach - 1, -1, -1):
-        to_back = lax.ppermute(to_back.astype(jnp.bfloat16), axes, back).astype(jnp.float32)
-        to_ahead = lax.ppermute(to_ahead.astype(jnp.bfloat16), axes, ahead).astype(jnp.float32)
-        if hop == reach - 1:
-            empty = jnp.zeros((rows - half, features), jnp.float32)
-            to_back = jnp.concatenate([to_back, empty], axis=0)
-            to_ahead = jnp.concatenate([empty, to_ahead], axis=0)
-        if hop > 0:
-            to_back = to_back + outs[hop - 1][0]
-            to_ahead = to_ahead + outs[hop - 1][1]
-    return mine + to_back + to_ahead
+        to_back = lax.ppermute(to_back, axes, back)
+        to_ahead = lax.ppermute(to_ahead, axes, ahead)
+        if hop == 0:
+            break
+        sums = []
+        for came, first, share in [(to_back, 0, outs[hop - 1][0]), (to_ahead, half, outs[hop - 1][1])]:
+            came = came.astype(jnp.float32)
+            if hop == reach - 1:
+                came = jnp.pad(came, ((first, rows - half - first), (0, 0)))
+            sums.append(lax.optimization_barrier((came + share).astype(jnp.bfloat16)))
+        to_back, to_ahead = sums
+    return mine, to_back, to_ahead
 
 
 def sparse_experts(widened, normed, gate_up, w_down, expert_ids, gates, features):
@@ -404,7 +558,6 @@
     gates,
 ):
     n_ep, n_hd, n_sub = lax.axis_size("ep"), lax.axis_size("hd"), lax.axis_size("sub")
-    sub = lax.axis_index("sub")
     query_rows = queries.shape[0]
     heads_here = queries.shape[1] // HD
     kv_heads = max(1, heads_here // (QH // KVH))
@@ -424,7 +577,8 @@
     )
     query_blocks = queries.reshape(n_hd, n_sub, rows, heads_here * HD)
     projections = sub_copies(out_proj)
-    residual_parts = sub_exchange(residual, 0)
+    residual_parts = hand_over(split_rows(residual, n_sub))
+    gate_table = gates_by_expert(expert_ids, gates, rows) if dense else None
     if dense:
         gate_up_parts = sub_copies(gate_up[0])
         w_down_parts = sub_copies(w_down[0])
@@ -447,20 +601,11 @@
     sent = states[-1][-1]
     if n_hd == 2:
         came = lax.ppermute(sent, "hd", cycle(n_hd))
-        projected = earlier + came.astype(jnp.float32)
     else:
-        projected = lax.psum_scatter(sent, "hd", scatter_dimension=0, tiled=True).astype(
-            jnp.float32
-        )
-    residual_rows = jnp.concatenate(residual_parts, axis=1).astype(jnp.float32)
-    hidden = (residual_rows + projected).astype(jnp.bfloat16)
-    hidden = jnp.concatenate(by_sub(jnp.split(hidden, n_sub, axis=1)), axis=1)
-    widened = hidden.astype(jnp.float32)
-    square_sum = jnp.sum(widened * widened, axis=1, keepdims=True)
-    normed = (
-        widened * lax.rsqrt(square_sum / features + EPSILON) * norm_gain.astype(jnp.float32)
-    ).astype(jnp.bfloat16)
-
+        came = lax.psum_scatter(sent, "hd", scatter_dimension=0, tiled=True)
+    hidden, normed = normalise(
+        earlier if n_hd == 2 else None, came, residual_parts, norm_gain, gate_table
+    )
     if not dense:
         own_columns = [
             jnp.concatenate(by_sub(sub_exchange(x, 1)), axis=0) for x in (hidden, normed)
@@ -474,19 +619,8 @@
             gates,
             features,
         )
-    ids_here = lax.dynamic_slice_in_dim(expert_ids, sub * rows, rows, 0)
-    gates_here = lax.dynamic_slice_in_dim(gates, sub * rows, rows, 0).astype(jnp.float32)
-    gate_table = jnp.sum(
-        jnp.where(
-            ids_here[:, :, None] == jnp.arange(LANES, dtype=jnp.int32)[None, None, :],
-            gates_here[:, :, None],
-            0.0,
-        ),
-        axis=1,
-    ).astype(jnp.bfloat16)
-    mixture = dense_experts(normed, gate_table, gate_up_parts, w_down_parts)
-    layer_rows = (widened + mixture).astype(jnp.bfloat16)
-    return jnp.concatenate(by_sub(sub_exchange(layer_rows, 1)), axis=0)
+    mine, to_back, to_ahead = dense_experts(normed, gate_up_parts, w_down_parts)
+    return stack_rows(hand_over(add_up(hidden, mine, to_back, to_ahead, n_sub)))
 
 
 def solution(mesh):

time: 124 us -> 112 us (0.903)
  waiting for transfers between devices: 39.8 us -> 59.5 us
  local copies, waits for them, and re-layouts: 16.6 us -> 6.14 us
  Pallas kernels: 29.7 us -> 19.3 us
  starting transfers between devices: 30.6 us -> 25.6 us
  other arithmetic: 5.22 us -> 0.31 us
    ppermute x6, waiting for transfers between devices: 1.97 us -> 13.7 us  [shards(): lax.ppermute(x, 'ep', cycle(n_ep))]
    ppermute x4, waiting for transfers between devices: 5.62 us -> 13.5 us  [dense_experts(): behind = lax.ppermute(behind, axes, ahead)]
    unnamed x42 -> x26, local copies, waits for them, and re-layouts: 13.4 us -> 6.1 us
    ppermute x4, waiting for transfers between devices: 6.89 us -> 0.49 us  [dense_experts(): before = lax.ppermute(before, axes, back)]
    pallas_call x5, Pallas kernels: 13.3 us -> 7.64 us  [apply_expert(): pl.pallas_call(kernel, out_shape=jax.ShapeDtypeStruct((rows, features), j...]
    ppermute x4, starting transfers between devices: 6.75 us -> 1.41 us  [dense_experts(): behind = lax.ppermute(behind, axes, ahead)]
    ppermute x4, starting transfers between devices: 1.92 us -> 6.84 us  [dense_experts(): before = lax.ppermute(before, axes, back)]
    ppermute x6, starting transfers between devices: 9.69 us -> 5.05 us  [shards(): lax.ppermute(x, 'ep', cycle(n_ep))]
  transfers between devices with their start and end apart: 36 -> 36, of which waited for: 18 -> 22; matrix products, arithmetic and copies ran while one was open for 6% -> 0% of each run, Pallas kernels for 22% -> 15%
where the time goes in v3:
time: 112 us
  waiting for transfers between devices  59.5 us (53%)
  starting transfers between devices  25.6 us (23%)
  Pallas kernels  19.3 us (17%)
  local copies, waits for them, and re-layouts  6.14 us (5%)
    ppermute x4, waiting for transfers between devices, dense_experts(): to_back = lax.ppermute(to_back, axes, back)  21.8 us
    ppermute x6, waiting for transfers between devices, shards(): lax.ppermute(x, 'ep', cycle(n_ep))  13.7 us
    ppermute x4, waiting for transfers between devices, dense_experts(): behind = lax.ppermute(behind, axes, ahead)  13.5 us
    pallas_call x8, Pallas kernels, attend(): pl.pallas_call(kernel, out_shape=out_shape, in_specs=in_specs, out_specs=...  10.3 us
    pallas_call x5, Pallas kernels, apply_expert(): pl.pallas_call(kernel, out_shape=jax.ShapeDtypeStruct((rows, features), j...  7.64 us
    ppermute x4, starting transfers between devices, dense_experts(): before = lax.ppermute(before, axes, back)  6.84 us
    unnamed x26, local copies, waits for them, and re-layouts  6.1 us
    ppermute x1, waiting for transfers between devices, shards(): came = lax.ppermute(sent, 'hd', cycle(n_hd))  5.51 us
  transfers between devices with their start and end apart: 36, of which 22 were waited for; matrix products, arithmetic and copies ran while one was open for 0% of the time, Pallas kernels for 15%

profile of v3, /device:TPU:0, one launch (start us, length us, event | category | flops | bytes accessed | tf_op | source)
XLA Modules:
  0.0 111.8 jit_solution(1805703287031931456)
XLA Ops:
  5.5 2.6 %collective-permute-start.8 = (bf16[272,256]{1,0:T(8,128)(2,1)S(1)}, bf16[272,256]{1,0:T(8,128)(2,1)S(1)}, u32[]{:S(2)}, u32[]{:S(2)}) collective-permute-start(bf16[272,256]{1,0:T(8,128)(2,1)S(1)} %get-tuple-element.69.refs_1_), channel_id=1, source_target_pairs={{0,4},{4,8},{8,12},{12,0},{1,5},{5,9},{9,13},{13,1},{2,6},{6,10},{... | collective-permute-start | bytes 417800 | tf_op jit(solution)/shard_map/ppermute | solution.py:590
  8.3 2.3 %collective-permute-start = (bf16[272,256]{1,0:T(8,128)(2,1)S(1)}, bf16[272,256]{1,0:T(8,128)(2,1)S(1)}, u32[]{:S(2)}, u32[]{:S(2)}) collective-permute-start(bf16[272,256]{1,0:T(8,128)(2,1)S(1)} %get-tuple-element.53.refs_1_), channel_id=1, source_target_pairs={{0,4},{4,8},{8,12},{12,0},{1,5},{5,9},{9,13},{13,1},{2,6},{6,10},{... | collective-permute-start | bytes 417800 | tf_op jit(solution)/shard_map/ppermute | solution.py:590
  12.8 1.9 %collective-permute-done.8.refs_1_ = bf16[272,256]{1,0:T(8,128)(2,1)S(1)} collective-permute-done((bf16[272,256]{1,0:T(8,128)(2,1)S(1)}, bf16[272,256]{1,0:T(8,128)(2,1)S(1)}, u32[]{:S(2)}, u32[]{:S(2)}) %collective-permute-start.8) | collective-permute-done | bytes 139296 | tf_op jit(solution)/shard_map/ppermute | solution.py:590
  15.7 1.7 %collective-permute-done.refs_1_ = bf16[272,256]{1,0:T(8,128)(2,1)S(1)} collective-permute-done((bf16[272,256]{1,0:T(8,128)(2,1)S(1)}, bf16[272,256]{1,0:T(8,128)(2,1)S(1)}, u32[]{:S(2)}, u32[]{:S(2)}) %collective-permute-start) | collective-permute-done | bytes 139296 | tf_op jit(solution)/shard_map/ppermute | solution.py:590
  19.8 3.0 %collective-permute-done.10.refs_1_ = bf16[272,256]{1,0:T(8,128)(2,1)S(1)} collective-permute-done((bf16[272,256]{1,0:T(8,128)(2,1)S(1)}, bf16[272,256]{1,0:T(8,128)(2,1)S(1)}, u32[]{:S(2)}, u32[]{:S(2)}) %collective-permute-start.10) | collective-permute-done | bytes 139296 | tf_op jit(solution)/shard_map/ppermute | solution.py:590
  23.9 1.7 %collective-permute-done.2.refs_1_ = bf16[272,256]{1,0:T(8,128)(2,1)S(1)} collective-permute-done((bf16[272,256]{1,0:T(8,128)(2,1)S(1)}, bf16[272,256]{1,0:T(8,128)(2,1)S(1)}, u32[]{:S(2)}, u32[]{:S(2)}) %collective-permute-start.2) | collective-permute-done | bytes 139296 | tf_op jit(solution)/shard_map/ppermute | solution.py:590
  25.6 5.2 %collective-permute-done.12.refs_1_ = bf16[272,256]{1,0:T(8,128)(2,1)S(1)} collective-permute-done((bf16[272,256]{1,0:T(8,128)(2,1)S(1)}, bf16[272,256]{1,0:T(8,128)(2,1)S(1)}, u32[]{:S(2)}, u32[]{:S(2)}) %collective-permute-start.12) | collective-permute-done | bytes 139296 | tf_op jit(solution)/shard_map/ppermute | solution.py:590
  33.7 2.1 %attend.14.refs_7_ = f32[128,2048]{1,0:T(8,128)S(1)} custom-call(bf16[2,2,64,2048]{3,2,1,0:T(8,128)(2,1)S(1)} %bitcast.17, bf16[272,256]{1,0:T(8,128)(2,1)S(1)} %collective-permute-done.12.refs_1_, bf16[272,256]{1,0:T(8,128)(2,1)S(1)} %collective-permute-done.14.refs_2_, f32[1024,128]{1,0:T(8,128)S(1)} %get-tuple-element.83.refs_3_, ...), custom_call_target="tpu_custom_call" | custom-call | flops 402653184 | bytes 4194304 | tf_op jit(solution)/shard_map/attend/pallas_call | solution.py:389
  35.8 2.1 %attend.15 = (f32[64,2048]{1,0:T(8,128)S(1)}, bf16[64,2048]{1,0:T(8,128)(2,1)S(1)}) custom-call(bf16[2,2,64,2048]{3,2,1,0:T(8,128)(2,1)S(1)} %bitcast.18, bf16[272,256]{1,0:T(8,128)(2,1)S(1)} %collective-permute-done.4.refs_1_, bf16[272,256]{1,0:T(8,128)(2,1)S(1)} %collective-permute-done.6.refs_2_, f32[1024,128]{1,0:T(8,128)S(1)} %get-tuple-element.67.refs_3_, ...), custom_call_target="tpu_custom_call" | custom-call | flops 402653184 | bytes 4194304 | tf_op jit(solution)/shard_map/attend/pallas_call | solution.py:389
  37.9 1.9 %collective-permute-start.15 = (bf16[64,2048]{1,0:T(8,128)(2,1)S(1)}, bf16[64,2048]{1,0:T(8,128)(2,1)S(1)}, u32[]{:S(2)}, u32[]{:S(2)}) collective-permute-start(bf16[64,2048]{1,0:T(8,128)(2,1)S(1)} %get-tuple-element.86), channel_id=1, source_target_pairs={{0,2},{2,0},{1,3},{3,1},{4,6},{6,4},{5,7},{7,5},{8,10},{10,8},{9,1... | collective-permute-start | bytes 786440 | tf_op jit(solution)/shard_map/ppermute | solution.py:603
  41.2 5.5 %collective-permute-done.15.refs_1_ = bf16[64,2048]{1,0:T(8,128)(2,1)S(1)} collective-permute-done((bf16[64,2048]{1,0:T(8,128)(2,1)S(1)}, bf16[64,2048]{1,0:T(8,128)(2,1)S(1)}, u32[]{:S(2)}, u32[]{:S(2)}) %collective-permute-start.15) | collective-permute-done | bytes 262176 | tf_op jit(solution)/shard_map/ppermute | solution.py:603
  47.0 2.0 %collective-permute-start.21 = (bf16[64,2176]{1,0:T(8,128)(2,1)S(1)}, bf16[64,2176]{1,0:T(8,128)(2,1)S(1)}, u32[]{:S(2)}, u32[]{:S(2)}) collective-permute-start(bf16[64,2176]{1,0:T(8,128)(2,1)S(1)} %get-tuple-element.90.refs_0_), channel_id=1, source_target_pairs={{4,0},{8,4},{12,8},{14,12},{10,14},{6,10},{2,6},{0,2},{5,1},{9,5},... | collective-permute-start | bytes 835592 | tf_op jit(solution)/shard_map/ppermute | solution.py:467
  49.0 1.5 %apply_expert.5.mine_ref = f32[64,2048]{1,0:T(8,128)S(1)} custom-call(bf16[64,2176]{1,0:T(8,128)(2,1)S(1)} %get-tuple-element.90.refs_0_, bf16[2,192,2048]{2,1,0:T(8,128)(2,1)S(1)} %bitcast.6, bf16[2,192,2048]{2,1,0:T(8,128)(2,1)S(1)} %collective-permute-done.18.refs_2_.refs_3_, bf16[192,2048]{1,0:T(8,128)(2,1)S(1)} %bitcast.20, ...), custom_call_target="tpu_custom_call" | custom-call | flops 301989888 | bytes 6291456 | tf_op jit(solution)/shard_map/apply_expert/pallas_call | solution.py:431
  50.6 4.8 %collective-permute-done.17.refs_0_ = bf16[64,2176]{1,0:T(8,128)(2,1)S(1)} collective-permute-done((bf16[64,2176]{1,0:T(8,128)(2,1)S(1)}, bf16[64,2176]{1,0:T(8,128)(2,1)S(1)}, u32[]{:S(2)}, u32[]{:S(2)}) %collective-permute-start.17) | collective-permute-done | bytes 278560 | tf_op jit(solution)/shard_map/ppermute | solution.py:466
  55.6 1.7 %collective-permute-start.23 = (bf16[64,2176]{1,0:T(8,128)(2,1)S(1)}, bf16[64,2176]{1,0:T(8,128)(2,1)S(1)}, u32[]{:S(2)}, u32[]{:S(2)}) collective-permute-start(bf16[64,2176]{1,0:T(8,128)(2,1)S(1)} %collective-permute-done.21.refs_1_), channel_id=1, source_target_pairs={{4,0},{8,4},{12,8},{14,12},{10,14},{6,10},{2,6},{0,2},{5,1},{9,5},... | collective-permute-start | bytes 835592 | tf_op jit(solution)/shard_map/ppermute | solution.py:467
  57.4 1.5 %apply_expert.6 = f32[128,2048]{1,0:T(8,128)S(1)} custom-call(bf16[64,2176]{1,0:T(8,128)(2,1)S(1)} %collective-permute-done.17.refs_0_, bf16[64,2176]{1,0:T(8,128)(2,1)S(1)} %collective-permute-done.21.refs_1_, bf16[2,192,2048]{2,1,0:T(8,128)(2,1)S(1)} %bitcast.7, bf16[2,192,2048]{2,1,0:T(8,128)(2,1)S(1)} %collective-permute-done.18.refs_2_.refs_3_, ...), custom_call_target="tpu_custom_call" | custom-call | flops 603979776 | bytes 6291456 | tf_op jit(solution)/shard_map/apply_expert/pallas_call | solution.py:431
  58.9 3.9 %collective-permute-done.20.refs_0_ = bf16[64,2176]{1,0:T(8,128)(2,1)S(1)} collective-permute-done((bf16[64,2176]{1,0:T(8,128)(2,1)S(1)}, bf16[64,2176]{1,0:T(8,128)(2,1)S(1)}, u32[]{:S(2)}, u32[]{:S(2)}) %collective-permute-start.20) | collective-permute-done | bytes 278560 | tf_op jit(solution)/shard_map/ppermute | solution.py:466
  63.4 1.4 %collective-permute-start.25 = (bf16[64,2176]{1,0:T(8,128)(2,1)S(1)}, bf16[64,2176]{1,0:T(8,128)(2,1)S(1)}, u32[]{:S(2)}, u32[]{:S(2)}) collective-permute-start(bf16[64,2176]{1,0:T(8,128)(2,1)S(1)} %collective-permute-done.23.refs_1_), channel_id=1, source_target_pairs={{4,0},{8,4},{12,8},{14,12},{10,14},{6,10},{2,6},{0,2},{5,1},{9,5},... | collective-permute-start | bytes 835592 | tf_op jit(solution)/shard_map/ppermute | solution.py:467
  64.8 1.6 %apply_expert.7 = f32[128,2048]{1,0:T(8,128)S(1)} custom-call(bf16[64,2176]{1,0:T(8,128)(2,1)S(1)} %collective-permute-done.20.refs_0_, bf16[64,2176]{1,0:T(8,128)(2,1)S(1)} %collective-permute-done.23.refs_1_, bf16[2,192,2048]{2,1,0:T(8,128)(2,1)S(1)} %bitcast.8, bf16[2,192,2048]{2,1,0:T(8,128)(2,1)S(1)} %collective-permute-done.18.refs_2_.refs_3_, ...), custom_call_target="tpu_custom_call" | custom-call | flops 603979776 | bytes 6291456 | tf_op jit(solution)/shard_map/apply_expert/pallas_call | solution.py:431
  66.4 3.4 %collective-permute-done.22.refs_0_ = bf16[64,2176]{1,0:T(8,128)(2,1)S(1)} collective-permute-done((bf16[64,2176]{1,0:T(8,128)(2,1)S(1)}, bf16[64,2176]{1,0:T(8,128)(2,1)S(1)}, u32[]{:S(2)}, u32[]{:S(2)}) %collective-permute-start.22) | collective-permute-done | bytes 278560 | tf_op jit(solution)/shard_map/ppermute | solution.py:466
  70.3 1.7 %collective-permute-start.26 = (bf16[32,2176]{1,0:T(8,128)(2,1)S(1)}, bf16[32,2176]{1,0:T(8,128)(2,1)S(1)}, u32[]{:S(2)}, u32[]{:S(2)}) collective-permute-start(bf16[32,2176]{1,0:T(8,128)(2,1)S(1)} %slice.42), channel_id=1, source_target_pairs={{4,0},{8,4},{12,8},{14,12},{10,14},{6,10},{2,6},{0,2},{5,1},{9,5},... | collective-permute-start | bytes 417800 | tf_op jit(solution)/shard_map/ppermute | solution.py:467
  71.9 1.5 %apply_expert.8 = f32[128,2048]{1,0:T(8,128)S(1)} custom-call(bf16[64,2176]{1,0:T(8,128)(2,1)S(1)} %collective-permute-done.22.refs_0_, bf16[64,2176]{1,0:T(8,128)(2,1)S(1)} %collective-permute-done.25.refs_1_, bf16[2,192,2048]{2,1,0:T(8,128)(2,1)S(1)} %bitcast.9, bf16[2,192,2048]{2,1,0:T(8,128)(2,1)S(1)} %collective-permute-done.18.refs_2_.refs_3_, ...), custom_call_target="tpu_custom_call" | custom-call | flops 603979776 | bytes 6291456 | tf_op jit(solution)/shard_map/apply_expert/pallas_call | solution.py:431
  75.4 1.5 %apply_expert.9 = f32[64,2048]{1,0:T(8,128)S(1)} custom-call(bf16[32,2176]{1,0:T(8,128)(2,1)S(1)} %collective-permute-done.24.refs_0_, bf16[32,2176]{1,0:T(8,128)(2,1)S(1)} %collective-permute-done.26.refs_1_, bf16[2,192,2048]{2,1,0:T(8,128)(2,1)S(1)} %bitcast.10, bf16[2,192,2048]{2,1,0:T(8,128)(2,1)S(1)} %collective-permute-done.18.refs_2_.refs_3_, ...), custom_call_target="tpu_custom_call" | custom-call | flops 301989888 | bytes 6291456 | tf_op jit(solution)/shard_map/apply_expert/pallas_call | solution.py:431
  77.0 1.7 %collective-permute-start.27 = (bf16[32,2048]{1,0:T(8,128)(2,1)S(1)}, bf16[32,2048]{1,0:T(8,128)(2,1)S(1)}, u32[]{:S(2)}, u32[]{:S(2)}) collective-permute-start(bf16[32,2048]{1,0:T(8,128)(2,1)S(1)} %get-tuple-element.108), channel_id=1, source_target_pairs={{4,0},{8,4},{12,8},{14,12},{10,14},{6,10},{2,6},{0,2},{5,1},{9,5},... | collective-permute-start | bytes 393224 | tf_op jit(solution)/shard_map/ppermute | solution.py:477
  79.0 4.3 %collective-permute-done.27 = bf16[32,2048]{1,0:T(8,128)(2,1)S(1)} collective-permute-done((bf16[32,2048]{1,0:T(8,128)(2,1)S(1)}, bf16[32,2048]{1,0:T(8,128)(2,1)S(1)}, u32[]{:S(2)}, u32[]{:S(2)}) %collective-permute-start.27) | collective-permute-done | bytes 131104 | tf_op jit(solution)/shard_map/ppermute | solution.py:477
  83.4 1.6 %collective-permute-done.31 = bf16[32,2048]{1,0:T(8,128)(2,1)S(1)} collective-permute-done((bf16[32,2048]{1,0:T(8,128)(2,1)S(1)}, bf16[32,2048]{1,0:T(8,128)(2,1)S(1)}, u32[]{:S(2)}, u32[]{:S(2)}) %collective-permute-start.31) | collective-permute-done | bytes 131104 | tf_op jit(solution)/shard_map/ppermute | solution.py:478
  85.1 1.6 %collective-permute-start.28 = (bf16[64,2048]{1,0:T(8,128)(2,1)S(1)}, bf16[64,2048]{1,0:T(8,128)(2,1)S(1)}, u32[]{:S(2)}, u32[]{:S(2)}) collective-permute-start(bf16[64,2048]{1,0:T(8,128)(2,1)S(1)} %get-tuple-element.106), channel_id=1, source_target_pairs={{4,0},{8,4},{12,8},{14,12},{10,14},{6,10},{2,6},{0,2},{5,1},{9,5},... | collective-permute-start | bytes 786440 | tf_op jit(solution)/shard_map/ppermute | solution.py:477
  87.1 7.1 %collective-permute-done.28 = bf16[64,2048]{1,0:T(8,128)(2,1)S(1)} collective-permute-done((bf16[64,2048]{1,0:T(8,128)(2,1)S(1)}, bf16[64,2048]{1,0:T(8,128)(2,1)S(1)}, u32[]{:S(2)}, u32[]{:S(2)}) %collective-permute-start.28) | collective-permute-done | bytes 262176 | tf_op jit(solution)/shard_map/ppermute | solution.py:477
  95.2 1.5 %collective-permute-start.33 = (bf16[64,2048]{1,0:T(8,128)(2,1)S(1)}, bf16[64,2048]{1,0:T(8,128)(2,1)S(1)}, u32[]{:S(2)}, u32[]{:S(2)}) collective-permute-start(bf16[64,2048]{1,0:T(8,128)(2,1)S(1)} %get-tuple-element.103), channel_id=1, source_target_pairs={{0,4},{4,8},{8,12},{12,14},{14,10},{10,6},{6,2},{2,0},{1,5},{5,9},... | collective-permute-start | bytes 786440 | tf_op jit(solution)/shard_map/ppermute | solution.py:478
  96.8 6.0 %collective-permute-done.29 = bf16[64,2048]{1,0:T(8,128)(2,1)S(1)} collective-permute-done((bf16[64,2048]{1,0:T(8,128)(2,1)S(1)}, bf16[64,2048]{1,0:T(8,128)(2,1)S(1)}, u32[]{:S(2)}, u32[]{:S(2)}) %collective-permute-start.29) | collective-permute-done | bytes 262176 | tf_op jit(solution)/shard_map/ppermute | solution.py:477
  103.2 1.8 %collective-permute-start.34 = (bf16[64,2048]{1,0:T(8,128)(2,1)S(1)}, bf16[64,2048]{1,0:T(8,128)(2,1)S(1)}, u32[]{:S(2)}, u32[]{:S(2)}) collective-permute-start(bf16[64,2048]{1,0:T(8,128)(2,1)S(1)} %get-tuple-element.101), channel_id=1, source_target_pairs={{0,4},{4,8},{8,12},{12,14},{14,10},{10,6},{6,2},{2,0},{1,5},{5,9},... | collective-permute-start | bytes 786440 | tf_op jit(solution)/shard_map/ppermute | solution.py:478
  105.0 4.3 %collective-permute-done.30.back_ref = bf16[64,2048]{1,0:T(8,128)(2,1)S(1)} collective-permute-done((bf16[64,2048]{1,0:T(8,128)(2,1)S(1)}, bf16[64,2048]{1,0:T(8,128)(2,1)S(1)}, u32[]{:S(2)}, u32[]{:S(2)}) %collective-permute-start.30) | collective-permute-done | bytes 262176 | tf_op jit(solution)/shard_map/ppermute | solution.py:477
  (93 shorter events, 24.3 us)
Async XLA Ops:
  0.0 33.6 %collective-permute-start.7 = (bf16[2048,1024]{1,0:T(8,128)(2,1)}, bf16[2048,1024]{1,0:T(8,128)(2,1)S(1)}, u32[]{:S(2)}, u32[]{:S(2)}) collective-permute-start(bf16[2048,1024]{1,0:T(8,128)(2,1)} %refs_5_.3), channel_id=1, source_target_pairs={{0,1},{1,0},{2,3},{3,2},{4,5},{5,4},{6,7},{7,6},{8,9},{9,8},{10,11... | collective-permute-start | bytes 12582920 | tf_op jit(solution)/shard_map/ppermute | solution.py:34
  0.5 48.6 %collective-permute-start.18 = (bf16[2,192,2048]{2,1,0:T(8,128)(2,1)}, bf16[2,192,2048]{2,1,0:T(8,128)(2,1)S(1)}, u32[]{:S(2)}, u32[]{:S(2)}) collective-permute-start(bf16[2,192,2048]{2,1,0:T(8,128)(2,1)} %bitcast.5), channel_id=1, source_target_pairs={{0,1},{1,0},{2,3},{3,2},{4,5},{5,4},{6,7},{7,6},{8,9},{9,8},{10,11... | collective-permute-start | bytes 4718600 | tf_op jit(solution)/shard_map/ppermute | solution.py:34
  5.0 3.3 %collective-permute-start.9 = (bf16[272,256]{1,0:T(8,128)(2,1)S(1)}, bf16[272,256]{1,0:T(8,128)(2,1)S(1)}, u32[]{:S(2)}, u32[]{:S(2)}) collective-permute-start(bf16[272,256]{1,0:T(8,128)(2,1)S(1)} %get-tuple-element.69.refs_1_), channel_id=1, source_target_pairs={{0,1},{1,0},{2,3},{3,2},{4,5},{5,4},{6,7},{7,6},{8,9},{9,8},{10,11... | collective-permute-start | bytes 417800 | tf_op jit(solution)/shard_map/ppermute | solution.py:34
  5.5 9.2 %collective-permute-start.8 = (bf16[272,256]{1,0:T(8,128)(2,1)S(1)}, bf16[272,256]{1,0:T(8,128)(2,1)S(1)}, u32[]{:S(2)}, u32[]{:S(2)}) collective-permute-start(bf16[272,256]{1,0:T(8,128)(2,1)S(1)} %get-tuple-element.69.refs_1_), channel_id=1, source_target_pairs={{0,4},{4,8},{8,12},{12,0},{1,5},{5,9},{9,13},{13,1},{2,6},{6,10},{... | collective-permute-start | bytes 417800 | tf_op jit(solution)/shard_map/ppermute | solution.py:590
  8.1 6.6 %collective-permute-start.1 = (bf16[272,256]{1,0:T(8,128)(2,1)S(1)}, bf16[272,256]{1,0:T(8,128)(2,1)S(1)}, u32[]{:S(2)}, u32[]{:S(2)}) collective-permute-start(bf16[272,256]{1,0:T(8,128)(2,1)S(1)} %get-tuple-element.53.refs_1_), channel_id=1, source_target_pairs={{0,1},{1,0},{2,3},{3,2},{4,5},{5,4},{6,7},{7,6},{8,9},{9,8},{10,11... | collective-permute-start | bytes 417800 | tf_op jit(solution)/shard_map/ppermute | solution.py:34
  8.3 9.1 %collective-permute-start = (bf16[272,256]{1,0:T(8,128)(2,1)S(1)}, bf16[272,256]{1,0:T(8,128)(2,1)S(1)}, u32[]{:S(2)}, u32[]{:S(2)}) collective-permute-start(bf16[272,256]{1,0:T(8,128)(2,1)S(1)} %get-tuple-element.53.refs_1_), channel_id=1, source_target_pairs={{0,4},{4,8},{8,12},{12,0},{1,5},{5,9},{9,13},{13,1},{2,6},{6,10},{... | collective-permute-start | bytes 417800 | tf_op jit(solution)/shard_map/ppermute | solution.py:590
  14.7 2.7 %collective-permute-start.11 = (bf16[272,256]{1,0:T(8,128)(2,1)S(1)}, bf16[272,256]{1,0:T(8,128)(2,1)S(1)}, u32[]{:S(2)}, u32[]{:S(2)}) collective-permute-start(bf16[272,256]{1,0:T(8,128)(2,1)S(1)} %collective-permute-done.8.refs_1_), channel_id=1, source_target_pairs={{0,1},{1,0},{2,3},{3,2},{4,5},{5,4},{6,7},{7,6},{8,9},{9,8},{10,11... | collective-permute-start | bytes 417800 | tf_op jit(solution)/shard_map/ppermute | solution.py:34
  14.7 8.1 %collective-permute-start.10 = (bf16[272,256]{1,0:T(8,128)(2,1)S(1)}, bf16[272,256]{1,0:T(8,128)(2,1)S(1)}, u32[]{:S(2)}, u32[]{:S(2)}) collective-permute-start(bf16[272,256]{1,0:T(8,128)(2,1)S(1)} %collective-permute-done.8.refs_1_), channel_id=1, source_target_pairs={{0,4},{4,8},{8,12},{12,0},{1,5},{5,9},{9,13},{13,1},{2,6},{6,10},{... | collective-permute-start | bytes 417800 | tf_op jit(solution)/shard_map/ppermute | solution.py:590
  17.4 5.3 %collective-permute-start.3 = (bf16[272,256]{1,0:T(8,128)(2,1)S(1)}, bf16[272,256]{1,0:T(8,128)(2,1)S(1)}, u32[]{:S(2)}, u32[]{:S(2)}) collective-permute-start(bf16[272,256]{1,0:T(8,128)(2,1)S(1)} %collective-permute-done.refs_1_), channel_id=1, source_target_pairs={{0,1},{1,0},{2,3},{3,2},{4,5},{5,4},{6,7},{7,6},{8,9},{9,8},{10,11... | collective-permute-start | bytes 417800 | tf_op jit(solution)/shard_map/ppermute | solution.py:34
  17.4 8.1 %collective-permute-start.2 = (bf16[272,256]{1,0:T(8,128)(2,1)S(1)}, bf16[272,256]{1,0:T(8,128)(2,1)S(1)}, u32[]{:S(2)}, u32[]{:S(2)}) collective-permute-start(bf16[272,256]{1,0:T(8,128)(2,1)S(1)} %collective-permute-done.refs_1_), channel_id=1, source_target_pairs={{0,4},{4,8},{8,12},{12,0},{1,5},{5,9},{9,13},{13,1},{2,6},{6,10},{... | collective-permute-start | bytes 417800 | tf_op jit(solution)/shard_map/ppermute | solution.py:590
  22.8 2.8 %collective-permute-start.13 = (bf16[272,256]{1,0:T(8,128)(2,1)S(1)}, bf16[272,256]{1,0:T(8,128)(2,1)S(1)}, u32[]{:S(2)}, u32[]{:S(2)}) collective-permute-start(bf16[272,256]{1,0:T(8,128)(2,1)S(1)} %collective-permute-done.10.refs_1_), channel_id=1, source_target_pairs={{0,1},{1,0},{2,3},{3,2},{4,5},{5,4},{6,7},{7,6},{8,9},{9,8},{10,11... | collective-permute-start | bytes 417800 | tf_op jit(solution)/shard_map/ppermute | solution.py:34
  22.8 8.0 %collective-permute-start.12 = (bf16[272,256]{1,0:T(8,128)(2,1)S(1)}, bf16[272,256]{1,0:T(8,128)(2,1)S(1)}, u32[]{:S(2)}, u32[]{:S(2)}) collective-permute-start(bf16[272,256]{1,0:T(8,128)(2,1)S(1)} %collective-permute-done.10.refs_1_), channel_id=1, source_target_pairs={{0,4},{4,8},{8,12},{12,0},{1,5},{5,9},{9,13},{13,1},{2,6},{6,10},{... | collective-permute-start | bytes 417800 | tf_op jit(solution)/shard_map/ppermute | solution.py:590
  25.6 6.2 %collective-permute-start.5 = (bf16[272,256]{1,0:T(8,128)(2,1)S(1)}, bf16[272,256]{1,0:T(8,128)(2,1)S(1)}, u32[]{:S(2)}, u32[]{:S(2)}) collective-permute-start(bf16[272,256]{1,0:T(8,128)(2,1)S(1)} %collective-permute-done.2.refs_1_), channel_id=1, source_target_pairs={{0,1},{1,0},{2,3},{3,2},{4,5},{5,4},{6,7},{7,6},{8,9},{9,8},{10,11... | collective-permute-start | bytes 417800 | tf_op jit(solution)/shard_map/ppermute | solution.py:34
  25.6 8.1 %collective-permute-start.4 = (bf16[272,256]{1,0:T(8,128)(2,1)S(1)}, bf16[272,256]{1,0:T(8,128)(2,1)S(1)}, u32[]{:S(2)}, u32[]{:S(2)}) collective-permute-start(bf16[272,256]{1,0:T(8,128)(2,1)S(1)} %collective-permute-done.2.refs_1_), channel_id=1, source_target_pairs={{0,4},{4,8},{8,12},{12,0},{1,5},{5,9},{9,13},{13,1},{2,6},{6,10},{... | collective-permute-start | bytes 417800 | tf_op jit(solution)/shard_map/ppermute | solution.py:590
  30.8 18.3 %collective-permute-start.19 = (bf16[192,2048]{1,0:T(8,128)(2,1)S(1)}, bf16[192,2048]{1,0:T(8,128)(2,1)S(1)}, u32[]{:S(2)}, u32[]{:S(2)}) collective-permute-start(bf16[192,2048]{1,0:T(8,128)(2,1)S(1)} %bitcast.19), channel_id=1, source_target_pairs={{0,1},{1,0},{2,3},{3,2},{4,5},{5,4},{6,7},{7,6},{8,9},{9,8},{10,11... | collective-permute-start | bytes 2359304 | tf_op jit(solution)/shard_map/ppermute | solution.py:34
  37.9 8.8 %collective-permute-start.15 = (bf16[64,2048]{1,0:T(8,128)(2,1)S(1)}, bf16[64,2048]{1,0:T(8,128)(2,1)S(1)}, u32[]{:S(2)}, u32[]{:S(2)}) collective-permute-start(bf16[64,2048]{1,0:T(8,128)(2,1)S(1)} %get-tuple-element.86), channel_id=1, source_target_pairs={{0,2},{2,0},{1,3},{3,1},{4,6},{6,4},{5,7},{7,5},{8,10},{10,8},{9,1... | collective-permute-start | bytes 786440 | tf_op jit(solution)/shard_map/ppermute | solution.py:603
  47.0 8.4 %collective-permute-start.17 = (bf16[64,2176]{1,0:T(8,128)(2,1)S(1)}, bf16[64,2176]{1,0:T(8,128)(2,1)S(1)}, u32[]{:S(2)}, u32[]{:S(2)}) collective-permute-start(bf16[64,2176]{1,0:T(8,128)(2,1)S(1)} %get-tuple-element.90.refs_0_), channel_id=1, source_target_pairs={{0,4},{4,8},{8,12},{12,14},{14,10},{10,6},{6,2},{2,0},{1,5},{5,9},... | collective-permute-start | bytes 835592 | tf_op jit(solution)/shard_map/ppermute | solution.py:466
  47.0 8.6 %collective-permute-start.21 = (bf16[64,2176]{1,0:T(8,128)(2,1)S(1)}, bf16[64,2176]{1,0:T(8,128)(2,1)S(1)}, u32[]{:S(2)}, u32[]{:S(2)}) collective-permute-start(bf16[64,2176]{1,0:T(8,128)(2,1)S(1)} %get-tuple-element.90.refs_0_), channel_id=1, source_target_pairs={{4,0},{8,4},{12,8},{14,12},{10,14},{6,10},{2,6},{0,2},{5,1},{9,5},... | collective-permute-start | bytes 835592 | tf_op jit(solution)/shard_map/ppermute | solution.py:467
  55.3 7.4 %collective-permute-start.20 = (bf16[64,2176]{1,0:T(8,128)(2,1)S(1)}, bf16[64,2176]{1,0:T(8,128)(2,1)S(1)}, u32[]{:S(2)}, u32[]{:S(2)}) collective-permute-start(bf16[64,2176]{1,0:T(8,128)(2,1)S(1)} %collective-permute-done.17.refs_0_), channel_id=1, source_target_pairs={{0,4},{4,8},{8,12},{12,14},{14,10},{10,6},{6,2},{2,0},{1,5},{5,9},... | collective-permute-start | bytes 835592 | tf_op jit(solution)/shard_map/ppermute | solution.py:466
  55.6 7.8 %collective-permute-start.23 = (bf16[64,2176]{1,0:T(8,128)(2,1)S(1)}, bf16[64,2176]{1,0:T(8,128)(2,1)S(1)}, u32[]{:S(2)}, u32[]{:S(2)}) collective-permute-start(bf16[64,2176]{1,0:T(8,128)(2,1)S(1)} %collective-permute-done.21.refs_1_), channel_id=1, source_target_pairs={{4,0},{8,4},{12,8},{14,12},{10,14},{6,10},{2,6},{0,2},{5,1},{9,5},... | collective-permute-start | bytes 835592 | tf_op jit(solution)/shard_map/ppermute | solution.py:467
  62.8 7.0 %collective-permute-start.22 = (bf16[64,2176]{1,0:T(8,128)(2,1)S(1)}, bf16[64,2176]{1,0:T(8,128)(2,1)S(1)}, u32[]{:S(2)}, u32[]{:S(2)}) collective-permute-start(bf16[64,2176]{1,0:T(8,128)(2,1)S(1)} %collective-permute-done.20.refs_0_), channel_id=1, source_target_pairs={{0,4},{4,8},{8,12},{12,14},{14,10},{10,6},{6,2},{2,0},{1,5},{5,9},... | collective-permute-start | bytes 835592 | tf_op jit(solution)/shard_map/ppermute | solution.py:466
  63.4 6.9 %collective-permute-start.25 = (bf16[64,2176]{1,0:T(8,128)(2,1)S(1)}, bf16[64,2176]{1,0:T(8,128)(2,1)S(1)}, u32[]{:S(2)}, u32[]{:S(2)}) collective-permute-start(bf16[64,2176]{1,0:T(8,128)(2,1)S(1)} %collective-permute-done.23.refs_1_), channel_id=1, source_target_pairs={{4,0},{8,4},{12,8},{14,12},{10,14},{6,10},{2,6},{0,2},{5,1},{9,5},... | collective-permute-start | bytes 835592 | tf_op jit(solution)/shard_map/ppermute | solution.py:467
  69.8 5.1 %collective-permute-start.24 = (bf16[32,2176]{1,0:T(8,128)(2,1)S(1)}, bf16[32,2176]{1,0:T(8,128)(2,1)S(1)}, u32[]{:S(2)}, u32[]{:S(2)}) collective-permute-start(bf16[32,2176]{1,0:T(8,128)(2,1)S(1)} %slice.32), channel_id=1, source_target_pairs={{0,4},{4,8},{8,12},{12,14},{14,10},{10,6},{6,2},{2,0},{1,5},{5,9},... | collective-permute-start | bytes 417800 | tf_op jit(solution)/shard_map/ppermute | solution.py:466
  70.3 5.1 %collective-permute-start.26 = (bf16[32,2176]{1,0:T(8,128)(2,1)S(1)}, bf16[32,2176]{1,0:T(8,128)(2,1)S(1)}, u32[]{:S(2)}, u32[]{:S(2)}) collective-permute-start(bf16[32,2176]{1,0:T(8,128)(2,1)S(1)} %slice.42), channel_id=1, source_target_pairs={{4,0},{8,4},{12,8},{14,12},{10,14},{6,10},{2,6},{0,2},{5,1},{9,5},... | collective-permute-start | bytes 417800 | tf_op jit(solution)/shard_map/ppermute | solution.py:467
  77.0 6.4 %collective-permute-start.27 = (bf16[32,2048]{1,0:T(8,128)(2,1)S(1)}, bf16[32,2048]{1,0:T(8,128)(2,1)S(1)}, u32[]{:S(2)}, u32[]{:S(2)}) collective-permute-start(bf16[32,2048]{1,0:T(8,128)(2,1)S(1)} %get-tuple-element.108), channel_id=1, source_target_pairs={{4,0},{8,4},{12,8},{14,12},{10,14},{6,10},{2,6},{0,2},{5,1},{9,5},... | collective-permute-start | bytes 393224 | tf_op jit(solution)/shard_map/ppermute | solution.py:477
  78.7 6.3 %collective-permute-start.31 = (bf16[32,2048]{1,0:T(8,128)(2,1)S(1)}, bf16[32,2048]{1,0:T(8,128)(2,1)S(1)}, u32[]{:S(2)}, u32[]{:S(2)}) collective-permute-start(bf16[32,2048]{1,0:T(8,128)(2,1)S(1)} %get-tuple-element.107), channel_id=1, source_target_pairs={{0,4},{4,8},{8,12},{12,14},{14,10},{10,6},{6,2},{2,0},{1,5},{5,9},... | collective-permute-start | bytes 393224 | tf_op jit(solution)/shard_map/ppermute | solution.py:478
  85.1 9.2 %collective-permute-start.28 = (bf16[64,2048]{1,0:T(8,128)(2,1)S(1)}, bf16[64,2048]{1,0:T(8,128)(2,1)S(1)}, u32[]{:S(2)}, u32[]{:S(2)}) collective-permute-start(bf16[64,2048]{1,0:T(8,128)(2,1)S(1)} %get-tuple-element.106), channel_id=1, source_target_pairs={{4,0},{8,4},{12,8},{14,12},{10,14},{6,10},{2,6},{0,2},{5,1},{9,5},... | collective-permute-start | bytes 786440 | tf_op jit(solution)/shard_map/ppermute | solution.py:477
  86.7 7.9 %collective-permute-start.32 = (bf16[64,2048]{1,0:T(8,128)(2,1)S(1)}, bf16[64,2048]{1,0:T(8,128)(2,1)S(1)}, u32[]{:S(2)}, u32[]{:S(2)}) collective-permute-start(bf16[64,2048]{1,0:T(8,128)(2,1)S(1)} %get-tuple-element.105), channel_id=1, source_target_pairs={{0,4},{4,8},{8,12},{12,14},{14,10},{10,6},{6,2},{2,0},{1,5},{5,9},... | collective-permute-start | bytes 786440 | tf_op jit(solution)/shard_map/ppermute | solution.py:478
  94.7 8.1 %collective-permute-start.29 = (bf16[64,2048]{1,0:T(8,128)(2,1)S(1)}, bf16[64,2048]{1,0:T(8,128)(2,1)S(1)}, u32[]{:S(2)}, u32[]{:S(2)}) collective-permute-start(bf16[64,2048]{1,0:T(8,128)(2,1)S(1)} %get-tuple-element.104), channel_id=1, source_target_pairs={{4,0},{8,4},{12,8},{14,12},{10,14},{6,10},{2,6},{0,2},{5,1},{9,5},... | collective-permute-start | bytes 786440 | tf_op jit(solution)/shard_map/ppermute | solution.py:477
  95.2 7.6 %collective-permute-start.33 = (bf16[64,2048]{1,0:T(8,128)(2,1)S(1)}, bf16[64,2048]{1,0:T(8,128)(2,1)S(1)}, u32[]{:S(2)}, u32[]{:S(2)}) collective-permute-start(bf16[64,2048]{1,0:T(8,128)(2,1)S(1)} %get-tuple-element.103), channel_id=1, source_target_pairs={{0,4},{4,8},{8,12},{12,14},{14,10},{10,6},{6,2},{2,0},{1,5},{5,9},... | collective-permute-start | bytes 786440 | tf_op jit(solution)/shard_map/ppermute | solution.py:478
  102.9 6.4 %collective-permute-start.30 = (bf16[64,2048]{1,0:T(8,128)(2,1)S(1)}, bf16[64,2048]{1,0:T(8,128)(2,1)S(1)}, u32[]{:S(2)}, u32[]{:S(2)}) collective-permute-start(bf16[64,2048]{1,0:T(8,128)(2,1)S(1)} %get-tuple-element.102), channel_id=1, source_target_pairs={{4,0},{8,4},{12,8},{14,12},{10,14},{6,10},{2,6},{0,2},{5,1},{9,5},... | collective-permute-start | bytes 786440 | tf_op jit(solution)/shard_map/ppermute | solution.py:477
  103.2 6.4 %collective-permute-start.34 = (bf16[64,2048]{1,0:T(8,128)(2,1)S(1)}, bf16[64,2048]{1,0:T(8,128)(2,1)S(1)}, u32[]{:S(2)}, u32[]{:S(2)}) collective-permute-start(bf16[64,2048]{1,0:T(8,128)(2,1)S(1)} %get-tuple-element.101), channel_id=1, source_target_pairs={{0,4},{4,8},{8,12},{12,14},{14,10},{10,6},{6,2},{2,0},{1,5},{5,9},... | collective-permute-start | bytes 786440 | tf_op jit(solution)/shard_map/ppermute | solution.py:478
  (17 other events, 73.0 us)

commit v4 on v3

--- a/solution.py
+++ b/solution.py
@@ -65,45 +65,24 @@
     group_width = QH // KVH
     rows = cache_rows + new_rows + MASK_ROWS
 
-    def kernel(page_ref, ck_ref, cv_ref, nk_ref, nv_ref, *refs):
-        out_refs, (mask_ref, sems) = refs[:kv_heads], refs[kv_heads:]
+    def kernel(page_ref, ck_ref, cv_ref, nk_ref, nv_ref, *out_refs):
         first = lax.axis_index("hd") * heads_here // group_width
-        copies = []
+        lane = lax.broadcasted_iota(jnp.int32, (MASK_ROWS, 2 * HD), 1)
+        bias = jnp.where(lane < page_ref[0], 0.0, NEG_FILL).astype(jnp.bfloat16)
         for kv, out_ref in enumerate(out_refs):
             columns = pl.ds(pl.multiple_of((first + kv) * HD, HD), HD)
-            cached, new = pl.ds(0, cache_rows), pl.ds(cache_rows, new_rows)
-            for i, (ref, here, lanes) in enumerate(
-                [(ck_ref, cached, 0), (cv_ref, cached, HD), (nk_ref, new, 0), (nv_ref, new, HD)]
-            ):
-                copies.append(
-                    pltpu.make_async_copy(
-                        ref.at[:, columns], out_ref.at[here, pl.ds(lanes, HD)], sems.at[kv, i]
-                    )
-                )
-                copies[-1].start()
-        lane = lax.broadcasted_iota(jnp.int32, (MASK_ROWS, 2 * HD), 1)
-        mask_ref[...] = jnp.where(lane < page_ref[0], 0.0, NEG_FILL).astype(jnp.bfloat16)
-        for kv, out_ref in enumerate(out_refs):
-            copies.append(
-                pltpu.make_async_copy(
-                    mask_ref, out_ref.at[pl.ds(cache_rows + new_rows, MASK_ROWS), :], sems.at[kv, 4]
-                )
-            )
-            copies[-1].start()
-        for copy in copies:
-            copy.wait()
-
-    anywhere = pl.BlockSpec(memory_space=pl.ANY)
+            out_ref[:cache_rows, :HD] = ck_ref[:, columns]
+            out_ref[:cache_rows, HD:] = cv_ref[:, columns]
+            out_ref[cache_rows : cache_rows + new_rows, :HD] = nk_ref[:, columns]
+            out_ref[cache_rows : cache_rows + new_rows, HD:] = nv_ref[:, columns]
+            out_ref[cache_rows + new_rows :, :] = bias
+
+    vmem = pl.BlockSpec(memory_space=pltpu.VMEM)
     return pl.pallas_call(
         kernel,
         out_shape=[jax.ShapeDtypeStruct((rows, 2 * HD), cache_keys.dtype)] * kv_heads,
-        in_specs=[pl.BlockSpec(memory_space=pltpu.SMEM)] + [anywhere] * 4,
-        out_specs=[anywhere] * kv_heads,
-        scratch_shapes=[
-            pltpu.VMEM((MASK_ROWS, 2 * HD), jnp.bfloat16),
-            pltpu.SemaphoreType.DMA((kv_heads, 5)),
-        ],
-        compiler_params=pltpu.CompilerParams(vmem_limit_bytes=4 * MIB),
+        in_specs=[pl.BlockSpec(memory_space=pltpu.SMEM)] + [vmem] * 4,
+        out_specs=[vmem] * kv_heads,
         name="pack_keys",
     )(page_len, cache_keys, cache_values, new_keys, new_values)
 
@@ -126,6 +105,35 @@
     return [parts[0]] + [
         lax.ppermute(part, "sub", cycle(size, step)) for step, part in enumerate(parts) if step
     ]
+
+
+def choose_queries(queries):
+    n_hd, n_sub, rows, columns = queries.shape
+
+    def kernel(in_ref, out_ref, sems):
+        sub = lax.axis_index("sub")
+        hd = lax.axis_index("hd")
+        copies = []
+        for j in range(n_hd):
+            place = (hd + j) % n_hd if n_hd == 2 else j
+            copies.append(
+                pltpu.make_async_copy(
+                    in_ref.at[place, sub], out_ref.at[pl.ds(j * rows, rows), :], sems.at[j]
+                )
+            )
+            copies[-1].start()
+        for copy in copies:
+            copy.wait()
+
+    return pl.pallas_call(
+        kernel,
+        out_shape=jax.ShapeDtypeStruct((n_hd * rows, columns), queries.dtype),
+        in_specs=[pl.BlockSpec(memory_space=pltpu.HBM)],
+        out_specs=pl.BlockSpec(memory_space=pltpu.VMEM),
+        scratch_shapes=[pltpu.SemaphoreType.DMA((n_hd,))],
+        compiler_params=pltpu.CompilerParams(vmem_limit_bytes=8 * MIB),
+        name="choose_queries",
+    )(queries)
 
 
 def split_rows(residual, n_sub):
@@ -162,9 +170,10 @@
     return small_kernel(kernel, [shape], [expert_ids.T, gates.T], "gates_by_expert")[0]
 
 
-def normalise(kept, came, residual_parts, gain, gate_table):
+def normalise(kept, came, residual_parts, gain, gate_table, first):
     n_sub = len(residual_parts)
-    rows, width = residual_parts[0].shape
+    rows, width = came.shape[0], residual_parts[0].shape[1]
+    chunk = slice(first, first + rows)
     features = n_sub * width
     extra = 0 if gate_table is None else LANES
 
@@ -184,7 +193,7 @@
             projected = came_ref[:, here].astype(jnp.float32)
             if kept is not None:
                 projected = kept_ref[:, here] + projected
-            value = (part_ref[...].astype(jnp.float32) + projected).astype(jnp.bfloat16)
+            value = (part_ref[chunk, :].astype(jnp.float32) + projected).astype(jnp.bfloat16)
             hidden.append(value)
             place = pl.ds(pl.multiple_of((sub - step) % n_sub * width, width), width)
             places.append(place)
@@ -196,7 +205,7 @@
             normed = value.astype(jnp.float32) * scale * gain_ref[:, place].astype(jnp.float32)
             normed_ref[:, place] = normed.astype(jnp.bfloat16)
         if extra:
-            normed_ref[:, features:] = gate_ref[...]
+            normed_ref[:, features:] = gate_ref[chunk, :]
 
     operands = ([kept] if kept is not None else []) + [came] + list(residual_parts)
     operands.append(gain.reshape(1, features))
@@ -210,20 +219,25 @@
 
 
 def add_up(hidden, mine, to_back, to_ahead, n_sub):
-    rows, features = hidden.shape
+    chunks = len(hidden)
+    rows, features = hidden[0].shape
     width = features // n_sub
 
-    def kernel(hidden_ref, mine_ref, back_ref, ahead_ref, *out_refs):
+    def kernel(*refs):
+        terms, out_refs = refs[: 4 * chunks], refs[4 * chunks :]
         sub = lax.axis_index("sub")
         for step, out_ref in enumerate(out_refs):
             place = pl.ds(pl.multiple_of((sub + step) % n_sub * width, width), width)
-            mixture = mine_ref[:, place] + back_ref[:, place].astype(jnp.float32)
-            mixture = mixture + ahead_ref[:, place].astype(jnp.float32)
-            total = hidden_ref[:, place].astype(jnp.float32) + mixture
-            out_ref[...] = total.astype(jnp.bfloat16)
-
-    shape = jax.ShapeDtypeStruct((rows, width), jnp.bfloat16)
-    return small_kernel(kernel, [shape] * n_sub, [hidden, mine, to_back, to_ahead], "add_up")
+            for chunk in range(chunks):
+                hidden_ref, mine_ref, back_ref, ahead_ref = terms[chunk::chunks]
+                mixture = mine_ref[:, place] + back_ref[:, place].astype(jnp.float32)
+                mixture = mixture + ahead_ref[:, place].astype(jnp.float32)
+                total = hidden_ref[:, place].astype(jnp.float32) + mixture
+                out_ref[chunk * rows : (chunk + 1) * rows, :] = total.astype(jnp.bfloat16)
+
+    shape = jax.ShapeDtypeStruct((chunks * rows, width), jnp.bfloat16)
+    operands = [*hidden, *mine, *to_back, *to_ahead]
+    return small_kernel(kernel, [shape] * n_sub, operands, "add_up")
 
 
 def stack_rows(parts):
@@ -240,11 +254,11 @@
     return small_kernel(kernel, [shape], parts, "stack_rows")[0]
 
 
-def attend(queries, kv, hop, blocks, state, cache_rows, kv_heads, finish=None):
-    n_hd, n_sub, rows, columns = queries.shape
+def attend(queries, kv, hop, blocks, state, cache_rows, kv_heads, n_hd, chunks, finish=None):
+    all_rows, columns = queries.shape
+    rows, n_sub = all_rows // n_hd, len(blocks)
     per_kv = columns // HD // kv_heads
     stack = 2 if per_kv % 2 == 0 else 1
-    all_rows = n_hd * rows
     part = stack * all_rows
     new_rows = blocks[0].shape[0] - cache_rows - MASK_ROWS
     keys = cache_rows + new_rows
@@ -255,6 +269,7 @@
     head_columns = per_kv * HD
     final = last and kv == kv_heads - 1
     kept_rows = rows if relative else 0
+    chunk_rows = rows // chunks if relative else all_rows
 
     def kernel(*refs):
         q_ref, refs = refs[0], refs[1:]
@@ -265,7 +280,7 @@
         if earlier is not None:
             earlier_ref, refs = refs[0], refs[1:]
         if last:
-            results = 1 + (kept_rows > 0 and final)
+            results = len(out_shape)
             result_refs, refs = refs[:results], refs[results:]
             head_ref, refs = refs[0], refs[1:]
             held_refs, sems = refs[: len(weights)], refs[len(weights)]
@@ -312,9 +327,7 @@
         for index in range(per_kv // stack):
             here = slice(index * part, (index + 1) * part)
             heads = range(kv * per_kv + index * stack, kv * per_kv + (index + 1) * stack)
-            q = jnp.concatenate(
-                [q_ref[p, sub, :, h * HD : (h + 1) * HD] for h in heads for p in places], axis=0
-            )
+            q = jnp.concatenate([q_ref[:, h * HD : (h + 1) * HD] for h in heads], axis=0)
             terms = [
                 lax.dot_general(q, k, CONTRACT_LAST, preferred_element_type=jnp.float32) * factor
                 + bias
@@ -353,9 +366,9 @@
                 if earlier is not None:
                     product = product + earlier_ref[:, here]
                 if final:
-                    result_refs[-1][:, here] = product[kept_rows:].astype(jnp.bfloat16)
-                    if kept_rows:
-                        result_refs[0][:, here] = product[:kept_rows]
+                    for j, result_ref in enumerate(result_refs):
+                        share = product[j * chunk_rows : (j + 1) * chunk_rows]
+                        result_ref[:, here] = share.astype(result_ref.dtype)
                 else:
                     result_refs[0][:, here] = product
 
@@ -365,10 +378,14 @@
     if last:
         features = sum(w.shape[1] for w in weights)
         if final:
-            out_shape = (
-                jax.ShapeDtypeStruct((kept_rows, features), jnp.float32),
-                jax.ShapeDtypeStruct((all_rows - kept_rows, features), jnp.bfloat16),
-            )[0 if kept_rows else 1 :]
+            out_shape = [
+                jax.ShapeDtypeStruct((chunk_rows, features), kind)
+                for kind, count in [
+                    (jnp.float32, kept_rows // chunk_rows),
+                    (jnp.bfloat16, (all_rows - kept_rows) // chunk_rows),
+                ]
+                for _ in range(count)
+            ]
         else:
             out_shape = (jax.ShapeDtypeStruct((all_rows, features), jnp.float32),)
         scratch = [pltpu.VMEM((all_rows, head_columns), jnp.bfloat16)]
@@ -408,7 +425,7 @@
     def kernel(*refs):
         x_refs, refs = refs[: len(inputs)], refs[len(inputs) :]
         gu_refs, refs = refs[: len(gate_up)], refs[len(gate_up) :]
-        down_refs, (out_ref,) = refs[: len(w_down)], refs[len(w_down) :]
+        down_refs, out_refs = refs[: len(w_down)], refs[len(w_down) :]
         mine = lax.axis_index("ep") * lax.axis_size("hd") + lax.axis_index("hd")
         joined = jnp.concatenate([x[...] for x in x_refs], axis=0)
         x = joined[:, :features]
@@ -424,15 +441,19 @@
             activation = (gate_part / (1.0 + jnp.exp(-gate_part)) * up_part).astype(jnp.bfloat16)
             product = jnp.dot(activation, down[...], preferred_element_type=jnp.float32)
             total = product if total is None else total + product
-        out_ref[...] = gate * total.astype(jnp.bfloat16).astype(jnp.float32)
+        total = gate * total.astype(jnp.bfloat16).astype(jnp.float32)
+        first = 0
+        for out_ref in out_refs:
+            out_ref[...] = total[first : first + out_ref.shape[0]]
+            first += out_ref.shape[0]
 
     vmem = pl.BlockSpec(memory_space=pltpu.VMEM)
     operands = list(inputs) + list(gate_up) + list(w_down)
     return pl.pallas_call(
         kernel,
-        out_shape=jax.ShapeDtypeStruct((rows, features), jnp.float32),
+        out_shape=[jax.ShapeDtypeStruct((x.shape[0], features), jnp.float32) for x in inputs],
         in_specs=[vmem] * len(operands),
-        out_specs=vmem,
+        out_specs=[vmem] * len(inputs),
         compiler_params=pltpu.CompilerParams(vmem_limit_bytes=16 * MIB),
         cost_estimate=pl.CostEstimate(
             flops=6 * rows * hidden * len(w_down) * features,
@@ -449,43 +470,55 @@
     return list(range(n_ep * n_hd))
 
 
+def add_share(came, share):
+    def kernel(came_ref, share_ref, out_ref):
+        total = came_ref[...].astype(jnp.float32) + share_ref[...]
+        out_ref[...] = total.astype(jnp.bfloat16)
+
+    shape = jax.ShapeDtypeStruct(share.shape, jnp.bfloat16)
+    return small_kernel(kernel, [shape], [came, share], "add_share")[0]
+
+
 def dense_experts(own, gate_up, w_down):
     axes = ("ep", "hd")
     walk = chip_ring(lax.axis_size("ep"), lax.axis_size("hd"))
     size = len(walk)
     ahead = [(walk[i], walk[(i + 1) % size]) for i in range(size)]
     back = [(b, a) for a, b in ahead]
-    rows, features = own.shape[0], w_down[0].shape[1]
-    half = rows // 2
     reach = size // 2
-    behind, before, waiting = own, own, [own]
-    outs = []
+    behind, before, waiting = list(own), list(own), None
+    outs = [None]
     for hop in range(1, reach + 1):
-        if hop == reach:
-            behind, before = behind[:half], before[half:]
-        behind = lax.ppermute(behind, axes, ahead)
-        before = lax.ppermute(before, axes, back)
-        out = apply_expert(waiting, gate_up, w_down)
-        behind, out = lax.optimization_barrier((behind, out))
-        outs.append(out)
-        waiting = [behind, before]
+        behind[0] = lax.ppermute(behind[0], axes, ahead)
+        before[1] = lax.ppermute(before[1], axes, back)
+        if hop < reach:
+            behind[1] = lax.ppermute(behind[1], axes, ahead)
+            before[0] = lax.ppermute(before[0], axes, back)
+        if waiting:
+            out = apply_expert(waiting, gate_up, w_down)
+            behind[0], out = lax.optimization_barrier((behind[0], out))
+            outs.append(out)
+        waiting = [behind[0], before[1]] + ([behind[1], before[0]] if hop < reach else [])
     outs.append(apply_expert(waiting, gate_up, w_down))
-    mine = outs[0]
-    outs = [(x[: x.shape[0] // 2], x[x.shape[0] // 2 :]) for x in outs[1:]]
-    to_back, to_ahead = [x.astype(jnp.bfloat16) for x in outs[-1]]
-    for hop in range(reach - 1, -1, -1):
-        to_back = lax.ppermute(to_back, axes, back)
-        to_ahead = lax.ppermute(to_ahead, axes, ahead)
-        if hop == 0:
-            break
-        sums = []
-        for came, first, share in [(to_back, 0, outs[hop - 1][0]), (to_ahead, half, outs[hop - 1][1])]:
-            came = came.astype(jnp.float32)
-            if hop == reach - 1:
-                came = jnp.pad(came, ((first, rows - half - first), (0, 0)))
-            sums.append(lax.optimization_barrier((came + share).astype(jnp.bfloat16)))
-        to_back, to_ahead = sums
-    return mine, to_back, to_ahead
+    to_back, to_ahead = [None, None], [None, None]
+    for hop in range(reach, 0, -1):
+        shares = outs[hop]
+        for chunks, chunk, way, share in [
+            (to_back, 0, back, 0),
+            (to_ahead, 1, ahead, 1),
+            (to_back, 1, back, 2),
+            (to_ahead, 0, ahead, 3),
+        ]:
+            if share >= len(shares):
+                continue
+            if chunks[chunk] is None:
+                sum_here = shares[share].astype(jnp.bfloat16)
+            else:
+                sum_here = add_share(chunks[chunk], shares[share])
+            chunks[chunk] = lax.ppermute(sum_here, axes, way)
+            if hop == min(2, reach) and share == 0:
+                chunks[chunk], own = lax.optimization_barrier((chunks[chunk], own))
+    return apply_expert(own, gate_up, w_down), to_back, to_ahead
 
 
 def sparse_experts(widened, normed, gate_up, w_down, expert_ids, gates, features):
@@ -572,43 +605,67 @@
         and rows % 32 == 0
     )
 
+    projections = sub_copies(out_proj)
     packed = pack_keys(
         cache_keys, cache_values, new_keys, new_values, page_len, kv_heads, heads_here
     )
-    query_blocks = queries.reshape(n_hd, n_sub, rows, heads_here * HD)
-    projections = sub_copies(out_proj)
-    residual_parts = hand_over(split_rows(residual, n_sub))
-    gate_table = gates_by_expert(expert_ids, gates, rows) if dense else None
-    if dense:
-        gate_up_parts = sub_copies(gate_up[0])
-        w_down_parts = sub_copies(w_down[0])
+    query_rows_here = choose_queries(queries.reshape(n_hd, n_sub, rows, heads_here * HD))
     travelling = list(packed)
     states = [None] * kv_heads
     earlier = None
     for hop in range(n_ep):
         blocks = [sub_copies(x) for x in travelling]
         onward = [lax.ppermute(x, "ep", cycle(n_ep)) for x in travelling] if hop < n_ep - 1 else []
+        if hop == min(2, n_ep - 1):
+            residual, gate_up, w_down, blocks = lax.optimization_barrier(
+                (residual, gate_up, w_down, blocks)
+            )
+            residual_parts = hand_over(split_rows(residual, n_sub))
+            gate_table = gates_by_expert(expert_ids, gates, rows) if dense else None
+            if dense:
+                gate_up_parts = sub_copies(gate_up[0])
+                w_down_parts = sub_copies(w_down[0])
         for kv in range(kv_heads):
             finish = (projections, earlier) if hop == n_ep - 1 else None
             states[kv] = attend(
-                query_blocks, kv, hop, blocks[kv], states[kv], cache_rows, kv_heads, finish
+                query_rows_here,
+                kv,
+                hop,
+                blocks[kv],
+                states[kv],
+                cache_rows,
+                kv_heads,
+                n_hd,
+                2 if dense else 1,
+                finish,
             )
             if finish:
                 earlier = states[kv][0]
             else:
                 onward[kv], states[kv] = lax.optimization_barrier((onward[kv], states[kv]))
         travelling = onward
-    sent = states[-1][-1]
+    parts = states[-1]
     if n_hd == 2:
-        came = lax.ppermute(sent, "hd", cycle(n_hd))
+        kept, sent = parts[: len(parts) // 2], parts[len(parts) // 2 :]
+        came = [lax.ppermute(x, "hd", cycle(n_hd)) for x in sent]
     else:
-        came = lax.psum_scatter(sent, "hd", scatter_dimension=0, tiled=True)
-    hidden, normed = normalise(
-        earlier if n_hd == 2 else None, came, residual_parts, norm_gain, gate_table
-    )
+        kept = [None]
+        came = [lax.psum_scatter(parts[0], "hd", scatter_dimension=0, tiled=True)]
+    hidden, normed = [], []
+    for index, (kept_chunk, came_chunk) in enumerate(zip(kept, came)):
+        pair = normalise(
+            kept_chunk,
+            came_chunk,
+            residual_parts,
+            norm_gain,
+            gate_table,
+            index * came_chunk.shape[0],
+        )
+        hidden.append(pair[0])
+        normed.append(pair[1])
     if not dense:
         own_columns = [
-            jnp.concatenate(by_sub(sub_exchange(x, 1)), axis=0) for x in (hidden, normed)
+            jnp.concatenate(by_sub(sub_exchange(x, 1)), axis=0) for x in (hidden[0], normed[0])
         ]
         return sparse_experts(
             own_columns[0].astype(jnp.float32),

time: 112 us -> 103 us (0.920)
  waiting for transfers between devices: 59.5 us -> 35.8 us
  starting transfers between devices: 25.6 us -> 39.2 us
  Pallas kernels: 19.3 us -> 23 us
  local copies, waits for them, and re-layouts: 6.14 us -> 3.23 us
    ppermute x17 -> x30, waiting for transfers between devices: 43.5 us -> 17.9 us  [the longest x2 6.55 us: shards(): came = [lax.ppermute(x, 'hd', cycle(n_hd)) for x in sent]]
    ppermute x17 -> x30, starting transfers between devices: 18.4 us -> 31 us  [the longest x14 14.9 us: dense_experts(): chunks[chunk] = lax.ppermute(sum_here, axes, way)]
    unnamed x26 -> x20, local copies, waits for them, and re-layouts: 6.1 us -> 3.23 us
    pallas_call x1, Pallas kernels: 0.18 us -> 1.84 us  [pack_keys(): pl.pallas_call(kernel, out_shape=[jax.ShapeDtypeStruct((rows, 2 * HD), ca...]
    pallas_call x8, Pallas kernels: 10.3 us -> 11.8 us  [attend(): pl.pallas_call(kernel, out_shape=out_shape, in_specs=in_specs, out_specs=...]
    ppermute x6, waiting for transfers between devices: 13.7 us -> 15.1 us  [shards(): lax.ppermute(x, 'ep', cycle(n_ep))]
    ppermute x11, waiting for transfers between devices: 0.03 us -> 1.38 us  [sub_copies(): lax.ppermute(x, 'sub', cycle(size, step))]
    ppermute x6, starting transfers between devices: 5.05 us -> 6.37 us  [shards(): lax.ppermute(x, 'ep', cycle(n_ep))]
  transfers between devices with their start and end apart: 36 -> 49, of which waited for: 22 -> 22; matrix products, arithmetic and copies ran while one was open for 0% -> 0% of each run, Pallas kernels for 15% -> 20%
where the time goes in v4:
time: 103 us; the launch traced here: 102 us
  starting transfers between devices  39.2 us (38%)
  waiting for transfers between devices  35.8 us (35%)
  Pallas kernels  23 us (22%)
  local copies, waits for them, and re-layouts  3.23 us (3%)
  between operations  1.1 us (1%)
    ppermute x6, waiting for transfers between devices, shards(): lax.ppermute(x, 'ep', cycle(n_ep))  15.1 us
    ppermute x14, starting transfers between devices, dense_experts(): chunks[chunk] = lax.ppermute(sum_here, axes, way)  14.9 us
    pallas_call x8, Pallas kernels, attend(): pl.pallas_call(kernel, out_shape=out_shape, in_specs=in_specs, out_specs=...  11.8 us
    pallas_call x5, Pallas kernels, apply_expert(): pl.pallas_call(kernel, out_shape=[jax.ShapeDtypeStruct((x.shape[0], featu...  7.7 us
    ppermute x2, waiting for transfers between devices, shards(): came = [lax.ppermute(x, 'hd', cycle(n_hd)) for x in sent]  6.55 us
    ppermute x6, starting transfers between devices, shards(): lax.ppermute(x, 'ep', cycle(n_ep))  6.37 us
    ppermute x4, starting transfers between devices, dense_experts(): before[1] = lax.ppermute(before[1], axes, back)  5.96 us
    ppermute x14, waiting for transfers between devices, dense_experts(): chunks[chunk] = lax.ppermute(sum_here, axes, way)  5.76 us
  transfers between devices with their start and end apart: 49, of which 22 were waited for; matrix products, arithmetic and copies ran while one was open for 0% of the time, Pallas kernels for 20%

profile of v4, /device:TPU:0, one launch (start us, length us, event | category | flops | bytes accessed | tf_op | source)
XLA Modules:
  0.0 102.4 jit_solution(7163641984672205587)
XLA Ops:
  1.1 1.8 %pack_keys.1 = (bf16[272,256]{1,0:T(8,128)(2,1)}, bf16[272,256]{1,0:T(8,128)(2,1)}) custom-call(s32[1]{0:T(128)S(6)} %copy.14.page_ref, bf16[128,512]{1,0:T(8,128)(2,1)} %ck_ref.1, bf16[128,512]{1,0:T(8,128)(2,1)} %cv_ref.1, bf16[128,512]{1,0:T(8,128)(2,1)} %nk_ref.1, bf16[128,512]{1,0:T(8,128)(2,1)} %nv_ref.1), custom_call_target="tpu_custom_call" | custom-call | tf_op jit(solution)/shard_map/pack_keys/pallas_call | solution.py:81
  3.0 3.0 %collective-permute-start.5 = (bf16[272,256]{1,0:T(8,128)(2,1)}, bf16[272,256]{1,0:T(8,128)(2,1)S(1)}, u32[]{:S(2)}, u32[]{:S(2)}) collective-permute-start(bf16[272,256]{1,0:T(8,128)(2,1)} %get-tuple-element.99.refs_1_), channel_id=1, source_target_pairs={{0,4},{4,8},{8,12},{12,0},{1,5},{5,9},{9,13},{13,1},{2,6},{6,10},{... | collective-permute-start | bytes 417800 | tf_op jit(solution)/shard_map/ppermute | solution.py:618
  6.0 1.6 %collective-permute-start = (bf16[272,256]{1,0:T(8,128)(2,1)}, bf16[272,256]{1,0:T(8,128)(2,1)S(1)}, u32[]{:S(2)}, u32[]{:S(2)}) collective-permute-start(bf16[272,256]{1,0:T(8,128)(2,1)} %get-tuple-element.90.refs_1_), channel_id=1, source_target_pairs={{0,4},{4,8},{8,12},{12,0},{1,5},{5,9},{9,13},{13,1},{2,6},{6,10},{... | collective-permute-start | bytes 417800 | tf_op jit(solution)/shard_map/ppermute | solution.py:618
  11.0 1.8 %collective-permute-done.5.refs_1_ = bf16[272,256]{1,0:T(8,128)(2,1)S(1)} collective-permute-done((bf16[272,256]{1,0:T(8,128)(2,1)}, bf16[272,256]{1,0:T(8,128)(2,1)S(1)}, u32[]{:S(2)}, u32[]{:S(2)}) %collective-permute-start.5) | collective-permute-done | bytes 139296 | tf_op jit(solution)/shard_map/ppermute | solution.py:618
  17.6 3.5 %collective-permute-done.7.refs_1_ = bf16[272,256]{1,0:T(8,128)(2,1)S(1)} collective-permute-done((bf16[272,256]{1,0:T(8,128)(2,1)S(1)}, bf16[272,256]{1,0:T(8,128)(2,1)S(1)}, u32[]{:S(2)}, u32[]{:S(2)}) %collective-permute-start.7) | collective-permute-done | bytes 139296 | tf_op jit(solution)/shard_map/ppermute | solution.py:618
  22.1 1.6 %collective-permute-done.2.refs_1_ = bf16[272,256]{1,0:T(8,128)(2,1)S(1)} collective-permute-done((bf16[272,256]{1,0:T(8,128)(2,1)S(1)}, bf16[272,256]{1,0:T(8,128)(2,1)S(1)}, u32[]{:S(2)}, u32[]{:S(2)}) %collective-permute-start.2) | collective-permute-done | bytes 139296 | tf_op jit(solution)/shard_map/ppermute | solution.py:618
  26.9 6.9 %collective-permute-done.13.refs_1_ = bf16[272,256]{1,0:T(8,128)(2,1)S(1)} collective-permute-done((bf16[272,256]{1,0:T(8,128)(2,1)S(1)}, bf16[272,256]{1,0:T(8,128)(2,1)S(1)}, u32[]{:S(2)}, u32[]{:S(2)}) %collective-permute-start.13) | collective-permute-done | bytes 139296 | tf_op jit(solution)/shard_map/ppermute | solution.py:618
  36.6 2.5 %attend.14.refs_7_ = f32[128,2048]{1,0:T(8,128)S(1)} custom-call(bf16[128,2048]{1,0:T(8,128)(2,1)S(1)} %choose_queries.1.refs_0_, bf16[272,256]{1,0:T(8,128)(2,1)S(1)} %collective-permute-done.13.refs_1_, bf16[272,256]{1,0:T(8,128)(2,1)S(1)} %collective-permute-done.14.refs_2_, f32[1024,128]{1,0:T(8,128)S(1)} %get-tuple-element.124.refs_3_, ...), custom_call_target="tpu_custom_call" | custom-call | flops 402653184 | bytes 4194304 | tf_op jit(solution)/shard_map/attend/pallas_call | solution.py:406
  39.2 3.2 %attend.15 = (f32[32,2048]{1,0:T(8,128)S(1)}, f32[32,2048]{1,0:T(8,128)S(1)}, bf16[32,2048]{1,0:T(8,128)(2,1)S(1)}, bf16[32,2048]{1,0:T(8,128)(2,1)S(1)}) custom-call(bf16[128,2048]{1,0:T(8,128)(2,1)S(1)} %choose_queries.1.refs_0_, bf16[272,256]{1,0:T(8,128)(2,1)S(1)} %collective-permute-done.4.refs_1_, ...), custom_call_target="tpu_custom_call" | custom-call | flops 402653184 | bytes 4194304 | tf_op jit(solution)/shard_map/attend/pallas_call | solution.py:406
  42.4 1.8 %collective-permute-start.15 = (bf16[32,2048]{1,0:T(8,128)(2,1)S(1)}, bf16[32,2048]{1,0:T(8,128)(2,1)S(1)}, u32[]{:S(2)}, u32[]{:S(2)}) collective-permute-start(bf16[32,2048]{1,0:T(8,128)(2,1)S(1)} %get-tuple-element.127), channel_id=1, source_target_pairs={{0,2},{2,0},{1,3},{3,1},{4,6},{6,4},{5,7},{7,5},{8,10},{10,8},{9,1... | collective-permute-start | bytes 393224 | tf_op jit(solution)/shard_map/ppermute | solution.py:650
  44.7 4.2 %collective-permute-done.15.refs_1_ = bf16[32,2048]{1,0:T(8,128)(2,1)S(1)} collective-permute-done((bf16[32,2048]{1,0:T(8,128)(2,1)S(1)}, bf16[32,2048]{1,0:T(8,128)(2,1)S(1)}, u32[]{:S(2)}, u32[]{:S(2)}) %collective-permute-start.15) | collective-permute-done | bytes 131104 | tf_op jit(solution)/shard_map/ppermute | solution.py:650
  49.1 2.4 %collective-permute-done.17.refs_1_ = bf16[32,2048]{1,0:T(8,128)(2,1)S(1)} collective-permute-done((bf16[32,2048]{1,0:T(8,128)(2,1)S(1)}, bf16[32,2048]{1,0:T(8,128)(2,1)S(1)}, u32[]{:S(2)}, u32[]{:S(2)}) %collective-permute-start.17) | collective-permute-done | bytes 131104 | tf_op jit(solution)/shard_map/ppermute | solution.py:650
  55.8 1.8 %collective-permute-done.20.refs_1_ = bf16[32,2176]{1,0:T(8,128)(2,1)S(1)} collective-permute-done((bf16[32,2176]{1,0:T(8,128)(2,1)S(1)}, bf16[32,2176]{1,0:T(8,128)(2,1)S(1)}, u32[]{:S(2)}, u32[]{:S(2)}) %collective-permute-start.20) | collective-permute-done | bytes 139296 | tf_op jit(solution)/shard_map/ppermute | solution.py:493
  57.5 1.6 %collective-permute-start.26 = (bf16[32,2176]{1,0:T(8,128)(2,1)S(1)}, bf16[32,2176]{1,0:T(8,128)(2,1)S(1)}, u32[]{:S(2)}, u32[]{:S(2)}) collective-permute-start(bf16[32,2176]{1,0:T(8,128)(2,1)S(1)} %collective-permute-done.20.refs_1_), channel_id=1, source_target_pairs={{4,0},{8,4},{12,8},{14,12},{10,14},{6,10},{2,6},{0,2},{5,1},{9,5},... | collective-permute-start | bytes 417800 | tf_op jit(solution)/shard_map/ppermute | solution.py:493
  60.5 1.6 %collective-permute-start.28 = (bf16[32,2176]{1,0:T(8,128)(2,1)S(1)}, bf16[32,2176]{1,0:T(8,128)(2,1)S(1)}, u32[]{:S(2)}, u32[]{:S(2)}) collective-permute-start(bf16[32,2176]{1,0:T(8,128)(2,1)S(1)} %collective-permute-done.22.refs_3_), channel_id=1, source_target_pairs={{4,0},{8,4},{12,8},{14,12},{10,14},{6,10},{2,6},{0,2},{5,1},{9,5},... | collective-permute-start | bytes 417800 | tf_op jit(solution)/shard_map/ppermute | solution.py:496
  62.1 1.6 %apply_expert.5 = (f32[32,2048]{1,0:T(8,128)S(1)}, f32[32,2048]{1,0:T(8,128)S(1)}, f32[32,2048]{1,0:T(8,128)S(1)}, f32[32,2048]{1,0:T(8,128)S(1)}) custom-call(bf16[32,2176]{1,0:T(8,128)(2,1)S(1)} %collective-permute-done.18.refs_0_, bf16[32,2176]{1,0:T(8,128)(2,1)S(1)} %collective-permute-done.20.refs_1_, ...), custom_call_target="tpu_custom_call" | custom-call | flops 603979776 | bytes 6291456 | tf_op jit(solution)/shard_map/apply_expert/pallas_call | solution.py:452
  64.2 1.6 %collective-permute-start.30 = (bf16[32,2176]{1,0:T(8,128)(2,1)S(1)}, bf16[32,2176]{1,0:T(8,128)(2,1)S(1)}, u32[]{:S(2)}, u32[]{:S(2)}) collective-permute-start(bf16[32,2176]{1,0:T(8,128)(2,1)S(1)} %collective-permute-done.26.refs_1_), channel_id=1, source_target_pairs={{4,0},{8,4},{12,8},{14,12},{10,14},{6,10},{2,6},{0,2},{5,1},{9,5},... | collective-permute-start | bytes 417800 | tf_op jit(solution)/shard_map/ppermute | solution.py:493
  67.1 1.6 %collective-permute-start.32 = (bf16[32,2176]{1,0:T(8,128)(2,1)S(1)}, bf16[32,2176]{1,0:T(8,128)(2,1)S(1)}, u32[]{:S(2)}, u32[]{:S(2)}) collective-permute-start(bf16[32,2176]{1,0:T(8,128)(2,1)S(1)} %collective-permute-done.28.refs_3_), channel_id=1, source_target_pairs={{4,0},{8,4},{12,8},{14,12},{10,14},{6,10},{2,6},{0,2},{5,1},{9,5},... | collective-permute-start | bytes 417800 | tf_op jit(solution)/shard_map/ppermute | solution.py:496
  68.7 1.6 %apply_expert.6 = (f32[32,2048]{1,0:T(8,128)S(1)}, f32[32,2048]{1,0:T(8,128)S(1)}, f32[32,2048]{1,0:T(8,128)S(1)}, f32[32,2048]{1,0:T(8,128)S(1)}) custom-call(bf16[32,2176]{1,0:T(8,128)(2,1)S(1)} %collective-permute-done.19.refs_0_, bf16[32,2176]{1,0:T(8,128)(2,1)S(1)} %collective-permute-done.26.refs_1_, ...), custom_call_target="tpu_custom_call" | custom-call | flops 603979776 | bytes 6291456 | tf_op jit(solution)/shard_map/apply_expert/pallas_call | solution.py:452
  70.7 1.6 %collective-permute-start.33 = (bf16[32,2176]{1,0:T(8,128)(2,1)S(1)}, bf16[32,2176]{1,0:T(8,128)(2,1)S(1)}, u32[]{:S(2)}, u32[]{:S(2)}) collective-permute-start(bf16[32,2176]{1,0:T(8,128)(2,1)S(1)} %collective-permute-done.30.refs_1_), channel_id=1, source_target_pairs={{4,0},{8,4},{12,8},{14,12},{10,14},{6,10},{2,6},{0,2},{5,1},{9,5},... | collective-permute-start | bytes 417800 | tf_op jit(solution)/shard_map/ppermute | solution.py:493
  72.4 1.6 %apply_expert.7 = (f32[32,2048]{1,0:T(8,128)S(1)}, f32[32,2048]{1,0:T(8,128)S(1)}, f32[32,2048]{1,0:T(8,128)S(1)}, f32[32,2048]{1,0:T(8,128)S(1)}) custom-call(bf16[32,2176]{1,0:T(8,128)(2,1)S(1)} %collective-permute-done.25.refs_0_, bf16[32,2176]{1,0:T(8,128)(2,1)S(1)} %collective-permute-done.30.refs_1_, ...), custom_call_target="tpu_custom_call" | custom-call | flops 603979776 | bytes 6291456 | tf_op jit(solution)/shard_map/apply_expert/pallas_call | solution.py:452
  74.0 1.5 %collective-permute-done.29.refs_0_ = bf16[32,2176]{1,0:T(8,128)(2,1)S(1)} collective-permute-done((bf16[32,2176]{1,0:T(8,128)(2,1)S(1)}, bf16[32,2176]{1,0:T(8,128)(2,1)S(1)}, u32[]{:S(2)}, u32[]{:S(2)}) %collective-permute-start.29) | collective-permute-done | bytes 139296 | tf_op jit(solution)/shard_map/ppermute | solution.py:492
  76.0 1.5 %apply_expert.8 = (f32[32,2048]{1,0:T(8,128)S(1)}, f32[32,2048]{1,0:T(8,128)S(1)}) custom-call(bf16[32,2176]{1,0:T(8,128)(2,1)S(1)} %collective-permute-done.29.refs_0_, bf16[32,2176]{1,0:T(8,128)(2,1)S(1)} %collective-permute-done.33.refs_1_, bf16[2,192,2048]{2,1,0:T(8,128)(2,1)S(1)} %bitcast.9, ...), custom_call_target="tpu_custom_call" | custom-call | flops 301989888 | bytes 6291456 | tf_op jit(solution)/shard_map/apply_expert/pallas_call | solution.py:452
  77.6 2.1 %collective-permute-start.34 = (bf16[32,2048]{1,0:T(8,128)(2,1)S(1)}, bf16[32,2048]{1,0:T(8,128)(2,1)S(1)}, u32[]{:S(2)}, u32[]{:S(2)}) collective-permute-start(bf16[32,2048]{1,0:T(8,128)(2,1)S(1)} %convert_element_type.12), channel_id=1, source_target_pairs={{4,0},{8,4},{12,8},{14,12},{10,14},{6,10},{2,6},{0,2},{5,1},{9,5},... | collective-permute-start | bytes 393224 | tf_op jit(solution)/shard_map/ppermute | solution.py:518
  79.8 2.1 %collective-permute-start.38 = (bf16[32,2048]{1,0:T(8,128)(2,1)S(1)}, bf16[32,2048]{1,0:T(8,128)(2,1)S(1)}, u32[]{:S(2)}, u32[]{:S(2)}) collective-permute-start(bf16[32,2048]{1,0:T(8,128)(2,1)S(1)} %convert_element_type.13), channel_id=1, source_target_pairs={{4,0},{8,4},{12,8},{14,12},{10,14},{6,10},{2,6},{0,2},{5,1},{9,5},... | collective-permute-start | bytes 393224 | tf_op jit(solution)/shard_map/ppermute | solution.py:518
  81.8 2.1 %collective-permute-done.44.came_ref = bf16[32,2048]{1,0:T(8,128)(2,1)S(1)} collective-permute-done((bf16[32,2048]{1,0:T(8,128)(2,1)S(1)}, bf16[32,2048]{1,0:T(8,128)(2,1)S(1)}, u32[]{:S(2)}, u32[]{:S(2)}) %collective-permute-start.44) | collective-permute-done | bytes 131104 | tf_op jit(solution)/shard_map/ppermute | solution.py:518
  84.0 2.1 %collective-permute-start.35 = (bf16[32,2048]{1,0:T(8,128)(2,1)S(1)}, bf16[32,2048]{1,0:T(8,128)(2,1)S(1)}, u32[]{:S(2)}, u32[]{:S(2)}) collective-permute-start(bf16[32,2048]{1,0:T(8,128)(2,1)S(1)} %add_share.10), channel_id=1, source_target_pairs={{4,0},{8,4},{12,8},{14,12},{10,14},{6,10},{2,6},{0,2},{5,1},{9,5},... | collective-permute-start | bytes 393224 | tf_op jit(solution)/shard_map/ppermute | solution.py:518
  86.8 2.1 %collective-permute-start.39 = (bf16[32,2048]{1,0:T(8,128)(2,1)S(1)}, bf16[32,2048]{1,0:T(8,128)(2,1)S(1)}, u32[]{:S(2)}, u32[]{:S(2)}) collective-permute-start(bf16[32,2048]{1,0:T(8,128)(2,1)S(1)} %add_share.13), channel_id=1, source_target_pairs={{4,0},{8,4},{12,8},{14,12},{10,14},{6,10},{2,6},{0,2},{5,1},{9,5},... | collective-permute-start | bytes 393224 | tf_op jit(solution)/shard_map/ppermute | solution.py:518
  90.0 1.8 %collective-permute-start.36 = (bf16[32,2048]{1,0:T(8,128)(2,1)S(1)}, bf16[32,2048]{1,0:T(8,128)(2,1)S(1)}, u32[]{:S(2)}, u32[]{:S(2)}) collective-permute-start(bf16[32,2048]{1,0:T(8,128)(2,1)S(1)} %add_share.11), channel_id=1, source_target_pairs={{4,0},{8,4},{12,8},{14,12},{10,14},{6,10},{2,6},{0,2},{5,1},{9,5},... | collective-permute-start | bytes 393224 | tf_op jit(solution)/shard_map/ppermute | solution.py:518
  92.8 1.8 %collective-permute-start.40 = (bf16[32,2048]{1,0:T(8,128)(2,1)S(1)}, bf16[32,2048]{1,0:T(8,128)(2,1)S(1)}, u32[]{:S(2)}, u32[]{:S(2)}) collective-permute-start(bf16[32,2048]{1,0:T(8,128)(2,1)S(1)} %add_share.14), channel_id=1, source_target_pairs={{4,0},{8,4},{12,8},{14,12},{10,14},{6,10},{2,6},{0,2},{5,1},{9,5},... | collective-permute-start | bytes 393224 | tf_op jit(solution)/shard_map/ppermute | solution.py:518
  95.1 1.8 %collective-permute-start.37 = (bf16[32,2048]{1,0:T(8,128)(2,1)S(1)}, bf16[32,2048]{1,0:T(8,128)(2,1)S(1)}, u32[]{:S(2)}, u32[]{:S(2)}) collective-permute-start(bf16[32,2048]{1,0:T(8,128)(2,1)S(1)} %add_share.12), channel_id=1, source_target_pairs={{4,0},{8,4},{12,8},{14,12},{10,14},{6,10},{2,6},{0,2},{5,1},{9,5},... | collective-permute-start | bytes 393224 | tf_op jit(solution)/shard_map/ppermute | solution.py:518
  96.8 1.5 %apply_expert.9 = (f32[32,2048]{1,0:T(8,128)S(1)}, f32[32,2048]{1,0:T(8,128)S(1)}) custom-call(bf16[32,2176]{1,0:T(8,128)(2,1)S(1)} %get-tuple-element.157.refs_0_, bf16[32,2176]{1,0:T(8,128)(2,1)S(1)} %get-tuple-element.158.refs_1_, bf16[2,192,2048]{2,1,0:T(8,128)(2,1)S(1)} %bitcast.10, bf16[2,192,2048]{2,1,0:T(8,128)(2,1)S(1)} %collective-permute-done.23.refs_5_.refs_3_, ...), custom_call_target="tpu_custom_call" | custom-call | flops 301989888 | bytes 6291456 | tf_op jit(solution)/shard_map/apply_expert/pallas_call | solution.py:452
  (122 shorter events, 32.4 us)
Async XLA Ops:
  0.0 36.6 %collective-permute-start.12 = (bf16[2048,1024]{1,0:T(8,128)(2,1)}, bf16[2048,1024]{1,0:T(8,128)(2,1)}, u32[]{:S(2)}, u32[]{:S(2)}) collective-permute-start(bf16[2048,1024]{1,0:T(8,128)(2,1)} %refs_5_.3), channel_id=1, source_target_pairs={{0,1},{1,0},{2,3},{3,2},{4,5},{5,4},{6,7},{7,6},{8,9},{9,8},{10,11... | collective-permute-start | bytes 12582920 | tf_op jit(solution)/shard_map/ppermute | solution.py:34
  2.9 6.0 %collective-permute-start.6 = (bf16[272,256]{1,0:T(8,128)(2,1)}, bf16[272,256]{1,0:T(8,128)(2,1)S(1)}, u32[]{:S(2)}, u32[]{:S(2)}) collective-permute-start(bf16[272,256]{1,0:T(8,128)(2,1)} %get-tuple-element.99.refs_1_), channel_id=1, source_target_pairs={{0,1},{1,0},{2,3},{3,2},{4,5},{5,4},{6,7},{7,6},{8,9},{9,8},{10,11... | collective-permute-start | bytes 417800 | tf_op jit(solution)/shard_map/ppermute | solution.py:34
  3.0 9.7 %collective-permute-start.5 = (bf16[272,256]{1,0:T(8,128)(2,1)}, bf16[272,256]{1,0:T(8,128)(2,1)S(1)}, u32[]{:S(2)}, u32[]{:S(2)}) collective-permute-start(bf16[272,256]{1,0:T(8,128)(2,1)} %get-tuple-element.99.refs_1_), channel_id=1, source_target_pairs={{0,4},{4,8},{8,12},{12,0},{1,5},{5,9},{9,13},{13,1},{2,6},{6,10},{... | collective-permute-start | bytes 417800 | tf_op jit(solution)/shard_map/ppermute | solution.py:618
  6.0 6.8 %collective-permute-start.1 = (bf16[272,256]{1,0:T(8,128)(2,1)}, bf16[272,256]{1,0:T(8,128)(2,1)S(1)}, u32[]{:S(2)}, u32[]{:S(2)}) collective-permute-start(bf16[272,256]{1,0:T(8,128)(2,1)} %get-tuple-element.90.refs_1_), channel_id=1, source_target_pairs={{0,1},{1,0},{2,3},{3,2},{4,5},{5,4},{6,7},{7,6},{8,9},{9,8},{10,11... | collective-permute-start | bytes 417800 | tf_op jit(solution)/shard_map/ppermute | solution.py:34
  6.0 9.1 %collective-permute-start = (bf16[272,256]{1,0:T(8,128)(2,1)}, bf16[272,256]{1,0:T(8,128)(2,1)S(1)}, u32[]{:S(2)}, u32[]{:S(2)}) collective-permute-start(bf16[272,256]{1,0:T(8,128)(2,1)} %get-tuple-element.90.refs_1_), channel_id=1, source_target_pairs={{0,4},{4,8},{8,12},{12,0},{1,5},{5,9},{9,13},{13,1},{2,6},{6,10},{... | collective-permute-start | bytes 417800 | tf_op jit(solution)/shard_map/ppermute | solution.py:618
  12.7 8.3 %collective-permute-start.7 = (bf16[272,256]{1,0:T(8,128)(2,1)S(1)}, bf16[272,256]{1,0:T(8,128)(2,1)S(1)}, u32[]{:S(2)}, u32[]{:S(2)}) collective-permute-start(bf16[272,256]{1,0:T(8,128)(2,1)S(1)} %collective-permute-done.5.refs_1_), channel_id=1, source_target_pairs={{0,4},{4,8},{8,12},{12,0},{1,5},{5,9},{9,13},{13,1},{2,6},{6,10},{... | collective-permute-start | bytes 417800 | tf_op jit(solution)/shard_map/ppermute | solution.py:618
  15.1 5.9 %collective-permute-start.3 = (bf16[272,256]{1,0:T(8,128)(2,1)S(1)}, bf16[272,256]{1,0:T(8,128)(2,1)S(1)}, u32[]{:S(2)}, u32[]{:S(2)}) collective-permute-start(bf16[272,256]{1,0:T(8,128)(2,1)S(1)} %collective-permute-done.refs_1_), channel_id=1, source_target_pairs={{0,1},{1,0},{2,3},{3,2},{4,5},{5,4},{6,7},{7,6},{8,9},{9,8},{10,11... | collective-permute-start | bytes 417800 | tf_op jit(solution)/shard_map/ppermute | solution.py:34
  15.3 8.4 %collective-permute-start.2 = (bf16[272,256]{1,0:T(8,128)(2,1)S(1)}, bf16[272,256]{1,0:T(8,128)(2,1)S(1)}, u32[]{:S(2)}, u32[]{:S(2)}) collective-permute-start(bf16[272,256]{1,0:T(8,128)(2,1)S(1)} %collective-permute-done.refs_1_), channel_id=1, source_target_pairs={{0,4},{4,8},{8,12},{12,0},{1,5},{5,9},{9,13},{13,1},{2,6},{6,10},{... | collective-permute-start | bytes 417800 | tf_op jit(solution)/shard_map/ppermute | solution.py:618
  25.0 37.2 %collective-permute-start.23 = (bf16[2,192,2048]{2,1,0:T(8,128)(2,1)S(1)}, bf16[2,192,2048]{2,1,0:T(8,128)(2,1)S(1)}, u32[]{:S(2)}, u32[]{:S(2)}) collective-permute-start(bf16[2,192,2048]{2,1,0:T(8,128)(2,1)S(1)} %bitcast.5), channel_id=1, source_target_pairs={{0,1},{1,0},{2,3},{3,2},{4,5},{5,4},{6,7},{7,6},{8,9},{9,8},{10,11... | collective-permute-start | bytes 4718600 | tf_op jit(solution)/shard_map/ppermute | solution.py:34
  25.1 28.6 %collective-permute-start.24 = (bf16[192,2048]{1,0:T(8,128)(2,1)S(1)}, bf16[192,2048]{1,0:T(8,128)(2,1)S(1)}, u32[]{:S(2)}, u32[]{:S(2)}) collective-permute-start(bf16[192,2048]{1,0:T(8,128)(2,1)S(1)} %bitcast.11), channel_id=1, source_target_pairs={{0,1},{1,0},{2,3},{3,2},{4,5},{5,4},{6,7},{7,6},{8,9},{9,8},{10,11... | collective-permute-start | bytes 2359304 | tf_op jit(solution)/shard_map/ppermute | solution.py:34
  25.5 8.3 %collective-permute-start.13 = (bf16[272,256]{1,0:T(8,128)(2,1)S(1)}, bf16[272,256]{1,0:T(8,128)(2,1)S(1)}, u32[]{:S(2)}, u32[]{:S(2)}) collective-permute-start(bf16[272,256]{1,0:T(8,128)(2,1)S(1)} %collective-permute-done.7.refs_1_), channel_id=1, source_target_pairs={{0,4},{4,8},{8,12},{12,0},{1,5},{5,9},{9,13},{13,1},{2,6},{6,10},{... | collective-permute-start | bytes 417800 | tf_op jit(solution)/shard_map/ppermute | solution.py:618
  25.5 10.5 %collective-permute-start.4 = (bf16[272,256]{1,0:T(8,128)(2,1)S(1)}, bf16[272,256]{1,0:T(8,128)(2,1)S(1)}, u32[]{:S(2)}, u32[]{:S(2)}) collective-permute-start(bf16[272,256]{1,0:T(8,128)(2,1)S(1)} %collective-permute-done.2.refs_1_), channel_id=1, source_target_pairs={{0,4},{4,8},{8,12},{12,0},{1,5},{5,9},{9,13},{13,1},{2,6},{6,10},{... | collective-permute-start | bytes 417800 | tf_op jit(solution)/shard_map/ppermute | solution.py:618
  36.0 8.7 %collective-permute-start.16 = (bf16[64,1024]{1,0:T(8,128)(2,1)S(1)}, bf16[64,1024]{1,0:T(8,128)(2,1)S(1)}, u32[]{:S(2)}, u32[]{:S(2)}) collective-permute-start(bf16[64,1024]{1,0:T(8,128)(2,1)S(1)} %get-tuple-element.130), channel_id=1, source_target_pairs={{0,1},{1,0},{2,3},{3,2},{4,5},{5,4},{6,7},{7,6},{8,9},{9,8},{10,11... | collective-permute-start | bytes 393224 | tf_op jit(solution)/shard_map/ppermute | solution.py:106
  42.4 6.4 %collective-permute-start.15 = (bf16[32,2048]{1,0:T(8,128)(2,1)S(1)}, bf16[32,2048]{1,0:T(8,128)(2,1)S(1)}, u32[]{:S(2)}, u32[]{:S(2)}) collective-permute-start(bf16[32,2048]{1,0:T(8,128)(2,1)S(1)} %get-tuple-element.127), channel_id=1, source_target_pairs={{0,2},{2,0},{1,3},{3,1},{4,6},{6,4},{5,7},{7,5},{8,10},{10,8},{9,1... | collective-permute-start | bytes 393224 | tf_op jit(solution)/shard_map/ppermute | solution.py:650
  44.2 7.3 %collective-permute-start.17 = (bf16[32,2048]{1,0:T(8,128)(2,1)S(1)}, bf16[32,2048]{1,0:T(8,128)(2,1)S(1)}, u32[]{:S(2)}, u32[]{:S(2)}) collective-permute-start(bf16[32,2048]{1,0:T(8,128)(2,1)S(1)} %get-tuple-element.133), channel_id=1, source_target_pairs={{0,2},{2,0},{1,3},{3,1},{4,6},{6,4},{5,7},{7,5},{8,10},{10,8},{9,1... | collective-permute-start | bytes 393224 | tf_op jit(solution)/shard_map/ppermute | solution.py:650
  51.7 5.9 %collective-permute-start.20 = (bf16[32,2176]{1,0:T(8,128)(2,1)S(1)}, bf16[32,2176]{1,0:T(8,128)(2,1)S(1)}, u32[]{:S(2)}, u32[]{:S(2)}) collective-permute-start(bf16[32,2176]{1,0:T(8,128)(2,1)S(1)} %get-tuple-element.158.refs_1_), channel_id=1, source_target_pairs={{4,0},{8,4},{12,8},{14,12},{10,14},{6,10},{2,6},{0,2},{5,1},{9,5},... | collective-permute-start | bytes 417800 | tf_op jit(solution)/shard_map/ppermute | solution.py:493
  52.7 6.5 %collective-permute-start.21 = (bf16[32,2176]{1,0:T(8,128)(2,1)S(1)}, bf16[32,2176]{1,0:T(8,128)(2,1)S(1)}, u32[]{:S(2)}, u32[]{:S(2)}) collective-permute-start(bf16[32,2176]{1,0:T(8,128)(2,1)S(1)} %get-tuple-element.158.refs_1_), channel_id=1, source_target_pairs={{0,4},{4,8},{8,12},{12,14},{14,10},{10,6},{6,2},{2,0},{1,5},{5,9},... | collective-permute-start | bytes 417800 | tf_op jit(solution)/shard_map/ppermute | solution.py:495
  53.7 6.8 %collective-permute-start.22 = (bf16[32,2176]{1,0:T(8,128)(2,1)S(1)}, bf16[32,2176]{1,0:T(8,128)(2,1)S(1)}, u32[]{:S(2)}, u32[]{:S(2)}) collective-permute-start(bf16[32,2176]{1,0:T(8,128)(2,1)S(1)} %get-tuple-element.157.refs_0_), channel_id=1, source_target_pairs={{4,0},{8,4},{12,8},{14,12},{10,14},{6,10},{2,6},{0,2},{5,1},{9,5},... | collective-permute-start | bytes 417800 | tf_op jit(solution)/shard_map/ppermute | solution.py:496
  54.7 9.0 %collective-permute-start.19 = (bf16[32,2176]{1,0:T(8,128)(2,1)S(1)}, bf16[32,2176]{1,0:T(8,128)(2,1)S(1)}, u32[]{:S(2)}, u32[]{:S(2)}) collective-permute-start(bf16[32,2176]{1,0:T(8,128)(2,1)S(1)} %collective-permute-done.18.refs_0_), channel_id=1, source_target_pairs={{0,4},{4,8},{8,12},{12,14},{14,10},{10,6},{6,2},{2,0},{1,5},{5,9},... | collective-permute-start | bytes 417800 | tf_op jit(solution)/shard_map/ppermute | solution.py:492
  57.5 6.7 %collective-permute-start.26 = (bf16[32,2176]{1,0:T(8,128)(2,1)S(1)}, bf16[32,2176]{1,0:T(8,128)(2,1)S(1)}, u32[]{:S(2)}, u32[]{:S(2)}) collective-permute-start(bf16[32,2176]{1,0:T(8,128)(2,1)S(1)} %collective-permute-done.20.refs_1_), channel_id=1, source_target_pairs={{4,0},{8,4},{12,8},{14,12},{10,14},{6,10},{2,6},{0,2},{5,1},{9,5},... | collective-permute-start | bytes 417800 | tf_op jit(solution)/shard_map/ppermute | solution.py:493
  59.2 6.7 %collective-permute-start.27 = (bf16[32,2176]{1,0:T(8,128)(2,1)S(1)}, bf16[32,2176]{1,0:T(8,128)(2,1)S(1)}, u32[]{:S(2)}, u32[]{:S(2)}) collective-permute-start(bf16[32,2176]{1,0:T(8,128)(2,1)S(1)} %collective-permute-done.21.refs_2_), channel_id=1, source_target_pairs={{0,4},{4,8},{8,12},{12,14},{14,10},{10,6},{6,2},{2,0},{1,5},{5,9},... | collective-permute-start | bytes 417800 | tf_op jit(solution)/shard_map/ppermute | solution.py:495
  60.5 6.6 %collective-permute-start.28 = (bf16[32,2176]{1,0:T(8,128)(2,1)S(1)}, bf16[32,2176]{1,0:T(8,128)(2,1)S(1)}, u32[]{:S(2)}, u32[]{:S(2)}) collective-permute-start(bf16[32,2176]{1,0:T(8,128)(2,1)S(1)} %collective-permute-done.22.refs_3_), channel_id=1, source_target_pairs={{4,0},{8,4},{12,8},{14,12},{10,14},{6,10},{2,6},{0,2},{5,1},{9,5},... | collective-permute-start | bytes 417800 | tf_op jit(solution)/shard_map/ppermute | solution.py:496
  63.7 6.6 %collective-permute-start.25 = (bf16[32,2176]{1,0:T(8,128)(2,1)S(1)}, bf16[32,2176]{1,0:T(8,128)(2,1)S(1)}, u32[]{:S(2)}, u32[]{:S(2)}) collective-permute-start(bf16[32,2176]{1,0:T(8,128)(2,1)S(1)} %collective-permute-done.19.refs_0_), channel_id=1, source_target_pairs={{0,4},{4,8},{8,12},{12,14},{14,10},{10,6},{6,2},{2,0},{1,5},{5,9},... | collective-permute-start | bytes 417800 | tf_op jit(solution)/shard_map/ppermute | solution.py:492
  64.2 6.6 %collective-permute-start.30 = (bf16[32,2176]{1,0:T(8,128)(2,1)S(1)}, bf16[32,2176]{1,0:T(8,128)(2,1)S(1)}, u32[]{:S(2)}, u32[]{:S(2)}) collective-permute-start(bf16[32,2176]{1,0:T(8,128)(2,1)S(1)} %collective-permute-done.26.refs_1_), channel_id=1, source_target_pairs={{4,0},{8,4},{12,8},{14,12},{10,14},{6,10},{2,6},{0,2},{5,1},{9,5},... | collective-permute-start | bytes 417800 | tf_op jit(solution)/shard_map/ppermute | solution.py:493
  65.8 6.6 %collective-permute-start.31 = (bf16[32,2176]{1,0:T(8,128)(2,1)S(1)}, bf16[32,2176]{1,0:T(8,128)(2,1)S(1)}, u32[]{:S(2)}, u32[]{:S(2)}) collective-permute-start(bf16[32,2176]{1,0:T(8,128)(2,1)S(1)} %collective-permute-done.27.refs_2_), channel_id=1, source_target_pairs={{0,4},{4,8},{8,12},{12,14},{14,10},{10,6},{6,2},{2,0},{1,5},{5,9},... | collective-permute-start | bytes 417800 | tf_op jit(solution)/shard_map/ppermute | solution.py:495
  77.5 6.4 %collective-permute-start.44 = (bf16[32,2048]{1,0:T(8,128)(2,1)S(1)}, bf16[32,2048]{1,0:T(8,128)(2,1)S(1)}, u32[]{:S(2)}, u32[]{:S(2)}) collective-permute-start(bf16[32,2048]{1,0:T(8,128)(2,1)S(1)} %convert_element_type.15), channel_id=1, source_target_pairs={{0,4},{4,8},{8,12},{12,14},{14,10},{10,6},{6,2},{2,0},{1,5},{5,9},... | collective-permute-start | bytes 393224 | tf_op jit(solution)/shard_map/ppermute | solution.py:518
  77.6 6.4 %collective-permute-start.34 = (bf16[32,2048]{1,0:T(8,128)(2,1)S(1)}, bf16[32,2048]{1,0:T(8,128)(2,1)S(1)}, u32[]{:S(2)}, u32[]{:S(2)}) collective-permute-start(bf16[32,2048]{1,0:T(8,128)(2,1)S(1)} %convert_element_type.12), channel_id=1, source_target_pairs={{4,0},{8,4},{12,8},{14,12},{10,14},{6,10},{2,6},{0,2},{5,1},{9,5},... | collective-permute-start | bytes 393224 | tf_op jit(solution)/shard_map/ppermute | solution.py:518
  79.7 7.0 %collective-permute-start.41 = (bf16[32,2048]{1,0:T(8,128)(2,1)S(1)}, bf16[32,2048]{1,0:T(8,128)(2,1)S(1)}, u32[]{:S(2)}, u32[]{:S(2)}) collective-permute-start(bf16[32,2048]{1,0:T(8,128)(2,1)S(1)} %convert_element_type.14), channel_id=1, source_target_pairs={{0,4},{4,8},{8,12},{12,14},{14,10},{10,6},{6,2},{2,0},{1,5},{5,9},... | collective-permute-start | bytes 393224 | tf_op jit(solution)/shard_map/ppermute | solution.py:518
  79.8 7.0 %collective-permute-start.38 = (bf16[32,2048]{1,0:T(8,128)(2,1)S(1)}, bf16[32,2048]{1,0:T(8,128)(2,1)S(1)}, u32[]{:S(2)}, u32[]{:S(2)}) collective-permute-start(bf16[32,2048]{1,0:T(8,128)(2,1)S(1)} %convert_element_type.13), channel_id=1, source_target_pairs={{4,0},{8,4},{12,8},{14,12},{10,14},{6,10},{2,6},{0,2},{5,1},{9,5},... | collective-permute-start | bytes 393224 | tf_op jit(solution)/shard_map/ppermute | solution.py:518
  84.0 6.0 %collective-permute-start.35 = (bf16[32,2048]{1,0:T(8,128)(2,1)S(1)}, bf16[32,2048]{1,0:T(8,128)(2,1)S(1)}, u32[]{:S(2)}, u32[]{:S(2)}) collective-permute-start(bf16[32,2048]{1,0:T(8,128)(2,1)S(1)} %add_share.10), channel_id=1, source_target_pairs={{4,0},{8,4},{12,8},{14,12},{10,14},{6,10},{2,6},{0,2},{5,1},{9,5},... | collective-permute-start | bytes 393224 | tf_op jit(solution)/shard_map/ppermute | solution.py:518
  86.8 5.9 %collective-permute-start.39 = (bf16[32,2048]{1,0:T(8,128)(2,1)S(1)}, bf16[32,2048]{1,0:T(8,128)(2,1)S(1)}, u32[]{:S(2)}, u32[]{:S(2)}) collective-permute-start(bf16[32,2048]{1,0:T(8,128)(2,1)S(1)} %add_share.13), channel_id=1, source_target_pairs={{4,0},{8,4},{12,8},{14,12},{10,14},{6,10},{2,6},{0,2},{5,1},{9,5},... | collective-permute-start | bytes 393224 | tf_op jit(solution)/shard_map/ppermute | solution.py:518
  92.4 6.0 %collective-permute-start.43 = (bf16[32,2048]{1,0:T(8,128)(2,1)S(1)}, bf16[32,2048]{1,0:T(8,128)(2,1)S(1)}, u32[]{:S(2)}, u32[]{:S(2)}) collective-permute-start(bf16[32,2048]{1,0:T(8,128)(2,1)S(1)} %add_share.16), channel_id=1, source_target_pairs={{0,4},{4,8},{8,12},{12,14},{14,10},{10,6},{6,2},{2,0},{1,5},{5,9},... | collective-permute-start | bytes 393224 | tf_op jit(solution)/shard_map/ppermute | solution.py:518
  (27 other events, 164.5 us)

commit v5 on v4

--- a/solution.py
+++ b/solution.py
@@ -254,9 +254,11 @@
     return small_kernel(kernel, [shape], parts, "stack_rows")[0]
 
 
-def attend(queries, kv, hop, blocks, state, cache_rows, kv_heads, n_hd, chunks, finish=None):
+def attend(queries, kv, stages, state, cache_rows, kv_heads, n_hd, chunks, finish=None):
     all_rows, columns = queries.shape
-    rows, n_sub = all_rows // n_hd, len(blocks)
+    rows, n_sub = all_rows // n_hd, len(stages[0][1])
+    blocks = [block for _, stage_blocks in stages for block in stage_blocks]
+    origins = [(hop, step) for hop, _ in stages for step in range(n_sub)]
     per_kv = columns // HD // kv_heads
     stack = 2 if per_kv % 2 == 0 else 1
     part = stack * all_rows
@@ -299,7 +301,7 @@
         hd = lax.axis_index("hd")
         places = [(hd + j) % n_hd if relative else j for j in range(n_hd)]
         biases = []
-        for step, block in enumerate(block_refs):
+        for (hop, step), block in zip(origins, block_refs):
             cache_bias = block[keys : keys + 1, :cache_rows].astype(jnp.float32)
             if hop == 0:
                 key_id = ((sub - step) % n_sub) * new_rows + lax.broadcasted_iota(
@@ -605,33 +607,36 @@
         and rows % 32 == 0
     )
 
-    projections = sub_copies(out_proj)
     packed = pack_keys(
         cache_keys, cache_values, new_keys, new_values, page_len, kv_heads, heads_here
     )
     query_rows_here = choose_queries(queries.reshape(n_hd, n_sub, rows, heads_here * HD))
-    travelling = list(packed)
+    reach = n_ep // 2
+    up, down = list(packed), list(packed)
+    arrived = [[(0, x)] for x in packed]
     states = [None] * kv_heads
     earlier = None
-    for hop in range(n_ep):
-        blocks = [sub_copies(x) for x in travelling]
-        onward = [lax.ppermute(x, "ep", cycle(n_ep)) for x in travelling] if hop < n_ep - 1 else []
-        if hop == min(2, n_ep - 1):
-            residual, gate_up, w_down, blocks = lax.optimization_barrier(
-                (residual, gate_up, w_down, blocks)
-            )
-            residual_parts = hand_over(split_rows(residual, n_sub))
-            gate_table = gates_by_expert(expert_ids, gates, rows) if dense else None
-            if dense:
-                gate_up_parts = sub_copies(gate_up[0])
-                w_down_parts = sub_copies(w_down[0])
+    for distance in range(reach + 1):
+        stages = [[(hop, sub_copies(x)) for hop, x in blocks] for blocks in arrived]
+        if distance == 0:
+            out_proj, packed = lax.optimization_barrier((out_proj, packed))
+            projections = sub_copies(out_proj)
+        onward = [[] for _ in packed]
+        if distance < reach:
+            opposite = 2 * (distance + 1) == n_ep
+            for kv in range(kv_heads):
+                if not opposite or kv % 2 == 0:
+                    up[kv] = lax.ppermute(up[kv], "ep", cycle(n_ep))
+                    onward[kv].append((distance + 1, up[kv]))
+                if not opposite or kv % 2 == 1:
+                    down[kv] = lax.ppermute(down[kv], "ep", cycle(n_ep, n_ep - 1))
+                    onward[kv].append((n_ep - distance - 1, down[kv]))
         for kv in range(kv_heads):
-            finish = (projections, earlier) if hop == n_ep - 1 else None
+            finish = (projections, earlier) if distance == reach else None
             states[kv] = attend(
                 query_rows_here,
                 kv,
-                hop,
-                blocks[kv],
+                stages[kv],
                 states[kv],
                 cache_rows,
                 kv_heads,
@@ -641,9 +646,24 @@
             )
             if finish:
                 earlier = states[kv][0]
-            else:
-                onward[kv], states[kv] = lax.optimization_barrier((onward[kv], states[kv]))
-        travelling = onward
+                continue
+            came = [x for _, x in onward[kv]]
+            came, states[kv] = lax.optimization_barrier((came, states[kv]))
+            onward[kv] = [(hop, x) for (hop, _), x in zip(onward[kv], came)]
+            for hop, x in onward[kv]:
+                if hop == distance + 1:
+                    up[kv] = x
+                else:
+                    down[kv] = x
+        if distance == 0:
+            residual, states[0] = lax.optimization_barrier((residual, states[0]))
+            residual_parts = hand_over(split_rows(residual, n_sub))
+            gate_table = gates_by_expert(expert_ids, gates, rows) if dense else None
+        arrived = onward
+    if dense:
+        gate_up, w_down, states[-1] = lax.optimization_barrier((gate_up, w_down, states[-1]))
+        gate_up_parts = sub_copies(gate_up[0])
+        w_down_parts = sub_copies(w_down[0])
     parts = states[-1]
     if n_hd == 2:
         kept, sent = parts[: len(parts) // 2], parts[len(parts) // 2 :]

time: 103 us -> 99.6 us (0.967)
  waiting for transfers between devices: 35.8 us -> 25.2 us
  starting transfers between devices: 39.2 us -> 49 us
  Pallas kernels: 23 us -> 20.9 us
    ppermute x6, waiting for transfers between devices: 15.1 us -> 3.26 us  [the longest x3 3.25 us: shards(): down[kv] = lax.ppermute(down[kv], 'ep', cycle(n_ep, n_ep - 1))]
    ppermute x6, starting transfers between devices: 6.37 us -> 13.1 us  [the longest x3 7.05 us: shards(): down[kv] = lax.ppermute(down[kv], 'ep', cycle(n_ep, n_ep - 1))]
    ppermute x2, waiting for transfers between devices: 6.55 us -> 2.63 us  [shards(): came = [lax.ppermute(x, 'hd', cycle(n_hd)) for x in sent]]
    ppermute x4, waiting for transfers between devices: 1.46 us -> 4.92 us  [dense_experts(): behind[0] = lax.ppermute(behind[0], axes, ahead)]
    ppermute x3, waiting for transfers between devices: 0.01 us -> 2.19 us  [dense_experts(): behind[1] = lax.ppermute(behind[1], axes, ahead)]
    pallas_call x8 -> x6, Pallas kernels: 11.8 us -> 9.72 us  [attend(): pl.pallas_call(kernel, out_shape=out_shape, in_specs=in_specs, out_specs=...]
    ppermute x4, starting transfers between devices: 5.96 us -> 7.92 us  [dense_experts(): before[1] = lax.ppermute(before[1], axes, back)]
    ppermute x3, starting transfers between devices: 4.27 us -> 5.83 us  [dense_experts(): before[0] = lax.ppermute(before[0], axes, back)]
  transfers between devices with their start and end apart: 49 -> 49, of which waited for: 22 -> 18; matrix products, arithmetic and copies ran while one was open for 0% -> 0% of each run, Pallas kernels for 20% -> 15%
where the time goes in v5:
time: 99.6 us; the launch traced here: 99.4 us
  starting transfers between devices  49 us (49%)
  waiting for transfers between devices  25.2 us (25%)
  Pallas kernels  20.9 us (21%)
  local copies, waits for them, and re-layouts  3.09 us (3%)
  between operations  1.13 us (1%)
    ppermute x14, starting transfers between devices, dense_experts(): chunks[chunk] = lax.ppermute(sum_here, axes, way)  15.5 us
    pallas_call x6, Pallas kernels, attend(): pl.pallas_call(kernel, out_shape=out_shape, in_specs=in_specs, out_specs=...  9.72 us
    ppermute x4, starting transfers between devices, dense_experts(): before[1] = lax.ppermute(before[1], axes, back)  7.92 us
    pallas_call x5, Pallas kernels, apply_expert(): pl.pallas_call(kernel, out_shape=[jax.ShapeDtypeStruct((x.shape[0], featu...  7.66 us
    ppermute x3, starting transfers between devices, shards(): down[kv] = lax.ppermute(down[kv], 'ep', cycle(n_ep, n_ep - 1))  7.05 us
    ppermute x3, starting transfers between devices, shards(): up[kv] = lax.ppermute(up[kv], 'ep', cycle(n_ep))  6.03 us
    ppermute x3, starting transfers between devices, dense_experts(): before[0] = lax.ppermute(before[0], axes, back)  5.83 us
    ppermute x14, waiting for transfers between devices, dense_experts(): chunks[chunk] = lax.ppermute(sum_here, axes, way)  5.23 us
  transfers between devices with their start and end apart: 49, of which 18 were waited for; matrix products, arithmetic and copies ran while one was open for 0% of the time, Pallas kernels for 15%

profile of v5, /device:TPU:0, one launch (start us, length us, event | category | flops | bytes accessed | tf_op | source)
XLA Modules:
  0.0 99.4 jit_solution(13667259836664102457)
XLA Ops:
  0.7 1.9 %pack_keys.1 = (bf16[272,256]{1,0:T(8,128)(2,1)}, bf16[272,256]{1,0:T(8,128)(2,1)}) custom-call(s32[1]{0:T(128)S(6)} %copy.14.page_ref, bf16[128,512]{1,0:T(8,128)(2,1)} %ck_ref.1, bf16[128,512]{1,0:T(8,128)(2,1)} %cv_ref.1, bf16[128,512]{1,0:T(8,128)(2,1)} %nk_ref.1, bf16[128,512]{1,0:T(8,128)(2,1)} %nv_ref.1), custom_call_target="tpu_custom_call" | custom-call | tf_op jit(solution)/shard_map/pack_keys/pallas_call | solution.py:81
  3.0 3.0 %collective-permute-start.8 = (bf16[272,256]{1,0:T(8,128)(2,1)}, bf16[272,256]{1,0:T(8,128)(2,1)S(1)}, u32[]{:S(2)}, u32[]{:S(2)}) collective-permute-start(bf16[272,256]{1,0:T(8,128)(2,1)} %get-tuple-element.97.refs_1_), channel_id=1, source_target_pairs={{0,4},{4,8},{8,12},{12,0},{1,5},{5,9},{9,13},{13,1},{2,6},{6,10},{... | collective-permute-start | bytes 417800 | tf_op jit(solution)/shard_map/ppermute | solution.py:629
  6.0 2.0 %collective-permute-start.9 = (bf16[272,256]{1,0:T(8,128)(2,1)}, bf16[272,256]{1,0:T(8,128)(2,1)S(1)}, u32[]{:S(2)}, u32[]{:S(2)}) collective-permute-start(bf16[272,256]{1,0:T(8,128)(2,1)} %get-tuple-element.97.refs_1_), channel_id=1, source_target_pairs={{0,12},{4,0},{8,4},{12,8},{1,13},{5,1},{9,5},{13,9},{2,14},{6,2},{... | collective-permute-start | bytes 417800 | tf_op jit(solution)/shard_map/ppermute | solution.py:632
  10.2 2.9 %collective-permute-start = (bf16[272,256]{1,0:T(8,128)(2,1)}, bf16[272,256]{1,0:T(8,128)(2,1)S(1)}, u32[]{:S(2)}, u32[]{:S(2)}) collective-permute-start(bf16[272,256]{1,0:T(8,128)(2,1)} %get-tuple-element.85.refs_1_), channel_id=1, source_target_pairs={{0,4},{4,8},{8,12},{12,0},{1,5},{5,9},{9,13},{13,1},{2,6},{6,10},{... | collective-permute-start | bytes 417800 | tf_op jit(solution)/shard_map/ppermute | solution.py:629
  15.0 2.1 %collective-permute-start.1 = (bf16[272,256]{1,0:T(8,128)(2,1)}, bf16[272,256]{1,0:T(8,128)(2,1)S(1)}, u32[]{:S(2)}, u32[]{:S(2)}) collective-permute-start(bf16[272,256]{1,0:T(8,128)(2,1)} %get-tuple-element.85.refs_1_), channel_id=1, source_target_pairs={{0,12},{4,0},{8,4},{12,8},{1,13},{5,1},{9,5},{13,9},{2,14},{6,2},{... | collective-permute-start | bytes 417800 | tf_op jit(solution)/shard_map/ppermute | solution.py:632
  19.6 2.7 %collective-permute-done.1.refs_3_ = bf16[272,256]{1,0:T(8,128)(2,1)S(1)} collective-permute-done((bf16[272,256]{1,0:T(8,128)(2,1)}, bf16[272,256]{1,0:T(8,128)(2,1)S(1)}, u32[]{:S(2)}, u32[]{:S(2)}) %collective-permute-start.1) | collective-permute-done | bytes 139296 | tf_op jit(solution)/shard_map/ppermute | solution.py:632
  22.8 2.9 %collective-permute-start.3 = (bf16[272,256]{1,0:T(8,128)(2,1)S(1)}, bf16[272,256]{1,0:T(8,128)(2,1)S(1)}, u32[]{:S(2)}, u32[]{:S(2)}) collective-permute-start(bf16[272,256]{1,0:T(8,128)(2,1)S(1)} %collective-permute-done.1.refs_3_), channel_id=1, source_target_pairs={{0,12},{4,0},{8,4},{12,8},{1,13},{5,1},{9,5},{13,9},{2,14},{6,2},{... | collective-permute-start | bytes 417800 | tf_op jit(solution)/shard_map/ppermute | solution.py:632
  25.7 1.8 %attend.9 = (f32[1024,128]{1,0:T(8,128)S(1)}, f32[1024,256]{1,0:T(8,128)S(1)}) custom-call(bf16[128,2048]{1,0:T(8,128)(2,1)S(1)} %choose_queries.1.refs_0_, bf16[272,256]{1,0:T(8,128)(2,1)S(1)} %collective-permute-done.8.refs_1_, bf16[272,256]{1,0:T(8,128)(2,1)S(1)} %collective-permute-done.12.refs_2_, bf16[272,256]{1,0:T(8,128)(2,1)S(1)} %collective-permute-done.9.refs_3_, ...), custom_call_target="tpu_custom_call" | custom-call | flops 805306368 | bytes 4194304 | tf_op jit(solution)/shard_map/attend/pallas_call | solution.py:408
  27.7 1.8 %attend.7 = (f32[1024,128]{1,0:T(8,128)S(1)}, f32[1024,256]{1,0:T(8,128)S(1)}) custom-call(bf16[128,2048]{1,0:T(8,128)(2,1)S(1)} %choose_queries.1.refs_0_, bf16[272,256]{1,0:T(8,128)(2,1)S(1)} %collective-permute-done.refs_1_, bf16[272,256]{1,0:T(8,128)(2,1)S(1)} %collective-permute-done.4.refs_2_, bf16[272,256]{1,0:T(8,128)(2,1)S(1)} %collective-permute-done.1.refs_3_, ...), custom_call_target="tpu_custom_call" | custom-call | flops 805306368 | bytes 4194304 | tf_op jit(solution)/shard_map/attend/pallas_call | solution.py:408
  30.0 2.1 %attend.10.refs_7_ = f32[128,2048]{1,0:T(8,128)S(1)} custom-call(bf16[128,2048]{1,0:T(8,128)(2,1)S(1)} %choose_queries.1.refs_0_, bf16[272,256]{1,0:T(8,128)(2,1)S(1)} %collective-permute-done.11.refs_1_, bf16[272,256]{1,0:T(8,128)(2,1)S(1)} %collective-permute-done.14.refs_2_, f32[1024,128]{1,0:T(8,128)S(1)} %get-tuple-element.110.refs_3_, ...), custom_call_target="tpu_custom_call" | custom-call | flops 402653184 | bytes 4194304 | tf_op jit(solution)/shard_map/attend/pallas_call | solution.py:408
  32.2 2.1 %attend.11 = (f32[32,2048]{1,0:T(8,128)S(1)}, f32[32,2048]{1,0:T(8,128)S(1)}, bf16[32,2048]{1,0:T(8,128)(2,1)S(1)}, bf16[32,2048]{1,0:T(8,128)(2,1)S(1)}) custom-call(bf16[128,2048]{1,0:T(8,128)(2,1)S(1)} %choose_queries.1.refs_0_, bf16[272,256]{1,0:T(8,128)(2,1)S(1)} %collective-permute-done.3.refs_1_, bf16[272,256]{1,0:T(8,128)(2,1)S(1)} %collective-permute-done.6.refs_2_, ...), custom_call_target="tpu_custom_call" | custom-call | flops 402653184 | bytes 4194304 | tf_op jit(solution)/shard_map/attend/pallas_call | solution.py:408
  35.5 1.7 %collective-permute-start.17 = (bf16[32,2048]{1,0:T(8,128)(2,1)S(1)}, bf16[32,2048]{1,0:T(8,128)(2,1)S(1)}, u32[]{:S(2)}, u32[]{:S(2)}) collective-permute-start(bf16[32,2048]{1,0:T(8,128)(2,1)S(1)} %get-tuple-element.123), channel_id=1, source_target_pairs={{0,2},{2,0},{1,3},{3,1},{4,6},{6,4},{5,7},{7,5},{8,10},{10,8},{9,1... | collective-permute-start | bytes 393224 | tf_op jit(solution)/shard_map/ppermute | solution.py:670
  37.7 1.6 %collective-permute-done.16.refs_3_ = bf16[64,1024]{1,0:T(8,128)(2,1)S(1)} collective-permute-done((bf16[64,1024]{1,0:T(8,128)(2,1)S(1)}, bf16[64,1024]{1,0:T(8,128)(2,1)S(1)}, u32[]{:S(2)}, u32[]{:S(2)}) %collective-permute-start.16) | collective-permute-done | bytes 131104 | tf_op jit(solution)/shard_map/ppermute | solution.py:106
  39.2 2.6 %collective-permute-done.17.refs_1_ = bf16[32,2048]{1,0:T(8,128)(2,1)S(1)} collective-permute-done((bf16[32,2048]{1,0:T(8,128)(2,1)S(1)}, bf16[32,2048]{1,0:T(8,128)(2,1)S(1)}, u32[]{:S(2)}, u32[]{:S(2)}) %collective-permute-start.17) | collective-permute-done | bytes 131104 | tf_op jit(solution)/shard_map/ppermute | solution.py:670
  42.0 1.8 %collective-permute-start.20 = (bf16[32,2176]{1,0:T(8,128)(2,1)S(1)}, bf16[32,2176]{1,0:T(8,128)(2,1)S(1)}, u32[]{:S(2)}, u32[]{:S(2)}) collective-permute-start(bf16[32,2176]{1,0:T(8,128)(2,1)S(1)} %get-tuple-element.148.refs_1_), channel_id=1, source_target_pairs={{4,0},{8,4},{12,8},{14,12},{10,14},{6,10},{2,6},{0,2},{5,1},{9,5},... | collective-permute-start | bytes 417800 | tf_op jit(solution)/shard_map/ppermute | solution.py:495
  45.1 2.0 %collective-permute-done.20.refs_1_ = bf16[32,2176]{1,0:T(8,128)(2,1)S(1)} collective-permute-done((bf16[32,2176]{1,0:T(8,128)(2,1)S(1)}, bf16[32,2176]{1,0:T(8,128)(2,1)S(1)}, u32[]{:S(2)}, u32[]{:S(2)}) %collective-permute-start.20) | collective-permute-done | bytes 139296 | tf_op jit(solution)/shard_map/ppermute | solution.py:495
  47.1 1.7 %collective-permute-start.22 = (bf16[32,2176]{1,0:T(8,128)(2,1)S(1)}, bf16[32,2176]{1,0:T(8,128)(2,1)S(1)}, u32[]{:S(2)}, u32[]{:S(2)}) collective-permute-start(bf16[32,2176]{1,0:T(8,128)(2,1)S(1)} %get-tuple-element.147.refs_0_), channel_id=1, source_target_pairs={{4,0},{8,4},{12,8},{14,12},{10,14},{6,10},{2,6},{0,2},{5,1},{9,5},... | collective-permute-start | bytes 417800 | tf_op jit(solution)/shard_map/ppermute | solution.py:498
  48.8 2.1 %collective-permute-done.18.refs_0_ = bf16[32,2176]{1,0:T(8,128)(2,1)S(1)} collective-permute-done((bf16[32,2176]{1,0:T(8,128)(2,1)S(1)}, bf16[32,2176]{1,0:T(8,128)(2,1)S(1)}, u32[]{:S(2)}, u32[]{:S(2)}) %collective-permute-start.18) | collective-permute-done | bytes 139296 | tf_op jit(solution)/shard_map/ppermute | solution.py:494
  51.2 2.2 %collective-permute-done.21.refs_2_ = bf16[32,2176]{1,0:T(8,128)(2,1)S(1)} collective-permute-done((bf16[32,2176]{1,0:T(8,128)(2,1)S(1)}, bf16[32,2176]{1,0:T(8,128)(2,1)S(1)}, u32[]{:S(2)}, u32[]{:S(2)}) %collective-permute-start.21) | collective-permute-done | bytes 139296 | tf_op jit(solution)/shard_map/ppermute | solution.py:497
  53.3 2.1 %collective-permute-start.26 = (bf16[32,2176]{1,0:T(8,128)(2,1)S(1)}, bf16[32,2176]{1,0:T(8,128)(2,1)S(1)}, u32[]{:S(2)}, u32[]{:S(2)}) collective-permute-start(bf16[32,2176]{1,0:T(8,128)(2,1)S(1)} %collective-permute-done.20.refs_1_), channel_id=1, source_target_pairs={{4,0},{8,4},{12,8},{14,12},{10,14},{6,10},{2,6},{0,2},{5,1},{9,5},... | collective-permute-start | bytes 417800 | tf_op jit(solution)/shard_map/ppermute | solution.py:495
  55.4 2.0 %collective-permute-start.28 = (bf16[32,2176]{1,0:T(8,128)(2,1)S(1)}, bf16[32,2176]{1,0:T(8,128)(2,1)S(1)}, u32[]{:S(2)}, u32[]{:S(2)}) collective-permute-start(bf16[32,2176]{1,0:T(8,128)(2,1)S(1)} %collective-permute-done.22.refs_3_), channel_id=1, source_target_pairs={{4,0},{8,4},{12,8},{14,12},{10,14},{6,10},{2,6},{0,2},{5,1},{9,5},... | collective-permute-start | bytes 417800 | tf_op jit(solution)/shard_map/ppermute | solution.py:498
  59.8 2.1 %collective-permute-start.30 = (bf16[32,2176]{1,0:T(8,128)(2,1)S(1)}, bf16[32,2176]{1,0:T(8,128)(2,1)S(1)}, u32[]{:S(2)}, u32[]{:S(2)}) collective-permute-start(bf16[32,2176]{1,0:T(8,128)(2,1)S(1)} %collective-permute-done.26.refs_1_), channel_id=1, source_target_pairs={{4,0},{8,4},{12,8},{14,12},{10,14},{6,10},{2,6},{0,2},{5,1},{9,5},... | collective-permute-start | bytes 417800 | tf_op jit(solution)/shard_map/ppermute | solution.py:495
  62.8 2.1 %collective-permute-start.32 = (bf16[32,2176]{1,0:T(8,128)(2,1)S(1)}, bf16[32,2176]{1,0:T(8,128)(2,1)S(1)}, u32[]{:S(2)}, u32[]{:S(2)}) collective-permute-start(bf16[32,2176]{1,0:T(8,128)(2,1)S(1)} %collective-permute-done.28.refs_3_), channel_id=1, source_target_pairs={{4,0},{8,4},{12,8},{14,12},{10,14},{6,10},{2,6},{0,2},{5,1},{9,5},... | collective-permute-start | bytes 417800 | tf_op jit(solution)/shard_map/ppermute | solution.py:498
  66.5 2.0 %collective-permute-start.33 = (bf16[32,2176]{1,0:T(8,128)(2,1)S(1)}, bf16[32,2176]{1,0:T(8,128)(2,1)S(1)}, u32[]{:S(2)}, u32[]{:S(2)}) collective-permute-start(bf16[32,2176]{1,0:T(8,128)(2,1)S(1)} %collective-permute-done.30.refs_1_), channel_id=1, source_target_pairs={{4,0},{8,4},{12,8},{14,12},{10,14},{6,10},{2,6},{0,2},{5,1},{9,5},... | collective-permute-start | bytes 417800 | tf_op jit(solution)/shard_map/ppermute | solution.py:495
  70.1 2.9 %collective-permute-done.29.refs_0_ = bf16[32,2176]{1,0:T(8,128)(2,1)S(1)} collective-permute-done((bf16[32,2176]{1,0:T(8,128)(2,1)S(1)}, bf16[32,2176]{1,0:T(8,128)(2,1)S(1)}, u32[]{:S(2)}, u32[]{:S(2)}) %collective-permute-start.29) | collective-permute-done | bytes 139296 | tf_op jit(solution)/shard_map/ppermute | solution.py:494
  74.6 2.1 %collective-permute-start.34 = (bf16[32,2048]{1,0:T(8,128)(2,1)S(1)}, bf16[32,2048]{1,0:T(8,128)(2,1)S(1)}, u32[]{:S(2)}, u32[]{:S(2)}) collective-permute-start(bf16[32,2048]{1,0:T(8,128)(2,1)S(1)} %convert_element_type.12), channel_id=1, source_target_pairs={{4,0},{8,4},{12,8},{14,12},{10,14},{6,10},{2,6},{0,2},{5,1},{9,5},... | collective-permute-start | bytes 393224 | tf_op jit(solution)/shard_map/ppermute | solution.py:520
  76.8 2.1 %collective-permute-start.38 = (bf16[32,2048]{1,0:T(8,128)(2,1)S(1)}, bf16[32,2048]{1,0:T(8,128)(2,1)S(1)}, u32[]{:S(2)}, u32[]{:S(2)}) collective-permute-start(bf16[32,2048]{1,0:T(8,128)(2,1)S(1)} %convert_element_type.13), channel_id=1, source_target_pairs={{4,0},{8,4},{12,8},{14,12},{10,14},{6,10},{2,6},{0,2},{5,1},{9,5},... | collective-permute-start | bytes 393224 | tf_op jit(solution)/shard_map/ppermute | solution.py:520
  81.0 1.9 %collective-permute-start.35 = (bf16[32,2048]{1,0:T(8,128)(2,1)S(1)}, bf16[32,2048]{1,0:T(8,128)(2,1)S(1)}, u32[]{:S(2)}, u32[]{:S(2)}) collective-permute-start(bf16[32,2048]{1,0:T(8,128)(2,1)S(1)} %add_share.10), channel_id=1, source_target_pairs={{4,0},{8,4},{12,8},{14,12},{10,14},{6,10},{2,6},{0,2},{5,1},{9,5},... | collective-permute-start | bytes 393224 | tf_op jit(solution)/shard_map/ppermute | solution.py:520
  83.8 1.9 %collective-permute-start.39 = (bf16[32,2048]{1,0:T(8,128)(2,1)S(1)}, bf16[32,2048]{1,0:T(8,128)(2,1)S(1)}, u32[]{:S(2)}, u32[]{:S(2)}) collective-permute-start(bf16[32,2048]{1,0:T(8,128)(2,1)S(1)} %add_share.13), channel_id=1, source_target_pairs={{4,0},{8,4},{12,8},{14,12},{10,14},{6,10},{2,6},{0,2},{5,1},{9,5},... | collective-permute-start | bytes 393224 | tf_op jit(solution)/shard_map/ppermute | solution.py:520
  87.0 2.1 %collective-permute-start.36 = (bf16[32,2048]{1,0:T(8,128)(2,1)S(1)}, bf16[32,2048]{1,0:T(8,128)(2,1)S(1)}, u32[]{:S(2)}, u32[]{:S(2)}) collective-permute-start(bf16[32,2048]{1,0:T(8,128)(2,1)S(1)} %add_share.11), channel_id=1, source_target_pairs={{4,0},{8,4},{12,8},{14,12},{10,14},{6,10},{2,6},{0,2},{5,1},{9,5},... | collective-permute-start | bytes 393224 | tf_op jit(solution)/shard_map/ppermute | solution.py:520
  89.2 2.1 %collective-permute-start.40 = (bf16[32,2048]{1,0:T(8,128)(2,1)S(1)}, bf16[32,2048]{1,0:T(8,128)(2,1)S(1)}, u32[]{:S(2)}, u32[]{:S(2)}) collective-permute-start(bf16[32,2048]{1,0:T(8,128)(2,1)S(1)} %add_share.14), channel_id=1, source_target_pairs={{4,0},{8,4},{12,8},{14,12},{10,14},{6,10},{2,6},{0,2},{5,1},{9,5},... | collective-permute-start | bytes 393224 | tf_op jit(solution)/shard_map/ppermute | solution.py:520
  92.1 2.1 %collective-permute-start.37 = (bf16[32,2048]{1,0:T(8,128)(2,1)S(1)}, bf16[32,2048]{1,0:T(8,128)(2,1)S(1)}, u32[]{:S(2)}, u32[]{:S(2)}) collective-permute-start(bf16[32,2048]{1,0:T(8,128)(2,1)S(1)} %add_share.12), channel_id=1, source_target_pairs={{4,0},{8,4},{12,8},{14,12},{10,14},{6,10},{2,6},{0,2},{5,1},{9,5},... | collective-permute-start | bytes 393224 | tf_op jit(solution)/shard_map/ppermute | solution.py:520
  (120 shorter events, 30.2 us)
Async XLA Ops:
  2.5 27.5 %collective-permute-start.7 = (bf16[2048,1024]{1,0:T(8,128)(2,1)}, bf16[2048,1024]{1,0:T(8,128)(2,1)S(1)}, u32[]{:S(2)}, u32[]{:S(2)}) collective-permute-start(bf16[2048,1024]{1,0:T(8,128)(2,1)} %refs_5_.1), channel_id=1, source_target_pairs={{0,1},{1,0},{2,3},{3,2},{4,5},{5,4},{6,7},{7,6},{8,9},{9,8},{10,11... | collective-permute-start | bytes 12582920 | tf_op jit(solution)/shard_map/ppermute | solution.py:34
  3.0 7.2 %collective-permute-start.10 = (bf16[272,256]{1,0:T(8,128)(2,1)}, bf16[272,256]{1,0:T(8,128)(2,1)S(1)}, u32[]{:S(2)}, u32[]{:S(2)}) collective-permute-start(bf16[272,256]{1,0:T(8,128)(2,1)} %get-tuple-element.97.refs_1_), channel_id=1, source_target_pairs={{0,1},{1,0},{2,3},{3,2},{4,5},{5,4},{6,7},{7,6},{8,9},{9,8},{10,11... | collective-permute-start | bytes 417800 | tf_op jit(solution)/shard_map/ppermute | solution.py:34
  3.0 12.0 %collective-permute-start.8 = (bf16[272,256]{1,0:T(8,128)(2,1)}, bf16[272,256]{1,0:T(8,128)(2,1)S(1)}, u32[]{:S(2)}, u32[]{:S(2)}) collective-permute-start(bf16[272,256]{1,0:T(8,128)(2,1)} %get-tuple-element.97.refs_1_), channel_id=1, source_target_pairs={{0,4},{4,8},{8,12},{12,0},{1,5},{5,9},{9,13},{13,1},{2,6},{6,10},{... | collective-permute-start | bytes 417800 | tf_op jit(solution)/shard_map/ppermute | solution.py:629
  6.0 11.0 %collective-permute-start.9 = (bf16[272,256]{1,0:T(8,128)(2,1)}, bf16[272,256]{1,0:T(8,128)(2,1)S(1)}, u32[]{:S(2)}, u32[]{:S(2)}) collective-permute-start(bf16[272,256]{1,0:T(8,128)(2,1)} %get-tuple-element.97.refs_1_), channel_id=1, source_target_pairs={{0,12},{4,0},{8,4},{12,8},{1,13},{5,1},{9,5},{13,9},{2,14},{6,2},{... | collective-permute-start | bytes 417800 | tf_op jit(solution)/shard_map/ppermute | solution.py:632
  8.1 9.0 %collective-permute-start.2 = (bf16[272,256]{1,0:T(8,128)(2,1)}, bf16[272,256]{1,0:T(8,128)(2,1)S(1)}, u32[]{:S(2)}, u32[]{:S(2)}) collective-permute-start(bf16[272,256]{1,0:T(8,128)(2,1)} %get-tuple-element.85.refs_1_), channel_id=1, source_target_pairs={{0,1},{1,0},{2,3},{3,2},{4,5},{5,4},{6,7},{7,6},{8,9},{9,8},{10,11... | collective-permute-start | bytes 417800 | tf_op jit(solution)/shard_map/ppermute | solution.py:34
  10.2 9.3 %collective-permute-start = (bf16[272,256]{1,0:T(8,128)(2,1)}, bf16[272,256]{1,0:T(8,128)(2,1)S(1)}, u32[]{:S(2)}, u32[]{:S(2)}) collective-permute-start(bf16[272,256]{1,0:T(8,128)(2,1)} %get-tuple-element.85.refs_1_), channel_id=1, source_target_pairs={{0,4},{4,8},{8,12},{12,0},{1,5},{5,9},{9,13},{13,1},{2,6},{6,10},{... | collective-permute-start | bytes 417800 | tf_op jit(solution)/shard_map/ppermute | solution.py:629
  15.0 7.3 %collective-permute-start.1 = (bf16[272,256]{1,0:T(8,128)(2,1)}, bf16[272,256]{1,0:T(8,128)(2,1)S(1)}, u32[]{:S(2)}, u32[]{:S(2)}) collective-permute-start(bf16[272,256]{1,0:T(8,128)(2,1)} %get-tuple-element.85.refs_1_), channel_id=1, source_target_pairs={{0,12},{4,0},{8,4},{12,8},{1,13},{5,1},{9,5},{13,9},{2,14},{6,2},{... | collective-permute-start | bytes 417800 | tf_op jit(solution)/shard_map/ppermute | solution.py:632
  19.5 8.1 %collective-permute-start.11 = (bf16[272,256]{1,0:T(8,128)(2,1)S(1)}, bf16[272,256]{1,0:T(8,128)(2,1)S(1)}, u32[]{:S(2)}, u32[]{:S(2)}) collective-permute-start(bf16[272,256]{1,0:T(8,128)(2,1)S(1)} %collective-permute-done.8.refs_1_), channel_id=1, source_target_pairs={{0,4},{4,8},{8,12},{12,0},{1,5},{5,9},{9,13},{13,1},{2,6},{6,10},{... | collective-permute-start | bytes 417800 | tf_op jit(solution)/shard_map/ppermute | solution.py:629
  22.8 7.2 %collective-permute-start.3 = (bf16[272,256]{1,0:T(8,128)(2,1)S(1)}, bf16[272,256]{1,0:T(8,128)(2,1)S(1)}, u32[]{:S(2)}, u32[]{:S(2)}) collective-permute-start(bf16[272,256]{1,0:T(8,128)(2,1)S(1)} %collective-permute-done.1.refs_3_), channel_id=1, source_target_pairs={{0,12},{4,0},{8,4},{12,8},{1,13},{5,1},{9,5},{13,9},{2,14},{6,2},{... | collective-permute-start | bytes 417800 | tf_op jit(solution)/shard_map/ppermute | solution.py:632
  34.3 23.1 %collective-permute-start.23 = (bf16[2,192,2048]{2,1,0:T(8,128)(2,1)S(1)}, bf16[2,192,2048]{2,1,0:T(8,128)(2,1)S(1)}, u32[]{:S(2)}, u32[]{:S(2)}) collective-permute-start(bf16[2,192,2048]{2,1,0:T(8,128)(2,1)S(1)} %bitcast.5), channel_id=1, source_target_pairs={{0,1},{1,0},{2,3},{3,2},{4,5},{5,4},{6,7},{7,6},{8,9},{9,8},{10,11... | collective-permute-start | bytes 4718600 | tf_op jit(solution)/shard_map/ppermute | solution.py:34
  34.9 20.5 %collective-permute-start.24 = (bf16[192,2048]{1,0:T(8,128)(2,1)S(1)}, bf16[192,2048]{1,0:T(8,128)(2,1)S(1)}, u32[]{:S(2)}, u32[]{:S(2)}) collective-permute-start(bf16[192,2048]{1,0:T(8,128)(2,1)S(1)} %bitcast.11), channel_id=1, source_target_pairs={{0,1},{1,0},{2,3},{3,2},{4,5},{5,4},{6,7},{7,6},{8,9},{9,8},{10,11... | collective-permute-start | bytes 2359304 | tf_op jit(solution)/shard_map/ppermute | solution.py:34
  35.5 6.4 %collective-permute-start.17 = (bf16[32,2048]{1,0:T(8,128)(2,1)S(1)}, bf16[32,2048]{1,0:T(8,128)(2,1)S(1)}, u32[]{:S(2)}, u32[]{:S(2)}) collective-permute-start(bf16[32,2048]{1,0:T(8,128)(2,1)S(1)} %get-tuple-element.123), channel_id=1, source_target_pairs={{0,2},{2,0},{1,3},{3,1},{4,6},{6,4},{5,7},{7,5},{8,10},{10,8},{9,1... | collective-permute-start | bytes 393224 | tf_op jit(solution)/shard_map/ppermute | solution.py:670
  37.2 6.6 %collective-permute-start.15 = (bf16[32,2048]{1,0:T(8,128)(2,1)S(1)}, bf16[32,2048]{1,0:T(8,128)(2,1)S(1)}, u32[]{:S(2)}, u32[]{:S(2)}) collective-permute-start(bf16[32,2048]{1,0:T(8,128)(2,1)S(1)} %get-tuple-element.117), channel_id=1, source_target_pairs={{0,2},{2,0},{1,3},{3,1},{4,6},{6,4},{5,7},{7,5},{8,10},{10,8},{9,1... | collective-permute-start | bytes 393224 | tf_op jit(solution)/shard_map/ppermute | solution.py:670
  43.9 6.9 %collective-permute-start.18 = (bf16[32,2176]{1,0:T(8,128)(2,1)S(1)}, bf16[32,2176]{1,0:T(8,128)(2,1)S(1)}, u32[]{:S(2)}, u32[]{:S(2)}) collective-permute-start(bf16[32,2176]{1,0:T(8,128)(2,1)S(1)} %get-tuple-element.147.refs_0_), channel_id=1, source_target_pairs={{0,4},{4,8},{8,12},{12,14},{14,10},{10,6},{6,2},{2,0},{1,5},{5,9},... | collective-permute-start | bytes 417800 | tf_op jit(solution)/shard_map/ppermute | solution.py:494
  44.6 8.8 %collective-permute-start.21 = (bf16[32,2176]{1,0:T(8,128)(2,1)S(1)}, bf16[32,2176]{1,0:T(8,128)(2,1)S(1)}, u32[]{:S(2)}, u32[]{:S(2)}) collective-permute-start(bf16[32,2176]{1,0:T(8,128)(2,1)S(1)} %get-tuple-element.148.refs_1_), channel_id=1, source_target_pairs={{0,4},{4,8},{8,12},{12,14},{14,10},{10,6},{6,2},{2,0},{1,5},{5,9},... | collective-permute-start | bytes 417800 | tf_op jit(solution)/shard_map/ppermute | solution.py:497
  47.1 8.3 %collective-permute-start.22 = (bf16[32,2176]{1,0:T(8,128)(2,1)S(1)}, bf16[32,2176]{1,0:T(8,128)(2,1)S(1)}, u32[]{:S(2)}, u32[]{:S(2)}) collective-permute-start(bf16[32,2176]{1,0:T(8,128)(2,1)S(1)} %get-tuple-element.147.refs_0_), channel_id=1, source_target_pairs={{4,0},{8,4},{12,8},{14,12},{10,14},{6,10},{2,6},{0,2},{5,1},{9,5},... | collective-permute-start | bytes 417800 | tf_op jit(solution)/shard_map/ppermute | solution.py:498
  50.9 8.1 %collective-permute-start.19 = (bf16[32,2176]{1,0:T(8,128)(2,1)S(1)}, bf16[32,2176]{1,0:T(8,128)(2,1)S(1)}, u32[]{:S(2)}, u32[]{:S(2)}) collective-permute-start(bf16[32,2176]{1,0:T(8,128)(2,1)S(1)} %collective-permute-done.18.refs_0_), channel_id=1, source_target_pairs={{0,4},{4,8},{8,12},{12,14},{14,10},{10,6},{6,2},{2,0},{1,5},{5,9},... | collective-permute-start | bytes 417800 | tf_op jit(solution)/shard_map/ppermute | solution.py:494
  53.3 6.4 %collective-permute-start.26 = (bf16[32,2176]{1,0:T(8,128)(2,1)S(1)}, bf16[32,2176]{1,0:T(8,128)(2,1)S(1)}, u32[]{:S(2)}, u32[]{:S(2)}) collective-permute-start(bf16[32,2176]{1,0:T(8,128)(2,1)S(1)} %collective-permute-done.20.refs_1_), channel_id=1, source_target_pairs={{4,0},{8,4},{12,8},{14,12},{10,14},{6,10},{2,6},{0,2},{5,1},{9,5},... | collective-permute-start | bytes 417800 | tf_op jit(solution)/shard_map/ppermute | solution.py:495
  55.4 6.5 %collective-permute-start.27 = (bf16[32,2176]{1,0:T(8,128)(2,1)S(1)}, bf16[32,2176]{1,0:T(8,128)(2,1)S(1)}, u32[]{:S(2)}, u32[]{:S(2)}) collective-permute-start(bf16[32,2176]{1,0:T(8,128)(2,1)S(1)} %collective-permute-done.21.refs_2_), channel_id=1, source_target_pairs={{0,4},{4,8},{8,12},{12,14},{14,10},{10,6},{6,2},{2,0},{1,5},{5,9},... | collective-permute-start | bytes 417800 | tf_op jit(solution)/shard_map/ppermute | solution.py:497
  55.4 7.3 %collective-permute-start.28 = (bf16[32,2176]{1,0:T(8,128)(2,1)S(1)}, bf16[32,2176]{1,0:T(8,128)(2,1)S(1)}, u32[]{:S(2)}, u32[]{:S(2)}) collective-permute-start(bf16[32,2176]{1,0:T(8,128)(2,1)S(1)} %collective-permute-done.22.refs_3_), channel_id=1, source_target_pairs={{4,0},{8,4},{12,8},{14,12},{10,14},{6,10},{2,6},{0,2},{5,1},{9,5},... | collective-permute-start | bytes 417800 | tf_op jit(solution)/shard_map/ppermute | solution.py:498
  59.0 7.4 %collective-permute-start.25 = (bf16[32,2176]{1,0:T(8,128)(2,1)S(1)}, bf16[32,2176]{1,0:T(8,128)(2,1)S(1)}, u32[]{:S(2)}, u32[]{:S(2)}) collective-permute-start(bf16[32,2176]{1,0:T(8,128)(2,1)S(1)} %collective-permute-done.19.refs_0_), channel_id=1, source_target_pairs={{0,4},{4,8},{8,12},{12,14},{14,10},{10,6},{6,2},{2,0},{1,5},{5,9},... | collective-permute-start | bytes 417800 | tf_op jit(solution)/shard_map/ppermute | solution.py:494
  59.8 6.7 %collective-permute-start.30 = (bf16[32,2176]{1,0:T(8,128)(2,1)S(1)}, bf16[32,2176]{1,0:T(8,128)(2,1)S(1)}, u32[]{:S(2)}, u32[]{:S(2)}) collective-permute-start(bf16[32,2176]{1,0:T(8,128)(2,1)S(1)} %collective-permute-done.26.refs_1_), channel_id=1, source_target_pairs={{4,0},{8,4},{12,8},{14,12},{10,14},{6,10},{2,6},{0,2},{5,1},{9,5},... | collective-permute-start | bytes 417800 | tf_op jit(solution)/shard_map/ppermute | solution.py:495
  61.9 6.6 %collective-permute-start.31 = (bf16[32,2176]{1,0:T(8,128)(2,1)S(1)}, bf16[32,2176]{1,0:T(8,128)(2,1)S(1)}, u32[]{:S(2)}, u32[]{:S(2)}) collective-permute-start(bf16[32,2176]{1,0:T(8,128)(2,1)S(1)} %collective-permute-done.27.refs_2_), channel_id=1, source_target_pairs={{0,4},{4,8},{8,12},{12,14},{14,10},{10,6},{6,2},{2,0},{1,5},{5,9},... | collective-permute-start | bytes 417800 | tf_op jit(solution)/shard_map/ppermute | solution.py:497
  66.4 6.5 %collective-permute-start.29 = (bf16[32,2176]{1,0:T(8,128)(2,1)S(1)}, bf16[32,2176]{1,0:T(8,128)(2,1)S(1)}, u32[]{:S(2)}, u32[]{:S(2)}) collective-permute-start(bf16[32,2176]{1,0:T(8,128)(2,1)S(1)} %collective-permute-done.25.refs_0_), channel_id=1, source_target_pairs={{0,4},{4,8},{8,12},{12,14},{14,10},{10,6},{6,2},{2,0},{1,5},{5,9},... | collective-permute-start | bytes 417800 | tf_op jit(solution)/shard_map/ppermute | solution.py:494
  66.5 6.4 %collective-permute-start.33 = (bf16[32,2176]{1,0:T(8,128)(2,1)S(1)}, bf16[32,2176]{1,0:T(8,128)(2,1)S(1)}, u32[]{:S(2)}, u32[]{:S(2)}) collective-permute-start(bf16[32,2176]{1,0:T(8,128)(2,1)S(1)} %collective-permute-done.30.refs_1_), channel_id=1, source_target_pairs={{4,0},{8,4},{12,8},{14,12},{10,14},{6,10},{2,6},{0,2},{5,1},{9,5},... | collective-permute-start | bytes 417800 | tf_op jit(solution)/shard_map/ppermute | solution.py:495
  74.6 6.4 %collective-permute-start.34 = (bf16[32,2048]{1,0:T(8,128)(2,1)S(1)}, bf16[32,2048]{1,0:T(8,128)(2,1)S(1)}, u32[]{:S(2)}, u32[]{:S(2)}) collective-permute-start(bf16[32,2048]{1,0:T(8,128)(2,1)S(1)} %convert_element_type.12), channel_id=1, source_target_pairs={{4,0},{8,4},{12,8},{14,12},{10,14},{6,10},{2,6},{0,2},{5,1},{9,5},... | collective-permute-start | bytes 393224 | tf_op jit(solution)/shard_map/ppermute | solution.py:520
  76.7 6.5 %collective-permute-start.41 = (bf16[32,2048]{1,0:T(8,128)(2,1)S(1)}, bf16[32,2048]{1,0:T(8,128)(2,1)S(1)}, u32[]{:S(2)}, u32[]{:S(2)}) collective-permute-start(bf16[32,2048]{1,0:T(8,128)(2,1)S(1)} %convert_element_type.14), channel_id=1, source_target_pairs={{0,4},{4,8},{8,12},{12,14},{14,10},{10,6},{6,2},{2,0},{1,5},{5,9},... | collective-permute-start | bytes 393224 | tf_op jit(solution)/shard_map/ppermute | solution.py:520
  76.8 6.9 %collective-permute-start.38 = (bf16[32,2048]{1,0:T(8,128)(2,1)S(1)}, bf16[32,2048]{1,0:T(8,128)(2,1)S(1)}, u32[]{:S(2)}, u32[]{:S(2)}) collective-permute-start(bf16[32,2048]{1,0:T(8,128)(2,1)S(1)} %convert_element_type.13), channel_id=1, source_target_pairs={{4,0},{8,4},{12,8},{14,12},{10,14},{6,10},{2,6},{0,2},{5,1},{9,5},... | collective-permute-start | bytes 393224 | tf_op jit(solution)/shard_map/ppermute | solution.py:520
  80.3 6.6 %collective-permute-start.45 = (bf16[32,2048]{1,0:T(8,128)(2,1)S(1)}, bf16[32,2048]{1,0:T(8,128)(2,1)S(1)}, u32[]{:S(2)}, u32[]{:S(2)}) collective-permute-start(bf16[32,2048]{1,0:T(8,128)(2,1)S(1)} %add_share.17), channel_id=1, source_target_pairs={{0,4},{4,8},{8,12},{12,14},{14,10},{10,6},{6,2},{2,0},{1,5},{5,9},... | collective-permute-start | bytes 393224 | tf_op jit(solution)/shard_map/ppermute | solution.py:520
  81.0 6.0 %collective-permute-start.35 = (bf16[32,2048]{1,0:T(8,128)(2,1)S(1)}, bf16[32,2048]{1,0:T(8,128)(2,1)S(1)}, u32[]{:S(2)}, u32[]{:S(2)}) collective-permute-start(bf16[32,2048]{1,0:T(8,128)(2,1)S(1)} %add_share.10), channel_id=1, source_target_pairs={{4,0},{8,4},{12,8},{14,12},{10,14},{6,10},{2,6},{0,2},{5,1},{9,5},... | collective-permute-start | bytes 393224 | tf_op jit(solution)/shard_map/ppermute | solution.py:520
  89.1 6.5 %collective-permute-start.43 = (bf16[32,2048]{1,0:T(8,128)(2,1)S(1)}, bf16[32,2048]{1,0:T(8,128)(2,1)S(1)}, u32[]{:S(2)}, u32[]{:S(2)}) collective-permute-start(bf16[32,2048]{1,0:T(8,128)(2,1)S(1)} %add_share.16), channel_id=1, source_target_pairs={{0,4},{4,8},{8,12},{12,14},{14,10},{10,6},{6,2},{2,0},{1,5},{5,9},... | collective-permute-start | bytes 393224 | tf_op jit(solution)/shard_map/ppermute | solution.py:520
  89.2 6.4 %collective-permute-start.40 = (bf16[32,2048]{1,0:T(8,128)(2,1)S(1)}, bf16[32,2048]{1,0:T(8,128)(2,1)S(1)}, u32[]{:S(2)}, u32[]{:S(2)}) collective-permute-start(bf16[32,2048]{1,0:T(8,128)(2,1)S(1)} %add_share.14), channel_id=1, source_target_pairs={{4,0},{8,4},{12,8},{14,12},{10,14},{6,10},{2,6},{0,2},{5,1},{9,5},... | collective-permute-start | bytes 393224 | tf_op jit(solution)/shard_map/ppermute | solution.py:520
  (27 other events, 127.5 us)

commit v6 on v5

--- a/solution.py
+++ b/solution.py
@@ -285,15 +285,6 @@
             results = len(out_shape)
             result_refs, refs = refs[:results], refs[results:]
             head_ref, refs = refs[0], refs[1:]
-            held_refs, sems = refs[: len(weights)], refs[len(weights)]
-            copies = [
-                pltpu.make_async_copy(
-                    w.at[pl.ds(kv * head_columns, head_columns), :], held, sems.at[i]
-                )
-                for i, (w, held) in enumerate(zip(weight_refs, held_refs))
-            ]
-            for copy in copies:
-                copy.start()
         else:
             m_out, acc_out = refs
         sub = lax.axis_index("sub")
@@ -358,13 +349,14 @@
                 m_out[here, :] = top
                 acc_out[here, :] = acc
         if last:
-            for copy in copies:
-                copy.wait()
             source = head_ref[...]
-            width = held_refs[0].shape[1]
-            for i, held in enumerate(held_refs):
+            width = weight_refs[0].shape[1]
+            these = slice(kv * head_columns, (kv + 1) * head_columns)
+            for i, weight_ref in enumerate(weight_refs):
                 here = slice(i * width, (i + 1) * width)
-                product = jnp.dot(source, held[...], preferred_element_type=jnp.float32)
+                product = jnp.dot(
+                    source, weight_ref[these, :], preferred_element_type=jnp.float32
+                )
                 if earlier is not None:
                     product = product + earlier_ref[:, here]
                 if final:
@@ -375,7 +367,6 @@
                     result_refs[0][:, here] = product
 
     vmem = pl.BlockSpec(memory_space=pltpu.VMEM)
-    anywhere = pl.BlockSpec(memory_space=pl.ANY)
     scratch = []
     if last:
         features = sum(w.shape[1] for w in weights)
@@ -391,24 +382,20 @@
         else:
             out_shape = (jax.ShapeDtypeStruct((all_rows, features), jnp.float32),)
         scratch = [pltpu.VMEM((all_rows, head_columns), jnp.bfloat16)]
-        scratch += [pltpu.VMEM((head_columns, w.shape[1]), w.dtype) for w in weights]
-        scratch += [pltpu.SemaphoreType.DMA((len(weights),))]
     else:
         out_shape = (
             jax.ShapeDtypeStruct((per_kv * all_rows, LANES), jnp.float32),
             jax.ShapeDtypeStruct((per_kv * all_rows, 2 * HD), jnp.float32),
         )
     operands = [queries] + list(blocks) + (list(state) if state is not None else [])
-    in_specs = [vmem] * len(operands) + [anywhere] * len(weights)
     operands += list(weights)
     if earlier is not None:
         operands.append(earlier)
-        in_specs.append(vmem)
     scores = all_rows * per_kv * keys * len(blocks)
     return pl.pallas_call(
         kernel,
         out_shape=out_shape,
-        in_specs=in_specs,
+        in_specs=[vmem] * len(operands),
         out_specs=tuple(vmem for _ in out_shape),
         scratch_shapes=scratch,
         compiler_params=pltpu.CompilerParams(vmem_limit_bytes=16 * MIB),
@@ -621,6 +608,14 @@
         if distance == 0:
             out_proj, packed = lax.optimization_barrier((out_proj, packed))
             projections = sub_copies(out_proj)
+        if distance == reach and dense:
+            blocks = [x for kv_stages in stages for _, x in kv_stages]
+            gate_up, w_down, blocks = lax.optimization_barrier((gate_up, w_down, blocks))
+            stages = [
+                [(hop, blocks.pop(0)) for hop, _ in kv_stages] for kv_stages in stages
+            ]
+            gate_up_parts = sub_copies(gate_up[0])
+            w_down_parts = sub_copies(w_down[0])
         onward = [[] for _ in packed]
         if distance < reach:
             opposite = 2 * (distance + 1) == n_ep
@@ -660,10 +655,6 @@
             residual_parts = hand_over(split_rows(residual, n_sub))
             gate_table = gates_by_expert(expert_ids, gates, rows) if dense else None
         arrived = onward
-    if dense:
-        gate_up, w_down, states[-1] = lax.optimization_barrier((gate_up, w_down, states[-1]))
-        gate_up_parts = sub_copies(gate_up[0])
-        w_down_parts = sub_copies(w_down[0])
     parts = states[-1]
     if n_hd == 2:
         kept, sent = parts[: len(parts) // 2], parts[len(parts) // 2 :]

time: 99.6 us -> 97.7 us (0.981)
  starting transfers between devices: 49 us -> 46.8 us
  waiting for transfers between devices: 25.2 us -> 26.5 us
    ppermute x4, waiting for transfers between devices: 4.92 us -> 1.26 us  [dense_experts(): behind[0] = lax.ppermute(behind[0], axes, ahead)]
    ppermute x2, waiting for transfers between devices: 2.63 us -> 5.95 us  [shards(): came = [lax.ppermute(x, 'hd', cycle(n_hd)) for x in sent]]
    ppermute x4, starting transfers between devices: 7.92 us -> 5.28 us  [dense_experts(): before[1] = lax.ppermute(before[1], axes, back)]
    ppermute x3, waiting for transfers between devices: 2.19 us -> 0.01 us  [dense_experts(): behind[1] = lax.ppermute(behind[1], axes, ahead)]
    ppermute x3, starting transfers between devices: 5.83 us -> 3.9 us  [dense_experts(): before[0] = lax.ppermute(before[0], axes, back)]
    ppermute x14, waiting for transfers between devices: 5.23 us -> 6.97 us  [dense_experts(): chunks[chunk] = lax.ppermute(sum_here, axes, way)]
    ppermute x4, starting transfers between devices: 1.27 us -> 2.9 us  [dense_experts(): behind[0] = lax.ppermute(behind[0], axes, ahead)]
    ppermute x3, starting transfers between devices: 0.57 us -> 2.15 us  [dense_experts(): behind[1] = lax.ppermute(behind[1], axes, ahead)]
  transfers between devices with their start and end apart: 49 -> 49, of which waited for: 18 -> 23; matrix products, arithmetic and copies ran while one was open for 0% -> 0% of each run, Pallas kernels for 15% -> 16%
where the time goes in v6:
time: 97.7 us; the launch traced here: 97.4 us
  starting transfers between devices  46.8 us (48%)
  waiting for transfers between devices  26.5 us (27%)
  Pallas kernels  20 us (20%)
  local copies, waits for them, and re-layouts  3.09 us (3%)
  between operations  1.04 us (1%)
    ppermute x14, starting transfers between devices, dense_experts(): chunks[chunk] = lax.ppermute(sum_here, axes, way)  14.7 us
    pallas_call x6, Pallas kernels, attend(): pl.pallas_call(kernel, out_shape=out_shape, in_specs=[vmem] * len(operand...  8.78 us
    pallas_call x5, Pallas kernels, apply_expert(): pl.pallas_call(kernel, out_shape=[jax.ShapeDtypeStruct((x.shape[0], featu...  7.67 us
    ppermute x3, starting transfers between devices, shards(): down[kv] = lax.ppermute(down[kv], 'ep', cycle(n_ep, n_ep - 1))  7.06 us
    ppermute x14, waiting for transfers between devices, dense_experts(): chunks[chunk] = lax.ppermute(sum_here, axes, way)  6.97 us
    ppermute x3, starting transfers between devices, shards(): up[kv] = lax.ppermute(up[kv], 'ep', cycle(n_ep))  6.24 us
    ppermute x2, waiting for transfers between devices, shards(): came = [lax.ppermute(x, 'hd', cycle(n_hd)) for x in sent]  5.95 us
    ppermute x4, starting transfers between devices, dense_experts(): before[1] = lax.ppermute(before[1], axes, back)  5.28 us
  transfers between devices with their start and end apart: 49, of which 23 were waited for; matrix products, arithmetic and copies ran while one was open for 0% of the time, Pallas kernels for 16%

profile of v6, /device:TPU:0, one launch (start us, length us, event | category | flops | bytes accessed | tf_op | source)
XLA Modules:
  0.0 97.4 jit_solution(11665920235267623065)
XLA Ops:
  0.7 1.9 %pack_keys.1 = (bf16[272,256]{1,0:T(8,128)(2,1)}, bf16[272,256]{1,0:T(8,128)(2,1)}) custom-call(s32[1]{0:T(128)S(6)} %copy.14.page_ref, bf16[128,512]{1,0:T(8,128)(2,1)} %ck_ref.1, bf16[128,512]{1,0:T(8,128)(2,1)} %cv_ref.1, bf16[128,512]{1,0:T(8,128)(2,1)} %nk_ref.1, bf16[128,512]{1,0:T(8,128)(2,1)} %nv_ref.1), custom_call_target="tpu_custom_call" | custom-call | tf_op jit(solution)/shard_map/pack_keys/pallas_call | solution.py:81
  3.0 3.0 %collective-permute-start = (bf16[272,256]{1,0:T(8,128)(2,1)}, bf16[272,256]{1,0:T(8,128)(2,1)S(1)}, u32[]{:S(2)}, u32[]{:S(2)}) collective-permute-start(bf16[272,256]{1,0:T(8,128)(2,1)} %get-tuple-element.85.refs_1_), channel_id=1, source_target_pairs={{0,4},{4,8},{8,12},{12,0},{1,5},{5,9},{9,13},{13,1},{2,6},{6,10},{... | collective-permute-start | bytes 417800 | tf_op jit(solution)/shard_map/ppermute | solution.py:624
  6.0 2.0 %collective-permute-start.1 = (bf16[272,256]{1,0:T(8,128)(2,1)}, bf16[272,256]{1,0:T(8,128)(2,1)S(1)}, u32[]{:S(2)}, u32[]{:S(2)}) collective-permute-start(bf16[272,256]{1,0:T(8,128)(2,1)} %get-tuple-element.85.refs_1_), channel_id=1, source_target_pairs={{0,12},{4,0},{8,4},{12,8},{1,13},{5,1},{9,5},{13,9},{2,14},{6,2},{... | collective-permute-start | bytes 417800 | tf_op jit(solution)/shard_map/ppermute | solution.py:627
  10.2 2.9 %collective-permute-start.7 = (bf16[272,256]{1,0:T(8,128)(2,1)}, bf16[272,256]{1,0:T(8,128)(2,1)S(1)}, u32[]{:S(2)}, u32[]{:S(2)}) collective-permute-start(bf16[272,256]{1,0:T(8,128)(2,1)} %get-tuple-element.97.refs_1_), channel_id=1, source_target_pairs={{0,4},{4,8},{8,12},{12,0},{1,5},{5,9},{9,13},{13,1},{2,6},{6,10},{... | collective-permute-start | bytes 417800 | tf_op jit(solution)/shard_map/ppermute | solution.py:624
  15.0 2.1 %collective-permute-start.8 = (bf16[272,256]{1,0:T(8,128)(2,1)}, bf16[272,256]{1,0:T(8,128)(2,1)S(1)}, u32[]{:S(2)}, u32[]{:S(2)}) collective-permute-start(bf16[272,256]{1,0:T(8,128)(2,1)} %get-tuple-element.97.refs_1_), channel_id=1, source_target_pairs={{0,12},{4,0},{8,4},{12,8},{1,13},{5,1},{9,5},{13,9},{2,14},{6,2},{... | collective-permute-start | bytes 417800 | tf_op jit(solution)/shard_map/ppermute | solution.py:627
  19.8 2.5 %collective-permute-done.8.refs_3_ = bf16[272,256]{1,0:T(8,128)(2,1)S(1)} collective-permute-done((bf16[272,256]{1,0:T(8,128)(2,1)}, bf16[272,256]{1,0:T(8,128)(2,1)S(1)}, u32[]{:S(2)}, u32[]{:S(2)}) %collective-permute-start.8) | collective-permute-done | bytes 139296 | tf_op jit(solution)/shard_map/ppermute | solution.py:627
  22.8 2.9 %collective-permute-start.10 = (bf16[272,256]{1,0:T(8,128)(2,1)S(1)}, bf16[272,256]{1,0:T(8,128)(2,1)S(1)}, u32[]{:S(2)}, u32[]{:S(2)}) collective-permute-start(bf16[272,256]{1,0:T(8,128)(2,1)S(1)} %collective-permute-done.8.refs_3_), channel_id=1, source_target_pairs={{0,12},{4,0},{8,4},{12,8},{1,13},{5,1},{9,5},{13,9},{2,14},{6,2},{... | collective-permute-start | bytes 417800 | tf_op jit(solution)/shard_map/ppermute | solution.py:627
  25.8 1.8 %attend.7 = (f32[1024,128]{1,0:T(8,128)S(1)}, f32[1024,256]{1,0:T(8,128)S(1)}) custom-call(bf16[128,2048]{1,0:T(8,128)(2,1)S(1)} %choose_queries.1.refs_0_, bf16[272,256]{1,0:T(8,128)(2,1)S(1)} %collective-permute-done.refs_1_, bf16[272,256]{1,0:T(8,128)(2,1)S(1)} %collective-permute-done.4.refs_2_, bf16[272,256]{1,0:T(8,128)(2,1)S(1)} %collective-permute-done.1.refs_3_, ...), custom_call_target="tpu_custom_call" | custom-call | flops 805306368 | bytes 4194304 | tf_op jit(solution)/shard_map/attend/pallas_call | solution.py:395
  27.7 1.8 %attend.9 = (f32[1024,128]{1,0:T(8,128)S(1)}, f32[1024,256]{1,0:T(8,128)S(1)}) custom-call(bf16[128,2048]{1,0:T(8,128)(2,1)S(1)} %choose_queries.1.refs_0_, bf16[272,256]{1,0:T(8,128)(2,1)S(1)} %collective-permute-done.7.refs_1_, bf16[272,256]{1,0:T(8,128)(2,1)S(1)} %collective-permute-done.11.refs_2_, bf16[272,256]{1,0:T(8,128)(2,1)S(1)} %collective-permute-done.8.refs_3_, ...), custom_call_target="tpu_custom_call" | custom-call | flops 805306368 | bytes 4194304 | tf_op jit(solution)/shard_map/attend/pallas_call | solution.py:395
  30.0 1.3 %collective-permute-done.13.refs_2_ = bf16[272,256]{1,0:T(8,128)(2,1)S(1)} collective-permute-done((bf16[272,256]{1,0:T(8,128)(2,1)S(1)}, bf16[272,256]{1,0:T(8,128)(2,1)S(1)}, u32[]{:S(2)}, u32[]{:S(2)}) %collective-permute-start.13) | collective-permute-done | bytes 139296 | tf_op jit(solution)/shard_map/ppermute | solution.py:34
  32.1 1.6 %attend.10.refs_7_ = f32[128,2048]{1,0:T(8,128)S(1)} custom-call(bf16[128,2048]{1,0:T(8,128)(2,1)S(1)} %choose_queries.1.refs_0_, bf16[272,256]{1,0:T(8,128)(2,1)S(1)} %collective-permute-done.3.refs_1_, bf16[272,256]{1,0:T(8,128)(2,1)S(1)} %collective-permute-done.6.refs_2_, f32[1024,128]{1,0:T(8,128)S(1)} %get-tuple-element.114.refs_3_, ...), custom_call_target="tpu_custom_call" | custom-call | flops 402653184 | bytes 4194304 | tf_op jit(solution)/shard_map/attend/pallas_call | solution.py:395
  33.8 1.7 %attend.11 = (f32[32,2048]{1,0:T(8,128)S(1)}, f32[32,2048]{1,0:T(8,128)S(1)}, bf16[32,2048]{1,0:T(8,128)(2,1)S(1)}, bf16[32,2048]{1,0:T(8,128)(2,1)S(1)}) custom-call(bf16[128,2048]{1,0:T(8,128)(2,1)S(1)} %choose_queries.1.refs_0_, bf16[272,256]{1,0:T(8,128)(2,1)S(1)} %collective-permute-done.10.refs_1_, ...), custom_call_target="tpu_custom_call" | custom-call | flops 402653184 | bytes 4194304 | tf_op jit(solution)/shard_map/attend/pallas_call | solution.py:395
  35.4 1.8 %collective-permute-start.15 = (bf16[32,2048]{1,0:T(8,128)(2,1)S(1)}, bf16[32,2048]{1,0:T(8,128)(2,1)S(1)}, u32[]{:S(2)}, u32[]{:S(2)}) collective-permute-start(bf16[32,2048]{1,0:T(8,128)(2,1)S(1)} %get-tuple-element.117), channel_id=1, source_target_pairs={{0,2},{2,0},{1,3},{3,1},{4,6},{6,4},{5,7},{7,5},{8,10},{10,8},{9,1... | collective-permute-start | bytes 393224 | tf_op jit(solution)/shard_map/ppermute | solution.py:661
  37.7 4.1 %collective-permute-done.15.refs_1_ = bf16[32,2048]{1,0:T(8,128)(2,1)S(1)} collective-permute-done((bf16[32,2048]{1,0:T(8,128)(2,1)S(1)}, bf16[32,2048]{1,0:T(8,128)(2,1)S(1)}, u32[]{:S(2)}, u32[]{:S(2)}) %collective-permute-start.15) | collective-permute-done | bytes 131104 | tf_op jit(solution)/shard_map/ppermute | solution.py:661
  42.6 1.8 %collective-permute-done.17.refs_1_ = bf16[32,2048]{1,0:T(8,128)(2,1)S(1)} collective-permute-done((bf16[32,2048]{1,0:T(8,128)(2,1)S(1)}, bf16[32,2048]{1,0:T(8,128)(2,1)S(1)}, u32[]{:S(2)}, u32[]{:S(2)}) %collective-permute-start.17) | collective-permute-done | bytes 131104 | tf_op jit(solution)/shard_map/ppermute | solution.py:661
  44.6 1.4 %collective-permute-start.20 = (bf16[32,2176]{1,0:T(8,128)(2,1)S(1)}, bf16[32,2176]{1,0:T(8,128)(2,1)S(1)}, u32[]{:S(2)}, u32[]{:S(2)}) collective-permute-start(bf16[32,2176]{1,0:T(8,128)(2,1)S(1)} %get-tuple-element.148.refs_1_), channel_id=1, source_target_pairs={{4,0},{8,4},{12,8},{14,12},{10,14},{6,10},{2,6},{0,2},{5,1},{9,5},... | collective-permute-start | bytes 417800 | tf_op jit(solution)/shard_map/ppermute | solution.py:482
  46.7 1.3 %collective-permute-start.22 = (bf16[32,2176]{1,0:T(8,128)(2,1)S(1)}, bf16[32,2176]{1,0:T(8,128)(2,1)S(1)}, u32[]{:S(2)}, u32[]{:S(2)}) collective-permute-start(bf16[32,2176]{1,0:T(8,128)(2,1)S(1)} %get-tuple-element.147.refs_0_), channel_id=1, source_target_pairs={{4,0},{8,4},{12,8},{14,12},{10,14},{6,10},{2,6},{0,2},{5,1},{9,5},... | collective-permute-start | bytes 417800 | tf_op jit(solution)/shard_map/ppermute | solution.py:485
  48.8 2.5 %collective-permute-done.20.refs_1_ = bf16[32,2176]{1,0:T(8,128)(2,1)S(1)} collective-permute-done((bf16[32,2176]{1,0:T(8,128)(2,1)S(1)}, bf16[32,2176]{1,0:T(8,128)(2,1)S(1)}, u32[]{:S(2)}, u32[]{:S(2)}) %collective-permute-start.20) | collective-permute-done | bytes 139296 | tf_op jit(solution)/shard_map/ppermute | solution.py:482
  51.3 1.3 %collective-permute-start.26 = (bf16[32,2176]{1,0:T(8,128)(2,1)S(1)}, bf16[32,2176]{1,0:T(8,128)(2,1)S(1)}, u32[]{:S(2)}, u32[]{:S(2)}) collective-permute-start(bf16[32,2176]{1,0:T(8,128)(2,1)S(1)} %collective-permute-done.20.refs_1_), channel_id=1, source_target_pairs={{4,0},{8,4},{12,8},{14,12},{10,14},{6,10},{2,6},{0,2},{5,1},{9,5},... | collective-permute-start | bytes 417800 | tf_op jit(solution)/shard_map/ppermute | solution.py:482
  54.3 1.3 %collective-permute-start.28 = (bf16[32,2176]{1,0:T(8,128)(2,1)S(1)}, bf16[32,2176]{1,0:T(8,128)(2,1)S(1)}, u32[]{:S(2)}, u32[]{:S(2)}) collective-permute-start(bf16[32,2176]{1,0:T(8,128)(2,1)S(1)} %collective-permute-done.22.refs_3_), channel_id=1, source_target_pairs={{4,0},{8,4},{12,8},{14,12},{10,14},{6,10},{2,6},{0,2},{5,1},{9,5},... | collective-permute-start | bytes 417800 | tf_op jit(solution)/shard_map/ppermute | solution.py:485
  55.6 1.5 %apply_expert.5 = (f32[32,2048]{1,0:T(8,128)S(1)}, f32[32,2048]{1,0:T(8,128)S(1)}, f32[32,2048]{1,0:T(8,128)S(1)}, f32[32,2048]{1,0:T(8,128)S(1)}) custom-call(bf16[32,2176]{1,0:T(8,128)(2,1)S(1)} %collective-permute-done.18.refs_0_, bf16[32,2176]{1,0:T(8,128)(2,1)S(1)} %collective-permute-done.20.refs_1_, ...), custom_call_target="tpu_custom_call" | custom-call | flops 603979776 | bytes 6291456 | tf_op jit(solution)/shard_map/apply_expert/pallas_call | solution.py:441
  57.9 1.3 %collective-permute-start.30 = (bf16[32,2176]{1,0:T(8,128)(2,1)S(1)}, bf16[32,2176]{1,0:T(8,128)(2,1)S(1)}, u32[]{:S(2)}, u32[]{:S(2)}) collective-permute-start(bf16[32,2176]{1,0:T(8,128)(2,1)S(1)} %collective-permute-done.26.refs_1_), channel_id=1, source_target_pairs={{4,0},{8,4},{12,8},{14,12},{10,14},{6,10},{2,6},{0,2},{5,1},{9,5},... | collective-permute-start | bytes 417800 | tf_op jit(solution)/shard_map/ppermute | solution.py:482
  62.1 1.6 %apply_expert.6 = (f32[32,2048]{1,0:T(8,128)S(1)}, f32[32,2048]{1,0:T(8,128)S(1)}, f32[32,2048]{1,0:T(8,128)S(1)}, f32[32,2048]{1,0:T(8,128)S(1)}) custom-call(bf16[32,2176]{1,0:T(8,128)(2,1)S(1)} %collective-permute-done.19.refs_0_, bf16[32,2176]{1,0:T(8,128)(2,1)S(1)} %collective-permute-done.26.refs_1_, ...), custom_call_target="tpu_custom_call" | custom-call | flops 603979776 | bytes 6291456 | tf_op jit(solution)/shard_map/apply_expert/pallas_call | solution.py:441
  66.0 1.5 %apply_expert.7 = (f32[32,2048]{1,0:T(8,128)S(1)}, f32[32,2048]{1,0:T(8,128)S(1)}, f32[32,2048]{1,0:T(8,128)S(1)}, f32[32,2048]{1,0:T(8,128)S(1)}) custom-call(bf16[32,2176]{1,0:T(8,128)(2,1)S(1)} %collective-permute-done.25.refs_0_, bf16[32,2176]{1,0:T(8,128)(2,1)S(1)} %collective-permute-done.30.refs_1_, ...), custom_call_target="tpu_custom_call" | custom-call | flops 603979776 | bytes 6291456 | tf_op jit(solution)/shard_map/apply_expert/pallas_call | solution.py:441
  70.0 1.5 %apply_expert.8 = (f32[32,2048]{1,0:T(8,128)S(1)}, f32[32,2048]{1,0:T(8,128)S(1)}) custom-call(bf16[32,2176]{1,0:T(8,128)(2,1)S(1)} %collective-permute-done.29.refs_0_, bf16[32,2176]{1,0:T(8,128)(2,1)S(1)} %collective-permute-done.33.refs_1_, bf16[2,192,2048]{2,1,0:T(8,128)(2,1)S(1)} %bitcast.9, ...), custom_call_target="tpu_custom_call" | custom-call | flops 301989888 | bytes 6291456 | tf_op jit(solution)/shard_map/apply_expert/pallas_call | solution.py:441
  75.9 2.1 %collective-permute-done.34.came_ref = bf16[32,2048]{1,0:T(8,128)(2,1)S(1)} collective-permute-done((bf16[32,2048]{1,0:T(8,128)(2,1)S(1)}, bf16[32,2048]{1,0:T(8,128)(2,1)S(1)}, u32[]{:S(2)}, u32[]{:S(2)}) %collective-permute-start.34) | collective-permute-done | bytes 131104 | tf_op jit(solution)/shard_map/ppermute | solution.py:507
  83.6 1.5 %collective-permute-start.36 = (bf16[32,2048]{1,0:T(8,128)(2,1)S(1)}, bf16[32,2048]{1,0:T(8,128)(2,1)S(1)}, u32[]{:S(2)}, u32[]{:S(2)}) collective-permute-start(bf16[32,2048]{1,0:T(8,128)(2,1)S(1)} %add_share.11), channel_id=1, source_target_pairs={{4,0},{8,4},{12,8},{14,12},{10,14},{6,10},{2,6},{0,2},{5,1},{9,5},... | collective-permute-start | bytes 393224 | tf_op jit(solution)/shard_map/ppermute | solution.py:507
  86.4 1.3 %collective-permute-start.40 = (bf16[32,2048]{1,0:T(8,128)(2,1)S(1)}, bf16[32,2048]{1,0:T(8,128)(2,1)S(1)}, u32[]{:S(2)}, u32[]{:S(2)}) collective-permute-start(bf16[32,2048]{1,0:T(8,128)(2,1)S(1)} %add_share.14), channel_id=1, source_target_pairs={{4,0},{8,4},{12,8},{14,12},{10,14},{6,10},{2,6},{0,2},{5,1},{9,5},... | collective-permute-start | bytes 393224 | tf_op jit(solution)/shard_map/ppermute | solution.py:507
  88.7 1.5 %collective-permute-start.37 = (bf16[32,2048]{1,0:T(8,128)(2,1)S(1)}, bf16[32,2048]{1,0:T(8,128)(2,1)S(1)}, u32[]{:S(2)}, u32[]{:S(2)}) collective-permute-start(bf16[32,2048]{1,0:T(8,128)(2,1)S(1)} %add_share.12), channel_id=1, source_target_pairs={{4,0},{8,4},{12,8},{14,12},{10,14},{6,10},{2,6},{0,2},{5,1},{9,5},... | collective-permute-start | bytes 393224 | tf_op jit(solution)/shard_map/ppermute | solution.py:507
  90.8 1.5 %apply_expert.9 = (f32[32,2048]{1,0:T(8,128)S(1)}, f32[32,2048]{1,0:T(8,128)S(1)}) custom-call(bf16[32,2176]{1,0:T(8,128)(2,1)S(1)} %get-tuple-element.147.refs_0_, bf16[32,2176]{1,0:T(8,128)(2,1)S(1)} %get-tuple-element.148.refs_1_, bf16[2,192,2048]{2,1,0:T(8,128)(2,1)S(1)} %bitcast.10, bf16[2,192,2048]{2,1,0:T(8,128)(2,1)S(1)} %collective-permute-done.23.refs_5_.refs_3_, ...), custom_call_target="tpu_custom_call" | custom-call | flops 301989888 | bytes 6291456 | tf_op jit(solution)/shard_map/apply_expert/pallas_call | solution.py:441
  93.7 1.5 %collective-permute-done.47.refs_7_ = bf16[32,2048]{1,0:T(8,128)(2,1)S(1)} collective-permute-done((bf16[32,2048]{1,0:T(8,128)(2,1)S(1)}, bf16[32,2048]{1,0:T(8,128)(2,1)S(1)}, u32[]{:S(2)}, u32[]{:S(2)}) %collective-permute-start.47) | collective-permute-done | bytes 131104 | tf_op jit(solution)/shard_map/ppermute | solution.py:507
  95.4 1.3 %collective-permute-done.48.refs_1_ = bf16[64,1024]{1,0:T(8,128)(2,1)S(1)} collective-permute-done((bf16[64,1024]{1,0:T(8,128)(2,1)S(1)}, bf16[64,1024]{1,0:T(8,128)(2,1)S(1)}, u32[]{:S(2)}, u32[]{:S(2)}) %collective-permute-start.48) | collective-permute-done | bytes 131104 | tf_op jit(solution)/shard_map/ppermute | solution.py:106
  (120 shorter events, 37.1 us)
Async XLA Ops:
  2.5 29.6 %collective-permute-start.14 = (bf16[2048,1024]{1,0:T(8,128)(2,1)}, bf16[2048,1024]{1,0:T(8,128)(2,1)S(1)}, u32[]{:S(2)}, u32[]{:S(2)}) collective-permute-start(bf16[2048,1024]{1,0:T(8,128)(2,1)} %refs_5_.1), channel_id=1, source_target_pairs={{0,1},{1,0},{2,3},{3,2},{4,5},{5,4},{6,7},{7,6},{8,9},{9,8},{10,11... | collective-permute-start | bytes 12582920 | tf_op jit(solution)/shard_map/ppermute | solution.py:34
  3.0 7.2 %collective-permute-start.2 = (bf16[272,256]{1,0:T(8,128)(2,1)}, bf16[272,256]{1,0:T(8,128)(2,1)S(1)}, u32[]{:S(2)}, u32[]{:S(2)}) collective-permute-start(bf16[272,256]{1,0:T(8,128)(2,1)} %get-tuple-element.85.refs_1_), channel_id=1, source_target_pairs={{0,1},{1,0},{2,3},{3,2},{4,5},{5,4},{6,7},{7,6},{8,9},{9,8},{10,11... | collective-permute-start | bytes 417800 | tf_op jit(solution)/shard_map/ppermute | solution.py:34
  3.0 12.0 %collective-permute-start = (bf16[272,256]{1,0:T(8,128)(2,1)}, bf16[272,256]{1,0:T(8,128)(2,1)S(1)}, u32[]{:S(2)}, u32[]{:S(2)}) collective-permute-start(bf16[272,256]{1,0:T(8,128)(2,1)} %get-tuple-element.85.refs_1_), channel_id=1, source_target_pairs={{0,4},{4,8},{8,12},{12,0},{1,5},{5,9},{9,13},{13,1},{2,6},{6,10},{... | collective-permute-start | bytes 417800 | tf_op jit(solution)/shard_map/ppermute | solution.py:624
  6.0 11.1 %collective-permute-start.1 = (bf16[272,256]{1,0:T(8,128)(2,1)}, bf16[272,256]{1,0:T(8,128)(2,1)S(1)}, u32[]{:S(2)}, u32[]{:S(2)}) collective-permute-start(bf16[272,256]{1,0:T(8,128)(2,1)} %get-tuple-element.85.refs_1_), channel_id=1, source_target_pairs={{0,12},{4,0},{8,4},{12,8},{1,13},{5,1},{9,5},{13,9},{2,14},{6,2},{... | collective-permute-start | bytes 417800 | tf_op jit(solution)/shard_map/ppermute | solution.py:627
  8.1 9.0 %collective-permute-start.9 = (bf16[272,256]{1,0:T(8,128)(2,1)}, bf16[272,256]{1,0:T(8,128)(2,1)S(1)}, u32[]{:S(2)}, u32[]{:S(2)}) collective-permute-start(bf16[272,256]{1,0:T(8,128)(2,1)} %get-tuple-element.97.refs_1_), channel_id=1, source_target_pairs={{0,1},{1,0},{2,3},{3,2},{4,5},{5,4},{6,7},{7,6},{8,9},{9,8},{10,11... | collective-permute-start | bytes 417800 | tf_op jit(solution)/shard_map/ppermute | solution.py:34
  10.2 9.4 %collective-permute-start.7 = (bf16[272,256]{1,0:T(8,128)(2,1)}, bf16[272,256]{1,0:T(8,128)(2,1)S(1)}, u32[]{:S(2)}, u32[]{:S(2)}) collective-permute-start(bf16[272,256]{1,0:T(8,128)(2,1)} %get-tuple-element.97.refs_1_), channel_id=1, source_target_pairs={{0,4},{4,8},{8,12},{12,0},{1,5},{5,9},{9,13},{13,1},{2,6},{6,10},{... | collective-permute-start | bytes 417800 | tf_op jit(solution)/shard_map/ppermute | solution.py:624
  15.0 7.3 %collective-permute-start.8 = (bf16[272,256]{1,0:T(8,128)(2,1)}, bf16[272,256]{1,0:T(8,128)(2,1)S(1)}, u32[]{:S(2)}, u32[]{:S(2)}) collective-permute-start(bf16[272,256]{1,0:T(8,128)(2,1)} %get-tuple-element.97.refs_1_), channel_id=1, source_target_pairs={{0,12},{4,0},{8,4},{12,8},{1,13},{5,1},{9,5},{13,9},{2,14},{6,2},{... | collective-permute-start | bytes 417800 | tf_op jit(solution)/shard_map/ppermute | solution.py:627
  19.5 8.0 %collective-permute-start.3 = (bf16[272,256]{1,0:T(8,128)(2,1)S(1)}, bf16[272,256]{1,0:T(8,128)(2,1)S(1)}, u32[]{:S(2)}, u32[]{:S(2)}) collective-permute-start(bf16[272,256]{1,0:T(8,128)(2,1)S(1)} %collective-permute-done.refs_1_), channel_id=1, source_target_pairs={{0,4},{4,8},{8,12},{12,0},{1,5},{5,9},{9,13},{13,1},{2,6},{6,10},{... | collective-permute-start | bytes 417800 | tf_op jit(solution)/shard_map/ppermute | solution.py:624
  22.8 7.2 %collective-permute-start.10 = (bf16[272,256]{1,0:T(8,128)(2,1)S(1)}, bf16[272,256]{1,0:T(8,128)(2,1)S(1)}, u32[]{:S(2)}, u32[]{:S(2)}) collective-permute-start(bf16[272,256]{1,0:T(8,128)(2,1)S(1)} %collective-permute-done.8.refs_3_), channel_id=1, source_target_pairs={{0,12},{4,0},{8,4},{12,8},{1,13},{5,1},{9,5},{13,9},{2,14},{6,2},{... | collective-permute-start | bytes 417800 | tf_op jit(solution)/shard_map/ppermute | solution.py:627
  31.4 24.3 %collective-permute-start.23 = (bf16[2,192,2048]{2,1,0:T(8,128)(2,1)S(1)}, bf16[2,192,2048]{2,1,0:T(8,128)(2,1)S(1)}, u32[]{:S(2)}, u32[]{:S(2)}) collective-permute-start(bf16[2,192,2048]{2,1,0:T(8,128)(2,1)S(1)} %bitcast.5), channel_id=1, source_target_pairs={{0,1},{1,0},{2,3},{3,2},{4,5},{5,4},{6,7},{7,6},{8,9},{9,8},{10,11... | collective-permute-start | bytes 4718600 | tf_op jit(solution)/shard_map/ppermute | solution.py:34
  31.5 15.2 %collective-permute-start.24 = (bf16[192,2048]{1,0:T(8,128)(2,1)S(1)}, bf16[192,2048]{1,0:T(8,128)(2,1)S(1)}, u32[]{:S(2)}, u32[]{:S(2)}) collective-permute-start(bf16[192,2048]{1,0:T(8,128)(2,1)S(1)} %bitcast.11), channel_id=1, source_target_pairs={{0,1},{1,0},{2,3},{3,2},{4,5},{5,4},{6,7},{7,6},{8,9},{9,8},{10,11... | collective-permute-start | bytes 2359304 | tf_op jit(solution)/shard_map/ppermute | solution.py:34
  31.9 5.8 %collective-permute-start.16 = (bf16[64,1024]{1,0:T(8,128)(2,1)S(1)}, bf16[64,1024]{1,0:T(8,128)(2,1)S(1)}, u32[]{:S(2)}, u32[]{:S(2)}) collective-permute-start(bf16[64,1024]{1,0:T(8,128)(2,1)S(1)} %get-tuple-element.120), channel_id=1, source_target_pairs={{0,1},{1,0},{2,3},{3,2},{4,5},{5,4},{6,7},{7,6},{8,9},{9,8},{10,11... | collective-permute-start | bytes 393224 | tf_op jit(solution)/shard_map/ppermute | solution.py:106
  35.4 6.4 %collective-permute-start.15 = (bf16[32,2048]{1,0:T(8,128)(2,1)S(1)}, bf16[32,2048]{1,0:T(8,128)(2,1)S(1)}, u32[]{:S(2)}, u32[]{:S(2)}) collective-permute-start(bf16[32,2048]{1,0:T(8,128)(2,1)S(1)} %get-tuple-element.117), channel_id=1, source_target_pairs={{0,2},{2,0},{1,3},{3,1},{4,6},{6,4},{5,7},{7,5},{8,10},{10,8},{9,1... | collective-permute-start | bytes 393224 | tf_op jit(solution)/shard_map/ppermute | solution.py:661
  37.2 7.2 %collective-permute-start.17 = (bf16[32,2048]{1,0:T(8,128)(2,1)S(1)}, bf16[32,2048]{1,0:T(8,128)(2,1)S(1)}, u32[]{:S(2)}, u32[]{:S(2)}) collective-permute-start(bf16[32,2048]{1,0:T(8,128)(2,1)S(1)} %get-tuple-element.123), channel_id=1, source_target_pairs={{0,2},{2,0},{1,3},{3,1},{4,6},{6,4},{5,7},{7,5},{8,10},{10,8},{9,1... | collective-permute-start | bytes 393224 | tf_op jit(solution)/shard_map/ppermute | solution.py:661
  42.0 6.0 %collective-permute-start.18 = (bf16[32,2176]{1,0:T(8,128)(2,1)S(1)}, bf16[32,2176]{1,0:T(8,128)(2,1)S(1)}, u32[]{:S(2)}, u32[]{:S(2)}) collective-permute-start(bf16[32,2176]{1,0:T(8,128)(2,1)S(1)} %get-tuple-element.147.refs_0_), channel_id=1, source_target_pairs={{0,4},{4,8},{8,12},{12,14},{14,10},{10,6},{6,2},{2,0},{1,5},{5,9},... | collective-permute-start | bytes 417800 | tf_op jit(solution)/shard_map/ppermute | solution.py:481
  44.6 6.7 %collective-permute-start.20 = (bf16[32,2176]{1,0:T(8,128)(2,1)S(1)}, bf16[32,2176]{1,0:T(8,128)(2,1)S(1)}, u32[]{:S(2)}, u32[]{:S(2)}) collective-permute-start(bf16[32,2176]{1,0:T(8,128)(2,1)S(1)} %get-tuple-element.148.refs_1_), channel_id=1, source_target_pairs={{4,0},{8,4},{12,8},{14,12},{10,14},{6,10},{2,6},{0,2},{5,1},{9,5},... | collective-permute-start | bytes 417800 | tf_op jit(solution)/shard_map/ppermute | solution.py:482
  46.0 6.6 %collective-permute-start.21 = (bf16[32,2176]{1,0:T(8,128)(2,1)S(1)}, bf16[32,2176]{1,0:T(8,128)(2,1)S(1)}, u32[]{:S(2)}, u32[]{:S(2)}) collective-permute-start(bf16[32,2176]{1,0:T(8,128)(2,1)S(1)} %get-tuple-element.148.refs_1_), channel_id=1, source_target_pairs={{0,4},{4,8},{8,12},{12,14},{14,10},{10,6},{6,2},{2,0},{1,5},{5,9},... | collective-permute-start | bytes 417800 | tf_op jit(solution)/shard_map/ppermute | solution.py:484
  46.7 7.5 %collective-permute-start.22 = (bf16[32,2176]{1,0:T(8,128)(2,1)S(1)}, bf16[32,2176]{1,0:T(8,128)(2,1)S(1)}, u32[]{:S(2)}, u32[]{:S(2)}) collective-permute-start(bf16[32,2176]{1,0:T(8,128)(2,1)S(1)} %get-tuple-element.147.refs_0_), channel_id=1, source_target_pairs={{4,0},{8,4},{12,8},{14,12},{10,14},{6,10},{2,6},{0,2},{5,1},{9,5},... | collective-permute-start | bytes 417800 | tf_op jit(solution)/shard_map/ppermute | solution.py:485
  48.1 9.1 %collective-permute-start.19 = (bf16[32,2176]{1,0:T(8,128)(2,1)S(1)}, bf16[32,2176]{1,0:T(8,128)(2,1)S(1)}, u32[]{:S(2)}, u32[]{:S(2)}) collective-permute-start(bf16[32,2176]{1,0:T(8,128)(2,1)S(1)} %collective-permute-done.18.refs_0_), channel_id=1, source_target_pairs={{0,4},{4,8},{8,12},{12,14},{14,10},{10,6},{6,2},{2,0},{1,5},{5,9},... | collective-permute-start | bytes 417800 | tf_op jit(solution)/shard_map/ppermute | solution.py:481
  51.3 6.6 %collective-permute-start.26 = (bf16[32,2176]{1,0:T(8,128)(2,1)S(1)}, bf16[32,2176]{1,0:T(8,128)(2,1)S(1)}, u32[]{:S(2)}, u32[]{:S(2)}) collective-permute-start(bf16[32,2176]{1,0:T(8,128)(2,1)S(1)} %collective-permute-done.20.refs_1_), channel_id=1, source_target_pairs={{4,0},{8,4},{12,8},{14,12},{10,14},{6,10},{2,6},{0,2},{5,1},{9,5},... | collective-permute-start | bytes 417800 | tf_op jit(solution)/shard_map/ppermute | solution.py:482
  52.6 6.6 %collective-permute-start.27 = (bf16[32,2176]{1,0:T(8,128)(2,1)S(1)}, bf16[32,2176]{1,0:T(8,128)(2,1)S(1)}, u32[]{:S(2)}, u32[]{:S(2)}) collective-permute-start(bf16[32,2176]{1,0:T(8,128)(2,1)S(1)} %collective-permute-done.21.refs_2_), channel_id=1, source_target_pairs={{0,4},{4,8},{8,12},{12,14},{14,10},{10,6},{6,2},{2,0},{1,5},{5,9},... | collective-permute-start | bytes 417800 | tf_op jit(solution)/shard_map/ppermute | solution.py:484
  54.3 6.5 %collective-permute-start.28 = (bf16[32,2176]{1,0:T(8,128)(2,1)S(1)}, bf16[32,2176]{1,0:T(8,128)(2,1)S(1)}, u32[]{:S(2)}, u32[]{:S(2)}) collective-permute-start(bf16[32,2176]{1,0:T(8,128)(2,1)S(1)} %collective-permute-done.22.refs_3_), channel_id=1, source_target_pairs={{4,0},{8,4},{12,8},{14,12},{10,14},{6,10},{2,6},{0,2},{5,1},{9,5},... | collective-permute-start | bytes 417800 | tf_op jit(solution)/shard_map/ppermute | solution.py:485
  57.2 6.5 %collective-permute-start.25 = (bf16[32,2176]{1,0:T(8,128)(2,1)S(1)}, bf16[32,2176]{1,0:T(8,128)(2,1)S(1)}, u32[]{:S(2)}, u32[]{:S(2)}) collective-permute-start(bf16[32,2176]{1,0:T(8,128)(2,1)S(1)} %collective-permute-done.19.refs_0_), channel_id=1, source_target_pairs={{0,4},{4,8},{8,12},{12,14},{14,10},{10,6},{6,2},{2,0},{1,5},{5,9},... | collective-permute-start | bytes 417800 | tf_op jit(solution)/shard_map/ppermute | solution.py:481
  57.9 6.5 %collective-permute-start.30 = (bf16[32,2176]{1,0:T(8,128)(2,1)S(1)}, bf16[32,2176]{1,0:T(8,128)(2,1)S(1)}, u32[]{:S(2)}, u32[]{:S(2)}) collective-permute-start(bf16[32,2176]{1,0:T(8,128)(2,1)S(1)} %collective-permute-done.26.refs_1_), channel_id=1, source_target_pairs={{4,0},{8,4},{12,8},{14,12},{10,14},{6,10},{2,6},{0,2},{5,1},{9,5},... | collective-permute-start | bytes 417800 | tf_op jit(solution)/shard_map/ppermute | solution.py:482
  59.3 6.5 %collective-permute-start.31 = (bf16[32,2176]{1,0:T(8,128)(2,1)S(1)}, bf16[32,2176]{1,0:T(8,128)(2,1)S(1)}, u32[]{:S(2)}, u32[]{:S(2)}) collective-permute-start(bf16[32,2176]{1,0:T(8,128)(2,1)S(1)} %collective-permute-done.27.refs_2_), channel_id=1, source_target_pairs={{0,4},{4,8},{8,12},{12,14},{14,10},{10,6},{6,2},{2,0},{1,5},{5,9},... | collective-permute-start | bytes 417800 | tf_op jit(solution)/shard_map/ppermute | solution.py:484
  71.6 6.4 %collective-permute-start.34 = (bf16[32,2048]{1,0:T(8,128)(2,1)S(1)}, bf16[32,2048]{1,0:T(8,128)(2,1)S(1)}, u32[]{:S(2)}, u32[]{:S(2)}) collective-permute-start(bf16[32,2048]{1,0:T(8,128)(2,1)S(1)} %convert_element_type.12), channel_id=1, source_target_pairs={{4,0},{8,4},{12,8},{14,12},{10,14},{6,10},{2,6},{0,2},{5,1},{9,5},... | collective-permute-start | bytes 393224 | tf_op jit(solution)/shard_map/ppermute | solution.py:507
  72.5 6.4 %collective-permute-start.44 = (bf16[32,2048]{1,0:T(8,128)(2,1)S(1)}, bf16[32,2048]{1,0:T(8,128)(2,1)S(1)}, u32[]{:S(2)}, u32[]{:S(2)}) collective-permute-start(bf16[32,2048]{1,0:T(8,128)(2,1)S(1)} %convert_element_type.15), channel_id=1, source_target_pairs={{0,4},{4,8},{8,12},{12,14},{14,10},{10,6},{6,2},{2,0},{1,5},{5,9},... | collective-permute-start | bytes 393224 | tf_op jit(solution)/shard_map/ppermute | solution.py:507
  73.8 7.0 %collective-permute-start.38 = (bf16[32,2048]{1,0:T(8,128)(2,1)S(1)}, bf16[32,2048]{1,0:T(8,128)(2,1)S(1)}, u32[]{:S(2)}, u32[]{:S(2)}) collective-permute-start(bf16[32,2048]{1,0:T(8,128)(2,1)S(1)} %convert_element_type.13), channel_id=1, source_target_pairs={{4,0},{8,4},{12,8},{14,12},{10,14},{6,10},{2,6},{0,2},{5,1},{9,5},... | collective-permute-start | bytes 393224 | tf_op jit(solution)/shard_map/ppermute | solution.py:507
  74.7 7.0 %collective-permute-start.41 = (bf16[32,2048]{1,0:T(8,128)(2,1)S(1)}, bf16[32,2048]{1,0:T(8,128)(2,1)S(1)}, u32[]{:S(2)}, u32[]{:S(2)}) collective-permute-start(bf16[32,2048]{1,0:T(8,128)(2,1)S(1)} %convert_element_type.14), channel_id=1, source_target_pairs={{0,4},{4,8},{8,12},{12,14},{14,10},{10,6},{6,2},{2,0},{1,5},{5,9},... | collective-permute-start | bytes 393224 | tf_op jit(solution)/shard_map/ppermute | solution.py:507
  78.9 6.1 %collective-permute-start.45 = (bf16[32,2048]{1,0:T(8,128)(2,1)S(1)}, bf16[32,2048]{1,0:T(8,128)(2,1)S(1)}, u32[]{:S(2)}, u32[]{:S(2)}) collective-permute-start(bf16[32,2048]{1,0:T(8,128)(2,1)S(1)} %add_share.17), channel_id=1, source_target_pairs={{0,4},{4,8},{8,12},{12,14},{14,10},{10,6},{6,2},{2,0},{1,5},{5,9},... | collective-permute-start | bytes 393224 | tf_op jit(solution)/shard_map/ppermute | solution.py:507
  81.7 6.0 %collective-permute-start.42 = (bf16[32,2048]{1,0:T(8,128)(2,1)S(1)}, bf16[32,2048]{1,0:T(8,128)(2,1)S(1)}, u32[]{:S(2)}, u32[]{:S(2)}) collective-permute-start(bf16[32,2048]{1,0:T(8,128)(2,1)S(1)} %add_share.15), channel_id=1, source_target_pairs={{0,4},{4,8},{8,12},{12,14},{14,10},{10,6},{6,2},{2,0},{1,5},{5,9},... | collective-permute-start | bytes 393224 | tf_op jit(solution)/shard_map/ppermute | solution.py:507
  86.4 6.0 %collective-permute-start.40 = (bf16[32,2048]{1,0:T(8,128)(2,1)S(1)}, bf16[32,2048]{1,0:T(8,128)(2,1)S(1)}, u32[]{:S(2)}, u32[]{:S(2)}) collective-permute-start(bf16[32,2048]{1,0:T(8,128)(2,1)S(1)} %add_share.14), channel_id=1, source_target_pairs={{4,0},{8,4},{12,8},{14,12},{10,14},{6,10},{2,6},{0,2},{5,1},{9,5},... | collective-permute-start | bytes 393224 | tf_op jit(solution)/shard_map/ppermute | solution.py:507
  (27 other events, 177.1 us)

commit v7 on v6

--- a/solution.py
+++ b/solution.py
@@ -469,10 +469,14 @@
 
 
 def dense_experts(own, gate_up, w_down):
-    axes = ("ep", "hd")
+    axes = ("ep", "hd", "sub")
     walk = chip_ring(lax.axis_size("ep"), lax.axis_size("hd"))
-    size = len(walk)
-    ahead = [(walk[i], walk[(i + 1) % size]) for i in range(size)]
+    size, n_sub = len(walk), lax.axis_size("sub")
+    ahead = [
+        (walk[i] * n_sub + sub, walk[(i + 1) % size] * n_sub + (sub + 1) % n_sub)
+        for i in range(size)
+        for sub in range(n_sub)
+    ]
     back = [(b, a) for a, b in ahead]
     reach = size // 2
     behind, before, waiting = list(own), list(own), None
@@ -485,7 +489,8 @@
             before[0] = lax.ppermute(before[0], axes, back)
         if waiting:
             out = apply_expert(waiting, gate_up, w_down)
-            behind[0], out = lax.optimization_barrier((behind[0], out))
+            late = int(hop < reach)
+            behind[late], out = lax.optimization_barrier((behind[late], out))
             outs.append(out)
         waiting = [behind[0], before[1]] + ([behind[1], before[0]] if hop < reach else [])
     outs.append(apply_expert(waiting, gate_up, w_down))

time: 97.7 us -> 96.5 us (0.988)
  waiting for transfers between devices: 26.5 us -> 25.2 us
    ppermute x14, starting transfers between devices: 14.7 us -> 17 us  [dense_experts(): chunks[chunk] = lax.ppermute(sum_here, axes, way)]
    ppermute x14, waiting for transfers between devices: 6.97 us -> 5.55 us  [dense_experts(): chunks[chunk] = lax.ppermute(sum_here, axes, way)]
    ppermute x4, waiting for transfers between devices: 3.79 us -> 5.1 us  [dense_experts(): before[1] = lax.ppermute(before[1], axes, back)]
    ppermute x4, starting transfers between devices: 2.9 us -> 1.79 us  [dense_experts(): behind[0] = lax.ppermute(behind[0], axes, ahead)]
    ppermute x3, waiting for transfers between devices: 2.02 us -> 0.99 us  [dense_experts(): before[0] = lax.ppermute(before[0], axes, back)]
  transfers between devices with their start and end apart: 49 -> 49, of which waited for: 23 -> 21; matrix products, arithmetic and copies ran while one was open for 0% -> 0% of each run, Pallas kernels for 16% -> 16%
where the time goes in v7:
time: 96.5 us; the launch traced here: 96.3 us
  starting transfers between devices  47 us (49%)
  waiting for transfers between devices  25.2 us (26%)
  Pallas kernels  19.9 us (21%)
  local copies, waits for them, and re-layouts  3.09 us (3%)
  between operations  1.04 us (1%)
    ppermute x14, starting transfers between devices, dense_experts(): chunks[chunk] = lax.ppermute(sum_here, axes, way)  17 us
    pallas_call x6, Pallas kernels, attend(): pl.pallas_call(kernel, out_shape=out_shape, in_specs=[vmem] * len(operand...  8.78 us
    pallas_call x5, Pallas kernels, apply_expert(): pl.pallas_call(kernel, out_shape=[jax.ShapeDtypeStruct((x.shape[0], featu...  7.65 us
    ppermute x3, starting transfers between devices, shards(): down[kv] = lax.ppermute(down[kv], 'ep', cycle(n_ep, n_ep - 1))  7.06 us
    ppermute x3, starting transfers between devices, shards(): up[kv] = lax.ppermute(up[kv], 'ep', cycle(n_ep))  6.24 us
    ppermute x2, waiting for transfers between devices, shards(): came = [lax.ppermute(x, 'hd', cycle(n_hd)) for x in sent]  6.12 us
    ppermute x14, waiting for transfers between devices, dense_experts(): chunks[chunk] = lax.ppermute(sum_here, axes, way)  5.55 us
    ppermute x4, waiting for transfers between devices, dense_experts(): before[1] = lax.ppermute(before[1], axes, back)  5.1 us
  transfers between devices with their start and end apart: 49, of which 21 were waited for; matrix products, arithmetic and copies ran while one was open for 0% of the time, Pallas kernels for 16%

profile of v7, /device:TPU:0, one launch (start us, length us, event | category | flops | bytes accessed | tf_op | source)
XLA Modules:
  0.0 96.3 jit_solution(1331846867904188060)
XLA Ops:
  0.7 1.9 %pack_keys.1 = (bf16[272,256]{1,0:T(8,128)(2,1)}, bf16[272,256]{1,0:T(8,128)(2,1)}) custom-call(s32[1]{0:T(128)S(6)} %copy.14.page_ref, bf16[128,512]{1,0:T(8,128)(2,1)} %ck_ref.1, bf16[128,512]{1,0:T(8,128)(2,1)} %cv_ref.1, bf16[128,512]{1,0:T(8,128)(2,1)} %nk_ref.1, bf16[128,512]{1,0:T(8,128)(2,1)} %nv_ref.1), custom_call_target="tpu_custom_call" | custom-call | tf_op jit(solution)/shard_map/pack_keys/pallas_call | solution.py:81
  3.0 3.0 %collective-permute-start = (bf16[272,256]{1,0:T(8,128)(2,1)}, bf16[272,256]{1,0:T(8,128)(2,1)S(1)}, u32[]{:S(2)}, u32[]{:S(2)}) collective-permute-start(bf16[272,256]{1,0:T(8,128)(2,1)} %get-tuple-element.85.refs_1_), channel_id=1, source_target_pairs={{0,4},{4,8},{8,12},{12,0},{1,5},{5,9},{9,13},{13,1},{2,6},{6,10},{... | collective-permute-start | bytes 417800 | tf_op jit(solution)/shard_map/ppermute | solution.py:629
  6.0 2.0 %collective-permute-start.1 = (bf16[272,256]{1,0:T(8,128)(2,1)}, bf16[272,256]{1,0:T(8,128)(2,1)S(1)}, u32[]{:S(2)}, u32[]{:S(2)}) collective-permute-start(bf16[272,256]{1,0:T(8,128)(2,1)} %get-tuple-element.85.refs_1_), channel_id=1, source_target_pairs={{0,12},{4,0},{8,4},{12,8},{1,13},{5,1},{9,5},{13,9},{2,14},{6,2},{... | collective-permute-start | bytes 417800 | tf_op jit(solution)/shard_map/ppermute | solution.py:632
  10.2 2.9 %collective-permute-start.7 = (bf16[272,256]{1,0:T(8,128)(2,1)}, bf16[272,256]{1,0:T(8,128)(2,1)S(1)}, u32[]{:S(2)}, u32[]{:S(2)}) collective-permute-start(bf16[272,256]{1,0:T(8,128)(2,1)} %get-tuple-element.97.refs_1_), channel_id=1, source_target_pairs={{0,4},{4,8},{8,12},{12,0},{1,5},{5,9},{9,13},{13,1},{2,6},{6,10},{... | collective-permute-start | bytes 417800 | tf_op jit(solution)/shard_map/ppermute | solution.py:629
  15.0 2.1 %collective-permute-start.8 = (bf16[272,256]{1,0:T(8,128)(2,1)}, bf16[272,256]{1,0:T(8,128)(2,1)S(1)}, u32[]{:S(2)}, u32[]{:S(2)}) collective-permute-start(bf16[272,256]{1,0:T(8,128)(2,1)} %get-tuple-element.97.refs_1_), channel_id=1, source_target_pairs={{0,12},{4,0},{8,4},{12,8},{1,13},{5,1},{9,5},{13,9},{2,14},{6,2},{... | collective-permute-start | bytes 417800 | tf_op jit(solution)/shard_map/ppermute | solution.py:632
  19.8 2.5 %collective-permute-done.8.refs_3_ = bf16[272,256]{1,0:T(8,128)(2,1)S(1)} collective-permute-done((bf16[272,256]{1,0:T(8,128)(2,1)}, bf16[272,256]{1,0:T(8,128)(2,1)S(1)}, u32[]{:S(2)}, u32[]{:S(2)}) %collective-permute-start.8) | collective-permute-done | bytes 139296 | tf_op jit(solution)/shard_map/ppermute | solution.py:632
  22.8 2.9 %collective-permute-start.10 = (bf16[272,256]{1,0:T(8,128)(2,1)S(1)}, bf16[272,256]{1,0:T(8,128)(2,1)S(1)}, u32[]{:S(2)}, u32[]{:S(2)}) collective-permute-start(bf16[272,256]{1,0:T(8,128)(2,1)S(1)} %collective-permute-done.8.refs_3_), channel_id=1, source_target_pairs={{0,12},{4,0},{8,4},{12,8},{1,13},{5,1},{9,5},{13,9},{2,14},{6,2},{... | collective-permute-start | bytes 417800 | tf_op jit(solution)/shard_map/ppermute | solution.py:632
  25.8 1.8 %attend.7 = (f32[1024,128]{1,0:T(8,128)S(1)}, f32[1024,256]{1,0:T(8,128)S(1)}) custom-call(bf16[128,2048]{1,0:T(8,128)(2,1)S(1)} %choose_queries.1.refs_0_, bf16[272,256]{1,0:T(8,128)(2,1)S(1)} %collective-permute-done.refs_1_, bf16[272,256]{1,0:T(8,128)(2,1)S(1)} %collective-permute-done.4.refs_2_, bf16[272,256]{1,0:T(8,128)(2,1)S(1)} %collective-permute-done.1.refs_3_, ...), custom_call_target="tpu_custom_call" | custom-call | flops 805306368 | bytes 4194304 | tf_op jit(solution)/shard_map/attend/pallas_call | solution.py:395
  27.7 1.8 %attend.9 = (f32[1024,128]{1,0:T(8,128)S(1)}, f32[1024,256]{1,0:T(8,128)S(1)}) custom-call(bf16[128,2048]{1,0:T(8,128)(2,1)S(1)} %choose_queries.1.refs_0_, bf16[272,256]{1,0:T(8,128)(2,1)S(1)} %collective-permute-done.7.refs_1_, bf16[272,256]{1,0:T(8,128)(2,1)S(1)} %collective-permute-done.11.refs_2_, bf16[272,256]{1,0:T(8,128)(2,1)S(1)} %collective-permute-done.8.refs_3_, ...), custom_call_target="tpu_custom_call" | custom-call | flops 805306368 | bytes 4194304 | tf_op jit(solution)/shard_map/attend/pallas_call | solution.py:395
  30.0 1.3 %collective-permute-done.13.refs_2_ = bf16[272,256]{1,0:T(8,128)(2,1)S(1)} collective-permute-done((bf16[272,256]{1,0:T(8,128)(2,1)S(1)}, bf16[272,256]{1,0:T(8,128)(2,1)S(1)}, u32[]{:S(2)}, u32[]{:S(2)}) %collective-permute-start.13) | collective-permute-done | bytes 139296 | tf_op jit(solution)/shard_map/ppermute | solution.py:34
  32.1 1.6 %attend.10.refs_7_ = f32[128,2048]{1,0:T(8,128)S(1)} custom-call(bf16[128,2048]{1,0:T(8,128)(2,1)S(1)} %choose_queries.1.refs_0_, bf16[272,256]{1,0:T(8,128)(2,1)S(1)} %collective-permute-done.3.refs_1_, bf16[272,256]{1,0:T(8,128)(2,1)S(1)} %collective-permute-done.6.refs_2_, f32[1024,128]{1,0:T(8,128)S(1)} %get-tuple-element.114.refs_3_, ...), custom_call_target="tpu_custom_call" | custom-call | flops 402653184 | bytes 4194304 | tf_op jit(solution)/shard_map/attend/pallas_call | solution.py:395
  33.8 1.7 %attend.11 = (f32[32,2048]{1,0:T(8,128)S(1)}, f32[32,2048]{1,0:T(8,128)S(1)}, bf16[32,2048]{1,0:T(8,128)(2,1)S(1)}, bf16[32,2048]{1,0:T(8,128)(2,1)S(1)}) custom-call(bf16[128,2048]{1,0:T(8,128)(2,1)S(1)} %choose_queries.1.refs_0_, bf16[272,256]{1,0:T(8,128)(2,1)S(1)} %collective-permute-done.10.refs_1_, ...), custom_call_target="tpu_custom_call" | custom-call | flops 402653184 | bytes 4194304 | tf_op jit(solution)/shard_map/attend/pallas_call | solution.py:395
  35.4 1.8 %collective-permute-start.15 = (bf16[32,2048]{1,0:T(8,128)(2,1)S(1)}, bf16[32,2048]{1,0:T(8,128)(2,1)S(1)}, u32[]{:S(2)}, u32[]{:S(2)}) collective-permute-start(bf16[32,2048]{1,0:T(8,128)(2,1)S(1)} %get-tuple-element.117), channel_id=1, source_target_pairs={{0,2},{2,0},{1,3},{3,1},{4,6},{6,4},{5,7},{7,5},{8,10},{10,8},{9,1... | collective-permute-start | bytes 393224 | tf_op jit(solution)/shard_map/ppermute | solution.py:666
  37.7 4.1 %collective-permute-done.15.refs_1_ = bf16[32,2048]{1,0:T(8,128)(2,1)S(1)} collective-permute-done((bf16[32,2048]{1,0:T(8,128)(2,1)S(1)}, bf16[32,2048]{1,0:T(8,128)(2,1)S(1)}, u32[]{:S(2)}, u32[]{:S(2)}) %collective-permute-start.15) | collective-permute-done | bytes 131104 | tf_op jit(solution)/shard_map/ppermute | solution.py:666
  42.1 2.0 %collective-permute-done.17.refs_1_ = bf16[32,2048]{1,0:T(8,128)(2,1)S(1)} collective-permute-done((bf16[32,2048]{1,0:T(8,128)(2,1)S(1)}, bf16[32,2048]{1,0:T(8,128)(2,1)S(1)}, u32[]{:S(2)}, u32[]{:S(2)}) %collective-permute-start.17) | collective-permute-done | bytes 131104 | tf_op jit(solution)/shard_map/ppermute | solution.py:666
  48.3 2.0 %collective-permute-done.22.refs_1_ = bf16[32,2176]{1,0:T(8,128)(2,1)S(1)} collective-permute-done((bf16[32,2176]{1,0:T(8,128)(2,1)S(1)}, bf16[32,2176]{1,0:T(8,128)(2,1)S(1)}, u32[]{:S(2)}, u32[]{:S(2)}) %collective-permute-start.22) | collective-permute-done | bytes 139296 | tf_op jit(solution)/shard_map/ppermute | solution.py:486
  57.2 1.6 %apply_expert.5 = (f32[32,2048]{1,0:T(8,128)S(1)}, f32[32,2048]{1,0:T(8,128)S(1)}, f32[32,2048]{1,0:T(8,128)S(1)}, f32[32,2048]{1,0:T(8,128)S(1)}) custom-call(bf16[32,2176]{1,0:T(8,128)(2,1)S(1)} %collective-permute-done.18.refs_0_, bf16[32,2176]{1,0:T(8,128)(2,1)S(1)} %collective-permute-done.22.refs_1_, ...), custom_call_target="tpu_custom_call" | custom-call | flops 603979776 | bytes 6291456 | tf_op jit(solution)/shard_map/apply_expert/pallas_call | solution.py:441
  61.9 1.5 %collective-permute-start.33 = (bf16[32,2176]{1,0:T(8,128)(2,1)S(1)}, bf16[32,2176]{1,0:T(8,128)(2,1)S(1)}, u32[]{:S(2)}, u32[]{:S(2)}) collective-permute-start(bf16[32,2176]{1,0:T(8,128)(2,1)S(1)} %collective-permute-done.24.refs_1_), channel_id=1, source_target_pairs={{5,0},{4,1},{9,4},{8,5},{13,8},{12,9},{15,12},{14,13},{11,14},{10,... | collective-permute-start | bytes 417800 | tf_op jit(solution)/shard_map/ppermute | solution.py:486
  63.4 1.6 %apply_expert.6 = (f32[32,2048]{1,0:T(8,128)S(1)}, f32[32,2048]{1,0:T(8,128)S(1)}, f32[32,2048]{1,0:T(8,128)S(1)}, f32[32,2048]{1,0:T(8,128)S(1)}) custom-call(bf16[32,2176]{1,0:T(8,128)(2,1)S(1)} %collective-permute-done.19.refs_0_, bf16[32,2176]{1,0:T(8,128)(2,1)S(1)} %collective-permute-done.23.refs_1_, ...), custom_call_target="tpu_custom_call" | custom-call | flops 603979776 | bytes 6291456 | tf_op jit(solution)/shard_map/apply_expert/pallas_call | solution.py:441
  65.0 1.5 %apply_expert.7 = (f32[32,2048]{1,0:T(8,128)S(1)}, f32[32,2048]{1,0:T(8,128)S(1)}, f32[32,2048]{1,0:T(8,128)S(1)}, f32[32,2048]{1,0:T(8,128)S(1)}) custom-call(bf16[32,2176]{1,0:T(8,128)(2,1)S(1)} %collective-permute-done.20.refs_0_, bf16[32,2176]{1,0:T(8,128)(2,1)S(1)} %collective-permute-done.24.refs_1_, ...), custom_call_target="tpu_custom_call" | custom-call | flops 603979776 | bytes 6291456 | tf_op jit(solution)/shard_map/apply_expert/pallas_call | solution.py:441
  68.0 1.5 %apply_expert.8 = (f32[32,2048]{1,0:T(8,128)S(1)}, f32[32,2048]{1,0:T(8,128)S(1)}) custom-call(bf16[32,2176]{1,0:T(8,128)(2,1)S(1)} %collective-permute-done.21.refs_0_, bf16[32,2176]{1,0:T(8,128)(2,1)S(1)} %collective-permute-done.33.refs_1_, bf16[2,192,2048]{2,1,0:T(8,128)(2,1)S(1)} %bitcast.9, ...), custom_call_target="tpu_custom_call" | custom-call | flops 301989888 | bytes 6291456 | tf_op jit(solution)/shard_map/apply_expert/pallas_call | solution.py:441
  69.6 1.7 %collective-permute-start.34 = (bf16[32,2048]{1,0:T(8,128)(2,1)S(1)}, bf16[32,2048]{1,0:T(8,128)(2,1)S(1)}, u32[]{:S(2)}, u32[]{:S(2)}) collective-permute-start(bf16[32,2048]{1,0:T(8,128)(2,1)S(1)} %convert_element_type.12), channel_id=1, source_target_pairs={{5,0},{4,1},{9,4},{8,5},{13,8},{12,9},{15,12},{14,13},{11,14},{10,... | collective-permute-start | bytes 393224 | tf_op jit(solution)/shard_map/ppermute | solution.py:512
  71.4 1.8 %collective-permute-start.38 = (bf16[32,2048]{1,0:T(8,128)(2,1)S(1)}, bf16[32,2048]{1,0:T(8,128)(2,1)S(1)}, u32[]{:S(2)}, u32[]{:S(2)}) collective-permute-start(bf16[32,2048]{1,0:T(8,128)(2,1)S(1)} %convert_element_type.13), channel_id=1, source_target_pairs={{5,0},{4,1},{9,4},{8,5},{13,8},{12,9},{15,12},{14,13},{11,14},{10,... | collective-permute-start | bytes 393224 | tf_op jit(solution)/shard_map/ppermute | solution.py:512
  73.3 1.9 %collective-permute-done.34.came_ref = bf16[32,2048]{1,0:T(8,128)(2,1)S(1)} collective-permute-done((bf16[32,2048]{1,0:T(8,128)(2,1)S(1)}, bf16[32,2048]{1,0:T(8,128)(2,1)S(1)}, u32[]{:S(2)}, u32[]{:S(2)}) %collective-permute-start.34) | collective-permute-done | bytes 131104 | tf_op jit(solution)/shard_map/ppermute | solution.py:512
  75.2 2.3 %collective-permute-start.35 = (bf16[32,2048]{1,0:T(8,128)(2,1)S(1)}, bf16[32,2048]{1,0:T(8,128)(2,1)S(1)}, u32[]{:S(2)}, u32[]{:S(2)}) collective-permute-start(bf16[32,2048]{1,0:T(8,128)(2,1)S(1)} %add_share.10), channel_id=1, source_target_pairs={{5,0},{4,1},{9,4},{8,5},{13,8},{12,9},{15,12},{14,13},{11,14},{10,... | collective-permute-start | bytes 393224 | tf_op jit(solution)/shard_map/ppermute | solution.py:512
  77.9 1.8 %collective-permute-start.39 = (bf16[32,2048]{1,0:T(8,128)(2,1)S(1)}, bf16[32,2048]{1,0:T(8,128)(2,1)S(1)}, u32[]{:S(2)}, u32[]{:S(2)}) collective-permute-start(bf16[32,2048]{1,0:T(8,128)(2,1)S(1)} %add_share.13), channel_id=1, source_target_pairs={{5,0},{4,1},{9,4},{8,5},{13,8},{12,9},{15,12},{14,13},{11,14},{10,... | collective-permute-start | bytes 393224 | tf_op jit(solution)/shard_map/ppermute | solution.py:512
  80.5 2.3 %collective-permute-start.36 = (bf16[32,2048]{1,0:T(8,128)(2,1)S(1)}, bf16[32,2048]{1,0:T(8,128)(2,1)S(1)}, u32[]{:S(2)}, u32[]{:S(2)}) collective-permute-start(bf16[32,2048]{1,0:T(8,128)(2,1)S(1)} %add_share.11), channel_id=1, source_target_pairs={{5,0},{4,1},{9,4},{8,5},{13,8},{12,9},{15,12},{14,13},{11,14},{10,... | collective-permute-start | bytes 393224 | tf_op jit(solution)/shard_map/ppermute | solution.py:512
  83.7 2.2 %collective-permute-start.40 = (bf16[32,2048]{1,0:T(8,128)(2,1)S(1)}, bf16[32,2048]{1,0:T(8,128)(2,1)S(1)}, u32[]{:S(2)}, u32[]{:S(2)}) collective-permute-start(bf16[32,2048]{1,0:T(8,128)(2,1)S(1)} %add_share.14), channel_id=1, source_target_pairs={{5,0},{4,1},{9,4},{8,5},{13,8},{12,9},{15,12},{14,13},{11,14},{10,... | collective-permute-start | bytes 393224 | tf_op jit(solution)/shard_map/ppermute | solution.py:512
  86.2 2.2 %collective-permute-start.37 = (bf16[32,2048]{1,0:T(8,128)(2,1)S(1)}, bf16[32,2048]{1,0:T(8,128)(2,1)S(1)}, u32[]{:S(2)}, u32[]{:S(2)}) collective-permute-start(bf16[32,2048]{1,0:T(8,128)(2,1)S(1)} %add_share.12), channel_id=1, source_target_pairs={{5,0},{4,1},{9,4},{8,5},{13,8},{12,9},{15,12},{14,13},{11,14},{10,... | collective-permute-start | bytes 393224 | tf_op jit(solution)/shard_map/ppermute | solution.py:512
  88.5 1.3 %collective-permute-start.47 = (bf16[32,2048]{1,0:T(8,128)(2,1)S(1)}, bf16[32,2048]{1,0:T(8,128)(2,1)S(1)}, u32[]{:S(2)}, u32[]{:S(2)}) collective-permute-start(bf16[32,2048]{1,0:T(8,128)(2,1)S(1)} %add_share.19), channel_id=1, source_target_pairs={{0,5},{1,4},{4,9},{5,8},{8,13},{9,12},{12,15},{13,14},{14,11},{15,... | collective-permute-start | bytes 393224 | tf_op jit(solution)/shard_map/ppermute | solution.py:512
  89.8 1.5 %apply_expert.9 = (f32[32,2048]{1,0:T(8,128)S(1)}, f32[32,2048]{1,0:T(8,128)S(1)}) custom-call(bf16[32,2176]{1,0:T(8,128)(2,1)S(1)} %get-tuple-element.147.refs_0_, bf16[32,2176]{1,0:T(8,128)(2,1)S(1)} %get-tuple-element.148.refs_1_, bf16[2,192,2048]{2,1,0:T(8,128)(2,1)S(1)} %bitcast.10, bf16[2,192,2048]{2,1,0:T(8,128)(2,1)S(1)} %collective-permute-done.28.refs_5_.refs_3_, ...), custom_call_target="tpu_custom_call" | custom-call | flops 301989888 | bytes 6291456 | tf_op jit(solution)/shard_map/apply_expert/pallas_call | solution.py:441
  92.3 1.7 %collective-permute-done.47.refs_7_ = bf16[32,2048]{1,0:T(8,128)(2,1)S(1)} collective-permute-done((bf16[32,2048]{1,0:T(8,128)(2,1)S(1)}, bf16[32,2048]{1,0:T(8,128)(2,1)S(1)}, u32[]{:S(2)}, u32[]{:S(2)}) %collective-permute-start.47) | collective-permute-done | bytes 131104 | tf_op jit(solution)/shard_map/ppermute | solution.py:512
  (120 shorter events, 31.6 us)
Async XLA Ops:
  2.5 29.6 %collective-permute-start.14 = (bf16[2048,1024]{1,0:T(8,128)(2,1)}, bf16[2048,1024]{1,0:T(8,128)(2,1)S(1)}, u32[]{:S(2)}, u32[]{:S(2)}) collective-permute-start(bf16[2048,1024]{1,0:T(8,128)(2,1)} %refs_5_.1), channel_id=1, source_target_pairs={{0,1},{1,0},{2,3},{3,2},{4,5},{5,4},{6,7},{7,6},{8,9},{9,8},{10,11... | collective-permute-start | bytes 12582920 | tf_op jit(solution)/shard_map/ppermute | solution.py:34
  3.0 7.2 %collective-permute-start.2 = (bf16[272,256]{1,0:T(8,128)(2,1)}, bf16[272,256]{1,0:T(8,128)(2,1)S(1)}, u32[]{:S(2)}, u32[]{:S(2)}) collective-permute-start(bf16[272,256]{1,0:T(8,128)(2,1)} %get-tuple-element.85.refs_1_), channel_id=1, source_target_pairs={{0,1},{1,0},{2,3},{3,2},{4,5},{5,4},{6,7},{7,6},{8,9},{9,8},{10,11... | collective-permute-start | bytes 417800 | tf_op jit(solution)/shard_map/ppermute | solution.py:34
  3.0 12.0 %collective-permute-start = (bf16[272,256]{1,0:T(8,128)(2,1)}, bf16[272,256]{1,0:T(8,128)(2,1)S(1)}, u32[]{:S(2)}, u32[]{:S(2)}) collective-permute-start(bf16[272,256]{1,0:T(8,128)(2,1)} %get-tuple-element.85.refs_1_), channel_id=1, source_target_pairs={{0,4},{4,8},{8,12},{12,0},{1,5},{5,9},{9,13},{13,1},{2,6},{6,10},{... | collective-permute-start | bytes 417800 | tf_op jit(solution)/shard_map/ppermute | solution.py:629
  6.0 11.1 %collective-permute-start.1 = (bf16[272,256]{1,0:T(8,128)(2,1)}, bf16[272,256]{1,0:T(8,128)(2,1)S(1)}, u32[]{:S(2)}, u32[]{:S(2)}) collective-permute-start(bf16[272,256]{1,0:T(8,128)(2,1)} %get-tuple-element.85.refs_1_), channel_id=1, source_target_pairs={{0,12},{4,0},{8,4},{12,8},{1,13},{5,1},{9,5},{13,9},{2,14},{6,2},{... | collective-permute-start | bytes 417800 | tf_op jit(solution)/shard_map/ppermute | solution.py:632
  8.1 9.0 %collective-permute-start.9 = (bf16[272,256]{1,0:T(8,128)(2,1)}, bf16[272,256]{1,0:T(8,128)(2,1)S(1)}, u32[]{:S(2)}, u32[]{:S(2)}) collective-permute-start(bf16[272,256]{1,0:T(8,128)(2,1)} %get-tuple-element.97.refs_1_), channel_id=1, source_target_pairs={{0,1},{1,0},{2,3},{3,2},{4,5},{5,4},{6,7},{7,6},{8,9},{9,8},{10,11... | collective-permute-start | bytes 417800 | tf_op jit(solution)/shard_map/ppermute | solution.py:34
  10.2 9.4 %collective-permute-start.7 = (bf16[272,256]{1,0:T(8,128)(2,1)}, bf16[272,256]{1,0:T(8,128)(2,1)S(1)}, u32[]{:S(2)}, u32[]{:S(2)}) collective-permute-start(bf16[272,256]{1,0:T(8,128)(2,1)} %get-tuple-element.97.refs_1_), channel_id=1, source_target_pairs={{0,4},{4,8},{8,12},{12,0},{1,5},{5,9},{9,13},{13,1},{2,6},{6,10},{... | collective-permute-start | bytes 417800 | tf_op jit(solution)/shard_map/ppermute | solution.py:629
  15.0 7.3 %collective-permute-start.8 = (bf16[272,256]{1,0:T(8,128)(2,1)}, bf16[272,256]{1,0:T(8,128)(2,1)S(1)}, u32[]{:S(2)}, u32[]{:S(2)}) collective-permute-start(bf16[272,256]{1,0:T(8,128)(2,1)} %get-tuple-element.97.refs_1_), channel_id=1, source_target_pairs={{0,12},{4,0},{8,4},{12,8},{1,13},{5,1},{9,5},{13,9},{2,14},{6,2},{... | collective-permute-start | bytes 417800 | tf_op jit(solution)/shard_map/ppermute | solution.py:632
  19.5 8.0 %collective-permute-start.3 = (bf16[272,256]{1,0:T(8,128)(2,1)S(1)}, bf16[272,256]{1,0:T(8,128)(2,1)S(1)}, u32[]{:S(2)}, u32[]{:S(2)}) collective-permute-start(bf16[272,256]{1,0:T(8,128)(2,1)S(1)} %collective-permute-done.refs_1_), channel_id=1, source_target_pairs={{0,4},{4,8},{8,12},{12,0},{1,5},{5,9},{9,13},{13,1},{2,6},{6,10},{... | collective-permute-start | bytes 417800 | tf_op jit(solution)/shard_map/ppermute | solution.py:629
  22.8 7.2 %collective-permute-start.10 = (bf16[272,256]{1,0:T(8,128)(2,1)S(1)}, bf16[272,256]{1,0:T(8,128)(2,1)S(1)}, u32[]{:S(2)}, u32[]{:S(2)}) collective-permute-start(bf16[272,256]{1,0:T(8,128)(2,1)S(1)} %collective-permute-done.8.refs_3_), channel_id=1, source_target_pairs={{0,12},{4,0},{8,4},{12,8},{1,13},{5,1},{9,5},{13,9},{2,14},{6,2},{... | collective-permute-start | bytes 417800 | tf_op jit(solution)/shard_map/ppermute | solution.py:632
  31.4 25.8 %collective-permute-start.28 = (bf16[2,192,2048]{2,1,0:T(8,128)(2,1)S(1)}, bf16[2,192,2048]{2,1,0:T(8,128)(2,1)S(1)}, u32[]{:S(2)}, u32[]{:S(2)}) collective-permute-start(bf16[2,192,2048]{2,1,0:T(8,128)(2,1)S(1)} %bitcast.5), channel_id=1, source_target_pairs={{0,1},{1,0},{2,3},{3,2},{4,5},{5,4},{6,7},{7,6},{8,9},{9,8},{10,11... | collective-permute-start | bytes 4718600 | tf_op jit(solution)/shard_map/ppermute | solution.py:34
  31.5 14.5 %collective-permute-start.29 = (bf16[192,2048]{1,0:T(8,128)(2,1)S(1)}, bf16[192,2048]{1,0:T(8,128)(2,1)S(1)}, u32[]{:S(2)}, u32[]{:S(2)}) collective-permute-start(bf16[192,2048]{1,0:T(8,128)(2,1)S(1)} %bitcast.11), channel_id=1, source_target_pairs={{0,1},{1,0},{2,3},{3,2},{4,5},{5,4},{6,7},{7,6},{8,9},{9,8},{10,11... | collective-permute-start | bytes 2359304 | tf_op jit(solution)/shard_map/ppermute | solution.py:34
  31.9 5.8 %collective-permute-start.16 = (bf16[64,1024]{1,0:T(8,128)(2,1)S(1)}, bf16[64,1024]{1,0:T(8,128)(2,1)S(1)}, u32[]{:S(2)}, u32[]{:S(2)}) collective-permute-start(bf16[64,1024]{1,0:T(8,128)(2,1)S(1)} %get-tuple-element.120), channel_id=1, source_target_pairs={{0,1},{1,0},{2,3},{3,2},{4,5},{5,4},{6,7},{7,6},{8,9},{9,8},{10,11... | collective-permute-start | bytes 393224 | tf_op jit(solution)/shard_map/ppermute | solution.py:106
  35.4 6.4 %collective-permute-start.15 = (bf16[32,2048]{1,0:T(8,128)(2,1)S(1)}, bf16[32,2048]{1,0:T(8,128)(2,1)S(1)}, u32[]{:S(2)}, u32[]{:S(2)}) collective-permute-start(bf16[32,2048]{1,0:T(8,128)(2,1)S(1)} %get-tuple-element.117), channel_id=1, source_target_pairs={{0,2},{2,0},{1,3},{3,1},{4,6},{6,4},{5,7},{7,5},{8,10},{10,8},{9,1... | collective-permute-start | bytes 393224 | tf_op jit(solution)/shard_map/ppermute | solution.py:666
  37.2 6.9 %collective-permute-start.17 = (bf16[32,2048]{1,0:T(8,128)(2,1)S(1)}, bf16[32,2048]{1,0:T(8,128)(2,1)S(1)}, u32[]{:S(2)}, u32[]{:S(2)}) collective-permute-start(bf16[32,2048]{1,0:T(8,128)(2,1)S(1)} %get-tuple-element.123), channel_id=1, source_target_pairs={{0,2},{2,0},{1,3},{3,1},{4,6},{6,4},{5,7},{7,5},{8,10},{10,8},{9,1... | collective-permute-start | bytes 393224 | tf_op jit(solution)/shard_map/ppermute | solution.py:666
  44.3 6.0 %collective-permute-start.22 = (bf16[32,2176]{1,0:T(8,128)(2,1)S(1)}, bf16[32,2176]{1,0:T(8,128)(2,1)S(1)}, u32[]{:S(2)}, u32[]{:S(2)}) collective-permute-start(bf16[32,2176]{1,0:T(8,128)(2,1)S(1)} %get-tuple-element.148.refs_1_), channel_id=1, source_target_pairs={{5,0},{4,1},{9,4},{8,5},{13,8},{12,9},{15,12},{14,13},{11,14},{10,... | collective-permute-start | bytes 417800 | tf_op jit(solution)/shard_map/ppermute | solution.py:486
  45.2 6.0 %collective-permute-start.25 = (bf16[32,2176]{1,0:T(8,128)(2,1)S(1)}, bf16[32,2176]{1,0:T(8,128)(2,1)S(1)}, u32[]{:S(2)}, u32[]{:S(2)}) collective-permute-start(bf16[32,2176]{1,0:T(8,128)(2,1)S(1)} %get-tuple-element.148.refs_1_), channel_id=1, source_target_pairs={{0,5},{1,4},{4,9},{5,8},{8,13},{9,12},{12,15},{13,14},{14,11},{15,... | collective-permute-start | bytes 417800 | tf_op jit(solution)/shard_map/ppermute | solution.py:488
  46.1 6.9 %collective-permute-start.27 = (bf16[32,2176]{1,0:T(8,128)(2,1)S(1)}, bf16[32,2176]{1,0:T(8,128)(2,1)S(1)}, u32[]{:S(2)}, u32[]{:S(2)}) collective-permute-start(bf16[32,2176]{1,0:T(8,128)(2,1)S(1)} %get-tuple-element.147.refs_0_), channel_id=1, source_target_pairs={{5,0},{4,1},{9,4},{8,5},{13,8},{12,9},{15,12},{14,13},{11,14},{10,... | collective-permute-start | bytes 417800 | tf_op jit(solution)/shard_map/ppermute | solution.py:489
  47.8 6.4 %collective-permute-start.19 = (bf16[32,2176]{1,0:T(8,128)(2,1)S(1)}, bf16[32,2176]{1,0:T(8,128)(2,1)S(1)}, u32[]{:S(2)}, u32[]{:S(2)}) collective-permute-start(bf16[32,2176]{1,0:T(8,128)(2,1)S(1)} %collective-permute-done.18.refs_0_), channel_id=1, source_target_pairs={{0,5},{1,4},{4,9},{5,8},{8,13},{9,12},{12,15},{13,14},{14,11},{15,... | collective-permute-start | bytes 417800 | tf_op jit(solution)/shard_map/ppermute | solution.py:485
  51.2 7.6 %collective-permute-start.26 = (bf16[32,2176]{1,0:T(8,128)(2,1)S(1)}, bf16[32,2176]{1,0:T(8,128)(2,1)S(1)}, u32[]{:S(2)}, u32[]{:S(2)}) collective-permute-start(bf16[32,2176]{1,0:T(8,128)(2,1)S(1)} %collective-permute-done.25.refs_2_), channel_id=1, source_target_pairs={{0,5},{1,4},{4,9},{5,8},{8,13},{9,12},{12,15},{13,14},{14,11},{15,... | collective-permute-start | bytes 417800 | tf_op jit(solution)/shard_map/ppermute | solution.py:488
  53.0 6.4 %collective-permute-start.31 = (bf16[32,2176]{1,0:T(8,128)(2,1)S(1)}, bf16[32,2176]{1,0:T(8,128)(2,1)S(1)}, u32[]{:S(2)}, u32[]{:S(2)}) collective-permute-start(bf16[32,2176]{1,0:T(8,128)(2,1)S(1)} %collective-permute-done.27.refs_3_), channel_id=1, source_target_pairs={{5,0},{4,1},{9,4},{8,5},{13,8},{12,9},{15,12},{14,13},{11,14},{10,... | collective-permute-start | bytes 417800 | tf_op jit(solution)/shard_map/ppermute | solution.py:489
  54.1 6.4 %collective-permute-start.20 = (bf16[32,2176]{1,0:T(8,128)(2,1)S(1)}, bf16[32,2176]{1,0:T(8,128)(2,1)S(1)}, u32[]{:S(2)}, u32[]{:S(2)}) collective-permute-start(bf16[32,2176]{1,0:T(8,128)(2,1)S(1)} %collective-permute-done.19.refs_0_), channel_id=1, source_target_pairs={{0,5},{1,4},{4,9},{5,8},{8,13},{9,12},{12,15},{13,14},{14,11},{15,... | collective-permute-start | bytes 417800 | tf_op jit(solution)/shard_map/ppermute | solution.py:485
  56.0 5.9 %collective-permute-start.24 = (bf16[32,2176]{1,0:T(8,128)(2,1)S(1)}, bf16[32,2176]{1,0:T(8,128)(2,1)S(1)}, u32[]{:S(2)}, u32[]{:S(2)}) collective-permute-start(bf16[32,2176]{1,0:T(8,128)(2,1)S(1)} %collective-permute-done.23.refs_1_), channel_id=1, source_target_pairs={{5,0},{4,1},{9,4},{8,5},{13,8},{12,9},{15,12},{14,13},{11,14},{10,... | collective-permute-start | bytes 417800 | tf_op jit(solution)/shard_map/ppermute | solution.py:486
  58.7 6.2 %collective-permute-start.30 = (bf16[32,2176]{1,0:T(8,128)(2,1)S(1)}, bf16[32,2176]{1,0:T(8,128)(2,1)S(1)}, u32[]{:S(2)}, u32[]{:S(2)}) collective-permute-start(bf16[32,2176]{1,0:T(8,128)(2,1)S(1)} %collective-permute-done.26.refs_2_), channel_id=1, source_target_pairs={{0,5},{1,4},{4,9},{5,8},{8,13},{9,12},{12,15},{13,14},{14,11},{15,... | collective-permute-start | bytes 417800 | tf_op jit(solution)/shard_map/ppermute | solution.py:488
  60.5 6.4 %collective-permute-start.21 = (bf16[32,2176]{1,0:T(8,128)(2,1)S(1)}, bf16[32,2176]{1,0:T(8,128)(2,1)S(1)}, u32[]{:S(2)}, u32[]{:S(2)}) collective-permute-start(bf16[32,2176]{1,0:T(8,128)(2,1)S(1)} %collective-permute-done.20.refs_0_), channel_id=1, source_target_pairs={{0,5},{1,4},{4,9},{5,8},{8,13},{9,12},{12,15},{13,14},{14,11},{15,... | collective-permute-start | bytes 417800 | tf_op jit(solution)/shard_map/ppermute | solution.py:485
  61.9 6.1 %collective-permute-start.33 = (bf16[32,2176]{1,0:T(8,128)(2,1)S(1)}, bf16[32,2176]{1,0:T(8,128)(2,1)S(1)}, u32[]{:S(2)}, u32[]{:S(2)}) collective-permute-start(bf16[32,2176]{1,0:T(8,128)(2,1)S(1)} %collective-permute-done.24.refs_1_), channel_id=1, source_target_pairs={{5,0},{4,1},{9,4},{8,5},{13,8},{12,9},{15,12},{14,13},{11,14},{10,... | collective-permute-start | bytes 417800 | tf_op jit(solution)/shard_map/ppermute | solution.py:486
  71.3 6.2 %collective-permute-start.44 = (bf16[32,2048]{1,0:T(8,128)(2,1)S(1)}, bf16[32,2048]{1,0:T(8,128)(2,1)S(1)}, u32[]{:S(2)}, u32[]{:S(2)}) collective-permute-start(bf16[32,2048]{1,0:T(8,128)(2,1)S(1)} %convert_element_type.15), channel_id=1, source_target_pairs={{0,5},{1,4},{4,9},{5,8},{8,13},{9,12},{12,15},{13,14},{14,11},{15,... | collective-permute-start | bytes 393224 | tf_op jit(solution)/shard_map/ppermute | solution.py:512
  71.4 6.4 %collective-permute-start.38 = (bf16[32,2048]{1,0:T(8,128)(2,1)S(1)}, bf16[32,2048]{1,0:T(8,128)(2,1)S(1)}, u32[]{:S(2)}, u32[]{:S(2)}) collective-permute-start(bf16[32,2048]{1,0:T(8,128)(2,1)S(1)} %convert_element_type.13), channel_id=1, source_target_pairs={{5,0},{4,1},{9,4},{8,5},{13,8},{12,9},{15,12},{14,13},{11,14},{10,... | collective-permute-start | bytes 393224 | tf_op jit(solution)/shard_map/ppermute | solution.py:512
  73.2 6.5 %collective-permute-start.41 = (bf16[32,2048]{1,0:T(8,128)(2,1)S(1)}, bf16[32,2048]{1,0:T(8,128)(2,1)S(1)}, u32[]{:S(2)}, u32[]{:S(2)}) collective-permute-start(bf16[32,2048]{1,0:T(8,128)(2,1)S(1)} %convert_element_type.14), channel_id=1, source_target_pairs={{0,5},{1,4},{4,9},{5,8},{8,13},{9,12},{12,15},{13,14},{14,11},{15,... | collective-permute-start | bytes 393224 | tf_op jit(solution)/shard_map/ppermute | solution.py:512
  77.9 5.8 %collective-permute-start.39 = (bf16[32,2048]{1,0:T(8,128)(2,1)S(1)}, bf16[32,2048]{1,0:T(8,128)(2,1)S(1)}, u32[]{:S(2)}, u32[]{:S(2)}) collective-permute-start(bf16[32,2048]{1,0:T(8,128)(2,1)S(1)} %add_share.13), channel_id=1, source_target_pairs={{5,0},{4,1},{9,4},{8,5},{13,8},{12,9},{15,12},{14,13},{11,14},{10,... | collective-permute-start | bytes 393224 | tf_op jit(solution)/shard_map/ppermute | solution.py:512
  79.8 6.2 %collective-permute-start.42 = (bf16[32,2048]{1,0:T(8,128)(2,1)S(1)}, bf16[32,2048]{1,0:T(8,128)(2,1)S(1)}, u32[]{:S(2)}, u32[]{:S(2)}) collective-permute-start(bf16[32,2048]{1,0:T(8,128)(2,1)S(1)} %add_share.15), channel_id=1, source_target_pairs={{0,5},{1,4},{4,9},{5,8},{8,13},{9,12},{12,15},{13,14},{14,11},{15,... | collective-permute-start | bytes 393224 | tf_op jit(solution)/shard_map/ppermute | solution.py:512
  83.7 7.6 %collective-permute-start.40 = (bf16[32,2048]{1,0:T(8,128)(2,1)S(1)}, bf16[32,2048]{1,0:T(8,128)(2,1)S(1)}, u32[]{:S(2)}, u32[]{:S(2)}) collective-permute-start(bf16[32,2048]{1,0:T(8,128)(2,1)S(1)} %add_share.14), channel_id=1, source_target_pairs={{5,0},{4,1},{9,4},{8,5},{13,8},{12,9},{15,12},{14,13},{11,14},{10,... | collective-permute-start | bytes 393224 | tf_op jit(solution)/shard_map/ppermute | solution.py:512
  86.2 6.1 %collective-permute-start.37 = (bf16[32,2048]{1,0:T(8,128)(2,1)S(1)}, bf16[32,2048]{1,0:T(8,128)(2,1)S(1)}, u32[]{:S(2)}, u32[]{:S(2)}) collective-permute-start(bf16[32,2048]{1,0:T(8,128)(2,1)S(1)} %add_share.12), channel_id=1, source_target_pairs={{5,0},{4,1},{9,4},{8,5},{13,8},{12,9},{15,12},{14,13},{11,14},{10,... | collective-permute-start | bytes 393224 | tf_op jit(solution)/shard_map/ppermute | solution.py:512
  (27 other events, 180.6 us)

commit v8 on v7

--- a/solution.py
+++ b/solution.py
@@ -60,12 +60,13 @@
     return came
 
 
-def pack_keys(cache_keys, cache_values, new_keys, new_values, page_len, kv_heads, heads_here):
+def pack_keys(cache_keys, cache_values, new_keys, new_values, page_len, routing, kv_heads, heads_here):
     cache_rows, new_rows = cache_keys.shape[0], new_keys.shape[0]
     group_width = QH // KVH
     rows = cache_rows + new_rows + MASK_ROWS
 
-    def kernel(page_ref, ck_ref, cv_ref, nk_ref, nv_ref, *out_refs):
+    def kernel(page_ref, ck_ref, cv_ref, nk_ref, nv_ref, *refs):
+        routing_refs, out_refs = refs[: len(routing)], refs[len(routing) :]
         first = lax.axis_index("hd") * heads_here // group_width
         lane = lax.broadcasted_iota(jnp.int32, (MASK_ROWS, 2 * HD), 1)
         bias = jnp.where(lane < page_ref[0], 0.0, NEG_FILL).astype(jnp.bfloat16)
@@ -76,15 +77,23 @@
             out_ref[cache_rows : cache_rows + new_rows, :HD] = nk_ref[:, columns]
             out_ref[cache_rows : cache_rows + new_rows, HD:] = nv_ref[:, columns]
             out_ref[cache_rows + new_rows :, :] = bias
+        if routing:
+            ids = routing_refs[0][...]
+            gates = routing_refs[1][...].astype(jnp.float32)
+            expert = lax.broadcasted_iota(jnp.int32, (MASK_ROWS, ids.shape[1]), 0)
+            table = jnp.zeros(expert.shape, jnp.float32)
+            for k in range(ids.shape[0]):
+                table = table + jnp.where(ids[k : k + 1, :] == expert, gates[k : k + 1, :], 0.0)
+            out_refs[0][cache_rows + new_rows :, HD:] = table.astype(jnp.bfloat16)
 
     vmem = pl.BlockSpec(memory_space=pltpu.VMEM)
     return pl.pallas_call(
         kernel,
         out_shape=[jax.ShapeDtypeStruct((rows, 2 * HD), cache_keys.dtype)] * kv_heads,
-        in_specs=[pl.BlockSpec(memory_space=pltpu.SMEM)] + [vmem] * 4,
+        in_specs=[pl.BlockSpec(memory_space=pltpu.SMEM)] + [vmem] * (4 + len(routing)),
         out_specs=[vmem] * kv_heads,
         name="pack_keys",
-    )(page_len, cache_keys, cache_values, new_keys, new_values)
+    )(page_len, cache_keys, cache_values, new_keys, new_values, *routing)
 
 
 def small_kernel(kernel, out_shape, operands, name):
@@ -149,33 +158,38 @@
     return small_kernel(kernel, [shape] * n_sub, [residual], "split_rows")
 
 
-def gates_by_expert(expert_ids, gates, rows):
-    choices, block_rows = expert_ids.shape[1], expert_ids.shape[0]
-
-    def kernel(ids_ref, gates_ref, out_ref):
-        sub = lax.axis_index("sub")
-        expert = lax.broadcasted_iota(jnp.int32, (LANES, block_rows), 0)
-        weights = gates_ref[...].astype(jnp.float32)
-        ids = ids_ref[...]
+def walk_place(ep, hd, n_ep, n_hd):
+    if n_hd == 2:
+        return jnp.where(hd == 0, ep, 2 * n_ep - 1 - ep)
+    return ep * n_hd + hd
+
+
+def gates_by_chip(own, came, n_ep, n_hd):
+    block_rows = own.shape[1]
+
+    def kernel(own_ref, came_ref, out_ref):
+        ep, hd = lax.axis_index("ep"), lax.axis_index("hd")
+        mine = ep * n_hd + hd
+        expert = lax.broadcasted_iota(jnp.int32, (MASK_ROWS, block_rows), 0)
+        place = lax.broadcasted_iota(jnp.int32, (LANES, block_rows), 0)
         table = jnp.zeros((LANES, block_rows), jnp.float32)
-        for k in range(choices):
-            table = table + jnp.where(ids[k : k + 1, :] == expert, weights[k : k + 1, :], 0.0)
-        table = table.T
-        chosen = table[:rows]
-        for place in range(1, block_rows // rows):
-            chosen = jnp.where(sub == place, table[place * rows : (place + 1) * rows], chosen)
-        out_ref[...] = chosen.astype(jnp.bfloat16)
-
-    shape = jax.ShapeDtypeStruct((rows, LANES), jnp.bfloat16)
-    return small_kernel(kernel, [shape], [expert_ids.T, gates.T], "gates_by_expert")[0]
-
-
-def normalise(kept, came, residual_parts, gain, gate_table, first):
+        for ref, other in ((own_ref, hd), (came_ref, 1 - hd)):
+            for hop in range(n_ep):
+                tile = ref[hop * MASK_ROWS : (hop + 1) * MASK_ROWS, :].astype(jnp.float32)
+                row = jnp.sum(jnp.where(expert == mine, tile, 0.0), axis=0, keepdims=True)
+                chip = walk_place((ep - hop) % n_ep, other, n_ep, n_hd)
+                table = jnp.where(place == chip, row, table)
+        out_ref[...] = table.T
+
+    shape = jax.ShapeDtypeStruct((block_rows, LANES), jnp.float32)
+    return small_kernel(kernel, [shape], [own, came], "gates_by_chip")[0]
+
+
+def normalise(kept, came, residual_parts, gain, first):
     n_sub = len(residual_parts)
     rows, width = came.shape[0], residual_parts[0].shape[1]
     chunk = slice(first, first + rows)
     features = n_sub * width
-    extra = 0 if gate_table is None else LANES
 
     def kernel(*refs):
         refs = list(refs)
@@ -183,8 +197,6 @@
         came_ref = refs.pop(0)
         part_refs = [refs.pop(0) for _ in residual_parts]
         gain_ref = refs.pop(0)
-        if extra:
-            gate_ref = refs.pop(0)
         hidden_ref, normed_ref = refs
         sub = lax.axis_index("sub")
         hidden, places, squares = [], [], 0.0
@@ -204,17 +216,10 @@
         for value, place in zip(hidden, places):
             normed = value.astype(jnp.float32) * scale * gain_ref[:, place].astype(jnp.float32)
             normed_ref[:, place] = normed.astype(jnp.bfloat16)
-        if extra:
-            normed_ref[:, features:] = gate_ref[chunk, :]
 
     operands = ([kept] if kept is not None else []) + [came] + list(residual_parts)
     operands.append(gain.reshape(1, features))
-    if extra:
-        operands.append(gate_table)
-    out_shape = [
-        jax.ShapeDtypeStruct((rows, features), jnp.bfloat16),
-        jax.ShapeDtypeStruct((rows, features + extra), jnp.bfloat16),
-    ]
+    out_shape = [jax.ShapeDtypeStruct((rows, features), jnp.bfloat16)] * 2
     return small_kernel(kernel, out_shape, operands, "normalise")
 
 
@@ -406,21 +411,30 @@
     )(*operands)
 
 
-def apply_expert(inputs, gate_up, w_down):
+def apply_expert(inputs, origins, gate_table, gate_up, w_down):
     features = w_down[0].shape[1]
     hidden = w_down[0].shape[0]
     rows = sum(x.shape[0] for x in inputs)
+    n_ep, n_hd, n_sub = lax.axis_size("ep"), lax.axis_size("hd"), lax.axis_size("sub")
+    chunks = gate_table.shape[0] // n_sub // inputs[0].shape[0]
 
     def kernel(*refs):
         x_refs, refs = refs[: len(inputs)], refs[len(inputs) :]
+        gate_ref, refs = refs[0], refs[1:]
         gu_refs, refs = refs[: len(gate_up)], refs[len(gate_up) :]
         down_refs, out_refs = refs[: len(w_down)], refs[len(w_down) :]
-        mine = lax.axis_index("ep") * lax.axis_size("hd") + lax.axis_index("hd")
-        joined = jnp.concatenate([x[...] for x in x_refs], axis=0)
-        x = joined[:, :features]
-        table = joined[:, features:].astype(jnp.float32)
-        lane = lax.broadcasted_iota(jnp.int32, table.shape, 1)
-        gate = jnp.sum(jnp.where(lane == mine, table, 0.0), axis=1, keepdims=True)
+        x = jnp.concatenate([x[...] for x in x_refs], axis=0)
+        here = walk_place(lax.axis_index("ep"), lax.axis_index("hd"), n_ep, n_hd)
+        columns = []
+        for (steps, chunk), x_ref in zip(origins, x_refs):
+            count = x_ref.shape[0]
+            sub = (lax.axis_index("sub") + steps) % n_sub
+            first = pl.multiple_of((sub * chunks + chunk) * count, count)
+            table = gate_ref[pl.ds(first, count), :]
+            lane = lax.broadcasted_iota(jnp.int32, table.shape, 1)
+            chip = (here + steps) % (n_ep * n_hd)
+            columns.append(jnp.sum(jnp.where(lane == chip, table, 0.0), axis=1, keepdims=True))
+        gate = jnp.concatenate(columns, axis=0)
         total = None
         for gu, down in zip(gu_refs, down_refs):
             gate_part = lax.dot_general(
@@ -437,7 +451,7 @@
             first += out_ref.shape[0]
 
     vmem = pl.BlockSpec(memory_space=pltpu.VMEM)
-    operands = list(inputs) + list(gate_up) + list(w_down)
+    operands = list(inputs) + [gate_table] + list(gate_up) + list(w_down)
     return pl.pallas_call(
         kernel,
         out_shape=[jax.ShapeDtypeStruct((x.shape[0], features), jnp.float32) for x in inputs],
@@ -468,7 +482,7 @@
     return small_kernel(kernel, [shape], [came, share], "add_share")[0]
 
 
-def dense_experts(own, gate_up, w_down):
+def dense_experts(own, gate_table, gate_up, w_down):
     axes = ("ep", "hd", "sub")
     walk = chip_ring(lax.axis_size("ep"), lax.axis_size("hd"))
     size, n_sub = len(walk), lax.axis_size("sub")
@@ -488,12 +502,13 @@
             behind[1] = lax.ppermute(behind[1], axes, ahead)
             before[0] = lax.ppermute(before[0], axes, back)
         if waiting:
-            out = apply_expert(waiting, gate_up, w_down)
+            out = apply_expert(waiting, origins, gate_table, gate_up, w_down)
             late = int(hop < reach)
             behind[late], out = lax.optimization_barrier((behind[late], out))
             outs.append(out)
         waiting = [behind[0], before[1]] + ([behind[1], before[0]] if hop < reach else [])
-    outs.append(apply_expert(waiting, gate_up, w_down))
+        origins = [(-hop, 0), (hop, 1), (-hop, 1), (hop, 0)][: len(waiting)]
+    outs.append(apply_expert(waiting, origins, gate_table, gate_up, w_down))
     to_back, to_ahead = [None, None], [None, None]
     for hop in range(reach, 0, -1):
         shares = outs[hop]
@@ -512,7 +527,8 @@
             chunks[chunk] = lax.ppermute(sum_here, axes, way)
             if hop == min(2, reach) and share == 0:
                 chunks[chunk], own = lax.optimization_barrier((chunks[chunk], own))
-    return apply_expert(own, gate_up, w_down), to_back, to_ahead
+    mine = apply_expert(own, [(0, 0), (0, 1)], gate_table, gate_up, w_down)
+    return mine, to_back, to_ahead
 
 
 def sparse_experts(widened, normed, gate_up, w_down, expert_ids, gates, features):
@@ -595,17 +611,27 @@
     dense = (
         expert_ids.shape[1] == all_experts
         and gate_up.shape[0] == 1
-        and n_ep * n_hd % 2 == 0
+        and n_hd == 2
         and rows % 32 == 0
+        and all_experts <= MASK_ROWS
+        and expert_ids.shape[0] == LANES
     )
 
     packed = pack_keys(
-        cache_keys, cache_values, new_keys, new_values, page_len, kv_heads, heads_here
+        cache_keys,
+        cache_values,
+        new_keys,
+        new_values,
+        page_len,
+        [expert_ids.T, gates.T] if dense else [],
+        kv_heads,
+        heads_here,
     )
     query_rows_here = choose_queries(queries.reshape(n_hd, n_sub, rows, heads_here * HD))
     reach = n_ep // 2
     up, down = list(packed), list(packed)
     arrived = [[(0, x)] for x in packed]
+    tables = {}
     states = [None] * kv_heads
     earlier = None
     for distance in range(reach + 1):
@@ -621,6 +647,8 @@
             ]
             gate_up_parts = sub_copies(gate_up[0])
             w_down_parts = sub_copies(w_down[0])
+        for hop, x in arrived[0]:
+            tables[hop] = x[-MASK_ROWS:, HD:]
         onward = [[] for _ in packed]
         if distance < reach:
             opposite = 2 * (distance + 1) == n_ep
@@ -658,12 +686,16 @@
         if distance == 0:
             residual, states[0] = lax.optimization_barrier((residual, states[0]))
             residual_parts = hand_over(split_rows(residual, n_sub))
-            gate_table = gates_by_expert(expert_ids, gates, rows) if dense else None
         arrived = onward
     parts = states[-1]
     if n_hd == 2:
         kept, sent = parts[: len(parts) // 2], parts[len(parts) // 2 :]
         came = [lax.ppermute(x, "hd", cycle(n_hd)) for x in sent]
+        if dense:
+            own_tables = jnp.concatenate([tables[hop] for hop in range(n_ep)], axis=0)
+            other_tables = lax.ppermute(own_tables, "hd", cycle(n_hd))
+            gate_table = gates_by_chip(own_tables, other_tables, n_ep, n_hd)
+            came[0], gate_table = lax.optimization_barrier((came[0], gate_table))
     else:
         kept = [None]
         came = [lax.psum_scatter(parts[0], "hd", scatter_dimension=0, tiled=True)]
@@ -674,7 +706,6 @@
             came_chunk,
             residual_parts,
             norm_gain,
-            gate_table,
             index * came_chunk.shape[0],
         )
         hidden.append(pair[0])
@@ -692,7 +723,7 @@
             gates,
             features,
         )
-    mine, to_back, to_ahead = dense_experts(normed, gate_up_parts, w_down_parts)
+    mine, to_back, to_ahead = dense_experts(normed, gate_table, gate_up_parts, w_down_parts)
     return stack_rows(hand_over(add_up(hidden, mine, to_back, to_ahead, n_sub)))
 
 

time: 96.5 us -> 95.7 us (level)
  starting transfers between devices: 47 us -> 44.8 us
    ppermute x14, starting transfers between devices: 17 us -> 12.7 us  [dense_experts(): chunks[chunk] = lax.ppermute(sum_here, axes, way)]
    ppermute x14, waiting for transfers between devices: 5.55 us -> 8.37 us  [dense_experts(): chunks[chunk] = lax.ppermute(sum_here, axes, way)]
    ppermute x4, starting transfers between devices: 1.79 us -> 4.29 us  [dense_experts(): behind[0] = lax.ppermute(behind[0], axes, ahead)]
    ppermute x4, waiting for transfers between devices: 5.1 us -> 3.06 us  [dense_experts(): before[1] = lax.ppermute(before[1], axes, back)]
    ppermute x4, starting transfers between devices: 4.41 us -> 2.52 us  [dense_experts(): before[1] = lax.ppermute(before[1], axes, back)]
    ppermute x0 -> x1, starting transfers between devices: none -> 1.77 us  [shards(): other_tables = lax.ppermute(own_tables, 'hd', cycle(n_hd))]
    ppermute x3, starting transfers between devices: 2.44 us -> 3.63 us  [dense_experts(): behind[1] = lax.ppermute(behind[1], axes, ahead)]
    ppermute x3, starting transfers between devices: 3.16 us -> 1.98 us  [dense_experts(): before[0] = lax.ppermute(before[0], axes, back)]
  transfers between devices with their start and end apart: 49 -> 50, of which waited for: 21 -> 24; matrix products, arithmetic and copies ran while one was open for 0% -> 1% of each run, Pallas kernels for 16% -> 17%
where the time goes in v8:
time: 95.7 us; the launch traced here: 95.4 us
  starting transfers between devices  44.8 us (47%)
  waiting for transfers between devices  25.7 us (27%)
  Pallas kernels  20.1 us (21%)
  local copies, waits for them, and re-layouts  3.77 us (4%)
  between operations  1.06 us (1%)
    ppermute x14, starting transfers between devices, dense_experts(): chunks[chunk] = lax.ppermute(sum_here, axes, way)  12.7 us
    pallas_call x6, Pallas kernels, attend(): pl.pallas_call(kernel, out_shape=out_shape, in_specs=[vmem] * len(operand...  8.84 us
    ppermute x14, waiting for transfers between devices, dense_experts(): chunks[chunk] = lax.ppermute(sum_here, axes, way)  8.37 us
    pallas_call x5, Pallas kernels, apply_expert(): pl.pallas_call(kernel, out_shape=[jax.ShapeDtypeStruct((x.shape[0], featu...  7.75 us
    ppermute x3, starting transfers between devices, shards(): down[kv] = lax.ppermute(down[kv], 'ep', cycle(n_ep, n_ep - 1))  7.05 us
    ppermute x3, starting transfers between devices, shards(): up[kv] = lax.ppermute(up[kv], 'ep', cycle(n_ep))  6.03 us
    ppermute x2, waiting for transfers between devices, shards(): came = [lax.ppermute(x, 'hd', cycle(n_hd)) for x in sent]  5.5 us
    ppermute x4, starting transfers between devices, dense_experts(): behind[0] = lax.ppermute(behind[0], axes, ahead)  4.29 us
  transfers between devices with their start and end apart: 50, of which 24 were waited for; matrix products, arithmetic and copies ran while one was open for 1% of the time, Pallas kernels for 17%

profile of v8, /device:TPU:0, one launch (start us, length us, event | category | flops | bytes accessed | tf_op | source)
XLA Modules:
  0.0 95.4 jit_solution(18220677435065611751)
XLA Ops:
  0.7 1.9 %pack_keys.1 = (bf16[272,256]{1,0:T(8,128)(2,1)}, bf16[272,256]{1,0:T(8,128)(2,1)}) custom-call(s32[1]{0:T(128)S(6)} %copy.14.page_ref, bf16[128,512]{1,0:T(8,128)(2,1)} %ck_ref.1, bf16[128,512]{1,0:T(8,128)(2,1)} %cv_ref.1, bf16[128,512]{1,0:T(8,128)(2,1)} %nk_ref.1, bf16[128,512]{1,0:T(8,128)(2,1)} %nv_ref.1, s32[8,128]{1,0:T(8,128)} %bitcast.18, ...), custom_call_target="tpu_custom_call" | custom-call | tf_op jit(solution)/shard_map/pack_keys/pallas_call | solution.py:90
  3.0 3.0 %collective-permute-start = (bf16[272,256]{1,0:T(8,128)(2,1)}, bf16[272,256]{1,0:T(8,128)(2,1)S(1)}, u32[]{:S(2)}, u32[]{:S(2)}) collective-permute-start(bf16[272,256]{1,0:T(8,128)(2,1)} %get-tuple-element.87.refs_1_), channel_id=1, source_target_pairs={{0,4},{4,8},{8,12},{12,0},{1,5},{5,9},{9,13},{13,1},{2,6},{6,10},{... | collective-permute-start | bytes 417800 | tf_op jit(solution)/shard_map/ppermute | solution.py:657
  6.1 2.0 %collective-permute-start.1 = (bf16[272,256]{1,0:T(8,128)(2,1)}, bf16[272,256]{1,0:T(8,128)(2,1)S(1)}, u32[]{:S(2)}, u32[]{:S(2)}) collective-permute-start(bf16[272,256]{1,0:T(8,128)(2,1)} %get-tuple-element.87.refs_1_), channel_id=1, source_target_pairs={{0,12},{4,0},{8,4},{12,8},{1,13},{5,1},{9,5},{13,9},{2,14},{6,2},{... | collective-permute-start | bytes 417800 | tf_op jit(solution)/shard_map/ppermute | solution.py:660
  10.2 2.9 %collective-permute-start.7 = (bf16[272,256]{1,0:T(8,128)(2,1)}, bf16[272,256]{1,0:T(8,128)(2,1)S(1)}, u32[]{:S(2)}, u32[]{:S(2)}) collective-permute-start(bf16[272,256]{1,0:T(8,128)(2,1)} %get-tuple-element.99.refs_1_), channel_id=1, source_target_pairs={{0,4},{4,8},{8,12},{12,0},{1,5},{5,9},{9,13},{13,1},{2,6},{6,10},{... | collective-permute-start | bytes 417800 | tf_op jit(solution)/shard_map/ppermute | solution.py:657
  15.0 2.1 %collective-permute-start.8 = (bf16[272,256]{1,0:T(8,128)(2,1)}, bf16[272,256]{1,0:T(8,128)(2,1)S(1)}, u32[]{:S(2)}, u32[]{:S(2)}) collective-permute-start(bf16[272,256]{1,0:T(8,128)(2,1)} %get-tuple-element.99.refs_1_), channel_id=1, source_target_pairs={{0,12},{4,0},{8,4},{12,8},{1,13},{5,1},{9,5},{13,9},{2,14},{6,2},{... | collective-permute-start | bytes 417800 | tf_op jit(solution)/shard_map/ppermute | solution.py:660
  19.6 2.7 %collective-permute-done.8.refs_3_ = bf16[272,256]{1,0:T(8,128)(2,1)S(1)} collective-permute-done((bf16[272,256]{1,0:T(8,128)(2,1)}, bf16[272,256]{1,0:T(8,128)(2,1)S(1)}, u32[]{:S(2)}, u32[]{:S(2)}) %collective-permute-start.8) | collective-permute-done | bytes 139296 | tf_op jit(solution)/shard_map/ppermute | solution.py:660
  22.8 2.9 %collective-permute-start.10 = (bf16[272,256]{1,0:T(8,128)(2,1)S(1)}, bf16[272,256]{1,0:T(8,128)(2,1)S(1)}, u32[]{:S(2)}, u32[]{:S(2)}) collective-permute-start(bf16[272,256]{1,0:T(8,128)(2,1)S(1)} %collective-permute-done.8.refs_3_), channel_id=1, source_target_pairs={{0,12},{4,0},{8,4},{12,8},{1,13},{5,1},{9,5},{13,9},{2,14},{6,2},{... | collective-permute-start | bytes 417800 | tf_op jit(solution)/shard_map/ppermute | solution.py:660
  25.8 1.8 %attend.7 = (f32[1024,128]{1,0:T(8,128)S(1)}, f32[1024,256]{1,0:T(8,128)S(1)}) custom-call(bf16[128,2048]{1,0:T(8,128)(2,1)S(1)} %choose_queries.1.refs_0_, bf16[272,256]{1,0:T(8,128)(2,1)S(1)} %collective-permute-done.refs_1_, bf16[272,256]{1,0:T(8,128)(2,1)S(1)} %collective-permute-done.4.refs_2_, bf16[272,256]{1,0:T(8,128)(2,1)S(1)} %collective-permute-done.1.refs_3_, ...), custom_call_target="tpu_custom_call" | custom-call | flops 805306368 | bytes 4194304 | tf_op jit(solution)/shard_map/attend/pallas_call | solution.py:400
  27.7 1.8 %attend.9 = (f32[1024,128]{1,0:T(8,128)S(1)}, f32[1024,256]{1,0:T(8,128)S(1)}) custom-call(bf16[128,2048]{1,0:T(8,128)(2,1)S(1)} %choose_queries.1.refs_0_, bf16[272,256]{1,0:T(8,128)(2,1)S(1)} %collective-permute-done.7.refs_1_, bf16[272,256]{1,0:T(8,128)(2,1)S(1)} %collective-permute-done.11.refs_2_, bf16[272,256]{1,0:T(8,128)(2,1)S(1)} %collective-permute-done.8.refs_3_, ...), custom_call_target="tpu_custom_call" | custom-call | flops 805306368 | bytes 4194304 | tf_op jit(solution)/shard_map/attend/pallas_call | solution.py:400
  32.6 1.8 %collective-permute-start.16 = (bf16[64,128]{1,0:T(8,128)(2,1)S(1)}, bf16[64,128]{1,0:T(8,128)(2,1)S(1)}, u32[]{:S(2)}, u32[]{:S(2)}) collective-permute-start(bf16[64,128]{1,0:T(8,128)(2,1)S(1)} %pad_maximum_fusion.own_ref), channel_id=1, source_target_pairs={{0,2},{2,0},{1,3},{3,1},{4,6},{6,4},{5,7},{7,5},{8,10},{10,8},{9,1... | collective-permute-start | bytes 49160 | tf_op jit(solution)/shard_map/ppermute | solution.py:696
  34.4 1.7 %attend.10.refs_7_ = f32[128,2048]{1,0:T(8,128)S(1)} custom-call(bf16[128,2048]{1,0:T(8,128)(2,1)S(1)} %choose_queries.1.refs_0_, bf16[272,256]{1,0:T(8,128)(2,1)S(1)} %collective-permute-done.3.refs_1_, bf16[272,256]{1,0:T(8,128)(2,1)S(1)} %collective-permute-done.6.refs_2_, f32[1024,128]{1,0:T(8,128)S(1)} %get-tuple-element.116.refs_3_, ...), custom_call_target="tpu_custom_call" | custom-call | flops 402653184 | bytes 4194304 | tf_op jit(solution)/shard_map/attend/pallas_call | solution.py:400
  36.0 1.6 %attend.11 = (f32[32,2048]{1,0:T(8,128)S(1)}, f32[32,2048]{1,0:T(8,128)S(1)}, bf16[32,2048]{1,0:T(8,128)(2,1)S(1)}, bf16[32,2048]{1,0:T(8,128)(2,1)S(1)}) custom-call(bf16[128,2048]{1,0:T(8,128)(2,1)S(1)} %choose_queries.1.refs_0_, bf16[272,256]{1,0:T(8,128)(2,1)S(1)} %collective-permute-done.10.refs_1_, ...), custom_call_target="tpu_custom_call" | custom-call | flops 402653184 | bytes 4194304 | tf_op jit(solution)/shard_map/attend/pallas_call | solution.py:400
  38.2 1.8 %collective-permute-start.18 = (bf16[32,2048]{1,0:T(8,128)(2,1)S(1)}, bf16[32,2048]{1,0:T(8,128)(2,1)S(1)}, u32[]{:S(2)}, u32[]{:S(2)}) collective-permute-start(bf16[32,2048]{1,0:T(8,128)(2,1)S(1)} %get-tuple-element.126), channel_id=1, source_target_pairs={{0,2},{2,0},{1,3},{3,1},{4,6},{6,4},{5,7},{7,5},{8,10},{10,8},{9,1... | collective-permute-start | bytes 393224 | tf_op jit(solution)/shard_map/ppermute | solution.py:693
  40.1 4.0 %collective-permute-done.15.refs_1_ = bf16[32,2048]{1,0:T(8,128)(2,1)S(1)} collective-permute-done((bf16[32,2048]{1,0:T(8,128)(2,1)S(1)}, bf16[32,2048]{1,0:T(8,128)(2,1)S(1)}, u32[]{:S(2)}, u32[]{:S(2)}) %collective-permute-start.15) | collective-permute-done | bytes 131104 | tf_op jit(solution)/shard_map/ppermute | solution.py:693
  44.4 1.5 %collective-permute-done.18.refs_1_ = bf16[32,2048]{1,0:T(8,128)(2,1)S(1)} collective-permute-done((bf16[32,2048]{1,0:T(8,128)(2,1)S(1)}, bf16[32,2048]{1,0:T(8,128)(2,1)S(1)}, u32[]{:S(2)}, u32[]{:S(2)}) %collective-permute-start.18) | collective-permute-done | bytes 131104 | tf_op jit(solution)/shard_map/ppermute | solution.py:693
  46.3 1.5 %collective-permute-start.26 = (bf16[32,2048]{1,0:T(8,128)(2,1)S(1)}, bf16[32,2048]{1,0:T(8,128)(2,1)S(1)}, u32[]{:S(2)}, u32[]{:S(2)}) collective-permute-start(bf16[32,2048]{1,0:T(8,128)(2,1)S(1)} %get-tuple-element.152.refs_1_), channel_id=1, source_target_pairs={{0,5},{1,4},{4,9},{5,8},{8,13},{9,12},{12,15},{13,14},{14,11},{15,... | collective-permute-start | bytes 393224 | tf_op jit(solution)/shard_map/ppermute | solution.py:502
  48.7 1.7 %collective-permute-start.20 = (bf16[32,2048]{1,0:T(8,128)(2,1)S(1)}, bf16[32,2048]{1,0:T(8,128)(2,1)S(1)}, u32[]{:S(2)}, u32[]{:S(2)}) collective-permute-start(bf16[32,2048]{1,0:T(8,128)(2,1)S(1)} %collective-permute-done.19.refs_0_), channel_id=1, source_target_pairs={{0,5},{1,4},{4,9},{5,8},{8,13},{9,12},{12,15},{13,14},{14,11},{15,... | collective-permute-start | bytes 393224 | tf_op jit(solution)/shard_map/ppermute | solution.py:499
  50.4 1.3 %collective-permute-done.23.refs_1_ = bf16[32,2048]{1,0:T(8,128)(2,1)S(1)} collective-permute-done((bf16[32,2048]{1,0:T(8,128)(2,1)S(1)}, bf16[32,2048]{1,0:T(8,128)(2,1)S(1)}, u32[]{:S(2)}, u32[]{:S(2)}) %collective-permute-start.23) | collective-permute-done | bytes 131104 | tf_op jit(solution)/shard_map/ppermute | solution.py:500
  54.9 1.6 %collective-permute-start.21 = (bf16[32,2048]{1,0:T(8,128)(2,1)S(1)}, bf16[32,2048]{1,0:T(8,128)(2,1)S(1)}, u32[]{:S(2)}, u32[]{:S(2)}) collective-permute-start(bf16[32,2048]{1,0:T(8,128)(2,1)S(1)} %collective-permute-done.20.refs_0_), channel_id=1, source_target_pairs={{0,5},{1,4},{4,9},{5,8},{8,13},{9,12},{12,15},{13,14},{14,11},{15,... | collective-permute-start | bytes 393224 | tf_op jit(solution)/shard_map/ppermute | solution.py:499
  57.7 1.6 %apply_expert.5 = (f32[32,2048]{1,0:T(8,128)S(1)}, f32[32,2048]{1,0:T(8,128)S(1)}, f32[32,2048]{1,0:T(8,128)S(1)}, f32[32,2048]{1,0:T(8,128)S(1)}) custom-call(bf16[32,2048]{1,0:T(8,128)(2,1)S(1)} %collective-permute-done.19.refs_0_, bf16[32,2048]{1,0:T(8,128)(2,1)S(1)} %collective-permute-done.23.refs_1_, ...), custom_call_target="tpu_custom_call" | custom-call | flops 603979776 | bytes 6291456 | tf_op jit(solution)/shard_map/apply_expert/pallas_call | solution.py:455
  63.3 1.6 %apply_expert.6 = (f32[32,2048]{1,0:T(8,128)S(1)}, f32[32,2048]{1,0:T(8,128)S(1)}, f32[32,2048]{1,0:T(8,128)S(1)}, f32[32,2048]{1,0:T(8,128)S(1)}) custom-call(bf16[32,2048]{1,0:T(8,128)(2,1)S(1)} %collective-permute-done.20.refs_0_, bf16[32,2048]{1,0:T(8,128)(2,1)S(1)} %collective-permute-done.24.refs_1_, ...), custom_call_target="tpu_custom_call" | custom-call | flops 603979776 | bytes 6291456 | tf_op jit(solution)/shard_map/apply_expert/pallas_call | solution.py:455
  66.1 1.6 %apply_expert.7 = (f32[32,2048]{1,0:T(8,128)S(1)}, f32[32,2048]{1,0:T(8,128)S(1)}, f32[32,2048]{1,0:T(8,128)S(1)}, f32[32,2048]{1,0:T(8,128)S(1)}) custom-call(bf16[32,2048]{1,0:T(8,128)(2,1)S(1)} %collective-permute-done.21.refs_0_, bf16[32,2048]{1,0:T(8,128)(2,1)S(1)} %collective-permute-done.25.refs_1_, ...), custom_call_target="tpu_custom_call" | custom-call | flops 603979776 | bytes 6291456 | tf_op jit(solution)/shard_map/apply_expert/pallas_call | solution.py:455
  68.6 1.5 %apply_expert.8 = (f32[32,2048]{1,0:T(8,128)S(1)}, f32[32,2048]{1,0:T(8,128)S(1)}) custom-call(bf16[32,2048]{1,0:T(8,128)(2,1)S(1)} %collective-permute-done.22.refs_0_, bf16[32,2048]{1,0:T(8,128)(2,1)S(1)} %collective-permute-done.34.refs_1_, f32[128,128]{1,0:T(8,128)S(1)} %gates_by_chip.1.refs_4_.refs_2_, bf16[2,192,2048]{2,1,0:T(8,128)(2,1)S(1)} %bitcast.9, ...), custom_call_target="tpu_custom_call" | custom-call | flops 301989888 | bytes 6291456 | tf_op jit(solution)/shard_map/apply_expert/pallas_call | solution.py:455
  70.2 1.8 %collective-permute-start.45 = (bf16[32,2048]{1,0:T(8,128)(2,1)S(1)}, bf16[32,2048]{1,0:T(8,128)(2,1)S(1)}, u32[]{:S(2)}, u32[]{:S(2)}) collective-permute-start(bf16[32,2048]{1,0:T(8,128)(2,1)S(1)} %convert_element_type.15), channel_id=1, source_target_pairs={{0,5},{1,4},{4,9},{5,8},{8,13},{9,12},{12,15},{13,14},{14,11},{15,... | collective-permute-start | bytes 393224 | tf_op jit(solution)/shard_map/ppermute | solution.py:527
  72.1 1.8 %collective-permute-start.42 = (bf16[32,2048]{1,0:T(8,128)(2,1)S(1)}, bf16[32,2048]{1,0:T(8,128)(2,1)S(1)}, u32[]{:S(2)}, u32[]{:S(2)}) collective-permute-start(bf16[32,2048]{1,0:T(8,128)(2,1)S(1)} %convert_element_type.14), channel_id=1, source_target_pairs={{0,5},{1,4},{4,9},{5,8},{8,13},{9,12},{12,15},{13,14},{14,11},{15,... | collective-permute-start | bytes 393224 | tf_op jit(solution)/shard_map/ppermute | solution.py:527
  73.9 2.1 %collective-permute-done.35.came_ref = bf16[32,2048]{1,0:T(8,128)(2,1)S(1)} collective-permute-done((bf16[32,2048]{1,0:T(8,128)(2,1)S(1)}, bf16[32,2048]{1,0:T(8,128)(2,1)S(1)}, u32[]{:S(2)}, u32[]{:S(2)}) %collective-permute-start.35) | collective-permute-done | bytes 131104 | tf_op jit(solution)/shard_map/ppermute | solution.py:527
  76.4 1.8 %collective-permute-start.46 = (bf16[32,2048]{1,0:T(8,128)(2,1)S(1)}, bf16[32,2048]{1,0:T(8,128)(2,1)S(1)}, u32[]{:S(2)}, u32[]{:S(2)}) collective-permute-start(bf16[32,2048]{1,0:T(8,128)(2,1)S(1)} %add_share.17), channel_id=1, source_target_pairs={{0,5},{1,4},{4,9},{5,8},{8,13},{9,12},{12,15},{13,14},{14,11},{15,... | collective-permute-start | bytes 393224 | tf_op jit(solution)/shard_map/ppermute | solution.py:527
  78.9 1.8 %collective-permute-start.43 = (bf16[32,2048]{1,0:T(8,128)(2,1)S(1)}, bf16[32,2048]{1,0:T(8,128)(2,1)S(1)}, u32[]{:S(2)}, u32[]{:S(2)}) collective-permute-start(bf16[32,2048]{1,0:T(8,128)(2,1)S(1)} %add_share.15), channel_id=1, source_target_pairs={{0,5},{1,4},{4,9},{5,8},{8,13},{9,12},{12,15},{13,14},{14,11},{15,... | collective-permute-start | bytes 393224 | tf_op jit(solution)/shard_map/ppermute | solution.py:527
  85.0 1.3 %collective-permute-start.44 = (bf16[32,2048]{1,0:T(8,128)(2,1)S(1)}, bf16[32,2048]{1,0:T(8,128)(2,1)S(1)}, u32[]{:S(2)}, u32[]{:S(2)}) collective-permute-start(bf16[32,2048]{1,0:T(8,128)(2,1)S(1)} %add_share.16), channel_id=1, source_target_pairs={{0,5},{1,4},{4,9},{5,8},{8,13},{9,12},{12,15},{13,14},{14,11},{15,... | collective-permute-start | bytes 393224 | tf_op jit(solution)/shard_map/ppermute | solution.py:527
  87.7 1.7 %collective-permute-start.48 = (bf16[32,2048]{1,0:T(8,128)(2,1)S(1)}, bf16[32,2048]{1,0:T(8,128)(2,1)S(1)}, u32[]{:S(2)}, u32[]{:S(2)}) collective-permute-start(bf16[32,2048]{1,0:T(8,128)(2,1)S(1)} %add_share.19), channel_id=1, source_target_pairs={{0,5},{1,4},{4,9},{5,8},{8,13},{9,12},{12,15},{13,14},{14,11},{15,... | collective-permute-start | bytes 393224 | tf_op jit(solution)/shard_map/ppermute | solution.py:527
  89.4 1.5 %apply_expert.9 = (f32[32,2048]{1,0:T(8,128)S(1)}, f32[32,2048]{1,0:T(8,128)S(1)}) custom-call(bf16[32,2048]{1,0:T(8,128)(2,1)S(1)} %get-tuple-element.151.refs_0_, bf16[32,2048]{1,0:T(8,128)(2,1)S(1)} %get-tuple-element.152.refs_1_, f32[128,128]{1,0:T(8,128)S(1)} %gates_by_chip.1.refs_4_.refs_2_, bf16[2,192,2048]{2,1,0:T(8,128)(2,1)S(1)} %bitcast.10, ...), custom_call_target="tpu_custom_call" | custom-call | flops 301989888 | bytes 6291456 | tf_op jit(solution)/shard_map/apply_expert/pallas_call | solution.py:455
  90.9 1.6 %collective-permute-done.38.refs_4_ = bf16[32,2048]{1,0:T(8,128)(2,1)S(1)} collective-permute-done((bf16[32,2048]{1,0:T(8,128)(2,1)S(1)}, bf16[32,2048]{1,0:T(8,128)(2,1)S(1)}, u32[]{:S(2)}, u32[]{:S(2)}) %collective-permute-start.38) | collective-permute-done | bytes 131104 | tf_op jit(solution)/shard_map/ppermute | solution.py:527
  (123 shorter events, 33.1 us)
Async XLA Ops:
  2.5 31.8 %collective-permute-start.14 = (bf16[2048,1024]{1,0:T(8,128)(2,1)}, bf16[2048,1024]{1,0:T(8,128)(2,1)S(1)}, u32[]{:S(2)}, u32[]{:S(2)}) collective-permute-start(bf16[2048,1024]{1,0:T(8,128)(2,1)} %refs_5_.1), channel_id=1, source_target_pairs={{0,1},{1,0},{2,3},{3,2},{4,5},{5,4},{6,7},{7,6},{8,9},{9,8},{10,11... | collective-permute-start | bytes 12582920 | tf_op jit(solution)/shard_map/ppermute | solution.py:34
  3.0 7.2 %collective-permute-start.2 = (bf16[272,256]{1,0:T(8,128)(2,1)}, bf16[272,256]{1,0:T(8,128)(2,1)S(1)}, u32[]{:S(2)}, u32[]{:S(2)}) collective-permute-start(bf16[272,256]{1,0:T(8,128)(2,1)} %get-tuple-element.87.refs_1_), channel_id=1, source_target_pairs={{0,1},{1,0},{2,3},{3,2},{4,5},{5,4},{6,7},{7,6},{8,9},{9,8},{10,11... | collective-permute-start | bytes 417800 | tf_op jit(solution)/shard_map/ppermute | solution.py:34
  3.0 12.0 %collective-permute-start = (bf16[272,256]{1,0:T(8,128)(2,1)}, bf16[272,256]{1,0:T(8,128)(2,1)S(1)}, u32[]{:S(2)}, u32[]{:S(2)}) collective-permute-start(bf16[272,256]{1,0:T(8,128)(2,1)} %get-tuple-element.87.refs_1_), channel_id=1, source_target_pairs={{0,4},{4,8},{8,12},{12,0},{1,5},{5,9},{9,13},{13,1},{2,6},{6,10},{... | collective-permute-start | bytes 417800 | tf_op jit(solution)/shard_map/ppermute | solution.py:657
  6.1 11.0 %collective-permute-start.1 = (bf16[272,256]{1,0:T(8,128)(2,1)}, bf16[272,256]{1,0:T(8,128)(2,1)S(1)}, u32[]{:S(2)}, u32[]{:S(2)}) collective-permute-start(bf16[272,256]{1,0:T(8,128)(2,1)} %get-tuple-element.87.refs_1_), channel_id=1, source_target_pairs={{0,12},{4,0},{8,4},{12,8},{1,13},{5,1},{9,5},{13,9},{2,14},{6,2},{... | collective-permute-start | bytes 417800 | tf_op jit(solution)/shard_map/ppermute | solution.py:660
  8.1 9.0 %collective-permute-start.9 = (bf16[272,256]{1,0:T(8,128)(2,1)}, bf16[272,256]{1,0:T(8,128)(2,1)S(1)}, u32[]{:S(2)}, u32[]{:S(2)}) collective-permute-start(bf16[272,256]{1,0:T(8,128)(2,1)} %get-tuple-element.99.refs_1_), channel_id=1, source_target_pairs={{0,1},{1,0},{2,3},{3,2},{4,5},{5,4},{6,7},{7,6},{8,9},{9,8},{10,11... | collective-permute-start | bytes 417800 | tf_op jit(solution)/shard_map/ppermute | solution.py:34
  10.2 9.3 %collective-permute-start.7 = (bf16[272,256]{1,0:T(8,128)(2,1)}, bf16[272,256]{1,0:T(8,128)(2,1)S(1)}, u32[]{:S(2)}, u32[]{:S(2)}) collective-permute-start(bf16[272,256]{1,0:T(8,128)(2,1)} %get-tuple-element.99.refs_1_), channel_id=1, source_target_pairs={{0,4},{4,8},{8,12},{12,0},{1,5},{5,9},{9,13},{13,1},{2,6},{6,10},{... | collective-permute-start | bytes 417800 | tf_op jit(solution)/shard_map/ppermute | solution.py:657
  15.0 7.3 %collective-permute-start.8 = (bf16[272,256]{1,0:T(8,128)(2,1)}, bf16[272,256]{1,0:T(8,128)(2,1)S(1)}, u32[]{:S(2)}, u32[]{:S(2)}) collective-permute-start(bf16[272,256]{1,0:T(8,128)(2,1)} %get-tuple-element.99.refs_1_), channel_id=1, source_target_pairs={{0,12},{4,0},{8,4},{12,8},{1,13},{5,1},{9,5},{13,9},{2,14},{6,2},{... | collective-permute-start | bytes 417800 | tf_op jit(solution)/shard_map/ppermute | solution.py:660
  19.5 8.1 %collective-permute-start.3 = (bf16[272,256]{1,0:T(8,128)(2,1)S(1)}, bf16[272,256]{1,0:T(8,128)(2,1)S(1)}, u32[]{:S(2)}, u32[]{:S(2)}) collective-permute-start(bf16[272,256]{1,0:T(8,128)(2,1)S(1)} %collective-permute-done.refs_1_), channel_id=1, source_target_pairs={{0,4},{4,8},{8,12},{12,0},{1,5},{5,9},{9,13},{13,1},{2,6},{6,10},{... | collective-permute-start | bytes 417800 | tf_op jit(solution)/shard_map/ppermute | solution.py:657
  22.8 7.2 %collective-permute-start.10 = (bf16[272,256]{1,0:T(8,128)(2,1)S(1)}, bf16[272,256]{1,0:T(8,128)(2,1)S(1)}, u32[]{:S(2)}, u32[]{:S(2)}) collective-permute-start(bf16[272,256]{1,0:T(8,128)(2,1)S(1)} %collective-permute-done.8.refs_3_), channel_id=1, source_target_pairs={{0,12},{4,0},{8,4},{12,8},{1,13},{5,1},{9,5},{13,9},{2,14},{6,2},{... | collective-permute-start | bytes 417800 | tf_op jit(solution)/shard_map/ppermute | solution.py:660
  31.4 26.4 %collective-permute-start.29 = (bf16[2,192,2048]{2,1,0:T(8,128)(2,1)S(1)}, bf16[2,192,2048]{2,1,0:T(8,128)(2,1)S(1)}, u32[]{:S(2)}, u32[]{:S(2)}) collective-permute-start(bf16[2,192,2048]{2,1,0:T(8,128)(2,1)S(1)} %bitcast.5), channel_id=1, source_target_pairs={{0,1},{1,0},{2,3},{3,2},{4,5},{5,4},{6,7},{7,6},{8,9},{9,8},{10,11... | collective-permute-start | bytes 4718600 | tf_op jit(solution)/shard_map/ppermute | solution.py:34
  31.5 16.3 %collective-permute-start.30 = (bf16[192,2048]{1,0:T(8,128)(2,1)S(1)}, bf16[192,2048]{1,0:T(8,128)(2,1)S(1)}, u32[]{:S(2)}, u32[]{:S(2)}) collective-permute-start(bf16[192,2048]{1,0:T(8,128)(2,1)S(1)} %bitcast.11), channel_id=1, source_target_pairs={{0,1},{1,0},{2,3},{3,2},{4,5},{5,4},{6,7},{7,6},{8,9},{9,8},{10,11... | collective-permute-start | bytes 2359304 | tf_op jit(solution)/shard_map/ppermute | solution.py:34
  37.7 6.4 %collective-permute-start.15 = (bf16[32,2048]{1,0:T(8,128)(2,1)S(1)}, bf16[32,2048]{1,0:T(8,128)(2,1)S(1)}, u32[]{:S(2)}, u32[]{:S(2)}) collective-permute-start(bf16[32,2048]{1,0:T(8,128)(2,1)S(1)} %get-tuple-element.119), channel_id=1, source_target_pairs={{0,2},{2,0},{1,3},{3,1},{4,6},{6,4},{5,7},{7,5},{8,10},{10,8},{9,1... | collective-permute-start | bytes 393224 | tf_op jit(solution)/shard_map/ppermute | solution.py:693
  38.1 6.0 %collective-permute-start.17 = (bf16[64,1024]{1,0:T(8,128)(2,1)S(1)}, bf16[64,1024]{1,0:T(8,128)(2,1)S(1)}, u32[]{:S(2)}, u32[]{:S(2)}) collective-permute-start(bf16[64,1024]{1,0:T(8,128)(2,1)S(1)} %get-tuple-element.123), channel_id=1, source_target_pairs={{0,1},{1,0},{2,3},{3,2},{4,5},{5,4},{6,7},{7,6},{8,9},{9,8},{10,11... | collective-permute-start | bytes 393224 | tf_op jit(solution)/shard_map/ppermute | solution.py:115
  38.2 7.7 %collective-permute-start.18 = (bf16[32,2048]{1,0:T(8,128)(2,1)S(1)}, bf16[32,2048]{1,0:T(8,128)(2,1)S(1)}, u32[]{:S(2)}, u32[]{:S(2)}) collective-permute-start(bf16[32,2048]{1,0:T(8,128)(2,1)S(1)} %get-tuple-element.126), channel_id=1, source_target_pairs={{0,2},{2,0},{1,3},{3,1},{4,6},{6,4},{5,7},{7,5},{8,10},{10,8},{9,1... | collective-permute-start | bytes 393224 | tf_op jit(solution)/shard_map/ppermute | solution.py:693
  46.0 5.8 %collective-permute-start.23 = (bf16[32,2048]{1,0:T(8,128)(2,1)S(1)}, bf16[32,2048]{1,0:T(8,128)(2,1)S(1)}, u32[]{:S(2)}, u32[]{:S(2)}) collective-permute-start(bf16[32,2048]{1,0:T(8,128)(2,1)S(1)} %get-tuple-element.152.refs_1_), channel_id=1, source_target_pairs={{5,0},{4,1},{9,4},{8,5},{13,8},{12,9},{15,12},{14,13},{11,14},{10,... | collective-permute-start | bytes 393224 | tf_op jit(solution)/shard_map/ppermute | solution.py:500
  46.3 6.0 %collective-permute-start.26 = (bf16[32,2048]{1,0:T(8,128)(2,1)S(1)}, bf16[32,2048]{1,0:T(8,128)(2,1)S(1)}, u32[]{:S(2)}, u32[]{:S(2)}) collective-permute-start(bf16[32,2048]{1,0:T(8,128)(2,1)S(1)} %get-tuple-element.152.refs_1_), channel_id=1, source_target_pairs={{0,5},{1,4},{4,9},{5,8},{8,13},{9,12},{12,15},{13,14},{14,11},{15,... | collective-permute-start | bytes 393224 | tf_op jit(solution)/shard_map/ppermute | solution.py:502
  47.8 6.2 %collective-permute-start.28 = (bf16[32,2048]{1,0:T(8,128)(2,1)S(1)}, bf16[32,2048]{1,0:T(8,128)(2,1)S(1)}, u32[]{:S(2)}, u32[]{:S(2)}) collective-permute-start(bf16[32,2048]{1,0:T(8,128)(2,1)S(1)} %get-tuple-element.151.refs_0_), channel_id=1, source_target_pairs={{5,0},{4,1},{9,4},{8,5},{13,8},{12,9},{15,12},{14,13},{11,14},{10,... | collective-permute-start | bytes 393224 | tf_op jit(solution)/shard_map/ppermute | solution.py:503
  48.7 6.2 %collective-permute-start.20 = (bf16[32,2048]{1,0:T(8,128)(2,1)S(1)}, bf16[32,2048]{1,0:T(8,128)(2,1)S(1)}, u32[]{:S(2)}, u32[]{:S(2)}) collective-permute-start(bf16[32,2048]{1,0:T(8,128)(2,1)S(1)} %collective-permute-done.19.refs_0_), channel_id=1, source_target_pairs={{0,5},{1,4},{4,9},{5,8},{8,13},{9,12},{12,15},{13,14},{14,11},{15,... | collective-permute-start | bytes 393224 | tf_op jit(solution)/shard_map/ppermute | solution.py:499
  52.4 7.0 %collective-permute-start.27 = (bf16[32,2048]{1,0:T(8,128)(2,1)S(1)}, bf16[32,2048]{1,0:T(8,128)(2,1)S(1)}, u32[]{:S(2)}, u32[]{:S(2)}) collective-permute-start(bf16[32,2048]{1,0:T(8,128)(2,1)S(1)} %collective-permute-done.26.refs_2_), channel_id=1, source_target_pairs={{0,5},{1,4},{4,9},{5,8},{8,13},{9,12},{12,15},{13,14},{14,11},{15,... | collective-permute-start | bytes 393224 | tf_op jit(solution)/shard_map/ppermute | solution.py:502
  54.0 6.2 %collective-permute-start.32 = (bf16[32,2048]{1,0:T(8,128)(2,1)S(1)}, bf16[32,2048]{1,0:T(8,128)(2,1)S(1)}, u32[]{:S(2)}, u32[]{:S(2)}) collective-permute-start(bf16[32,2048]{1,0:T(8,128)(2,1)S(1)} %collective-permute-done.28.refs_3_), channel_id=1, source_target_pairs={{5,0},{4,1},{9,4},{8,5},{13,8},{12,9},{15,12},{14,13},{11,14},{10,... | collective-permute-start | bytes 393224 | tf_op jit(solution)/shard_map/ppermute | solution.py:503
  54.9 6.2 %collective-permute-start.21 = (bf16[32,2048]{1,0:T(8,128)(2,1)S(1)}, bf16[32,2048]{1,0:T(8,128)(2,1)S(1)}, u32[]{:S(2)}, u32[]{:S(2)}) collective-permute-start(bf16[32,2048]{1,0:T(8,128)(2,1)S(1)} %collective-permute-done.20.refs_0_), channel_id=1, source_target_pairs={{0,5},{1,4},{4,9},{5,8},{8,13},{9,12},{12,15},{13,14},{14,11},{15,... | collective-permute-start | bytes 393224 | tf_op jit(solution)/shard_map/ppermute | solution.py:499
  60.3 5.8 %collective-permute-start.33 = (bf16[32,2048]{1,0:T(8,128)(2,1)S(1)}, bf16[32,2048]{1,0:T(8,128)(2,1)S(1)}, u32[]{:S(2)}, u32[]{:S(2)}) collective-permute-start(bf16[32,2048]{1,0:T(8,128)(2,1)S(1)} %collective-permute-done.32.refs_3_), channel_id=1, source_target_pairs={{5,0},{4,1},{9,4},{8,5},{13,8},{12,9},{15,12},{14,13},{11,14},{10,... | collective-permute-start | bytes 393224 | tf_op jit(solution)/shard_map/ppermute | solution.py:503
  61.1 6.5 %collective-permute-start.22 = (bf16[32,2048]{1,0:T(8,128)(2,1)S(1)}, bf16[32,2048]{1,0:T(8,128)(2,1)S(1)}, u32[]{:S(2)}, u32[]{:S(2)}) collective-permute-start(bf16[32,2048]{1,0:T(8,128)(2,1)S(1)} %collective-permute-done.21.refs_0_), channel_id=1, source_target_pairs={{0,5},{1,4},{4,9},{5,8},{8,13},{9,12},{12,15},{13,14},{14,11},{15,... | collective-permute-start | bytes 393224 | tf_op jit(solution)/shard_map/ppermute | solution.py:499
  62.5 6.1 %collective-permute-start.34 = (bf16[32,2048]{1,0:T(8,128)(2,1)S(1)}, bf16[32,2048]{1,0:T(8,128)(2,1)S(1)}, u32[]{:S(2)}, u32[]{:S(2)}) collective-permute-start(bf16[32,2048]{1,0:T(8,128)(2,1)S(1)} %collective-permute-done.25.refs_1_), channel_id=1, source_target_pairs={{5,0},{4,1},{9,4},{8,5},{13,8},{12,9},{15,12},{14,13},{11,14},{10,... | collective-permute-start | bytes 393224 | tf_op jit(solution)/shard_map/ppermute | solution.py:500
  70.2 5.8 %collective-permute-start.35 = (bf16[32,2048]{1,0:T(8,128)(2,1)S(1)}, bf16[32,2048]{1,0:T(8,128)(2,1)S(1)}, u32[]{:S(2)}, u32[]{:S(2)}) collective-permute-start(bf16[32,2048]{1,0:T(8,128)(2,1)S(1)} %convert_element_type.12), channel_id=1, source_target_pairs={{5,0},{4,1},{9,4},{8,5},{13,8},{12,9},{15,12},{14,13},{11,14},{10,... | collective-permute-start | bytes 393224 | tf_op jit(solution)/shard_map/ppermute | solution.py:527
  70.2 6.1 %collective-permute-start.45 = (bf16[32,2048]{1,0:T(8,128)(2,1)S(1)}, bf16[32,2048]{1,0:T(8,128)(2,1)S(1)}, u32[]{:S(2)}, u32[]{:S(2)}) collective-permute-start(bf16[32,2048]{1,0:T(8,128)(2,1)S(1)} %convert_element_type.15), channel_id=1, source_target_pairs={{0,5},{1,4},{4,9},{5,8},{8,13},{9,12},{12,15},{13,14},{14,11},{15,... | collective-permute-start | bytes 393224 | tf_op jit(solution)/shard_map/ppermute | solution.py:527
  72.0 6.8 %collective-permute-start.39 = (bf16[32,2048]{1,0:T(8,128)(2,1)S(1)}, bf16[32,2048]{1,0:T(8,128)(2,1)S(1)}, u32[]{:S(2)}, u32[]{:S(2)}) collective-permute-start(bf16[32,2048]{1,0:T(8,128)(2,1)S(1)} %convert_element_type.13), channel_id=1, source_target_pairs={{5,0},{4,1},{9,4},{8,5},{13,8},{12,9},{15,12},{14,13},{11,14},{10,... | collective-permute-start | bytes 393224 | tf_op jit(solution)/shard_map/ppermute | solution.py:527
  72.1 6.8 %collective-permute-start.42 = (bf16[32,2048]{1,0:T(8,128)(2,1)S(1)}, bf16[32,2048]{1,0:T(8,128)(2,1)S(1)}, u32[]{:S(2)}, u32[]{:S(2)}) collective-permute-start(bf16[32,2048]{1,0:T(8,128)(2,1)S(1)} %convert_element_type.14), channel_id=1, source_target_pairs={{0,5},{1,4},{4,9},{5,8},{8,13},{9,12},{12,15},{13,14},{14,11},{15,... | collective-permute-start | bytes 393224 | tf_op jit(solution)/shard_map/ppermute | solution.py:527
  76.4 5.8 %collective-permute-start.46 = (bf16[32,2048]{1,0:T(8,128)(2,1)S(1)}, bf16[32,2048]{1,0:T(8,128)(2,1)S(1)}, u32[]{:S(2)}, u32[]{:S(2)}) collective-permute-start(bf16[32,2048]{1,0:T(8,128)(2,1)S(1)} %add_share.17), channel_id=1, source_target_pairs={{0,5},{1,4},{4,9},{5,8},{8,13},{9,12},{12,15},{13,14},{14,11},{15,... | collective-permute-start | bytes 393224 | tf_op jit(solution)/shard_map/ppermute | solution.py:527
  78.9 6.0 %collective-permute-start.43 = (bf16[32,2048]{1,0:T(8,128)(2,1)S(1)}, bf16[32,2048]{1,0:T(8,128)(2,1)S(1)}, u32[]{:S(2)}, u32[]{:S(2)}) collective-permute-start(bf16[32,2048]{1,0:T(8,128)(2,1)S(1)} %add_share.15), channel_id=1, source_target_pairs={{0,5},{1,4},{4,9},{5,8},{8,13},{9,12},{12,15},{13,14},{14,11},{15,... | collective-permute-start | bytes 393224 | tf_op jit(solution)/shard_map/ppermute | solution.py:527
  84.4 6.5 %collective-permute-start.41 = (bf16[32,2048]{1,0:T(8,128)(2,1)S(1)}, bf16[32,2048]{1,0:T(8,128)(2,1)S(1)}, u32[]{:S(2)}, u32[]{:S(2)}) collective-permute-start(bf16[32,2048]{1,0:T(8,128)(2,1)S(1)} %add_share.14), channel_id=1, source_target_pairs={{5,0},{4,1},{9,4},{8,5},{13,8},{12,9},{15,12},{14,13},{11,14},{10,... | collective-permute-start | bytes 393224 | tf_op jit(solution)/shard_map/ppermute | solution.py:527
  85.0 5.9 %collective-permute-start.44 = (bf16[32,2048]{1,0:T(8,128)(2,1)S(1)}, bf16[32,2048]{1,0:T(8,128)(2,1)S(1)}, u32[]{:S(2)}, u32[]{:S(2)}) collective-permute-start(bf16[32,2048]{1,0:T(8,128)(2,1)S(1)} %add_share.16), channel_id=1, source_target_pairs={{0,5},{1,4},{4,9},{5,8},{8,13},{9,12},{12,15},{13,14},{14,11},{15,... | collective-permute-start | bytes 393224 | tf_op jit(solution)/shard_map/ppermute | solution.py:527
  (26 other events, 164.2 us)

commit v9 on v8

--- a/solution.py
+++ b/solution.py
@@ -15,6 +15,7 @@
 NEG_FILL = -1e30
 EPSILON = 1e-06
 MASK_ROWS = 16
+TABLE_ROWS = 8
 LANES = 128
 MIB = 1024 * 1024
 CONTRACT_LAST = (((1,), (1,)), ((), ()))
@@ -166,16 +167,19 @@
 
 def gates_by_chip(own, came, n_ep, n_hd):
     block_rows = own.shape[1]
+    places = slice(came.shape[1] - block_rows, came.shape[1])
 
     def kernel(own_ref, came_ref, out_ref):
         ep, hd = lax.axis_index("ep"), lax.axis_index("hd")
         mine = ep * n_hd + hd
-        expert = lax.broadcasted_iota(jnp.int32, (MASK_ROWS, block_rows), 0)
+        expert = lax.broadcasted_iota(jnp.int32, (TABLE_ROWS, block_rows), 0)
         place = lax.broadcasted_iota(jnp.int32, (LANES, block_rows), 0)
         table = jnp.zeros((LANES, block_rows), jnp.float32)
-        for ref, other in ((own_ref, hd), (came_ref, 1 - hd)):
+        tables = [(own_ref[...], hd), (came_ref[: n_ep * TABLE_ROWS, places], 1 - hd)]
+        for joint, other in tables:
+            joint = joint.astype(jnp.float32)
             for hop in range(n_ep):
-                tile = ref[hop * MASK_ROWS : (hop + 1) * MASK_ROWS, :].astype(jnp.float32)
+                tile = joint[hop * TABLE_ROWS : (hop + 1) * TABLE_ROWS, :]
                 row = jnp.sum(jnp.where(expert == mine, tile, 0.0), axis=0, keepdims=True)
                 chip = walk_place((ep - hop) % n_ep, other, n_ep, n_hd)
                 table = jnp.where(place == chip, row, table)
@@ -272,7 +276,7 @@
     factor = math.log2(math.e) / math.sqrt(HD)
     relative = n_hd == 2
     last = finish is not None
-    weights, earlier = finish if last else ([], None)
+    weights, earlier, tables = finish if last else ([], None, [])
     head_columns = per_kv * HD
     final = last and kv == kv_heads - 1
     kept_rows = rows if relative else 0
@@ -284,12 +288,26 @@
         if state is not None:
             (m_in, acc_in), refs = refs[:2], refs[2:]
         weight_refs, refs = refs[: len(weights)], refs[len(weights) :]
+        table_refs, refs = refs[: len(tables)], refs[len(tables) :]
         if earlier is not None:
             earlier_ref, refs = refs[0], refs[1:]
         if last:
             results = len(out_shape)
             result_refs, refs = refs[:results], refs[results:]
             head_ref, refs = refs[0], refs[1:]
+            copies = []
+            if tables:
+                result_refs, own_table_ref = result_refs[:-1], result_refs[-1]
+                held_ref, sems = refs
+                for i, table_ref in enumerate(table_refs):
+                    copies.append(
+                        pltpu.make_async_copy(
+                            table_ref.at[pl.ds(keys, MASK_ROWS), pl.ds(HD, HD)],
+                            held_ref.at[pl.ds(i * MASK_ROWS, MASK_ROWS), :],
+                            sems.at[i],
+                        )
+                    )
+                    copies[-1].start()
         else:
             m_out, acc_out = refs
         sub = lax.axis_index("sub")
@@ -370,6 +388,20 @@
                         result_ref[:, here] = share.astype(result_ref.dtype)
                 else:
                     result_refs[0][:, here] = product
+            if tables:
+                for copy in copies:
+                    copy.wait()
+                joint = jnp.concatenate(
+                    [
+                        held_ref[i * MASK_ROWS : (i + 1) * MASK_ROWS, :].astype(jnp.float32)[
+                            :TABLE_ROWS
+                        ]
+                        for i in range(len(tables))
+                    ],
+                    axis=0,
+                ).astype(jnp.bfloat16)
+                own_table_ref[...] = joint
+                result_refs[len(result_refs) // 2][: joint.shape[0], features:] = joint
 
     vmem = pl.BlockSpec(memory_space=pltpu.VMEM)
     scratch = []
@@ -387,6 +419,15 @@
         else:
             out_shape = (jax.ShapeDtypeStruct((all_rows, features), jnp.float32),)
         scratch = [pltpu.VMEM((all_rows, head_columns), jnp.bfloat16)]
+        if tables:
+            joint = (len(tables) * TABLE_ROWS, LANES)
+            first = len(out_shape) // 2
+            out_shape[first] = jax.ShapeDtypeStruct((chunk_rows, features + LANES), jnp.bfloat16)
+            out_shape.append(jax.ShapeDtypeStruct(joint, jnp.bfloat16))
+            scratch += [
+                pltpu.VMEM((len(tables) * MASK_ROWS, LANES), jnp.bfloat16),
+                pltpu.SemaphoreType.DMA((len(tables),)),
+            ]
     else:
         out_shape = (
             jax.ShapeDtypeStruct((per_kv * all_rows, LANES), jnp.float32),
@@ -394,13 +435,16 @@
         )
     operands = [queries] + list(blocks) + (list(state) if state is not None else [])
     operands += list(weights)
+    in_specs = [vmem] * len(operands) + [pl.BlockSpec(memory_space=pl.ANY)] * len(tables)
+    operands += list(tables)
     if earlier is not None:
         operands.append(earlier)
+        in_specs.append(vmem)
     scores = all_rows * per_kv * keys * len(blocks)
     return pl.pallas_call(
         kernel,
         out_shape=out_shape,
-        in_specs=[vmem] * len(operands),
+        in_specs=in_specs,
         out_specs=tuple(vmem for _ in out_shape),
         scratch_shapes=scratch,
         compiler_params=pltpu.CompilerParams(vmem_limit_bytes=16 * MIB),
@@ -613,7 +657,9 @@
         and gate_up.shape[0] == 1
         and n_hd == 2
         and rows % 32 == 0
-        and all_experts <= MASK_ROWS
+        and all_experts <= TABLE_ROWS
+        and cache_rows <= HD
+        and n_ep * TABLE_ROWS <= rows // 2
         and expert_ids.shape[0] == LANES
     )
 
@@ -648,7 +694,7 @@
             gate_up_parts = sub_copies(gate_up[0])
             w_down_parts = sub_copies(w_down[0])
         for hop, x in arrived[0]:
-            tables[hop] = x[-MASK_ROWS:, HD:]
+            tables[hop] = x
         onward = [[] for _ in packed]
         if distance < reach:
             opposite = 2 * (distance + 1) == n_ep
@@ -660,7 +706,10 @@
                     down[kv] = lax.ppermute(down[kv], "ep", cycle(n_ep, n_ep - 1))
                     onward[kv].append((n_ep - distance - 1, down[kv]))
         for kv in range(kv_heads):
-            finish = (projections, earlier) if distance == reach else None
+            finish = None
+            if distance == reach:
+                joint = [tables[hop] for hop in range(n_ep)] if dense and kv == kv_heads - 1 else []
+                finish = (projections, earlier, joint)
             states[kv] = attend(
                 query_rows_here,
                 kv,
@@ -688,14 +737,13 @@
             residual_parts = hand_over(split_rows(residual, n_sub))
         arrived = onward
     parts = states[-1]
+    if dense:
+        *parts, own_table = parts
     if n_hd == 2:
         kept, sent = parts[: len(parts) // 2], parts[len(parts) // 2 :]
         came = [lax.ppermute(x, "hd", cycle(n_hd)) for x in sent]
         if dense:
-            own_tables = jnp.concatenate([tables[hop] for hop in range(n_ep)], axis=0)
-            other_tables = lax.ppermute(own_tables, "hd", cycle(n_hd))
-            gate_table = gates_by_chip(own_tables, other_tables, n_ep, n_hd)
-            came[0], gate_table = lax.optimization_barrier((came[0], gate_table))
+            gate_table = gates_by_chip(own_table, came[0], n_ep, n_hd)
     else:
         kept = [None]
         came = [lax.psum_scatter(parts[0], "hd", scatter_dimension=0, tiled=True)]

time: 95.7 us -> 95.2 us (level)
    ppermute x14, starting transfers between devices: 12.7 us -> 16.3 us  [dense_experts(): chunks[chunk] = lax.ppermute(sum_here, axes, way)]
    ppermute x14, waiting for transfers between devices: 8.37 us -> 6 us  [dense_experts(): chunks[chunk] = lax.ppermute(sum_here, axes, way)]
    ppermute x4, starting transfers between devices: 4.29 us -> 2.48 us  [dense_experts(): behind[0] = lax.ppermute(behind[0], axes, ahead)]
    ppermute x1 -> x0, starting transfers between devices: 1.77 us -> none  [shards(): other_tables = lax.ppermute(own_tables, 'hd', cycle(n_hd))]
    ppermute x4, waiting for transfers between devices: 3.06 us -> 4.17 us  [dense_experts(): before[1] = lax.ppermute(before[1], axes, back)]
    ppermute x2, waiting for transfers between devices: 1.03 us -> 1.99 us  [hand_over(): lax.ppermute(part, 'sub', cycle(size, step))]
    unnamed x16 -> x18, local copies, waits for them, and re-layouts: 3.07 us -> 3.07 us
  transfers between devices with their start and end apart: 50 -> 49, of which waited for: 24 -> 21; matrix products, arithmetic and copies ran while one was open for 1% -> 0% of each run, Pallas kernels for 17% -> 17%
where the time goes in v9:
time: 95.2 us; the launch traced here: 95 us
  starting transfers between devices  45.4 us (48%)
  waiting for transfers between devices  25.3 us (27%)
  Pallas kernels  20.2 us (21%)
  local copies, waits for them, and re-layouts  3.08 us (3%)
  between operations  1.03 us (1%)
    ppermute x14, starting transfers between devices, dense_experts(): chunks[chunk] = lax.ppermute(sum_here, axes, way)  16.3 us
    pallas_call x6, Pallas kernels, attend(): pl.pallas_call(kernel, out_shape=out_shape, in_specs=in_specs, out_specs=...  8.92 us
    pallas_call x5, Pallas kernels, apply_expert(): pl.pallas_call(kernel, out_shape=[jax.ShapeDtypeStruct((x.shape[0], featu...  7.75 us
    ppermute x3, starting transfers between devices, shards(): down[kv] = lax.ppermute(down[kv], 'ep', cycle(n_ep, n_ep - 1))  7.04 us
    ppermute x3, starting transfers between devices, shards(): up[kv] = lax.ppermute(up[kv], 'ep', cycle(n_ep))  6.03 us
    ppermute x14, waiting for transfers between devices, dense_experts(): chunks[chunk] = lax.ppermute(sum_here, axes, way)  6 us
    ppermute x2, waiting for transfers between devices, shards(): came = [lax.ppermute(x, 'hd', cycle(n_hd)) for x in sent]  5.14 us
    ppermute x4, waiting for transfers between devices, dense_experts(): before[1] = lax.ppermute(before[1], axes, back)  4.17 us
  transfers between devices with their start and end apart: 49, of which 21 were waited for; matrix products, arithmetic and copies ran while one was open for 0% of the time, Pallas kernels for 17%

profile of v9, /device:TPU:0, one launch (start us, length us, event | category | flops | bytes accessed | tf_op | source)
XLA Modules:
  0.0 95.0 jit_solution(10185329656981786292)
XLA Ops:
  0.7 1.9 %pack_keys.1 = (bf16[272,256]{1,0:T(8,128)(2,1)}, bf16[272,256]{1,0:T(8,128)(2,1)}) custom-call(s32[1]{0:T(128)S(6)} %copy.14.page_ref, bf16[128,512]{1,0:T(8,128)(2,1)} %ck_ref.1, bf16[128,512]{1,0:T(8,128)(2,1)} %cv_ref.1, bf16[128,512]{1,0:T(8,128)(2,1)} %nk_ref.1, bf16[128,512]{1,0:T(8,128)(2,1)} %nv_ref.1, s32[8,128]{1,0:T(8,128)} %bitcast.18, ...), custom_call_target="tpu_custom_call" | custom-call | tf_op jit(solution)/shard_map/pack_keys/pallas_call | solution.py:91
  3.0 3.0 %collective-permute-start = (bf16[272,256]{1,0:T(8,128)(2,1)}, bf16[272,256]{1,0:T(8,128)(2,1)S(1)}, u32[]{:S(2)}, u32[]{:S(2)}) collective-permute-start(bf16[272,256]{1,0:T(8,128)(2,1)} %get-tuple-element.86.refs_1_.refs_7_), channel_id=1, source_target_pairs={{0,4},{4,8},{8,12},{12,0},{1,5},{5,9},{9,13},{13,1},{2,6},{6,10},{... | collective-permute-start | bytes 417800 | tf_op jit(solution)/shard_map/ppermute | solution.py:703
  6.1 2.0 %collective-permute-start.1 = (bf16[272,256]{1,0:T(8,128)(2,1)}, bf16[272,256]{1,0:T(8,128)(2,1)S(1)}, u32[]{:S(2)}, u32[]{:S(2)}) collective-permute-start(bf16[272,256]{1,0:T(8,128)(2,1)} %get-tuple-element.86.refs_1_.refs_7_), channel_id=1, source_target_pairs={{0,12},{4,0},{8,4},{12,8},{1,13},{5,1},{9,5},{13,9},{2,14},{6,2},{... | collective-permute-start | bytes 417800 | tf_op jit(solution)/shard_map/ppermute | solution.py:706
  8.1 1.2 %copy-done.3 = bf16[256,2048]{1,0:T(8,128)(2,1)S(1)} copy-done((bf16[256,2048]{1,0:T(8,128)(2,1)S(1)}, bf16[256,2048]{1,0:T(8,128)(2,1)}, u32[]{:S(2)}) %copy-start.3) | copy-done | bytes 1048600
  10.2 2.9 %collective-permute-start.7 = (bf16[272,256]{1,0:T(8,128)(2,1)}, bf16[272,256]{1,0:T(8,128)(2,1)S(1)}, u32[]{:S(2)}, u32[]{:S(2)}) collective-permute-start(bf16[272,256]{1,0:T(8,128)(2,1)} %get-tuple-element.98.refs_1_), channel_id=1, source_target_pairs={{0,4},{4,8},{8,12},{12,0},{1,5},{5,9},{9,13},{13,1},{2,6},{6,10},{... | collective-permute-start | bytes 417800 | tf_op jit(solution)/shard_map/ppermute | solution.py:703
  15.0 2.1 %collective-permute-start.8 = (bf16[272,256]{1,0:T(8,128)(2,1)}, bf16[272,256]{1,0:T(8,128)(2,1)S(1)}, u32[]{:S(2)}, u32[]{:S(2)}) collective-permute-start(bf16[272,256]{1,0:T(8,128)(2,1)} %get-tuple-element.98.refs_1_), channel_id=1, source_target_pairs={{0,12},{4,0},{8,4},{12,8},{1,13},{5,1},{9,5},{13,9},{2,14},{6,2},{... | collective-permute-start | bytes 417800 | tf_op jit(solution)/shard_map/ppermute | solution.py:706
  19.6 2.7 %collective-permute-done.8.refs_3_ = bf16[272,256]{1,0:T(8,128)(2,1)S(1)} collective-permute-done((bf16[272,256]{1,0:T(8,128)(2,1)}, bf16[272,256]{1,0:T(8,128)(2,1)S(1)}, u32[]{:S(2)}, u32[]{:S(2)}) %collective-permute-start.8) | collective-permute-done | bytes 139296 | tf_op jit(solution)/shard_map/ppermute | solution.py:706
  22.8 2.9 %collective-permute-start.10 = (bf16[272,256]{1,0:T(8,128)(2,1)S(1)}, bf16[272,256]{1,0:T(8,128)(2,1)S(1)}, u32[]{:S(2)}, u32[]{:S(2)}) collective-permute-start(bf16[272,256]{1,0:T(8,128)(2,1)S(1)} %collective-permute-done.8.refs_3_), channel_id=1, source_target_pairs={{0,12},{4,0},{8,4},{12,8},{1,13},{5,1},{9,5},{13,9},{2,14},{6,2},{... | collective-permute-start | bytes 417800 | tf_op jit(solution)/shard_map/ppermute | solution.py:706
  25.8 1.8 %attend.7 = (f32[1024,128]{1,0:T(8,128)S(1)}, f32[1024,256]{1,0:T(8,128)S(1)}) custom-call(bf16[128,2048]{1,0:T(8,128)(2,1)S(1)} %choose_queries.1.refs_0_, bf16[272,256]{1,0:T(8,128)(2,1)S(1)} %collective-permute-done.refs_1_.refs_8_, bf16[272,256]{1,0:T(8,128)(2,1)S(1)} %collective-permute-done.4.refs_2_, ...), custom_call_target="tpu_custom_call" | custom-call | flops 805306368 | bytes 4194304 | tf_op jit(solution)/shard_map/attend/pallas_call | solution.py:444
  27.7 1.8 %attend.9 = (f32[1024,128]{1,0:T(8,128)S(1)}, f32[1024,256]{1,0:T(8,128)S(1)}) custom-call(bf16[128,2048]{1,0:T(8,128)(2,1)S(1)} %choose_queries.1.refs_0_, bf16[272,256]{1,0:T(8,128)(2,1)S(1)} %collective-permute-done.7.refs_1_, bf16[272,256]{1,0:T(8,128)(2,1)S(1)} %collective-permute-done.11.refs_2_, bf16[272,256]{1,0:T(8,128)(2,1)S(1)} %collective-permute-done.8.refs_3_, ...), custom_call_target="tpu_custom_call" | custom-call | flops 805306368 | bytes 4194304 | tf_op jit(solution)/shard_map/attend/pallas_call | solution.py:444
  30.1 1.3 %collective-permute-done.13.refs_2_ = bf16[272,256]{1,0:T(8,128)(2,1)S(1)} collective-permute-done((bf16[272,256]{1,0:T(8,128)(2,1)S(1)}, bf16[272,256]{1,0:T(8,128)(2,1)S(1)}, u32[]{:S(2)}, u32[]{:S(2)}) %collective-permute-start.13) | collective-permute-done | bytes 139296 | tf_op jit(solution)/shard_map/ppermute | solution.py:35
  31.9 1.7 %attend.10.refs_11_ = f32[128,2048]{1,0:T(8,128)S(1)} custom-call(bf16[128,2048]{1,0:T(8,128)(2,1)S(1)} %choose_queries.1.refs_0_, bf16[272,256]{1,0:T(8,128)(2,1)S(1)} %collective-permute-done.3.refs_1_.refs_9_, bf16[272,256]{1,0:T(8,128)(2,1)S(1)} %collective-permute-done.6.refs_2_, f32[1024,128]{1,0:T(8,128)S(1)} %get-tuple-element.115.refs_3_, ...), custom_call_target="tpu_custom_call" | custom-call | flops 402653184 | bytes 4194304 | tf_op jit(solution)/shard_map/attend/pallas_call | solution.py:444
  33.6 1.7 %attend.11 = (f32[32,2048]{1,0:T(8,128)S(1)}, f32[32,2048]{1,0:T(8,128)S(1)}, bf16[32,2176]{1,0:T(8,128)(2,1)S(1)}, bf16[32,2048]{1,0:T(8,128)(2,1)S(1)}, bf16[32,128]{1,0:T(8,128)(2,1)S(1)}) custom-call(bf16[128,2048]{1,0:T(8,128)(2,1)S(1)} %choose_queries.1.refs_0_, bf16[272,256]{1,0:T(8,128)(2,1)S(1)} %collective-permute-done.10.refs_1_, ...), custom_call_target="tpu_custom_call" | custom-call | flops 402653184 | bytes 4194304 | tf_op jit(solution)/shard_map/attend/pallas_call | solution.py:444
  35.3 1.8 %collective-permute-start.15 = (bf16[32,2176]{1,0:T(8,128)(2,1)S(1)}, bf16[32,2176]{1,0:T(8,128)(2,1)S(1)}, u32[]{:S(2)}, u32[]{:S(2)}) collective-permute-start(bf16[32,2176]{1,0:T(8,128)(2,1)S(1)} %get-tuple-element.118), channel_id=1, source_target_pairs={{0,2},{2,0},{1,3},{3,1},{4,6},{6,4},{5,7},{7,5},{8,10},{10,8},{9,1... | collective-permute-start | bytes 417800 | tf_op jit(solution)/shard_map/ppermute | solution.py:744
  38.5 3.4 %collective-permute-done.15.refs_1_.came_ref = bf16[32,2176]{1,0:T(8,128)(2,1)S(1)} collective-permute-done((bf16[32,2176]{1,0:T(8,128)(2,1)S(1)}, bf16[32,2176]{1,0:T(8,128)(2,1)S(1)}, u32[]{:S(2)}, u32[]{:S(2)}) %collective-permute-start.15) | collective-permute-done | bytes 139296 | tf_op jit(solution)/shard_map/ppermute | solution.py:744
  42.1 1.8 %collective-permute-done.17.refs_1_ = bf16[32,2048]{1,0:T(8,128)(2,1)S(1)} collective-permute-done((bf16[32,2048]{1,0:T(8,128)(2,1)S(1)}, bf16[32,2048]{1,0:T(8,128)(2,1)S(1)}, u32[]{:S(2)}, u32[]{:S(2)}) %collective-permute-start.17) | collective-permute-done | bytes 131104 | tf_op jit(solution)/shard_map/ppermute | solution.py:744
  46.5 1.1 %collective-permute-done.18.refs_0_ = bf16[32,2048]{1,0:T(8,128)(2,1)S(1)} collective-permute-done((bf16[32,2048]{1,0:T(8,128)(2,1)S(1)}, bf16[32,2048]{1,0:T(8,128)(2,1)S(1)}, u32[]{:S(2)}, u32[]{:S(2)}) %collective-permute-start.18) | collective-permute-done | bytes 131104 | tf_op jit(solution)/shard_map/ppermute | solution.py:543
  48.2 1.5 %collective-permute-done.22.refs_1_ = bf16[32,2048]{1,0:T(8,128)(2,1)S(1)} collective-permute-done((bf16[32,2048]{1,0:T(8,128)(2,1)S(1)}, bf16[32,2048]{1,0:T(8,128)(2,1)S(1)}, u32[]{:S(2)}, u32[]{:S(2)}) %collective-permute-start.22) | collective-permute-done | bytes 131104 | tf_op jit(solution)/shard_map/ppermute | solution.py:544
  56.1 1.6 %apply_expert.5 = (f32[32,2048]{1,0:T(8,128)S(1)}, f32[32,2048]{1,0:T(8,128)S(1)}, f32[32,2048]{1,0:T(8,128)S(1)}, f32[32,2048]{1,0:T(8,128)S(1)}) custom-call(bf16[32,2048]{1,0:T(8,128)(2,1)S(1)} %collective-permute-done.18.refs_0_, bf16[32,2048]{1,0:T(8,128)(2,1)S(1)} %collective-permute-done.22.refs_1_, ...), custom_call_target="tpu_custom_call" | custom-call | flops 603979776 | bytes 6291456 | tf_op jit(solution)/shard_map/apply_expert/pallas_call | solution.py:499
  62.0 1.6 %apply_expert.6 = (f32[32,2048]{1,0:T(8,128)S(1)}, f32[32,2048]{1,0:T(8,128)S(1)}, f32[32,2048]{1,0:T(8,128)S(1)}, f32[32,2048]{1,0:T(8,128)S(1)}) custom-call(bf16[32,2048]{1,0:T(8,128)(2,1)S(1)} %collective-permute-done.19.refs_0_, bf16[32,2048]{1,0:T(8,128)(2,1)S(1)} %collective-permute-done.23.refs_1_, ...), custom_call_target="tpu_custom_call" | custom-call | flops 603979776 | bytes 6291456 | tf_op jit(solution)/shard_map/apply_expert/pallas_call | solution.py:499
  64.3 1.6 %apply_expert.7 = (f32[32,2048]{1,0:T(8,128)S(1)}, f32[32,2048]{1,0:T(8,128)S(1)}, f32[32,2048]{1,0:T(8,128)S(1)}, f32[32,2048]{1,0:T(8,128)S(1)}) custom-call(bf16[32,2048]{1,0:T(8,128)(2,1)S(1)} %collective-permute-done.20.refs_0_, bf16[32,2048]{1,0:T(8,128)(2,1)S(1)} %collective-permute-done.24.refs_1_, ...), custom_call_target="tpu_custom_call" | custom-call | flops 603979776 | bytes 6291456 | tf_op jit(solution)/shard_map/apply_expert/pallas_call | solution.py:499
  65.9 1.2 %collective-permute-done.33.refs_1_ = bf16[32,2048]{1,0:T(8,128)(2,1)S(1)} collective-permute-done((bf16[32,2048]{1,0:T(8,128)(2,1)S(1)}, bf16[32,2048]{1,0:T(8,128)(2,1)S(1)}, u32[]{:S(2)}, u32[]{:S(2)}) %collective-permute-start.33) | collective-permute-done | bytes 131104 | tf_op jit(solution)/shard_map/ppermute | solution.py:544
  67.1 1.5 %apply_expert.8 = (f32[32,2048]{1,0:T(8,128)S(1)}, f32[32,2048]{1,0:T(8,128)S(1)}) custom-call(bf16[32,2048]{1,0:T(8,128)(2,1)S(1)} %collective-permute-done.21.refs_0_, bf16[32,2048]{1,0:T(8,128)(2,1)S(1)} %collective-permute-done.33.refs_1_, f32[128,128]{1,0:T(8,128)S(1)} %gates_by_chip.1.refs_4_.refs_2_, bf16[2,192,2048]{2,1,0:T(8,128)(2,1)S(1)} %bitcast.9, ...), custom_call_target="tpu_custom_call" | custom-call | flops 301989888 | bytes 6291456 | tf_op jit(solution)/shard_map/apply_expert/pallas_call | solution.py:499
  68.6 1.2 %collective-permute-start.34 = (bf16[32,2048]{1,0:T(8,128)(2,1)S(1)}, bf16[32,2048]{1,0:T(8,128)(2,1)S(1)}, u32[]{:S(2)}, u32[]{:S(2)}) collective-permute-start(bf16[32,2048]{1,0:T(8,128)(2,1)S(1)} %convert_element_type.12), channel_id=1, source_target_pairs={{5,0},{4,1},{9,4},{8,5},{13,8},{12,9},{15,12},{14,13},{11,14},{10,... | collective-permute-start | bytes 393224 | tf_op jit(solution)/shard_map/ppermute | solution.py:571
  72.4 1.7 %collective-permute-done.34.came_ref = bf16[32,2048]{1,0:T(8,128)(2,1)S(1)} collective-permute-done((bf16[32,2048]{1,0:T(8,128)(2,1)S(1)}, bf16[32,2048]{1,0:T(8,128)(2,1)S(1)}, u32[]{:S(2)}, u32[]{:S(2)}) %collective-permute-start.34) | collective-permute-done | bytes 131104 | tf_op jit(solution)/shard_map/ppermute | solution.py:571
  74.2 1.7 %collective-permute-start.35 = (bf16[32,2048]{1,0:T(8,128)(2,1)S(1)}, bf16[32,2048]{1,0:T(8,128)(2,1)S(1)}, u32[]{:S(2)}, u32[]{:S(2)}) collective-permute-start(bf16[32,2048]{1,0:T(8,128)(2,1)S(1)} %add_share.10), channel_id=1, source_target_pairs={{5,0},{4,1},{9,4},{8,5},{13,8},{12,9},{15,12},{14,13},{11,14},{10,... | collective-permute-start | bytes 393224 | tf_op jit(solution)/shard_map/ppermute | solution.py:571
  77.0 1.7 %collective-permute-start.39 = (bf16[32,2048]{1,0:T(8,128)(2,1)S(1)}, bf16[32,2048]{1,0:T(8,128)(2,1)S(1)}, u32[]{:S(2)}, u32[]{:S(2)}) collective-permute-start(bf16[32,2048]{1,0:T(8,128)(2,1)S(1)} %add_share.13), channel_id=1, source_target_pairs={{5,0},{4,1},{9,4},{8,5},{13,8},{12,9},{15,12},{14,13},{11,14},{10,... | collective-permute-start | bytes 393224 | tf_op jit(solution)/shard_map/ppermute | solution.py:571
  79.5 2.3 %collective-permute-start.36 = (bf16[32,2048]{1,0:T(8,128)(2,1)S(1)}, bf16[32,2048]{1,0:T(8,128)(2,1)S(1)}, u32[]{:S(2)}, u32[]{:S(2)}) collective-permute-start(bf16[32,2048]{1,0:T(8,128)(2,1)S(1)} %add_share.11), channel_id=1, source_target_pairs={{5,0},{4,1},{9,4},{8,5},{13,8},{12,9},{15,12},{14,13},{11,14},{10,... | collective-permute-start | bytes 393224 | tf_op jit(solution)/shard_map/ppermute | solution.py:571
  82.5 2.0 %collective-permute-start.40 = (bf16[32,2048]{1,0:T(8,128)(2,1)S(1)}, bf16[32,2048]{1,0:T(8,128)(2,1)S(1)}, u32[]{:S(2)}, u32[]{:S(2)}) collective-permute-start(bf16[32,2048]{1,0:T(8,128)(2,1)S(1)} %add_share.14), channel_id=1, source_target_pairs={{5,0},{4,1},{9,4},{8,5},{13,8},{12,9},{15,12},{14,13},{11,14},{10,... | collective-permute-start | bytes 393224 | tf_op jit(solution)/shard_map/ppermute | solution.py:571
  85.3 2.1 %collective-permute-start.37 = (bf16[32,2048]{1,0:T(8,128)(2,1)S(1)}, bf16[32,2048]{1,0:T(8,128)(2,1)S(1)}, u32[]{:S(2)}, u32[]{:S(2)}) collective-permute-start(bf16[32,2048]{1,0:T(8,128)(2,1)S(1)} %add_share.12), channel_id=1, source_target_pairs={{5,0},{4,1},{9,4},{8,5},{13,8},{12,9},{15,12},{14,13},{11,14},{10,... | collective-permute-start | bytes 393224 | tf_op jit(solution)/shard_map/ppermute | solution.py:571
  87.9 1.5 %apply_expert.9 = (f32[32,2048]{1,0:T(8,128)S(1)}, f32[32,2048]{1,0:T(8,128)S(1)}) custom-call(bf16[32,2048]{1,0:T(8,128)(2,1)S(1)} %get-tuple-element.149.refs_0_, bf16[32,2048]{1,0:T(8,128)(2,1)S(1)} %get-tuple-element.150.refs_1_, f32[128,128]{1,0:T(8,128)S(1)} %gates_by_chip.1.refs_4_.refs_2_, bf16[2,192,2048]{2,1,0:T(8,128)(2,1)S(1)} %bitcast.10, ...), custom_call_target="tpu_custom_call" | custom-call | flops 301989888 | bytes 6291456 | tf_op jit(solution)/shard_map/apply_expert/pallas_call | solution.py:499
  90.1 1.6 %collective-permute-done.37.refs_4_ = bf16[32,2048]{1,0:T(8,128)(2,1)S(1)} collective-permute-done((bf16[32,2048]{1,0:T(8,128)(2,1)S(1)}, bf16[32,2048]{1,0:T(8,128)(2,1)S(1)}, u32[]{:S(2)}, u32[]{:S(2)}) %collective-permute-start.37) | collective-permute-done | bytes 131104 | tf_op jit(solution)/shard_map/ppermute | solution.py:571
  (118 shorter events, 34.2 us)
Async XLA Ops:
  2.5 29.4 %collective-permute-start.14 = (bf16[2048,1024]{1,0:T(8,128)(2,1)}, bf16[2048,1024]{1,0:T(8,128)(2,1)S(1)}, u32[]{:S(2)}, u32[]{:S(2)}) collective-permute-start(bf16[2048,1024]{1,0:T(8,128)(2,1)} %refs_5_.1), channel_id=1, source_target_pairs={{0,1},{1,0},{2,3},{3,2},{4,5},{5,4},{6,7},{7,6},{8,9},{9,8},{10,11... | collective-permute-start | bytes 12582920 | tf_op jit(solution)/shard_map/ppermute | solution.py:35
  3.0 7.2 %collective-permute-start.2 = (bf16[272,256]{1,0:T(8,128)(2,1)}, bf16[272,256]{1,0:T(8,128)(2,1)S(1)}, u32[]{:S(2)}, u32[]{:S(2)}) collective-permute-start(bf16[272,256]{1,0:T(8,128)(2,1)} %get-tuple-element.86.refs_1_.refs_7_), channel_id=1, source_target_pairs={{0,1},{1,0},{2,3},{3,2},{4,5},{5,4},{6,7},{7,6},{8,9},{9,8},{10,11... | collective-permute-start | bytes 417800 | tf_op jit(solution)/shard_map/ppermute | solution.py:35
  3.0 12.0 %collective-permute-start = (bf16[272,256]{1,0:T(8,128)(2,1)}, bf16[272,256]{1,0:T(8,128)(2,1)S(1)}, u32[]{:S(2)}, u32[]{:S(2)}) collective-permute-start(bf16[272,256]{1,0:T(8,128)(2,1)} %get-tuple-element.86.refs_1_.refs_7_), channel_id=1, source_target_pairs={{0,4},{4,8},{8,12},{12,0},{1,5},{5,9},{9,13},{13,1},{2,6},{6,10},{... | collective-permute-start | bytes 417800 | tf_op jit(solution)/shard_map/ppermute | solution.py:703
  6.1 11.1 %collective-permute-start.1 = (bf16[272,256]{1,0:T(8,128)(2,1)}, bf16[272,256]{1,0:T(8,128)(2,1)S(1)}, u32[]{:S(2)}, u32[]{:S(2)}) collective-permute-start(bf16[272,256]{1,0:T(8,128)(2,1)} %get-tuple-element.86.refs_1_.refs_7_), channel_id=1, source_target_pairs={{0,12},{4,0},{8,4},{12,8},{1,13},{5,1},{9,5},{13,9},{2,14},{6,2},{... | collective-permute-start | bytes 417800 | tf_op jit(solution)/shard_map/ppermute | solution.py:706
  8.1 9.0 %collective-permute-start.9 = (bf16[272,256]{1,0:T(8,128)(2,1)}, bf16[272,256]{1,0:T(8,128)(2,1)S(1)}, u32[]{:S(2)}, u32[]{:S(2)}) collective-permute-start(bf16[272,256]{1,0:T(8,128)(2,1)} %get-tuple-element.98.refs_1_), channel_id=1, source_target_pairs={{0,1},{1,0},{2,3},{3,2},{4,5},{5,4},{6,7},{7,6},{8,9},{9,8},{10,11... | collective-permute-start | bytes 417800 | tf_op jit(solution)/shard_map/ppermute | solution.py:35
  10.2 9.4 %collective-permute-start.7 = (bf16[272,256]{1,0:T(8,128)(2,1)}, bf16[272,256]{1,0:T(8,128)(2,1)S(1)}, u32[]{:S(2)}, u32[]{:S(2)}) collective-permute-start(bf16[272,256]{1,0:T(8,128)(2,1)} %get-tuple-element.98.refs_1_), channel_id=1, source_target_pairs={{0,4},{4,8},{8,12},{12,0},{1,5},{5,9},{9,13},{13,1},{2,6},{6,10},{... | collective-permute-start | bytes 417800 | tf_op jit(solution)/shard_map/ppermute | solution.py:703
  15.0 7.3 %collective-permute-start.8 = (bf16[272,256]{1,0:T(8,128)(2,1)}, bf16[272,256]{1,0:T(8,128)(2,1)S(1)}, u32[]{:S(2)}, u32[]{:S(2)}) collective-permute-start(bf16[272,256]{1,0:T(8,128)(2,1)} %get-tuple-element.98.refs_1_), channel_id=1, source_target_pairs={{0,12},{4,0},{8,4},{12,8},{1,13},{5,1},{9,5},{13,9},{2,14},{6,2},{... | collective-permute-start | bytes 417800 | tf_op jit(solution)/shard_map/ppermute | solution.py:706
  17.1 5.7 %collective-permute-start.5 = (bf16[272,256]{1,0:T(8,128)(2,1)S(1)}, bf16[272,256]{1,0:T(8,128)(2,1)S(1)}, u32[]{:S(2)}, u32[]{:S(2)}) collective-permute-start(bf16[272,256]{1,0:T(8,128)(2,1)S(1)} %collective-permute-done.1.refs_3_.refs_10_), channel_id=1, source_target_pairs={{0,1},{1,0},{2,3},{3,2},{4,5},{5,4},{6,7},{7,6},{8,9},{9,8},{10,11... | collective-permute-start | bytes 417800 | tf_op jit(solution)/shard_map/ppermute | solution.py:35
  19.5 8.1 %collective-permute-start.3 = (bf16[272,256]{1,0:T(8,128)(2,1)S(1)}, bf16[272,256]{1,0:T(8,128)(2,1)S(1)}, u32[]{:S(2)}, u32[]{:S(2)}) collective-permute-start(bf16[272,256]{1,0:T(8,128)(2,1)S(1)} %collective-permute-done.refs_1_.refs_8_), channel_id=1, source_target_pairs={{0,4},{4,8},{8,12},{12,0},{1,5},{5,9},{9,13},{13,1},{2,6},{6,10},{... | collective-permute-start | bytes 417800 | tf_op jit(solution)/shard_map/ppermute | solution.py:703
  22.8 7.2 %collective-permute-start.10 = (bf16[272,256]{1,0:T(8,128)(2,1)S(1)}, bf16[272,256]{1,0:T(8,128)(2,1)S(1)}, u32[]{:S(2)}, u32[]{:S(2)}) collective-permute-start(bf16[272,256]{1,0:T(8,128)(2,1)S(1)} %collective-permute-done.8.refs_3_), channel_id=1, source_target_pairs={{0,12},{4,0},{8,4},{12,8},{1,13},{5,1},{9,5},{13,9},{2,14},{6,2},{... | collective-permute-start | bytes 417800 | tf_op jit(solution)/shard_map/ppermute | solution.py:706
  31.4 24.7 %collective-permute-start.28 = (bf16[2,192,2048]{2,1,0:T(8,128)(2,1)S(1)}, bf16[2,192,2048]{2,1,0:T(8,128)(2,1)S(1)}, u32[]{:S(2)}, u32[]{:S(2)}) collective-permute-start(bf16[2,192,2048]{2,1,0:T(8,128)(2,1)S(1)} %bitcast.5), channel_id=1, source_target_pairs={{0,1},{1,0},{2,3},{3,2},{4,5},{5,4},{6,7},{7,6},{8,9},{9,8},{10,11... | collective-permute-start | bytes 4718600 | tf_op jit(solution)/shard_map/ppermute | solution.py:35
  31.5 14.3 %collective-permute-start.29 = (bf16[192,2048]{1,0:T(8,128)(2,1)S(1)}, bf16[192,2048]{1,0:T(8,128)(2,1)S(1)}, u32[]{:S(2)}, u32[]{:S(2)}) collective-permute-start(bf16[192,2048]{1,0:T(8,128)(2,1)S(1)} %bitcast.11), channel_id=1, source_target_pairs={{0,1},{1,0},{2,3},{3,2},{4,5},{5,4},{6,7},{7,6},{8,9},{9,8},{10,11... | collective-permute-start | bytes 2359304 | tf_op jit(solution)/shard_map/ppermute | solution.py:35
  35.3 6.6 %collective-permute-start.15 = (bf16[32,2176]{1,0:T(8,128)(2,1)S(1)}, bf16[32,2176]{1,0:T(8,128)(2,1)S(1)}, u32[]{:S(2)}, u32[]{:S(2)}) collective-permute-start(bf16[32,2176]{1,0:T(8,128)(2,1)S(1)} %get-tuple-element.118), channel_id=1, source_target_pairs={{0,2},{2,0},{1,3},{3,1},{4,6},{6,4},{5,7},{7,5},{8,10},{10,8},{9,1... | collective-permute-start | bytes 417800 | tf_op jit(solution)/shard_map/ppermute | solution.py:744
  37.2 6.7 %collective-permute-start.17 = (bf16[32,2048]{1,0:T(8,128)(2,1)S(1)}, bf16[32,2048]{1,0:T(8,128)(2,1)S(1)}, u32[]{:S(2)}, u32[]{:S(2)}) collective-permute-start(bf16[32,2048]{1,0:T(8,128)(2,1)S(1)} %get-tuple-element.124), channel_id=1, source_target_pairs={{0,2},{2,0},{1,3},{3,1},{4,6},{6,4},{5,7},{7,5},{8,10},{10,8},{9,1... | collective-permute-start | bytes 393224 | tf_op jit(solution)/shard_map/ppermute | solution.py:744
  44.8 5.7 %collective-permute-start.25 = (bf16[32,2048]{1,0:T(8,128)(2,1)S(1)}, bf16[32,2048]{1,0:T(8,128)(2,1)S(1)}, u32[]{:S(2)}, u32[]{:S(2)}) collective-permute-start(bf16[32,2048]{1,0:T(8,128)(2,1)S(1)} %get-tuple-element.150.refs_1_), channel_id=1, source_target_pairs={{0,5},{1,4},{4,9},{5,8},{8,13},{9,12},{12,15},{13,14},{14,11},{15,... | collective-permute-start | bytes 393224 | tf_op jit(solution)/shard_map/ppermute | solution.py:546
  45.9 6.4 %collective-permute-start.27 = (bf16[32,2048]{1,0:T(8,128)(2,1)S(1)}, bf16[32,2048]{1,0:T(8,128)(2,1)S(1)}, u32[]{:S(2)}, u32[]{:S(2)}) collective-permute-start(bf16[32,2048]{1,0:T(8,128)(2,1)S(1)} %get-tuple-element.149.refs_0_), channel_id=1, source_target_pairs={{5,0},{4,1},{9,4},{8,5},{13,8},{12,9},{15,12},{14,13},{11,14},{10,... | collective-permute-start | bytes 393224 | tf_op jit(solution)/shard_map/ppermute | solution.py:547
  47.6 5.6 %collective-permute-start.19 = (bf16[32,2048]{1,0:T(8,128)(2,1)S(1)}, bf16[32,2048]{1,0:T(8,128)(2,1)S(1)}, u32[]{:S(2)}, u32[]{:S(2)}) collective-permute-start(bf16[32,2048]{1,0:T(8,128)(2,1)S(1)} %collective-permute-done.18.refs_0_), channel_id=1, source_target_pairs={{0,5},{1,4},{4,9},{5,8},{8,13},{9,12},{12,15},{13,14},{14,11},{15,... | collective-permute-start | bytes 393224 | tf_op jit(solution)/shard_map/ppermute | solution.py:543
  50.4 7.3 %collective-permute-start.26 = (bf16[32,2048]{1,0:T(8,128)(2,1)S(1)}, bf16[32,2048]{1,0:T(8,128)(2,1)S(1)}, u32[]{:S(2)}, u32[]{:S(2)}) collective-permute-start(bf16[32,2048]{1,0:T(8,128)(2,1)S(1)} %collective-permute-done.25.refs_2_), channel_id=1, source_target_pairs={{0,5},{1,4},{4,9},{5,8},{8,13},{9,12},{12,15},{13,14},{14,11},{15,... | collective-permute-start | bytes 393224 | tf_op jit(solution)/shard_map/ppermute | solution.py:546
  52.2 6.5 %collective-permute-start.31 = (bf16[32,2048]{1,0:T(8,128)(2,1)S(1)}, bf16[32,2048]{1,0:T(8,128)(2,1)S(1)}, u32[]{:S(2)}, u32[]{:S(2)}) collective-permute-start(bf16[32,2048]{1,0:T(8,128)(2,1)S(1)} %collective-permute-done.27.refs_3_), channel_id=1, source_target_pairs={{5,0},{4,1},{9,4},{8,5},{13,8},{12,9},{15,12},{14,13},{11,14},{10,... | collective-permute-start | bytes 393224 | tf_op jit(solution)/shard_map/ppermute | solution.py:547
  53.2 6.3 %collective-permute-start.20 = (bf16[32,2048]{1,0:T(8,128)(2,1)S(1)}, bf16[32,2048]{1,0:T(8,128)(2,1)S(1)}, u32[]{:S(2)}, u32[]{:S(2)}) collective-permute-start(bf16[32,2048]{1,0:T(8,128)(2,1)S(1)} %collective-permute-done.19.refs_0_), channel_id=1, source_target_pairs={{0,5},{1,4},{4,9},{5,8},{8,13},{9,12},{12,15},{13,14},{14,11},{15,... | collective-permute-start | bytes 393224 | tf_op jit(solution)/shard_map/ppermute | solution.py:543
  55.2 5.8 %collective-permute-start.24 = (bf16[32,2048]{1,0:T(8,128)(2,1)S(1)}, bf16[32,2048]{1,0:T(8,128)(2,1)S(1)}, u32[]{:S(2)}, u32[]{:S(2)}) collective-permute-start(bf16[32,2048]{1,0:T(8,128)(2,1)S(1)} %collective-permute-done.23.refs_1_), channel_id=1, source_target_pairs={{5,0},{4,1},{9,4},{8,5},{13,8},{12,9},{15,12},{14,13},{11,14},{10,... | collective-permute-start | bytes 393224 | tf_op jit(solution)/shard_map/ppermute | solution.py:544
  57.7 5.8 %collective-permute-start.30 = (bf16[32,2048]{1,0:T(8,128)(2,1)S(1)}, bf16[32,2048]{1,0:T(8,128)(2,1)S(1)}, u32[]{:S(2)}, u32[]{:S(2)}) collective-permute-start(bf16[32,2048]{1,0:T(8,128)(2,1)S(1)} %collective-permute-done.26.refs_2_), channel_id=1, source_target_pairs={{0,5},{1,4},{4,9},{5,8},{8,13},{9,12},{12,15},{13,14},{14,11},{15,... | collective-permute-start | bytes 393224 | tf_op jit(solution)/shard_map/ppermute | solution.py:546
  59.5 6.3 %collective-permute-start.21 = (bf16[32,2048]{1,0:T(8,128)(2,1)S(1)}, bf16[32,2048]{1,0:T(8,128)(2,1)S(1)}, u32[]{:S(2)}, u32[]{:S(2)}) collective-permute-start(bf16[32,2048]{1,0:T(8,128)(2,1)S(1)} %collective-permute-done.20.refs_0_), channel_id=1, source_target_pairs={{0,5},{1,4},{4,9},{5,8},{8,13},{9,12},{12,15},{13,14},{14,11},{15,... | collective-permute-start | bytes 393224 | tf_op jit(solution)/shard_map/ppermute | solution.py:543
  61.0 6.1 %collective-permute-start.33 = (bf16[32,2048]{1,0:T(8,128)(2,1)S(1)}, bf16[32,2048]{1,0:T(8,128)(2,1)S(1)}, u32[]{:S(2)}, u32[]{:S(2)}) collective-permute-start(bf16[32,2048]{1,0:T(8,128)(2,1)S(1)} %collective-permute-done.24.refs_1_), channel_id=1, source_target_pairs={{5,0},{4,1},{9,4},{8,5},{13,8},{12,9},{15,12},{14,13},{11,14},{10,... | collective-permute-start | bytes 393224 | tf_op jit(solution)/shard_map/ppermute | solution.py:544
  69.8 6.2 %collective-permute-start.44 = (bf16[32,2048]{1,0:T(8,128)(2,1)S(1)}, bf16[32,2048]{1,0:T(8,128)(2,1)S(1)}, u32[]{:S(2)}, u32[]{:S(2)}) collective-permute-start(bf16[32,2048]{1,0:T(8,128)(2,1)S(1)} %convert_element_type.15), channel_id=1, source_target_pairs={{0,5},{1,4},{4,9},{5,8},{8,13},{9,12},{12,15},{13,14},{14,11},{15,... | collective-permute-start | bytes 393224 | tf_op jit(solution)/shard_map/ppermute | solution.py:571
  70.5 6.4 %collective-permute-start.38 = (bf16[32,2048]{1,0:T(8,128)(2,1)S(1)}, bf16[32,2048]{1,0:T(8,128)(2,1)S(1)}, u32[]{:S(2)}, u32[]{:S(2)}) collective-permute-start(bf16[32,2048]{1,0:T(8,128)(2,1)S(1)} %convert_element_type.13), channel_id=1, source_target_pairs={{5,0},{4,1},{9,4},{8,5},{13,8},{12,9},{15,12},{14,13},{11,14},{10,... | collective-permute-start | bytes 393224 | tf_op jit(solution)/shard_map/ppermute | solution.py:571
  71.7 7.0 %collective-permute-start.41 = (bf16[32,2048]{1,0:T(8,128)(2,1)S(1)}, bf16[32,2048]{1,0:T(8,128)(2,1)S(1)}, u32[]{:S(2)}, u32[]{:S(2)}) collective-permute-start(bf16[32,2048]{1,0:T(8,128)(2,1)S(1)} %convert_element_type.14), channel_id=1, source_target_pairs={{0,5},{1,4},{4,9},{5,8},{8,13},{9,12},{12,15},{13,14},{14,11},{15,... | collective-permute-start | bytes 393224 | tf_op jit(solution)/shard_map/ppermute | solution.py:571
  76.0 5.7 %collective-permute-start.45 = (bf16[32,2048]{1,0:T(8,128)(2,1)S(1)}, bf16[32,2048]{1,0:T(8,128)(2,1)S(1)}, u32[]{:S(2)}, u32[]{:S(2)}) collective-permute-start(bf16[32,2048]{1,0:T(8,128)(2,1)S(1)} %add_share.17), channel_id=1, source_target_pairs={{0,5},{1,4},{4,9},{5,8},{8,13},{9,12},{12,15},{13,14},{14,11},{15,... | collective-permute-start | bytes 393224 | tf_op jit(solution)/shard_map/ppermute | solution.py:571
  78.7 5.8 %collective-permute-start.42 = (bf16[32,2048]{1,0:T(8,128)(2,1)S(1)}, bf16[32,2048]{1,0:T(8,128)(2,1)S(1)}, u32[]{:S(2)}, u32[]{:S(2)}) collective-permute-start(bf16[32,2048]{1,0:T(8,128)(2,1)S(1)} %add_share.15), channel_id=1, source_target_pairs={{0,5},{1,4},{4,9},{5,8},{8,13},{9,12},{12,15},{13,14},{14,11},{15,... | collective-permute-start | bytes 393224 | tf_op jit(solution)/shard_map/ppermute | solution.py:571
  79.5 5.8 %collective-permute-start.36 = (bf16[32,2048]{1,0:T(8,128)(2,1)S(1)}, bf16[32,2048]{1,0:T(8,128)(2,1)S(1)}, u32[]{:S(2)}, u32[]{:S(2)}) collective-permute-start(bf16[32,2048]{1,0:T(8,128)(2,1)S(1)} %add_share.11), channel_id=1, source_target_pairs={{5,0},{4,1},{9,4},{8,5},{13,8},{12,9},{15,12},{14,13},{11,14},{10,... | collective-permute-start | bytes 393224 | tf_op jit(solution)/shard_map/ppermute | solution.py:571
  82.5 6.9 %collective-permute-start.40 = (bf16[32,2048]{1,0:T(8,128)(2,1)S(1)}, bf16[32,2048]{1,0:T(8,128)(2,1)S(1)}, u32[]{:S(2)}, u32[]{:S(2)}) collective-permute-start(bf16[32,2048]{1,0:T(8,128)(2,1)S(1)} %add_share.14), channel_id=1, source_target_pairs={{5,0},{4,1},{9,4},{8,5},{13,8},{12,9},{15,12},{14,13},{11,14},{10,... | collective-permute-start | bytes 393224 | tf_op jit(solution)/shard_map/ppermute | solution.py:571
  85.3 6.4 %collective-permute-start.37 = (bf16[32,2048]{1,0:T(8,128)(2,1)S(1)}, bf16[32,2048]{1,0:T(8,128)(2,1)S(1)}, u32[]{:S(2)}, u32[]{:S(2)}) collective-permute-start(bf16[32,2048]{1,0:T(8,128)(2,1)S(1)} %add_share.12), channel_id=1, source_target_pairs={{5,0},{4,1},{9,4},{8,5},{13,8},{12,9},{15,12},{14,13},{11,14},{10,... | collective-permute-start | bytes 393224 | tf_op jit(solution)/shard_map/ppermute | solution.py:571
  (26 other events, 156.8 us)

commit v10 on v9

--- a/solution.py
+++ b/solution.py
@@ -269,14 +269,14 @@
     blocks = [block for _, stage_blocks in stages for block in stage_blocks]
     origins = [(hop, step) for hop, _ in stages for step in range(n_sub)]
     per_kv = columns // HD // kv_heads
-    stack = 2 if per_kv % 2 == 0 else 1
+    stack = 1
     part = stack * all_rows
     new_rows = blocks[0].shape[0] - cache_rows - MASK_ROWS
     keys = cache_rows + new_rows
     factor = math.log2(math.e) / math.sqrt(HD)
     relative = n_hd == 2
     last = finish is not None
-    weights, earlier, tables = finish if last else ([], None, [])
+    weights, earlier, tables = finish if last else ([], [], [])
     head_columns = per_kv * HD
     final = last and kv == kv_heads - 1
     kept_rows = rows if relative else 0
@@ -289,8 +289,7 @@
             (m_in, acc_in), refs = refs[:2], refs[2:]
         weight_refs, refs = refs[: len(weights)], refs[len(weights) :]
         table_refs, refs = refs[: len(tables)], refs[len(tables) :]
-        if earlier is not None:
-            earlier_ref, refs = refs[0], refs[1:]
+        earlier_refs, refs = refs[: len(earlier)], refs[len(earlier) :]
         if last:
             results = len(out_shape)
             result_refs, refs = refs[:results], refs[results:]
@@ -372,22 +371,16 @@
                 m_out[here, :] = top
                 acc_out[here, :] = acc
         if last:
-            source = head_ref[...]
-            width = weight_refs[0].shape[1]
-            these = slice(kv * head_columns, (kv + 1) * head_columns)
+            source = jnp.concatenate([ref[...] for ref in earlier_refs] + [head_ref[...]], axis=1)
             for i, weight_ref in enumerate(weight_refs):
+                width = weight_ref.shape[1]
                 here = slice(i * width, (i + 1) * width)
-                product = jnp.dot(
-                    source, weight_ref[these, :], preferred_element_type=jnp.float32
-                )
-                if earlier is not None:
-                    product = product + earlier_ref[:, here]
-                if final:
-                    for j, result_ref in enumerate(result_refs):
-                        share = product[j * chunk_rows : (j + 1) * chunk_rows]
-                        result_ref[:, here] = share.astype(result_ref.dtype)
-                else:
-                    result_refs[0][:, here] = product
+                product = jnp.dot(source, weight_ref[...], preferred_element_type=jnp.float32)
+                for j, result_ref in enumerate(result_refs):
+                    share = product[j * chunk_rows : (j + 1) * chunk_rows]
+                    result_ref[:, here] = share.astype(result_ref.dtype)
+            if not final:
+                result_refs[0][...] = head_ref[...]
             if tables:
                 for copy in copies:
                     copy.wait()
@@ -417,7 +410,7 @@
                 for _ in range(count)
             ]
         else:
-            out_shape = (jax.ShapeDtypeStruct((all_rows, features), jnp.float32),)
+            out_shape = [jax.ShapeDtypeStruct((all_rows, head_columns), jnp.bfloat16)]
         scratch = [pltpu.VMEM((all_rows, head_columns), jnp.bfloat16)]
         if tables:
             joint = (len(tables) * TABLE_ROWS, LANES)
@@ -437,9 +430,8 @@
     operands += list(weights)
     in_specs = [vmem] * len(operands) + [pl.BlockSpec(memory_space=pl.ANY)] * len(tables)
     operands += list(tables)
-    if earlier is not None:
-        operands.append(earlier)
-        in_specs.append(vmem)
+    operands += list(earlier)
+    in_specs += [vmem] * len(earlier)
     scores = all_rows * per_kv * keys * len(blocks)
     return pl.pallas_call(
         kernel,
@@ -679,7 +671,7 @@
     arrived = [[(0, x)] for x in packed]
     tables = {}
     states = [None] * kv_heads
-    earlier = None
+    attended = []
     for distance in range(reach + 1):
         stages = [[(hop, sub_copies(x)) for hop, x in blocks] for blocks in arrived]
         if distance == 0:
@@ -709,7 +701,9 @@
             finish = None
             if distance == reach:
                 joint = [tables[hop] for hop in range(n_ep)] if dense and kv == kv_heads - 1 else []
-                finish = (projections, earlier, joint)
+                finish = (projections, list(attended), joint)
+                if kv < kv_heads - 1:
+                    finish = ([], [], [])
             states[kv] = attend(
                 query_rows_here,
                 kv,
@@ -722,7 +716,7 @@
                 finish,
             )
             if finish:
-                earlier = states[kv][0]
+                attended.append(states[kv][0])
                 continue
             came = [x for _, x in onward[kv]]
             came, states[kv] = lax.optimization_barrier((came, states[kv]))

time: 95.2 us -> 94.6 us (level)
  starting transfers between devices: 45.4 us -> 44.3 us
    ppermute x3, waiting for transfers between devices: 0.01 us -> 2.69 us  [shards(): up[kv] = lax.ppermute(up[kv], 'ep', cycle(n_ep))]
    ppermute x3, waiting for transfers between devices: 3.25 us -> 0.75 us  [shards(): down[kv] = lax.ppermute(down[kv], 'ep', cycle(n_ep, n_ep - 1))]
    ppermute x14, waiting for transfers between devices: 6 us -> 4.93 us  [dense_experts(): chunks[chunk] = lax.ppermute(sum_here, axes, way)]
    ppermute x3, starting transfers between devices: 6.03 us -> 7.03 us  [shards(): up[kv] = lax.ppermute(up[kv], 'ep', cycle(n_ep))]
  transfers between devices with their start and end apart: 49 -> 49, of which waited for: 21 -> 22; matrix products, arithmetic and copies ran while one was open for 0% -> 0% of each run, Pallas kernels for 17% -> 17%
where the time goes in v10:
time: 94.6 us; the launch traced here: 94.4 us
  starting transfers between devices  44.3 us (47%)
  waiting for transfers between devices  25.8 us (27%)
  Pallas kernels  20.1 us (21%)
  local copies, waits for them, and re-layouts  3.08 us (3%)
  between operations  1.05 us (1%)
    ppermute x14, starting transfers between devices, dense_experts(): chunks[chunk] = lax.ppermute(sum_here, axes, way)  16.1 us
    pallas_call x6, Pallas kernels, attend(): pl.pallas_call(kernel, out_shape=out_shape, in_specs=in_specs, out_specs=...  8.83 us
    pallas_call x5, Pallas kernels, apply_expert(): pl.pallas_call(kernel, out_shape=[jax.ShapeDtypeStruct((x.shape[0], featu...  7.73 us
    ppermute x3, starting transfers between devices, shards(): up[kv] = lax.ppermute(up[kv], 'ep', cycle(n_ep))  7.03 us
    ppermute x3, starting transfers between devices, shards(): down[kv] = lax.ppermute(down[kv], 'ep', cycle(n_ep, n_ep - 1))  6.18 us
    ppermute x2, waiting for transfers between devices, shards(): came = [lax.ppermute(x, 'hd', cycle(n_hd)) for x in sent]  5.37 us
    ppermute x14, waiting for transfers between devices, dense_experts(): chunks[chunk] = lax.ppermute(sum_here, axes, way)  4.93 us
    ppermute x4, waiting for transfers between devices, dense_experts(): before[1] = lax.ppermute(before[1], axes, back)  4.63 us
  transfers between devices with their start and end apart: 49, of which 22 were waited for; matrix products, arithmetic and copies ran while one was open for 0% of the time, Pallas kernels for 17%

profile of v10, /device:TPU:0, one launch (start us, length us, event | category | flops | bytes accessed | tf_op | source)
XLA Modules:
  0.0 94.4 jit_solution(13779098428792876124)
XLA Ops:
  0.7 1.9 %pack_keys.1 = (bf16[272,256]{1,0:T(8,128)(2,1)}, bf16[272,256]{1,0:T(8,128)(2,1)}) custom-call(s32[1]{0:T(128)S(6)} %copy.14.page_ref, bf16[128,512]{1,0:T(8,128)(2,1)} %ck_ref.1, bf16[128,512]{1,0:T(8,128)(2,1)} %cv_ref.1, bf16[128,512]{1,0:T(8,128)(2,1)} %nk_ref.1, bf16[128,512]{1,0:T(8,128)(2,1)} %nv_ref.1, s32[8,128]{1,0:T(8,128)} %bitcast.18, ...), custom_call_target="tpu_custom_call" | custom-call | tf_op jit(solution)/shard_map/pack_keys/pallas_call | solution.py:91
  3.0 3.0 %collective-permute-start.7 = (bf16[272,256]{1,0:T(8,128)(2,1)}, bf16[272,256]{1,0:T(8,128)(2,1)S(1)}, u32[]{:S(2)}, u32[]{:S(2)}) collective-permute-start(bf16[272,256]{1,0:T(8,128)(2,1)} %get-tuple-element.98.refs_1_), channel_id=1, source_target_pairs={{0,4},{4,8},{8,12},{12,0},{1,5},{5,9},{9,13},{13,1},{2,6},{6,10},{... | collective-permute-start | bytes 417800 | tf_op jit(solution)/shard_map/ppermute | solution.py:695
  6.1 2.0 %collective-permute-start.8 = (bf16[272,256]{1,0:T(8,128)(2,1)}, bf16[272,256]{1,0:T(8,128)(2,1)S(1)}, u32[]{:S(2)}, u32[]{:S(2)}) collective-permute-start(bf16[272,256]{1,0:T(8,128)(2,1)} %get-tuple-element.98.refs_1_), channel_id=1, source_target_pairs={{0,12},{4,0},{8,4},{12,8},{1,13},{5,1},{9,5},{13,9},{2,14},{6,2},{... | collective-permute-start | bytes 417800 | tf_op jit(solution)/shard_map/ppermute | solution.py:698
  10.2 2.9 %collective-permute-start = (bf16[272,256]{1,0:T(8,128)(2,1)}, bf16[272,256]{1,0:T(8,128)(2,1)S(1)}, u32[]{:S(2)}, u32[]{:S(2)}) collective-permute-start(bf16[272,256]{1,0:T(8,128)(2,1)} %get-tuple-element.86.refs_1_.refs_7_), channel_id=1, source_target_pairs={{0,4},{4,8},{8,12},{12,0},{1,5},{5,9},{9,13},{13,1},{2,6},{6,10},{... | collective-permute-start | bytes 417800 | tf_op jit(solution)/shard_map/ppermute | solution.py:695
  15.0 2.1 %collective-permute-start.1 = (bf16[272,256]{1,0:T(8,128)(2,1)}, bf16[272,256]{1,0:T(8,128)(2,1)S(1)}, u32[]{:S(2)}, u32[]{:S(2)}) collective-permute-start(bf16[272,256]{1,0:T(8,128)(2,1)} %get-tuple-element.86.refs_1_.refs_7_), channel_id=1, source_target_pairs={{0,12},{4,0},{8,4},{12,8},{1,13},{5,1},{9,5},{13,9},{2,14},{6,2},{... | collective-permute-start | bytes 417800 | tf_op jit(solution)/shard_map/ppermute | solution.py:698
  19.5 2.1 %collective-permute-start.10 = (bf16[272,256]{1,0:T(8,128)(2,1)S(1)}, bf16[272,256]{1,0:T(8,128)(2,1)S(1)}, u32[]{:S(2)}, u32[]{:S(2)}) collective-permute-start(bf16[272,256]{1,0:T(8,128)(2,1)S(1)} %collective-permute-done.8.refs_3_), channel_id=1, source_target_pairs={{0,12},{4,0},{8,4},{12,8},{1,13},{5,1},{9,5},{13,9},{2,14},{6,2},{... | collective-permute-start | bytes 417800 | tf_op jit(solution)/shard_map/ppermute | solution.py:698
  23.9 1.8 %attend.9 = (f32[1024,128]{1,0:T(8,128)S(1)}, f32[1024,256]{1,0:T(8,128)S(1)}) custom-call(bf16[128,2048]{1,0:T(8,128)(2,1)S(1)} %choose_queries.1.refs_0_, bf16[272,256]{1,0:T(8,128)(2,1)S(1)} %collective-permute-done.7.refs_1_, bf16[272,256]{1,0:T(8,128)(2,1)S(1)} %collective-permute-done.11.refs_2_, bf16[272,256]{1,0:T(8,128)(2,1)S(1)} %collective-permute-done.8.refs_3_, ...), custom_call_target="tpu_custom_call" | custom-call | flops 805306368 | bytes 4194304 | tf_op jit(solution)/shard_map/attend/pallas_call | solution.py:436
  25.8 1.8 %attend.7 = (f32[1024,128]{1,0:T(8,128)S(1)}, f32[1024,256]{1,0:T(8,128)S(1)}) custom-call(bf16[128,2048]{1,0:T(8,128)(2,1)S(1)} %choose_queries.1.refs_0_, bf16[272,256]{1,0:T(8,128)(2,1)S(1)} %collective-permute-done.refs_1_.refs_8_, bf16[272,256]{1,0:T(8,128)(2,1)S(1)} %collective-permute-done.4.refs_2_, ...), custom_call_target="tpu_custom_call" | custom-call | flops 805306368 | bytes 4194304 | tf_op jit(solution)/shard_map/attend/pallas_call | solution.py:436
  27.6 2.7 %collective-permute-done.3.refs_1_.refs_9_ = bf16[272,256]{1,0:T(8,128)(2,1)S(1)} collective-permute-done((bf16[272,256]{1,0:T(8,128)(2,1)S(1)}, bf16[272,256]{1,0:T(8,128)(2,1)S(1)}, u32[]{:S(2)}, u32[]{:S(2)}) %collective-permute-start.3) | collective-permute-done | bytes 139296 | tf_op jit(solution)/shard_map/ppermute | solution.py:695
  30.3 1.4 %collective-permute-done.6.refs_2_ = bf16[272,256]{1,0:T(8,128)(2,1)S(1)} collective-permute-done((bf16[272,256]{1,0:T(8,128)(2,1)S(1)}, bf16[272,256]{1,0:T(8,128)(2,1)S(1)}, u32[]{:S(2)}, u32[]{:S(2)}) %collective-permute-start.6) | collective-permute-done | bytes 139296 | tf_op jit(solution)/shard_map/ppermute | solution.py:35
  33.3 2.3 %attend.11 = (f32[32,2048]{1,0:T(8,128)S(1)}, f32[32,2048]{1,0:T(8,128)S(1)}, bf16[32,2176]{1,0:T(8,128)(2,1)S(1)}, bf16[32,2048]{1,0:T(8,128)(2,1)S(1)}, bf16[32,128]{1,0:T(8,128)(2,1)S(1)}) custom-call(bf16[128,2048]{1,0:T(8,128)(2,1)S(1)} %choose_queries.1.refs_0_, bf16[272,256]{1,0:T(8,128)(2,1)S(1)} %collective-permute-done.10.refs_1_, ...), custom_call_target="tpu_custom_call" | custom-call | flops 402653184 | bytes 4194304 | tf_op jit(solution)/shard_map/attend/pallas_call | solution.py:436
  35.6 1.5 %collective-permute-start.15 = (bf16[32,2176]{1,0:T(8,128)(2,1)S(1)}, bf16[32,2176]{1,0:T(8,128)(2,1)S(1)}, u32[]{:S(2)}, u32[]{:S(2)}) collective-permute-start(bf16[32,2176]{1,0:T(8,128)(2,1)S(1)} %get-tuple-element.118), channel_id=1, source_target_pairs={{0,2},{2,0},{1,3},{3,1},{4,6},{6,4},{5,7},{7,5},{8,10},{10,8},{9,1... | collective-permute-start | bytes 417800 | tf_op jit(solution)/shard_map/ppermute | solution.py:738
  38.5 3.6 %collective-permute-done.15.refs_1_.came_ref = bf16[32,2176]{1,0:T(8,128)(2,1)S(1)} collective-permute-done((bf16[32,2176]{1,0:T(8,128)(2,1)S(1)}, bf16[32,2176]{1,0:T(8,128)(2,1)S(1)}, u32[]{:S(2)}, u32[]{:S(2)}) %collective-permute-start.15) | collective-permute-done | bytes 139296 | tf_op jit(solution)/shard_map/ppermute | solution.py:738
  42.4 1.8 %collective-permute-done.17.refs_1_ = bf16[32,2048]{1,0:T(8,128)(2,1)S(1)} collective-permute-done((bf16[32,2048]{1,0:T(8,128)(2,1)S(1)}, bf16[32,2048]{1,0:T(8,128)(2,1)S(1)}, u32[]{:S(2)}, u32[]{:S(2)}) %collective-permute-start.17) | collective-permute-done | bytes 131104 | tf_op jit(solution)/shard_map/ppermute | solution.py:738
  46.5 1.6 %collective-permute-done.18.refs_0_ = bf16[32,2048]{1,0:T(8,128)(2,1)S(1)} collective-permute-done((bf16[32,2048]{1,0:T(8,128)(2,1)S(1)}, bf16[32,2048]{1,0:T(8,128)(2,1)S(1)}, u32[]{:S(2)}, u32[]{:S(2)}) %collective-permute-start.18) | collective-permute-done | bytes 131104 | tf_op jit(solution)/shard_map/ppermute | solution.py:535
  48.1 2.0 %collective-permute-done.22.refs_1_ = bf16[32,2048]{1,0:T(8,128)(2,1)S(1)} collective-permute-done((bf16[32,2048]{1,0:T(8,128)(2,1)S(1)}, bf16[32,2048]{1,0:T(8,128)(2,1)S(1)}, u32[]{:S(2)}, u32[]{:S(2)}) %collective-permute-start.22) | collective-permute-done | bytes 131104 | tf_op jit(solution)/shard_map/ppermute | solution.py:536
  50.4 1.4 %collective-permute-start.26 = (bf16[32,2048]{1,0:T(8,128)(2,1)S(1)}, bf16[32,2048]{1,0:T(8,128)(2,1)S(1)}, u32[]{:S(2)}, u32[]{:S(2)}) collective-permute-start(bf16[32,2048]{1,0:T(8,128)(2,1)S(1)} %collective-permute-done.25.refs_2_), channel_id=1, source_target_pairs={{0,5},{1,4},{4,9},{5,8},{8,13},{9,12},{12,15},{13,14},{14,11},{15,... | collective-permute-start | bytes 393224 | tf_op jit(solution)/shard_map/ppermute | solution.py:538
  56.1 1.6 %apply_expert.5 = (f32[32,2048]{1,0:T(8,128)S(1)}, f32[32,2048]{1,0:T(8,128)S(1)}, f32[32,2048]{1,0:T(8,128)S(1)}, f32[32,2048]{1,0:T(8,128)S(1)}) custom-call(bf16[32,2048]{1,0:T(8,128)(2,1)S(1)} %collective-permute-done.18.refs_0_, bf16[32,2048]{1,0:T(8,128)(2,1)S(1)} %collective-permute-done.22.refs_1_, ...), custom_call_target="tpu_custom_call" | custom-call | flops 603979776 | bytes 6291456 | tf_op jit(solution)/shard_map/apply_expert/pallas_call | solution.py:491
  62.0 1.6 %apply_expert.6 = (f32[32,2048]{1,0:T(8,128)S(1)}, f32[32,2048]{1,0:T(8,128)S(1)}, f32[32,2048]{1,0:T(8,128)S(1)}, f32[32,2048]{1,0:T(8,128)S(1)}) custom-call(bf16[32,2048]{1,0:T(8,128)(2,1)S(1)} %collective-permute-done.19.refs_0_, bf16[32,2048]{1,0:T(8,128)(2,1)S(1)} %collective-permute-done.23.refs_1_, ...), custom_call_target="tpu_custom_call" | custom-call | flops 603979776 | bytes 6291456 | tf_op jit(solution)/shard_map/apply_expert/pallas_call | solution.py:491
  64.5 1.6 %apply_expert.7 = (f32[32,2048]{1,0:T(8,128)S(1)}, f32[32,2048]{1,0:T(8,128)S(1)}, f32[32,2048]{1,0:T(8,128)S(1)}, f32[32,2048]{1,0:T(8,128)S(1)}) custom-call(bf16[32,2048]{1,0:T(8,128)(2,1)S(1)} %collective-permute-done.20.refs_0_, bf16[32,2048]{1,0:T(8,128)(2,1)S(1)} %collective-permute-done.24.refs_1_, ...), custom_call_target="tpu_custom_call" | custom-call | flops 603979776 | bytes 6291456 | tf_op jit(solution)/shard_map/apply_expert/pallas_call | solution.py:491
  67.3 1.5 %apply_expert.8 = (f32[32,2048]{1,0:T(8,128)S(1)}, f32[32,2048]{1,0:T(8,128)S(1)}) custom-call(bf16[32,2048]{1,0:T(8,128)(2,1)S(1)} %collective-permute-done.21.refs_0_, bf16[32,2048]{1,0:T(8,128)(2,1)S(1)} %collective-permute-done.33.refs_1_, f32[128,128]{1,0:T(8,128)S(1)} %gates_by_chip.1.refs_4_.refs_2_, bf16[2,192,2048]{2,1,0:T(8,128)(2,1)S(1)} %bitcast.9, ...), custom_call_target="tpu_custom_call" | custom-call | flops 301989888 | bytes 6291456 | tf_op jit(solution)/shard_map/apply_expert/pallas_call | solution.py:491
  69.0 1.8 %collective-permute-start.34 = (bf16[32,2048]{1,0:T(8,128)(2,1)S(1)}, bf16[32,2048]{1,0:T(8,128)(2,1)S(1)}, u32[]{:S(2)}, u32[]{:S(2)}) collective-permute-start(bf16[32,2048]{1,0:T(8,128)(2,1)S(1)} %convert_element_type.12), channel_id=1, source_target_pairs={{5,0},{4,1},{9,4},{8,5},{13,8},{12,9},{15,12},{14,13},{11,14},{10,... | collective-permute-start | bytes 393224 | tf_op jit(solution)/shard_map/ppermute | solution.py:563
  70.9 1.8 %collective-permute-start.38 = (bf16[32,2048]{1,0:T(8,128)(2,1)S(1)}, bf16[32,2048]{1,0:T(8,128)(2,1)S(1)}, u32[]{:S(2)}, u32[]{:S(2)}) collective-permute-start(bf16[32,2048]{1,0:T(8,128)(2,1)S(1)} %convert_element_type.13), channel_id=1, source_target_pairs={{5,0},{4,1},{9,4},{8,5},{13,8},{12,9},{15,12},{14,13},{11,14},{10,... | collective-permute-start | bytes 393224 | tf_op jit(solution)/shard_map/ppermute | solution.py:563
  72.6 1.8 %collective-permute-done.44.came_ref = bf16[32,2048]{1,0:T(8,128)(2,1)S(1)} collective-permute-done((bf16[32,2048]{1,0:T(8,128)(2,1)S(1)}, bf16[32,2048]{1,0:T(8,128)(2,1)S(1)}, u32[]{:S(2)}, u32[]{:S(2)}) %collective-permute-start.44) | collective-permute-done | bytes 131104 | tf_op jit(solution)/shard_map/ppermute | solution.py:563
  75.1 1.8 %collective-permute-start.35 = (bf16[32,2048]{1,0:T(8,128)(2,1)S(1)}, bf16[32,2048]{1,0:T(8,128)(2,1)S(1)}, u32[]{:S(2)}, u32[]{:S(2)}) collective-permute-start(bf16[32,2048]{1,0:T(8,128)(2,1)S(1)} %add_share.10), channel_id=1, source_target_pairs={{5,0},{4,1},{9,4},{8,5},{13,8},{12,9},{15,12},{14,13},{11,14},{10,... | collective-permute-start | bytes 393224 | tf_op jit(solution)/shard_map/ppermute | solution.py:563
  77.4 1.8 %collective-permute-start.39 = (bf16[32,2048]{1,0:T(8,128)(2,1)S(1)}, bf16[32,2048]{1,0:T(8,128)(2,1)S(1)}, u32[]{:S(2)}, u32[]{:S(2)}) collective-permute-start(bf16[32,2048]{1,0:T(8,128)(2,1)S(1)} %add_share.13), channel_id=1, source_target_pairs={{5,0},{4,1},{9,4},{8,5},{13,8},{12,9},{15,12},{14,13},{11,14},{10,... | collective-permute-start | bytes 393224 | tf_op jit(solution)/shard_map/ppermute | solution.py:563
  79.5 1.6 %collective-permute-start.46 = (bf16[32,2048]{1,0:T(8,128)(2,1)S(1)}, bf16[32,2048]{1,0:T(8,128)(2,1)S(1)}, u32[]{:S(2)}, u32[]{:S(2)}) collective-permute-start(bf16[32,2048]{1,0:T(8,128)(2,1)S(1)} %add_share.18), channel_id=1, source_target_pairs={{0,5},{1,4},{4,9},{5,8},{8,13},{9,12},{12,15},{13,14},{14,11},{15,... | collective-permute-start | bytes 393224 | tf_op jit(solution)/shard_map/ppermute | solution.py:563
  81.2 1.8 %collective-permute-start.36 = (bf16[32,2048]{1,0:T(8,128)(2,1)S(1)}, bf16[32,2048]{1,0:T(8,128)(2,1)S(1)}, u32[]{:S(2)}, u32[]{:S(2)}) collective-permute-start(bf16[32,2048]{1,0:T(8,128)(2,1)S(1)} %add_share.11), channel_id=1, source_target_pairs={{5,0},{4,1},{9,4},{8,5},{13,8},{12,9},{15,12},{14,13},{11,14},{10,... | collective-permute-start | bytes 393224 | tf_op jit(solution)/shard_map/ppermute | solution.py:563
  83.7 1.8 %collective-permute-start.40 = (bf16[32,2048]{1,0:T(8,128)(2,1)S(1)}, bf16[32,2048]{1,0:T(8,128)(2,1)S(1)}, u32[]{:S(2)}, u32[]{:S(2)}) collective-permute-start(bf16[32,2048]{1,0:T(8,128)(2,1)S(1)} %add_share.14), channel_id=1, source_target_pairs={{5,0},{4,1},{9,4},{8,5},{13,8},{12,9},{15,12},{14,13},{11,14},{10,... | collective-permute-start | bytes 393224 | tf_op jit(solution)/shard_map/ppermute | solution.py:563
  86.8 1.5 %collective-permute-start.37 = (bf16[32,2048]{1,0:T(8,128)(2,1)S(1)}, bf16[32,2048]{1,0:T(8,128)(2,1)S(1)}, u32[]{:S(2)}, u32[]{:S(2)}) collective-permute-start(bf16[32,2048]{1,0:T(8,128)(2,1)S(1)} %add_share.12), channel_id=1, source_target_pairs={{5,0},{4,1},{9,4},{8,5},{13,8},{12,9},{15,12},{14,13},{11,14},{10,... | collective-permute-start | bytes 393224 | tf_op jit(solution)/shard_map/ppermute | solution.py:563
  88.3 1.5 %apply_expert.9 = (f32[32,2048]{1,0:T(8,128)S(1)}, f32[32,2048]{1,0:T(8,128)S(1)}) custom-call(bf16[32,2048]{1,0:T(8,128)(2,1)S(1)} %get-tuple-element.149.refs_0_, bf16[32,2048]{1,0:T(8,128)(2,1)S(1)} %get-tuple-element.150.refs_1_, f32[128,128]{1,0:T(8,128)S(1)} %gates_by_chip.1.refs_4_.refs_2_, bf16[2,192,2048]{2,1,0:T(8,128)(2,1)S(1)} %bitcast.10, ...), custom_call_target="tpu_custom_call" | custom-call | flops 301989888 | bytes 6291456 | tf_op jit(solution)/shard_map/apply_expert/pallas_call | solution.py:491
  89.8 1.4 %collective-permute-done.47.refs_7_ = bf16[32,2048]{1,0:T(8,128)(2,1)S(1)} collective-permute-done((bf16[32,2048]{1,0:T(8,128)(2,1)S(1)}, bf16[32,2048]{1,0:T(8,128)(2,1)S(1)}, u32[]{:S(2)}, u32[]{:S(2)}) %collective-permute-start.47) | collective-permute-done | bytes 131104 | tf_op jit(solution)/shard_map/ppermute | solution.py:563
  (118 shorter events, 32.9 us)
Async XLA Ops:
  2.5 30.7 %collective-permute-start.14 = (bf16[2048,1024]{1,0:T(8,128)(2,1)}, bf16[2048,1024]{1,0:T(8,128)(2,1)S(1)}, u32[]{:S(2)}, u32[]{:S(2)}) collective-permute-start(bf16[2048,1024]{1,0:T(8,128)(2,1)} %refs_5_), channel_id=1, source_target_pairs={{0,1},{1,0},{2,3},{3,2},{4,5},{5,4},{6,7},{7,6},{8,9},{9,8},{10,11... | collective-permute-start | bytes 12582920 | tf_op jit(solution)/shard_map/ppermute | solution.py:35
  3.0 7.2 %collective-permute-start.9 = (bf16[272,256]{1,0:T(8,128)(2,1)}, bf16[272,256]{1,0:T(8,128)(2,1)S(1)}, u32[]{:S(2)}, u32[]{:S(2)}) collective-permute-start(bf16[272,256]{1,0:T(8,128)(2,1)} %get-tuple-element.98.refs_1_), channel_id=1, source_target_pairs={{0,1},{1,0},{2,3},{3,2},{4,5},{5,4},{6,7},{7,6},{8,9},{9,8},{10,11... | collective-permute-start | bytes 417800 | tf_op jit(solution)/shard_map/ppermute | solution.py:35
  3.0 11.9 %collective-permute-start.7 = (bf16[272,256]{1,0:T(8,128)(2,1)}, bf16[272,256]{1,0:T(8,128)(2,1)S(1)}, u32[]{:S(2)}, u32[]{:S(2)}) collective-permute-start(bf16[272,256]{1,0:T(8,128)(2,1)} %get-tuple-element.98.refs_1_), channel_id=1, source_target_pairs={{0,4},{4,8},{8,12},{12,0},{1,5},{5,9},{9,13},{13,1},{2,6},{6,10},{... | collective-permute-start | bytes 417800 | tf_op jit(solution)/shard_map/ppermute | solution.py:695
  6.1 11.0 %collective-permute-start.8 = (bf16[272,256]{1,0:T(8,128)(2,1)}, bf16[272,256]{1,0:T(8,128)(2,1)S(1)}, u32[]{:S(2)}, u32[]{:S(2)}) collective-permute-start(bf16[272,256]{1,0:T(8,128)(2,1)} %get-tuple-element.98.refs_1_), channel_id=1, source_target_pairs={{0,12},{4,0},{8,4},{12,8},{1,13},{5,1},{9,5},{13,9},{2,14},{6,2},{... | collective-permute-start | bytes 417800 | tf_op jit(solution)/shard_map/ppermute | solution.py:698
  8.1 9.0 %collective-permute-start.2 = (bf16[272,256]{1,0:T(8,128)(2,1)}, bf16[272,256]{1,0:T(8,128)(2,1)S(1)}, u32[]{:S(2)}, u32[]{:S(2)}) collective-permute-start(bf16[272,256]{1,0:T(8,128)(2,1)} %get-tuple-element.86.refs_1_.refs_7_), channel_id=1, source_target_pairs={{0,1},{1,0},{2,3},{3,2},{4,5},{5,4},{6,7},{7,6},{8,9},{9,8},{10,11... | collective-permute-start | bytes 417800 | tf_op jit(solution)/shard_map/ppermute | solution.py:35
  10.2 9.3 %collective-permute-start = (bf16[272,256]{1,0:T(8,128)(2,1)}, bf16[272,256]{1,0:T(8,128)(2,1)S(1)}, u32[]{:S(2)}, u32[]{:S(2)}) collective-permute-start(bf16[272,256]{1,0:T(8,128)(2,1)} %get-tuple-element.86.refs_1_.refs_7_), channel_id=1, source_target_pairs={{0,4},{4,8},{8,12},{12,0},{1,5},{5,9},{9,13},{13,1},{2,6},{6,10},{... | collective-permute-start | bytes 417800 | tf_op jit(solution)/shard_map/ppermute | solution.py:695
  15.0 7.3 %collective-permute-start.1 = (bf16[272,256]{1,0:T(8,128)(2,1)}, bf16[272,256]{1,0:T(8,128)(2,1)S(1)}, u32[]{:S(2)}, u32[]{:S(2)}) collective-permute-start(bf16[272,256]{1,0:T(8,128)(2,1)} %get-tuple-element.86.refs_1_.refs_7_), channel_id=1, source_target_pairs={{0,12},{4,0},{8,4},{12,8},{1,13},{5,1},{9,5},{13,9},{2,14},{6,2},{... | collective-permute-start | bytes 417800 | tf_op jit(solution)/shard_map/ppermute | solution.py:698
  17.1 5.8 %collective-permute-start.11 = (bf16[272,256]{1,0:T(8,128)(2,1)S(1)}, bf16[272,256]{1,0:T(8,128)(2,1)S(1)}, u32[]{:S(2)}, u32[]{:S(2)}) collective-permute-start(bf16[272,256]{1,0:T(8,128)(2,1)S(1)} %collective-permute-done.7.refs_1_), channel_id=1, source_target_pairs={{0,1},{1,0},{2,3},{3,2},{4,5},{5,4},{6,7},{7,6},{8,9},{9,8},{10,11... | collective-permute-start | bytes 417800 | tf_op jit(solution)/shard_map/ppermute | solution.py:35
  19.5 6.2 %collective-permute-start.10 = (bf16[272,256]{1,0:T(8,128)(2,1)S(1)}, bf16[272,256]{1,0:T(8,128)(2,1)S(1)}, u32[]{:S(2)}, u32[]{:S(2)}) collective-permute-start(bf16[272,256]{1,0:T(8,128)(2,1)S(1)} %collective-permute-done.8.refs_3_), channel_id=1, source_target_pairs={{0,12},{4,0},{8,4},{12,8},{1,13},{5,1},{9,5},{13,9},{2,14},{6,2},{... | collective-permute-start | bytes 417800 | tf_op jit(solution)/shard_map/ppermute | solution.py:698
  22.8 7.4 %collective-permute-start.3 = (bf16[272,256]{1,0:T(8,128)(2,1)S(1)}, bf16[272,256]{1,0:T(8,128)(2,1)S(1)}, u32[]{:S(2)}, u32[]{:S(2)}) collective-permute-start(bf16[272,256]{1,0:T(8,128)(2,1)S(1)} %collective-permute-done.refs_1_.refs_8_), channel_id=1, source_target_pairs={{0,4},{4,8},{8,12},{12,0},{1,5},{5,9},{9,13},{13,1},{2,6},{6,10},{... | collective-permute-start | bytes 417800 | tf_op jit(solution)/shard_map/ppermute | solution.py:695
  31.7 24.5 %collective-permute-start.28 = (bf16[2,192,2048]{2,1,0:T(8,128)(2,1)S(1)}, bf16[2,192,2048]{2,1,0:T(8,128)(2,1)S(1)}, u32[]{:S(2)}, u32[]{:S(2)}) collective-permute-start(bf16[2,192,2048]{2,1,0:T(8,128)(2,1)S(1)} %bitcast.5), channel_id=1, source_target_pairs={{0,1},{1,0},{2,3},{3,2},{4,5},{5,4},{6,7},{7,6},{8,9},{9,8},{10,11... | collective-permute-start | bytes 4718600 | tf_op jit(solution)/shard_map/ppermute | solution.py:35
  31.8 14.3 %collective-permute-start.29 = (bf16[192,2048]{1,0:T(8,128)(2,1)S(1)}, bf16[192,2048]{1,0:T(8,128)(2,1)S(1)}, u32[]{:S(2)}, u32[]{:S(2)}) collective-permute-start(bf16[192,2048]{1,0:T(8,128)(2,1)S(1)} %bitcast.11), channel_id=1, source_target_pairs={{0,1},{1,0},{2,3},{3,2},{4,5},{5,4},{6,7},{7,6},{8,9},{9,8},{10,11... | collective-permute-start | bytes 2359304 | tf_op jit(solution)/shard_map/ppermute | solution.py:35
  35.6 6.6 %collective-permute-start.15 = (bf16[32,2176]{1,0:T(8,128)(2,1)S(1)}, bf16[32,2176]{1,0:T(8,128)(2,1)S(1)}, u32[]{:S(2)}, u32[]{:S(2)}) collective-permute-start(bf16[32,2176]{1,0:T(8,128)(2,1)S(1)} %get-tuple-element.118), channel_id=1, source_target_pairs={{0,2},{2,0},{1,3},{3,1},{4,6},{6,4},{5,7},{7,5},{8,10},{10,8},{9,1... | collective-permute-start | bytes 417800 | tf_op jit(solution)/shard_map/ppermute | solution.py:738
  37.2 6.9 %collective-permute-start.17 = (bf16[32,2048]{1,0:T(8,128)(2,1)S(1)}, bf16[32,2048]{1,0:T(8,128)(2,1)S(1)}, u32[]{:S(2)}, u32[]{:S(2)}) collective-permute-start(bf16[32,2048]{1,0:T(8,128)(2,1)S(1)} %get-tuple-element.124), channel_id=1, source_target_pairs={{0,2},{2,0},{1,3},{3,1},{4,6},{6,4},{5,7},{7,5},{8,10},{10,8},{9,1... | collective-permute-start | bytes 393224 | tf_op jit(solution)/shard_map/ppermute | solution.py:738
  42.3 5.8 %collective-permute-start.18 = (bf16[32,2048]{1,0:T(8,128)(2,1)S(1)}, bf16[32,2048]{1,0:T(8,128)(2,1)S(1)}, u32[]{:S(2)}, u32[]{:S(2)}) collective-permute-start(bf16[32,2048]{1,0:T(8,128)(2,1)S(1)} %get-tuple-element.149.refs_0_), channel_id=1, source_target_pairs={{0,5},{1,4},{4,9},{5,8},{8,13},{9,12},{12,15},{13,14},{14,11},{15,... | collective-permute-start | bytes 393224 | tf_op jit(solution)/shard_map/ppermute | solution.py:535
  44.3 5.8 %collective-permute-start.22 = (bf16[32,2048]{1,0:T(8,128)(2,1)S(1)}, bf16[32,2048]{1,0:T(8,128)(2,1)S(1)}, u32[]{:S(2)}, u32[]{:S(2)}) collective-permute-start(bf16[32,2048]{1,0:T(8,128)(2,1)S(1)} %get-tuple-element.150.refs_1_), channel_id=1, source_target_pairs={{5,0},{4,1},{9,4},{8,5},{13,8},{12,9},{15,12},{14,13},{11,14},{10,... | collective-permute-start | bytes 393224 | tf_op jit(solution)/shard_map/ppermute | solution.py:536
  46.1 6.4 %collective-permute-start.27 = (bf16[32,2048]{1,0:T(8,128)(2,1)S(1)}, bf16[32,2048]{1,0:T(8,128)(2,1)S(1)}, u32[]{:S(2)}, u32[]{:S(2)}) collective-permute-start(bf16[32,2048]{1,0:T(8,128)(2,1)S(1)} %get-tuple-element.149.refs_0_), channel_id=1, source_target_pairs={{5,0},{4,1},{9,4},{8,5},{13,8},{12,9},{15,12},{14,13},{11,14},{10,... | collective-permute-start | bytes 393224 | tf_op jit(solution)/shard_map/ppermute | solution.py:539
  50.4 7.3 %collective-permute-start.26 = (bf16[32,2048]{1,0:T(8,128)(2,1)S(1)}, bf16[32,2048]{1,0:T(8,128)(2,1)S(1)}, u32[]{:S(2)}, u32[]{:S(2)}) collective-permute-start(bf16[32,2048]{1,0:T(8,128)(2,1)S(1)} %collective-permute-done.25.refs_2_), channel_id=1, source_target_pairs={{0,5},{1,4},{4,9},{5,8},{8,13},{9,12},{12,15},{13,14},{14,11},{15,... | collective-permute-start | bytes 393224 | tf_op jit(solution)/shard_map/ppermute | solution.py:538
  52.5 6.4 %collective-permute-start.31 = (bf16[32,2048]{1,0:T(8,128)(2,1)S(1)}, bf16[32,2048]{1,0:T(8,128)(2,1)S(1)}, u32[]{:S(2)}, u32[]{:S(2)}) collective-permute-start(bf16[32,2048]{1,0:T(8,128)(2,1)S(1)} %collective-permute-done.27.refs_3_), channel_id=1, source_target_pairs={{5,0},{4,1},{9,4},{8,5},{13,8},{12,9},{15,12},{14,13},{11,14},{10,... | collective-permute-start | bytes 393224 | tf_op jit(solution)/shard_map/ppermute | solution.py:539
  53.6 5.9 %collective-permute-start.20 = (bf16[32,2048]{1,0:T(8,128)(2,1)S(1)}, bf16[32,2048]{1,0:T(8,128)(2,1)S(1)}, u32[]{:S(2)}, u32[]{:S(2)}) collective-permute-start(bf16[32,2048]{1,0:T(8,128)(2,1)S(1)} %collective-permute-done.19.refs_0_), channel_id=1, source_target_pairs={{0,5},{1,4},{4,9},{5,8},{8,13},{9,12},{12,15},{13,14},{14,11},{15,... | collective-permute-start | bytes 393224 | tf_op jit(solution)/shard_map/ppermute | solution.py:535
  57.7 5.8 %collective-permute-start.30 = (bf16[32,2048]{1,0:T(8,128)(2,1)S(1)}, bf16[32,2048]{1,0:T(8,128)(2,1)S(1)}, u32[]{:S(2)}, u32[]{:S(2)}) collective-permute-start(bf16[32,2048]{1,0:T(8,128)(2,1)S(1)} %collective-permute-done.26.refs_2_), channel_id=1, source_target_pairs={{0,5},{1,4},{4,9},{5,8},{8,13},{9,12},{12,15},{13,14},{14,11},{15,... | collective-permute-start | bytes 393224 | tf_op jit(solution)/shard_map/ppermute | solution.py:538
  59.5 6.6 %collective-permute-start.21 = (bf16[32,2048]{1,0:T(8,128)(2,1)S(1)}, bf16[32,2048]{1,0:T(8,128)(2,1)S(1)}, u32[]{:S(2)}, u32[]{:S(2)}) collective-permute-start(bf16[32,2048]{1,0:T(8,128)(2,1)S(1)} %collective-permute-done.20.refs_0_), channel_id=1, source_target_pairs={{0,5},{1,4},{4,9},{5,8},{8,13},{9,12},{12,15},{13,14},{14,11},{15,... | collective-permute-start | bytes 393224 | tf_op jit(solution)/shard_map/ppermute | solution.py:535
  61.0 6.4 %collective-permute-start.33 = (bf16[32,2048]{1,0:T(8,128)(2,1)S(1)}, bf16[32,2048]{1,0:T(8,128)(2,1)S(1)}, u32[]{:S(2)}, u32[]{:S(2)}) collective-permute-start(bf16[32,2048]{1,0:T(8,128)(2,1)S(1)} %collective-permute-done.24.refs_1_), channel_id=1, source_target_pairs={{5,0},{4,1},{9,4},{8,5},{13,8},{12,9},{15,12},{14,13},{11,14},{10,... | collective-permute-start | bytes 393224 | tf_op jit(solution)/shard_map/ppermute | solution.py:536
  69.0 6.1 %collective-permute-start.34 = (bf16[32,2048]{1,0:T(8,128)(2,1)S(1)}, bf16[32,2048]{1,0:T(8,128)(2,1)S(1)}, u32[]{:S(2)}, u32[]{:S(2)}) collective-permute-start(bf16[32,2048]{1,0:T(8,128)(2,1)S(1)} %convert_element_type.12), channel_id=1, source_target_pairs={{5,0},{4,1},{9,4},{8,5},{13,8},{12,9},{15,12},{14,13},{11,14},{10,... | collective-permute-start | bytes 393224 | tf_op jit(solution)/shard_map/ppermute | solution.py:563
  70.8 6.5 %collective-permute-start.41 = (bf16[32,2048]{1,0:T(8,128)(2,1)S(1)}, bf16[32,2048]{1,0:T(8,128)(2,1)S(1)}, u32[]{:S(2)}, u32[]{:S(2)}) collective-permute-start(bf16[32,2048]{1,0:T(8,128)(2,1)S(1)} %convert_element_type.14), channel_id=1, source_target_pairs={{0,5},{1,4},{4,9},{5,8},{8,13},{9,12},{12,15},{13,14},{14,11},{15,... | collective-permute-start | bytes 393224 | tf_op jit(solution)/shard_map/ppermute | solution.py:563
  70.9 6.5 %collective-permute-start.38 = (bf16[32,2048]{1,0:T(8,128)(2,1)S(1)}, bf16[32,2048]{1,0:T(8,128)(2,1)S(1)}, u32[]{:S(2)}, u32[]{:S(2)}) collective-permute-start(bf16[32,2048]{1,0:T(8,128)(2,1)S(1)} %convert_element_type.13), channel_id=1, source_target_pairs={{5,0},{4,1},{9,4},{8,5},{13,8},{12,9},{15,12},{14,13},{11,14},{10,... | collective-permute-start | bytes 393224 | tf_op jit(solution)/shard_map/ppermute | solution.py:563
  75.1 6.1 %collective-permute-start.35 = (bf16[32,2048]{1,0:T(8,128)(2,1)S(1)}, bf16[32,2048]{1,0:T(8,128)(2,1)S(1)}, u32[]{:S(2)}, u32[]{:S(2)}) collective-permute-start(bf16[32,2048]{1,0:T(8,128)(2,1)S(1)} %add_share.10), channel_id=1, source_target_pairs={{5,0},{4,1},{9,4},{8,5},{13,8},{12,9},{15,12},{14,13},{11,14},{10,... | collective-permute-start | bytes 393224 | tf_op jit(solution)/shard_map/ppermute | solution.py:563
  77.4 6.3 %collective-permute-start.39 = (bf16[32,2048]{1,0:T(8,128)(2,1)S(1)}, bf16[32,2048]{1,0:T(8,128)(2,1)S(1)}, u32[]{:S(2)}, u32[]{:S(2)}) collective-permute-start(bf16[32,2048]{1,0:T(8,128)(2,1)S(1)} %add_share.13), channel_id=1, source_target_pairs={{5,0},{4,1},{9,4},{8,5},{13,8},{12,9},{15,12},{14,13},{11,14},{10,... | collective-permute-start | bytes 393224 | tf_op jit(solution)/shard_map/ppermute | solution.py:563
  79.5 5.9 %collective-permute-start.46 = (bf16[32,2048]{1,0:T(8,128)(2,1)S(1)}, bf16[32,2048]{1,0:T(8,128)(2,1)S(1)}, u32[]{:S(2)}, u32[]{:S(2)}) collective-permute-start(bf16[32,2048]{1,0:T(8,128)(2,1)S(1)} %add_share.18), channel_id=1, source_target_pairs={{0,5},{1,4},{4,9},{5,8},{8,13},{9,12},{12,15},{13,14},{14,11},{15,... | collective-permute-start | bytes 393224 | tf_op jit(solution)/shard_map/ppermute | solution.py:563
  83.0 6.8 %collective-permute-start.43 = (bf16[32,2048]{1,0:T(8,128)(2,1)S(1)}, bf16[32,2048]{1,0:T(8,128)(2,1)S(1)}, u32[]{:S(2)}, u32[]{:S(2)}) collective-permute-start(bf16[32,2048]{1,0:T(8,128)(2,1)S(1)} %add_share.16), channel_id=1, source_target_pairs={{0,5},{1,4},{4,9},{5,8},{8,13},{9,12},{12,15},{13,14},{14,11},{15,... | collective-permute-start | bytes 393224 | tf_op jit(solution)/shard_map/ppermute | solution.py:563
  83.7 6.1 %collective-permute-start.40 = (bf16[32,2048]{1,0:T(8,128)(2,1)S(1)}, bf16[32,2048]{1,0:T(8,128)(2,1)S(1)}, u32[]{:S(2)}, u32[]{:S(2)}) collective-permute-start(bf16[32,2048]{1,0:T(8,128)(2,1)S(1)} %add_share.14), channel_id=1, source_target_pairs={{5,0},{4,1},{9,4},{8,5},{13,8},{12,9},{15,12},{14,13},{11,14},{10,... | collective-permute-start | bytes 393224 | tf_op jit(solution)/shard_map/ppermute | solution.py:563
  85.5 5.7 %collective-permute-start.47 = (bf16[32,2048]{1,0:T(8,128)(2,1)S(1)}, bf16[32,2048]{1,0:T(8,128)(2,1)S(1)}, u32[]{:S(2)}, u32[]{:S(2)}) collective-permute-start(bf16[32,2048]{1,0:T(8,128)(2,1)S(1)} %add_share.19), channel_id=1, source_target_pairs={{0,5},{1,4},{4,9},{5,8},{8,13},{9,12},{12,15},{13,14},{14,11},{15,... | collective-permute-start | bytes 393224 | tf_op jit(solution)/shard_map/ppermute | solution.py:563
  (26 other events, 153.9 us)

commit v11 on v10

--- a/solution.py
+++ b/solution.py
@@ -447,7 +447,7 @@
     )(*operands)
 
 
-def apply_expert(inputs, origins, gate_table, gate_up, w_down):
+def apply_expert(inputs, origins, gate_table, gate_up, w_down, kind=jnp.float32):
     features = w_down[0].shape[1]
     hidden = w_down[0].shape[0]
     rows = sum(x.shape[0] for x in inputs)
@@ -483,14 +483,14 @@
         total = gate * total.astype(jnp.bfloat16).astype(jnp.float32)
         first = 0
         for out_ref in out_refs:
-            out_ref[...] = total[first : first + out_ref.shape[0]]
+            out_ref[...] = total[first : first + out_ref.shape[0]].astype(kind)
             first += out_ref.shape[0]
 
     vmem = pl.BlockSpec(memory_space=pltpu.VMEM)
     operands = list(inputs) + [gate_table] + list(gate_up) + list(w_down)
     return pl.pallas_call(
         kernel,
-        out_shape=[jax.ShapeDtypeStruct((x.shape[0], features), jnp.float32) for x in inputs],
+        out_shape=[jax.ShapeDtypeStruct((x.shape[0], features), kind) for x in inputs],
         in_specs=[vmem] * len(operands),
         out_specs=[vmem] * len(inputs),
         compiler_params=pltpu.CompilerParams(vmem_limit_bytes=16 * MIB),
@@ -544,7 +544,7 @@
             outs.append(out)
         waiting = [behind[0], before[1]] + ([behind[1], before[0]] if hop < reach else [])
         origins = [(-hop, 0), (hop, 1), (-hop, 1), (hop, 0)][: len(waiting)]
-    outs.append(apply_expert(waiting, origins, gate_table, gate_up, w_down))
+    outs.append(apply_expert(waiting, origins, gate_table, gate_up, w_down, jnp.bfloat16))
     to_back, to_ahead = [None, None], [None, None]
     for hop in range(reach, 0, -1):
         shares = outs[hop]

time: 94.6 us -> 94.6 us (level)
  transfers between devices with their start and end apart: 49 -> 49, of which waited for: 22 -> 23; matrix products, arithmetic and copies ran while one was open for 0% -> 0% of each run, Pallas kernels for 17% -> 17%
where the time goes in v11:
time: 94.6 us; the launch traced here: 94.3 us
  starting transfers between devices  44 us (47%)
  waiting for transfers between devices  26.2 us (28%)
  Pallas kernels  20.1 us (21%)
  local copies, waits for them, and re-layouts  3.08 us (3%)
  between operations  1.04 us (1%)
    ppermute x14, starting transfers between devices, dense_experts(): chunks[chunk] = lax.ppermute(sum_here, axes, way)  15.8 us
    pallas_call x6, Pallas kernels, attend(): pl.pallas_call(kernel, out_shape=out_shape, in_specs=in_specs, out_specs=...  8.83 us
    pallas_call x5, Pallas kernels, apply_expert(): pl.pallas_call(kernel, out_shape=[jax.ShapeDtypeStruct((x.shape[0], featu...  7.73 us
    ppermute x3, starting transfers between devices, shards(): up[kv] = lax.ppermute(up[kv], 'ep', cycle(n_ep))  7.03 us
    ppermute x3, starting transfers between devices, shards(): down[kv] = lax.ppermute(down[kv], 'ep', cycle(n_ep, n_ep - 1))  6.18 us
    ppermute x2, waiting for transfers between devices, shards(): came = [lax.ppermute(x, 'hd', cycle(n_hd)) for x in sent]  5.37 us
    ppermute x14, waiting for transfers between devices, dense_experts(): chunks[chunk] = lax.ppermute(sum_here, axes, way)  5.27 us
    ppermute x4, waiting for transfers between devices, dense_experts(): before[1] = lax.ppermute(before[1], axes, back)  4.63 us
  transfers between devices with their start and end apart: 49, of which 23 were waited for; matrix products, arithmetic and copies ran while one was open for 0% of the time, Pallas kernels for 17%

profile of v11, /device:TPU:0, one launch (start us, length us, event | category | flops | bytes accessed | tf_op | source)
XLA Modules:
  0.0 94.3 jit_solution(10976399830132070331)
XLA Ops:
  0.7 1.9 %pack_keys.1 = (bf16[272,256]{1,0:T(8,128)(2,1)}, bf16[272,256]{1,0:T(8,128)(2,1)}) custom-call(s32[1]{0:T(128)S(6)} %copy.14.page_ref, bf16[128,512]{1,0:T(8,128)(2,1)} %ck_ref.1, bf16[128,512]{1,0:T(8,128)(2,1)} %cv_ref.1, bf16[128,512]{1,0:T(8,128)(2,1)} %nk_ref.1, bf16[128,512]{1,0:T(8,128)(2,1)} %nv_ref.1, s32[8,128]{1,0:T(8,128)} %bitcast.18, ...), custom_call_target="tpu_custom_call" | custom-call | tf_op jit(solution)/shard_map/pack_keys/pallas_call | solution.py:91
  3.0 3.0 %collective-permute-start.7 = (bf16[272,256]{1,0:T(8,128)(2,1)}, bf16[272,256]{1,0:T(8,128)(2,1)S(1)}, u32[]{:S(2)}, u32[]{:S(2)}) collective-permute-start(bf16[272,256]{1,0:T(8,128)(2,1)} %get-tuple-element.98.refs_1_), channel_id=1, source_target_pairs={{0,4},{4,8},{8,12},{12,0},{1,5},{5,9},{9,13},{13,1},{2,6},{6,10},{... | collective-permute-start | bytes 417800 | tf_op jit(solution)/shard_map/ppermute | solution.py:695
  6.1 2.0 %collective-permute-start.8 = (bf16[272,256]{1,0:T(8,128)(2,1)}, bf16[272,256]{1,0:T(8,128)(2,1)S(1)}, u32[]{:S(2)}, u32[]{:S(2)}) collective-permute-start(bf16[272,256]{1,0:T(8,128)(2,1)} %get-tuple-element.98.refs_1_), channel_id=1, source_target_pairs={{0,12},{4,0},{8,4},{12,8},{1,13},{5,1},{9,5},{13,9},{2,14},{6,2},{... | collective-permute-start | bytes 417800 | tf_op jit(solution)/shard_map/ppermute | solution.py:698
  10.2 2.9 %collective-permute-start = (bf16[272,256]{1,0:T(8,128)(2,1)}, bf16[272,256]{1,0:T(8,128)(2,1)S(1)}, u32[]{:S(2)}, u32[]{:S(2)}) collective-permute-start(bf16[272,256]{1,0:T(8,128)(2,1)} %get-tuple-element.86.refs_1_.refs_7_), channel_id=1, source_target_pairs={{0,4},{4,8},{8,12},{12,0},{1,5},{5,9},{9,13},{13,1},{2,6},{6,10},{... | collective-permute-start | bytes 417800 | tf_op jit(solution)/shard_map/ppermute | solution.py:695
  15.0 2.1 %collective-permute-start.1 = (bf16[272,256]{1,0:T(8,128)(2,1)}, bf16[272,256]{1,0:T(8,128)(2,1)S(1)}, u32[]{:S(2)}, u32[]{:S(2)}) collective-permute-start(bf16[272,256]{1,0:T(8,128)(2,1)} %get-tuple-element.86.refs_1_.refs_7_), channel_id=1, source_target_pairs={{0,12},{4,0},{8,4},{12,8},{1,13},{5,1},{9,5},{13,9},{2,14},{6,2},{... | collective-permute-start | bytes 417800 | tf_op jit(solution)/shard_map/ppermute | solution.py:698
  19.5 2.1 %collective-permute-start.10 = (bf16[272,256]{1,0:T(8,128)(2,1)S(1)}, bf16[272,256]{1,0:T(8,128)(2,1)S(1)}, u32[]{:S(2)}, u32[]{:S(2)}) collective-permute-start(bf16[272,256]{1,0:T(8,128)(2,1)S(1)} %collective-permute-done.8.refs_3_), channel_id=1, source_target_pairs={{0,12},{4,0},{8,4},{12,8},{1,13},{5,1},{9,5},{13,9},{2,14},{6,2},{... | collective-permute-start | bytes 417800 | tf_op jit(solution)/shard_map/ppermute | solution.py:698
  23.9 1.8 %attend.9 = (f32[1024,128]{1,0:T(8,128)S(1)}, f32[1024,256]{1,0:T(8,128)S(1)}) custom-call(bf16[128,2048]{1,0:T(8,128)(2,1)S(1)} %choose_queries.1.refs_0_, bf16[272,256]{1,0:T(8,128)(2,1)S(1)} %collective-permute-done.7.refs_1_, bf16[272,256]{1,0:T(8,128)(2,1)S(1)} %collective-permute-done.11.refs_2_, bf16[272,256]{1,0:T(8,128)(2,1)S(1)} %collective-permute-done.8.refs_3_, ...), custom_call_target="tpu_custom_call" | custom-call | flops 805306368 | bytes 4194304 | tf_op jit(solution)/shard_map/attend/pallas_call | solution.py:436
  25.8 1.8 %attend.7 = (f32[1024,128]{1,0:T(8,128)S(1)}, f32[1024,256]{1,0:T(8,128)S(1)}) custom-call(bf16[128,2048]{1,0:T(8,128)(2,1)S(1)} %choose_queries.1.refs_0_, bf16[272,256]{1,0:T(8,128)(2,1)S(1)} %collective-permute-done.refs_1_.refs_8_, bf16[272,256]{1,0:T(8,128)(2,1)S(1)} %collective-permute-done.4.refs_2_, ...), custom_call_target="tpu_custom_call" | custom-call | flops 805306368 | bytes 4194304 | tf_op jit(solution)/shard_map/attend/pallas_call | solution.py:436
  27.6 2.7 %collective-permute-done.3.refs_1_.refs_9_ = bf16[272,256]{1,0:T(8,128)(2,1)S(1)} collective-permute-done((bf16[272,256]{1,0:T(8,128)(2,1)S(1)}, bf16[272,256]{1,0:T(8,128)(2,1)S(1)}, u32[]{:S(2)}, u32[]{:S(2)}) %collective-permute-start.3) | collective-permute-done | bytes 139296 | tf_op jit(solution)/shard_map/ppermute | solution.py:695
  30.3 1.4 %collective-permute-done.6.refs_2_ = bf16[272,256]{1,0:T(8,128)(2,1)S(1)} collective-permute-done((bf16[272,256]{1,0:T(8,128)(2,1)S(1)}, bf16[272,256]{1,0:T(8,128)(2,1)S(1)}, u32[]{:S(2)}, u32[]{:S(2)}) %collective-permute-start.6) | collective-permute-done | bytes 139296 | tf_op jit(solution)/shard_map/ppermute | solution.py:35
  33.3 2.3 %attend.11 = (f32[32,2048]{1,0:T(8,128)S(1)}, f32[32,2048]{1,0:T(8,128)S(1)}, bf16[32,2176]{1,0:T(8,128)(2,1)S(1)}, bf16[32,2048]{1,0:T(8,128)(2,1)S(1)}, bf16[32,128]{1,0:T(8,128)(2,1)S(1)}) custom-call(bf16[128,2048]{1,0:T(8,128)(2,1)S(1)} %choose_queries.1.refs_0_, bf16[272,256]{1,0:T(8,128)(2,1)S(1)} %collective-permute-done.10.refs_1_, ...), custom_call_target="tpu_custom_call" | custom-call | flops 402653184 | bytes 4194304 | tf_op jit(solution)/shard_map/attend/pallas_call | solution.py:436
  35.6 1.5 %collective-permute-start.15 = (bf16[32,2176]{1,0:T(8,128)(2,1)S(1)}, bf16[32,2176]{1,0:T(8,128)(2,1)S(1)}, u32[]{:S(2)}, u32[]{:S(2)}) collective-permute-start(bf16[32,2176]{1,0:T(8,128)(2,1)S(1)} %get-tuple-element.118), channel_id=1, source_target_pairs={{0,2},{2,0},{1,3},{3,1},{4,6},{6,4},{5,7},{7,5},{8,10},{10,8},{9,1... | collective-permute-start | bytes 417800 | tf_op jit(solution)/shard_map/ppermute | solution.py:738
  38.5 3.6 %collective-permute-done.15.refs_1_.came_ref = bf16[32,2176]{1,0:T(8,128)(2,1)S(1)} collective-permute-done((bf16[32,2176]{1,0:T(8,128)(2,1)S(1)}, bf16[32,2176]{1,0:T(8,128)(2,1)S(1)}, u32[]{:S(2)}, u32[]{:S(2)}) %collective-permute-start.15) | collective-permute-done | bytes 139296 | tf_op jit(solution)/shard_map/ppermute | solution.py:738
  42.4 1.8 %collective-permute-done.17.refs_1_ = bf16[32,2048]{1,0:T(8,128)(2,1)S(1)} collective-permute-done((bf16[32,2048]{1,0:T(8,128)(2,1)S(1)}, bf16[32,2048]{1,0:T(8,128)(2,1)S(1)}, u32[]{:S(2)}, u32[]{:S(2)}) %collective-permute-start.17) | collective-permute-done | bytes 131104 | tf_op jit(solution)/shard_map/ppermute | solution.py:738
  46.5 1.6 %collective-permute-done.18.refs_0_ = bf16[32,2048]{1,0:T(8,128)(2,1)S(1)} collective-permute-done((bf16[32,2048]{1,0:T(8,128)(2,1)S(1)}, bf16[32,2048]{1,0:T(8,128)(2,1)S(1)}, u32[]{:S(2)}, u32[]{:S(2)}) %collective-permute-start.18) | collective-permute-done | bytes 131104 | tf_op jit(solution)/shard_map/ppermute | solution.py:535
  48.1 2.0 %collective-permute-done.22.refs_1_ = bf16[32,2048]{1,0:T(8,128)(2,1)S(1)} collective-permute-done((bf16[32,2048]{1,0:T(8,128)(2,1)S(1)}, bf16[32,2048]{1,0:T(8,128)(2,1)S(1)}, u32[]{:S(2)}, u32[]{:S(2)}) %collective-permute-start.22) | collective-permute-done | bytes 131104 | tf_op jit(solution)/shard_map/ppermute | solution.py:536
  50.4 1.4 %collective-permute-start.26 = (bf16[32,2048]{1,0:T(8,128)(2,1)S(1)}, bf16[32,2048]{1,0:T(8,128)(2,1)S(1)}, u32[]{:S(2)}, u32[]{:S(2)}) collective-permute-start(bf16[32,2048]{1,0:T(8,128)(2,1)S(1)} %collective-permute-done.25.refs_2_), channel_id=1, source_target_pairs={{0,5},{1,4},{4,9},{5,8},{8,13},{9,12},{12,15},{13,14},{14,11},{15,... | collective-permute-start | bytes 393224 | tf_op jit(solution)/shard_map/ppermute | solution.py:538
  56.1 1.6 %apply_expert.5 = (f32[32,2048]{1,0:T(8,128)S(1)}, f32[32,2048]{1,0:T(8,128)S(1)}, f32[32,2048]{1,0:T(8,128)S(1)}, f32[32,2048]{1,0:T(8,128)S(1)}) custom-call(bf16[32,2048]{1,0:T(8,128)(2,1)S(1)} %collective-permute-done.18.refs_0_, bf16[32,2048]{1,0:T(8,128)(2,1)S(1)} %collective-permute-done.22.refs_1_, ...), custom_call_target="tpu_custom_call" | custom-call | flops 603979776 | bytes 6291456 | tf_op jit(solution)/shard_map/apply_expert/pallas_call | solution.py:491
  62.0 1.6 %apply_expert.6 = (f32[32,2048]{1,0:T(8,128)S(1)}, f32[32,2048]{1,0:T(8,128)S(1)}, f32[32,2048]{1,0:T(8,128)S(1)}, f32[32,2048]{1,0:T(8,128)S(1)}) custom-call(bf16[32,2048]{1,0:T(8,128)(2,1)S(1)} %collective-permute-done.19.refs_0_, bf16[32,2048]{1,0:T(8,128)(2,1)S(1)} %collective-permute-done.23.refs_1_, ...), custom_call_target="tpu_custom_call" | custom-call | flops 603979776 | bytes 6291456 | tf_op jit(solution)/shard_map/apply_expert/pallas_call | solution.py:491
  64.5 1.6 %apply_expert.7 = (f32[32,2048]{1,0:T(8,128)S(1)}, f32[32,2048]{1,0:T(8,128)S(1)}, f32[32,2048]{1,0:T(8,128)S(1)}, f32[32,2048]{1,0:T(8,128)S(1)}) custom-call(bf16[32,2048]{1,0:T(8,128)(2,1)S(1)} %collective-permute-done.20.refs_0_, bf16[32,2048]{1,0:T(8,128)(2,1)S(1)} %collective-permute-done.24.refs_1_, ...), custom_call_target="tpu_custom_call" | custom-call | flops 603979776 | bytes 6291456 | tf_op jit(solution)/shard_map/apply_expert/pallas_call | solution.py:491
  67.3 1.5 %apply_expert.8 = (bf16[32,2048]{1,0:T(8,128)(2,1)S(1)}, bf16[32,2048]{1,0:T(8,128)(2,1)S(1)}) custom-call(bf16[32,2048]{1,0:T(8,128)(2,1)S(1)} %collective-permute-done.21.refs_0_, bf16[32,2048]{1,0:T(8,128)(2,1)S(1)} %collective-permute-done.33.refs_1_, f32[128,128]{1,0:T(8,128)S(1)} %gates_by_chip.1.refs_4_.refs_2_, bf16[2,192,2048]{2,1,0:T(8,128)(2,1)S(1)} %bitcast.9, ...), custom_call_target="tpu_custom_call" | custom-call | flops 301989888 | bytes 6291456 | tf_op jit(solution)/shard_map/apply_expert/pallas_call | solution.py:491
  68.9 1.7 %collective-permute-start.34 = (bf16[32,2048]{1,0:T(8,128)(2,1)S(1)}, bf16[32,2048]{1,0:T(8,128)(2,1)S(1)}, u32[]{:S(2)}, u32[]{:S(2)}) collective-permute-start(bf16[32,2048]{1,0:T(8,128)(2,1)S(1)} %get-tuple-element.146), channel_id=1, source_target_pairs={{5,0},{4,1},{9,4},{8,5},{13,8},{12,9},{15,12},{14,13},{11,14},{10,... | collective-permute-start | bytes 393224 | tf_op jit(solution)/shard_map/ppermute | solution.py:563
  70.8 1.7 %collective-permute-start.38 = (bf16[32,2048]{1,0:T(8,128)(2,1)S(1)}, bf16[32,2048]{1,0:T(8,128)(2,1)S(1)}, u32[]{:S(2)}, u32[]{:S(2)}) collective-permute-start(bf16[32,2048]{1,0:T(8,128)(2,1)S(1)} %convert_element_type.6), channel_id=1, source_target_pairs={{5,0},{4,1},{9,4},{8,5},{13,8},{12,9},{15,12},{14,13},{11,14},{10,... | collective-permute-start | bytes 393224 | tf_op jit(solution)/shard_map/ppermute | solution.py:563
  72.5 1.9 %collective-permute-done.44.came_ref = bf16[32,2048]{1,0:T(8,128)(2,1)S(1)} collective-permute-done((bf16[32,2048]{1,0:T(8,128)(2,1)S(1)}, bf16[32,2048]{1,0:T(8,128)(2,1)S(1)}, u32[]{:S(2)}, u32[]{:S(2)}) %collective-permute-start.44) | collective-permute-done | bytes 131104 | tf_op jit(solution)/shard_map/ppermute | solution.py:563
  75.1 1.7 %collective-permute-start.35 = (bf16[32,2048]{1,0:T(8,128)(2,1)S(1)}, bf16[32,2048]{1,0:T(8,128)(2,1)S(1)}, u32[]{:S(2)}, u32[]{:S(2)}) collective-permute-start(bf16[32,2048]{1,0:T(8,128)(2,1)S(1)} %add_share.10), channel_id=1, source_target_pairs={{5,0},{4,1},{9,4},{8,5},{13,8},{12,9},{15,12},{14,13},{11,14},{10,... | collective-permute-start | bytes 393224 | tf_op jit(solution)/shard_map/ppermute | solution.py:563
  77.4 1.8 %collective-permute-start.39 = (bf16[32,2048]{1,0:T(8,128)(2,1)S(1)}, bf16[32,2048]{1,0:T(8,128)(2,1)S(1)}, u32[]{:S(2)}, u32[]{:S(2)}) collective-permute-start(bf16[32,2048]{1,0:T(8,128)(2,1)S(1)} %add_share.13), channel_id=1, source_target_pairs={{5,0},{4,1},{9,4},{8,5},{13,8},{12,9},{15,12},{14,13},{11,14},{10,... | collective-permute-start | bytes 393224 | tf_op jit(solution)/shard_map/ppermute | solution.py:563
  79.5 1.6 %collective-permute-start.46 = (bf16[32,2048]{1,0:T(8,128)(2,1)S(1)}, bf16[32,2048]{1,0:T(8,128)(2,1)S(1)}, u32[]{:S(2)}, u32[]{:S(2)}) collective-permute-start(bf16[32,2048]{1,0:T(8,128)(2,1)S(1)} %add_share.18), channel_id=1, source_target_pairs={{0,5},{1,4},{4,9},{5,8},{8,13},{9,12},{12,15},{13,14},{14,11},{15,... | collective-permute-start | bytes 393224 | tf_op jit(solution)/shard_map/ppermute | solution.py:563
  81.2 1.7 %collective-permute-start.36 = (bf16[32,2048]{1,0:T(8,128)(2,1)S(1)}, bf16[32,2048]{1,0:T(8,128)(2,1)S(1)}, u32[]{:S(2)}, u32[]{:S(2)}) collective-permute-start(bf16[32,2048]{1,0:T(8,128)(2,1)S(1)} %add_share.11), channel_id=1, source_target_pairs={{5,0},{4,1},{9,4},{8,5},{13,8},{12,9},{15,12},{14,13},{11,14},{10,... | collective-permute-start | bytes 393224 | tf_op jit(solution)/shard_map/ppermute | solution.py:563
  83.7 1.7 %collective-permute-start.40 = (bf16[32,2048]{1,0:T(8,128)(2,1)S(1)}, bf16[32,2048]{1,0:T(8,128)(2,1)S(1)}, u32[]{:S(2)}, u32[]{:S(2)}) collective-permute-start(bf16[32,2048]{1,0:T(8,128)(2,1)S(1)} %add_share.14), channel_id=1, source_target_pairs={{5,0},{4,1},{9,4},{8,5},{13,8},{12,9},{15,12},{14,13},{11,14},{10,... | collective-permute-start | bytes 393224 | tf_op jit(solution)/shard_map/ppermute | solution.py:563
  86.8 1.4 %collective-permute-start.37 = (bf16[32,2048]{1,0:T(8,128)(2,1)S(1)}, bf16[32,2048]{1,0:T(8,128)(2,1)S(1)}, u32[]{:S(2)}, u32[]{:S(2)}) collective-permute-start(bf16[32,2048]{1,0:T(8,128)(2,1)S(1)} %add_share.12), channel_id=1, source_target_pairs={{5,0},{4,1},{9,4},{8,5},{13,8},{12,9},{15,12},{14,13},{11,14},{10,... | collective-permute-start | bytes 393224 | tf_op jit(solution)/shard_map/ppermute | solution.py:563
  88.1 1.5 %apply_expert.9 = (f32[32,2048]{1,0:T(8,128)S(1)}, f32[32,2048]{1,0:T(8,128)S(1)}) custom-call(bf16[32,2048]{1,0:T(8,128)(2,1)S(1)} %get-tuple-element.149.refs_0_, bf16[32,2048]{1,0:T(8,128)(2,1)S(1)} %get-tuple-element.150.refs_1_, f32[128,128]{1,0:T(8,128)S(1)} %gates_by_chip.1.refs_4_.refs_2_, bf16[2,192,2048]{2,1,0:T(8,128)(2,1)S(1)} %bitcast.10, ...), custom_call_target="tpu_custom_call" | custom-call | flops 301989888 | bytes 6291456 | tf_op jit(solution)/shard_map/apply_expert/pallas_call | solution.py:491
  89.7 1.4 %collective-permute-done.47.refs_7_ = bf16[32,2048]{1,0:T(8,128)(2,1)S(1)} collective-permute-done((bf16[32,2048]{1,0:T(8,128)(2,1)S(1)}, bf16[32,2048]{1,0:T(8,128)(2,1)S(1)}, u32[]{:S(2)}, u32[]{:S(2)}) %collective-permute-start.47) | collective-permute-done | bytes 131104 | tf_op jit(solution)/shard_map/ppermute | solution.py:563
  (116 shorter events, 33.3 us)
Async XLA Ops:
  2.5 30.7 %collective-permute-start.14 = (bf16[2048,1024]{1,0:T(8,128)(2,1)}, bf16[2048,1024]{1,0:T(8,128)(2,1)S(1)}, u32[]{:S(2)}, u32[]{:S(2)}) collective-permute-start(bf16[2048,1024]{1,0:T(8,128)(2,1)} %refs_5_), channel_id=1, source_target_pairs={{0,1},{1,0},{2,3},{3,2},{4,5},{5,4},{6,7},{7,6},{8,9},{9,8},{10,11... | collective-permute-start | bytes 12582920 | tf_op jit(solution)/shard_map/ppermute | solution.py:35
  3.0 7.2 %collective-permute-start.9 = (bf16[272,256]{1,0:T(8,128)(2,1)}, bf16[272,256]{1,0:T(8,128)(2,1)S(1)}, u32[]{:S(2)}, u32[]{:S(2)}) collective-permute-start(bf16[272,256]{1,0:T(8,128)(2,1)} %get-tuple-element.98.refs_1_), channel_id=1, source_target_pairs={{0,1},{1,0},{2,3},{3,2},{4,5},{5,4},{6,7},{7,6},{8,9},{9,8},{10,11... | collective-permute-start | bytes 417800 | tf_op jit(solution)/shard_map/ppermute | solution.py:35
  3.0 11.9 %collective-permute-start.7 = (bf16[272,256]{1,0:T(8,128)(2,1)}, bf16[272,256]{1,0:T(8,128)(2,1)S(1)}, u32[]{:S(2)}, u32[]{:S(2)}) collective-permute-start(bf16[272,256]{1,0:T(8,128)(2,1)} %get-tuple-element.98.refs_1_), channel_id=1, source_target_pairs={{0,4},{4,8},{8,12},{12,0},{1,5},{5,9},{9,13},{13,1},{2,6},{6,10},{... | collective-permute-start | bytes 417800 | tf_op jit(solution)/shard_map/ppermute | solution.py:695
  6.1 11.0 %collective-permute-start.8 = (bf16[272,256]{1,0:T(8,128)(2,1)}, bf16[272,256]{1,0:T(8,128)(2,1)S(1)}, u32[]{:S(2)}, u32[]{:S(2)}) collective-permute-start(bf16[272,256]{1,0:T(8,128)(2,1)} %get-tuple-element.98.refs_1_), channel_id=1, source_target_pairs={{0,12},{4,0},{8,4},{12,8},{1,13},{5,1},{9,5},{13,9},{2,14},{6,2},{... | collective-permute-start | bytes 417800 | tf_op jit(solution)/shard_map/ppermute | solution.py:698
  8.1 9.0 %collective-permute-start.2 = (bf16[272,256]{1,0:T(8,128)(2,1)}, bf16[272,256]{1,0:T(8,128)(2,1)S(1)}, u32[]{:S(2)}, u32[]{:S(2)}) collective-permute-start(bf16[272,256]{1,0:T(8,128)(2,1)} %get-tuple-element.86.refs_1_.refs_7_), channel_id=1, source_target_pairs={{0,1},{1,0},{2,3},{3,2},{4,5},{5,4},{6,7},{7,6},{8,9},{9,8},{10,11... | collective-permute-start | bytes 417800 | tf_op jit(solution)/shard_map/ppermute | solution.py:35
  10.2 9.3 %collective-permute-start = (bf16[272,256]{1,0:T(8,128)(2,1)}, bf16[272,256]{1,0:T(8,128)(2,1)S(1)}, u32[]{:S(2)}, u32[]{:S(2)}) collective-permute-start(bf16[272,256]{1,0:T(8,128)(2,1)} %get-tuple-element.86.refs_1_.refs_7_), channel_id=1, source_target_pairs={{0,4},{4,8},{8,12},{12,0},{1,5},{5,9},{9,13},{13,1},{2,6},{6,10},{... | collective-permute-start | bytes 417800 | tf_op jit(solution)/shard_map/ppermute | solution.py:695
  15.0 7.3 %collective-permute-start.1 = (bf16[272,256]{1,0:T(8,128)(2,1)}, bf16[272,256]{1,0:T(8,128)(2,1)S(1)}, u32[]{:S(2)}, u32[]{:S(2)}) collective-permute-start(bf16[272,256]{1,0:T(8,128)(2,1)} %get-tuple-element.86.refs_1_.refs_7_), channel_id=1, source_target_pairs={{0,12},{4,0},{8,4},{12,8},{1,13},{5,1},{9,5},{13,9},{2,14},{6,2},{... | collective-permute-start | bytes 417800 | tf_op jit(solution)/shard_map/ppermute | solution.py:698
  17.1 5.8 %collective-permute-start.11 = (bf16[272,256]{1,0:T(8,128)(2,1)S(1)}, bf16[272,256]{1,0:T(8,128)(2,1)S(1)}, u32[]{:S(2)}, u32[]{:S(2)}) collective-permute-start(bf16[272,256]{1,0:T(8,128)(2,1)S(1)} %collective-permute-done.7.refs_1_), channel_id=1, source_target_pairs={{0,1},{1,0},{2,3},{3,2},{4,5},{5,4},{6,7},{7,6},{8,9},{9,8},{10,11... | collective-permute-start | bytes 417800 | tf_op jit(solution)/shard_map/ppermute | solution.py:35
  19.5 6.2 %collective-permute-start.10 = (bf16[272,256]{1,0:T(8,128)(2,1)S(1)}, bf16[272,256]{1,0:T(8,128)(2,1)S(1)}, u32[]{:S(2)}, u32[]{:S(2)}) collective-permute-start(bf16[272,256]{1,0:T(8,128)(2,1)S(1)} %collective-permute-done.8.refs_3_), channel_id=1, source_target_pairs={{0,12},{4,0},{8,4},{12,8},{1,13},{5,1},{9,5},{13,9},{2,14},{6,2},{... | collective-permute-start | bytes 417800 | tf_op jit(solution)/shard_map/ppermute | solution.py:698
  22.8 7.4 %collective-permute-start.3 = (bf16[272,256]{1,0:T(8,128)(2,1)S(1)}, bf16[272,256]{1,0:T(8,128)(2,1)S(1)}, u32[]{:S(2)}, u32[]{:S(2)}) collective-permute-start(bf16[272,256]{1,0:T(8,128)(2,1)S(1)} %collective-permute-done.refs_1_.refs_8_), channel_id=1, source_target_pairs={{0,4},{4,8},{8,12},{12,0},{1,5},{5,9},{9,13},{13,1},{2,6},{6,10},{... | collective-permute-start | bytes 417800 | tf_op jit(solution)/shard_map/ppermute | solution.py:695
  31.7 24.5 %collective-permute-start.28 = (bf16[2,192,2048]{2,1,0:T(8,128)(2,1)S(1)}, bf16[2,192,2048]{2,1,0:T(8,128)(2,1)S(1)}, u32[]{:S(2)}, u32[]{:S(2)}) collective-permute-start(bf16[2,192,2048]{2,1,0:T(8,128)(2,1)S(1)} %bitcast.5), channel_id=1, source_target_pairs={{0,1},{1,0},{2,3},{3,2},{4,5},{5,4},{6,7},{7,6},{8,9},{9,8},{10,11... | collective-permute-start | bytes 4718600 | tf_op jit(solution)/shard_map/ppermute | solution.py:35
  31.8 14.3 %collective-permute-start.29 = (bf16[192,2048]{1,0:T(8,128)(2,1)S(1)}, bf16[192,2048]{1,0:T(8,128)(2,1)S(1)}, u32[]{:S(2)}, u32[]{:S(2)}) collective-permute-start(bf16[192,2048]{1,0:T(8,128)(2,1)S(1)} %bitcast.11), channel_id=1, source_target_pairs={{0,1},{1,0},{2,3},{3,2},{4,5},{5,4},{6,7},{7,6},{8,9},{9,8},{10,11... | collective-permute-start | bytes 2359304 | tf_op jit(solution)/shard_map/ppermute | solution.py:35
  35.6 6.6 %collective-permute-start.15 = (bf16[32,2176]{1,0:T(8,128)(2,1)S(1)}, bf16[32,2176]{1,0:T(8,128)(2,1)S(1)}, u32[]{:S(2)}, u32[]{:S(2)}) collective-permute-start(bf16[32,2176]{1,0:T(8,128)(2,1)S(1)} %get-tuple-element.118), channel_id=1, source_target_pairs={{0,2},{2,0},{1,3},{3,1},{4,6},{6,4},{5,7},{7,5},{8,10},{10,8},{9,1... | collective-permute-start | bytes 417800 | tf_op jit(solution)/shard_map/ppermute | solution.py:738
  37.2 6.9 %collective-permute-start.17 = (bf16[32,2048]{1,0:T(8,128)(2,1)S(1)}, bf16[32,2048]{1,0:T(8,128)(2,1)S(1)}, u32[]{:S(2)}, u32[]{:S(2)}) collective-permute-start(bf16[32,2048]{1,0:T(8,128)(2,1)S(1)} %get-tuple-element.124), channel_id=1, source_target_pairs={{0,2},{2,0},{1,3},{3,1},{4,6},{6,4},{5,7},{7,5},{8,10},{10,8},{9,1... | collective-permute-start | bytes 393224 | tf_op jit(solution)/shard_map/ppermute | solution.py:738
  42.3 5.8 %collective-permute-start.18 = (bf16[32,2048]{1,0:T(8,128)(2,1)S(1)}, bf16[32,2048]{1,0:T(8,128)(2,1)S(1)}, u32[]{:S(2)}, u32[]{:S(2)}) collective-permute-start(bf16[32,2048]{1,0:T(8,128)(2,1)S(1)} %get-tuple-element.149.refs_0_), channel_id=1, source_target_pairs={{0,5},{1,4},{4,9},{5,8},{8,13},{9,12},{12,15},{13,14},{14,11},{15,... | collective-permute-start | bytes 393224 | tf_op jit(solution)/shard_map/ppermute | solution.py:535
  44.3 5.8 %collective-permute-start.22 = (bf16[32,2048]{1,0:T(8,128)(2,1)S(1)}, bf16[32,2048]{1,0:T(8,128)(2,1)S(1)}, u32[]{:S(2)}, u32[]{:S(2)}) collective-permute-start(bf16[32,2048]{1,0:T(8,128)(2,1)S(1)} %get-tuple-element.150.refs_1_), channel_id=1, source_target_pairs={{5,0},{4,1},{9,4},{8,5},{13,8},{12,9},{15,12},{14,13},{11,14},{10,... | collective-permute-start | bytes 393224 | tf_op jit(solution)/shard_map/ppermute | solution.py:536
  46.1 6.4 %collective-permute-start.27 = (bf16[32,2048]{1,0:T(8,128)(2,1)S(1)}, bf16[32,2048]{1,0:T(8,128)(2,1)S(1)}, u32[]{:S(2)}, u32[]{:S(2)}) collective-permute-start(bf16[32,2048]{1,0:T(8,128)(2,1)S(1)} %get-tuple-element.149.refs_0_), channel_id=1, source_target_pairs={{5,0},{4,1},{9,4},{8,5},{13,8},{12,9},{15,12},{14,13},{11,14},{10,... | collective-permute-start | bytes 393224 | tf_op jit(solution)/shard_map/ppermute | solution.py:539
  50.4 7.3 %collective-permute-start.26 = (bf16[32,2048]{1,0:T(8,128)(2,1)S(1)}, bf16[32,2048]{1,0:T(8,128)(2,1)S(1)}, u32[]{:S(2)}, u32[]{:S(2)}) collective-permute-start(bf16[32,2048]{1,0:T(8,128)(2,1)S(1)} %collective-permute-done.25.refs_2_), channel_id=1, source_target_pairs={{0,5},{1,4},{4,9},{5,8},{8,13},{9,12},{12,15},{13,14},{14,11},{15,... | collective-permute-start | bytes 393224 | tf_op jit(solution)/shard_map/ppermute | solution.py:538
  52.5 6.4 %collective-permute-start.31 = (bf16[32,2048]{1,0:T(8,128)(2,1)S(1)}, bf16[32,2048]{1,0:T(8,128)(2,1)S(1)}, u32[]{:S(2)}, u32[]{:S(2)}) collective-permute-start(bf16[32,2048]{1,0:T(8,128)(2,1)S(1)} %collective-permute-done.27.refs_3_), channel_id=1, source_target_pairs={{5,0},{4,1},{9,4},{8,5},{13,8},{12,9},{15,12},{14,13},{11,14},{10,... | collective-permute-start | bytes 393224 | tf_op jit(solution)/shard_map/ppermute | solution.py:539
  53.6 5.9 %collective-permute-start.20 = (bf16[32,2048]{1,0:T(8,128)(2,1)S(1)}, bf16[32,2048]{1,0:T(8,128)(2,1)S(1)}, u32[]{:S(2)}, u32[]{:S(2)}) collective-permute-start(bf16[32,2048]{1,0:T(8,128)(2,1)S(1)} %collective-permute-done.19.refs_0_), channel_id=1, source_target_pairs={{0,5},{1,4},{4,9},{5,8},{8,13},{9,12},{12,15},{13,14},{14,11},{15,... | collective-permute-start | bytes 393224 | tf_op jit(solution)/shard_map/ppermute | solution.py:535
  57.7 5.8 %collective-permute-start.30 = (bf16[32,2048]{1,0:T(8,128)(2,1)S(1)}, bf16[32,2048]{1,0:T(8,128)(2,1)S(1)}, u32[]{:S(2)}, u32[]{:S(2)}) collective-permute-start(bf16[32,2048]{1,0:T(8,128)(2,1)S(1)} %collective-permute-done.26.refs_2_), channel_id=1, source_target_pairs={{0,5},{1,4},{4,9},{5,8},{8,13},{9,12},{12,15},{13,14},{14,11},{15,... | collective-permute-start | bytes 393224 | tf_op jit(solution)/shard_map/ppermute | solution.py:538
  58.9 5.7 %collective-permute-start.32 = (bf16[32,2048]{1,0:T(8,128)(2,1)S(1)}, bf16[32,2048]{1,0:T(8,128)(2,1)S(1)}, u32[]{:S(2)}, u32[]{:S(2)}) collective-permute-start(bf16[32,2048]{1,0:T(8,128)(2,1)S(1)} %collective-permute-done.31.refs_3_), channel_id=1, source_target_pairs={{5,0},{4,1},{9,4},{8,5},{13,8},{12,9},{15,12},{14,13},{11,14},{10,... | collective-permute-start | bytes 393224 | tf_op jit(solution)/shard_map/ppermute | solution.py:539
  59.5 6.6 %collective-permute-start.21 = (bf16[32,2048]{1,0:T(8,128)(2,1)S(1)}, bf16[32,2048]{1,0:T(8,128)(2,1)S(1)}, u32[]{:S(2)}, u32[]{:S(2)}) collective-permute-start(bf16[32,2048]{1,0:T(8,128)(2,1)S(1)} %collective-permute-done.20.refs_0_), channel_id=1, source_target_pairs={{0,5},{1,4},{4,9},{5,8},{8,13},{9,12},{12,15},{13,14},{14,11},{15,... | collective-permute-start | bytes 393224 | tf_op jit(solution)/shard_map/ppermute | solution.py:535
  61.0 6.4 %collective-permute-start.33 = (bf16[32,2048]{1,0:T(8,128)(2,1)S(1)}, bf16[32,2048]{1,0:T(8,128)(2,1)S(1)}, u32[]{:S(2)}, u32[]{:S(2)}) collective-permute-start(bf16[32,2048]{1,0:T(8,128)(2,1)S(1)} %collective-permute-done.24.refs_1_), channel_id=1, source_target_pairs={{5,0},{4,1},{9,4},{8,5},{13,8},{12,9},{15,12},{14,13},{11,14},{10,... | collective-permute-start | bytes 393224 | tf_op jit(solution)/shard_map/ppermute | solution.py:536
  68.9 6.1 %collective-permute-start.34 = (bf16[32,2048]{1,0:T(8,128)(2,1)S(1)}, bf16[32,2048]{1,0:T(8,128)(2,1)S(1)}, u32[]{:S(2)}, u32[]{:S(2)}) collective-permute-start(bf16[32,2048]{1,0:T(8,128)(2,1)S(1)} %get-tuple-element.146), channel_id=1, source_target_pairs={{5,0},{4,1},{9,4},{8,5},{13,8},{12,9},{15,12},{14,13},{11,14},{10,... | collective-permute-start | bytes 393224 | tf_op jit(solution)/shard_map/ppermute | solution.py:563
  70.7 6.5 %collective-permute-start.41 = (bf16[32,2048]{1,0:T(8,128)(2,1)S(1)}, bf16[32,2048]{1,0:T(8,128)(2,1)S(1)}, u32[]{:S(2)}, u32[]{:S(2)}) collective-permute-start(bf16[32,2048]{1,0:T(8,128)(2,1)S(1)} %convert_element_type.7), channel_id=1, source_target_pairs={{0,5},{1,4},{4,9},{5,8},{8,13},{9,12},{12,15},{13,14},{14,11},{15,... | collective-permute-start | bytes 393224 | tf_op jit(solution)/shard_map/ppermute | solution.py:563
  70.8 6.5 %collective-permute-start.38 = (bf16[32,2048]{1,0:T(8,128)(2,1)S(1)}, bf16[32,2048]{1,0:T(8,128)(2,1)S(1)}, u32[]{:S(2)}, u32[]{:S(2)}) collective-permute-start(bf16[32,2048]{1,0:T(8,128)(2,1)S(1)} %convert_element_type.6), channel_id=1, source_target_pairs={{5,0},{4,1},{9,4},{8,5},{13,8},{12,9},{15,12},{14,13},{11,14},{10,... | collective-permute-start | bytes 393224 | tf_op jit(solution)/shard_map/ppermute | solution.py:563
  75.1 6.1 %collective-permute-start.35 = (bf16[32,2048]{1,0:T(8,128)(2,1)S(1)}, bf16[32,2048]{1,0:T(8,128)(2,1)S(1)}, u32[]{:S(2)}, u32[]{:S(2)}) collective-permute-start(bf16[32,2048]{1,0:T(8,128)(2,1)S(1)} %add_share.10), channel_id=1, source_target_pairs={{5,0},{4,1},{9,4},{8,5},{13,8},{12,9},{15,12},{14,13},{11,14},{10,... | collective-permute-start | bytes 393224 | tf_op jit(solution)/shard_map/ppermute | solution.py:563
  77.4 6.3 %collective-permute-start.39 = (bf16[32,2048]{1,0:T(8,128)(2,1)S(1)}, bf16[32,2048]{1,0:T(8,128)(2,1)S(1)}, u32[]{:S(2)}, u32[]{:S(2)}) collective-permute-start(bf16[32,2048]{1,0:T(8,128)(2,1)S(1)} %add_share.13), channel_id=1, source_target_pairs={{5,0},{4,1},{9,4},{8,5},{13,8},{12,9},{15,12},{14,13},{11,14},{10,... | collective-permute-start | bytes 393224 | tf_op jit(solution)/shard_map/ppermute | solution.py:563
  79.5 5.9 %collective-permute-start.46 = (bf16[32,2048]{1,0:T(8,128)(2,1)S(1)}, bf16[32,2048]{1,0:T(8,128)(2,1)S(1)}, u32[]{:S(2)}, u32[]{:S(2)}) collective-permute-start(bf16[32,2048]{1,0:T(8,128)(2,1)S(1)} %add_share.18), channel_id=1, source_target_pairs={{0,5},{1,4},{4,9},{5,8},{8,13},{9,12},{12,15},{13,14},{14,11},{15,... | collective-permute-start | bytes 393224 | tf_op jit(solution)/shard_map/ppermute | solution.py:563
  82.9 6.8 %collective-permute-start.43 = (bf16[32,2048]{1,0:T(8,128)(2,1)S(1)}, bf16[32,2048]{1,0:T(8,128)(2,1)S(1)}, u32[]{:S(2)}, u32[]{:S(2)}) collective-permute-start(bf16[32,2048]{1,0:T(8,128)(2,1)S(1)} %add_share.16), channel_id=1, source_target_pairs={{0,5},{1,4},{4,9},{5,8},{8,13},{9,12},{12,15},{13,14},{14,11},{15,... | collective-permute-start | bytes 393224 | tf_op jit(solution)/shard_map/ppermute | solution.py:563
  83.7 6.0 %collective-permute-start.40 = (bf16[32,2048]{1,0:T(8,128)(2,1)S(1)}, bf16[32,2048]{1,0:T(8,128)(2,1)S(1)}, u32[]{:S(2)}, u32[]{:S(2)}) collective-permute-start(bf16[32,2048]{1,0:T(8,128)(2,1)S(1)} %add_share.14), channel_id=1, source_target_pairs={{5,0},{4,1},{9,4},{8,5},{13,8},{12,9},{15,12},{14,13},{11,14},{10,... | collective-permute-start | bytes 393224 | tf_op jit(solution)/shard_map/ppermute | solution.py:563
  (26 other events, 153.7 us)
